TPU v7x, 32 devices: a whole 2x2x4 slice. The times are simulated.
32 devices in a mesh: blk: 16 (over z, y, core), wa: 2 (over x).
Axes of the slice: x: 2, y: 2, z: 4, core: 2. Of those that a mesh axis runs over, the one named last changes fastest.
Arguments:
- features: bfloat16 [53248, 2048], P(('blk', 'wa')), may hold values from -6 to 6
- weight: bfloat16 [2048, 2048], P(('blk', 'wa')), may hold values from -0.375 to 0.375
- bias: bfloat16 [2048], P(('blk', 'wa')), may hold values from -3 to 3
- neighbours: int32 [16, 53248], P(None, ('blk', 'wa')), may hold values from 0 to 3199, as said below
- degrees: int32 [53248], P(('blk', 'wa')), may hold values from 4 to 16
- cluster_sizes: int32 [16], P('blk'), may hold values from 603 to 3016
- cotangent: bfloat16 [53248, 2048], P(('blk', 'wa')), may hold values from -6 to 6
Outputs:
- output: float32 [53248, 2048], P(('blk', 'wa'))
- grad_features: float32 [53248, 2048], P(('blk', 'wa'))
- grad_weight: float32 [2048, 2048], P(('blk', 'wa'))
- grad_bias: float32 [2048], P(('blk', 'wa'))
Inputs may be any that keep to these rules, and one draw needn't show every extreme that they name: `neighbours`: an entry below 1664 names a live row of the same part; larger entries name leading rows of the cluster itself and of the two clusters beside it on the cycle. Slots past a node's degree hold entries of the same law.
All inputs are finite; a program needn't handle non-finite values.
Results may differ from a plain program's by a relative error of at most 0.0049.
Values may be sent and summed in bfloat16 or wider, within the bound.
No kernel may reach another device: no remote copies, remote signals or barrier semaphores. Data moves between devices by JAX's collectives and lax.ppermute only.
A program may use at most 192 MiB of HBM per device.

v0:
```python
import jax
import jax.numpy as jnp
from jax import lax
from jax.sharding import PartitionSpec as P

FANOUT = 16
BOUND = 256


def shifted(shard, axis, by):
    count = lax.axis_size(axis)
    return lax.ppermute(shard, axis, [(i, (i + by) % count) for i in range(count)])


def smooth(value):
    return jax.nn.gelu(value, approximate=True)


def body(features, weight, bias, neighbours, degrees, cluster_sizes, cotangent):
    node_count = features.shape[0]
    halves = lax.axis_size("wa")
    wa_index = lax.axis_index("wa")
    matrix, offset = (
        lax.all_gather(weight, ("blk", "wa"), axis=0, tiled=True),
        lax.all_gather(bias, ("blk", "wa"), axis=0, tiled=True),
    )
    node_ids = jnp.arange(node_count, dtype=jnp.int32)
    live_mask = (halves * node_ids + wa_index < cluster_sizes[0]).astype(jnp.float32)[:, None]
    edge_rows = features[:BOUND]
    own_pair = lax.all_gather(edge_rows, "wa", axis=0, tiled=True)
    prev_pair = shifted(own_pair, "blk", 1)
    next_pair = shifted(own_pair, "blk", -1)
    table = jnp.concatenate([features, own_pair, prev_pair, next_pair], axis=0)
    table_rows = table.shape[0]
    in_range = jnp.arange(FANOUT, dtype=jnp.int32)[:, None] < degrees[None, :]
    inverse = (1.0 / (degrees.astype(jnp.float32) + 1.0))[:, None]
    row_ids = jnp.arange(table_rows, dtype=jnp.int32)[None, :]
    counts = jnp.zeros((node_count, table_rows), jnp.float32)
    for column in range(FANOUT):
        hits = (neighbours[column][:, None] == row_ids) & in_range[column][:, None]
        counts = counts + hits.astype(jnp.float32)
    adjacency = counts.astype(jnp.bfloat16)
    gathered_sum = jnp.dot(adjacency, table, preferred_element_type=jnp.float32)
    summed = 2.0 * features.astype(jnp.float32) + gathered_sum
    blended = (summed * inverse).astype(jnp.bfloat16)
    product = (
        jnp.dot(blended, matrix, preferred_element_type=jnp.float32)
        + offset.astype(jnp.float32)[None, :]
    )
    activated, smooth_back = jax.vjp(smooth, product)
    output = live_mask * activated
    (grad_product,) = smooth_back(live_mask * cotangent.astype(jnp.float32))
    grad_low = grad_product.astype(jnp.bfloat16)
    bias_part = jnp.sum(grad_product, axis=0)
    weight_part = lax.dot_general(
        blended, grad_low, (((0,), (0,)), ((), ())), preferred_element_type=jnp.float32
    )
    grad_blended = lax.dot_general(
        grad_low, matrix, (((1,), (1,)), ((), ())), preferred_element_type=jnp.float32
    )
    grad_scaled = grad_blended * inverse
    collected = lax.dot_general(
        counts,
        grad_scaled,
        (((0,), (0,)), ((), ())),
        precision=lax.Precision.HIGHEST,
        preferred_element_type=jnp.float32,
    )
    pair_rows = halves * BOUND
    own_part = collected[node_count : node_count + pair_rows]
    prev_part = collected[node_count + pair_rows : node_count + 2 * pair_rows]
    next_part = collected[node_count + 2 * pair_rows :]
    from_after = shifted(prev_part, "blk", -1)
    from_before = shifted(next_part, "blk", 1)
    returned = lax.psum_scatter(
        own_part + from_after + from_before, "wa", scatter_dimension=0, tiled=True
    )
    grad_features = 2.0 * grad_scaled + collected[:node_count]
    grad_features = grad_features.at[:BOUND].add(returned)
    grad_weight, grad_bias = (
        lax.psum_scatter(weight_part, ("blk", "wa"), scatter_dimension=0, tiled=True),
        lax.psum_scatter(bias_part, ("blk", "wa"), scatter_dimension=0, tiled=True),
    )
    return (output, grad_features, grad_weight, grad_bias)


def solution(mesh):
    return jax.shard_map(
        body,
        mesh=mesh,
        in_specs=(
            P(("blk", "wa"), None),
            P(("blk", "wa"), None),
            P(("blk", "wa")),
            P(None, ("blk", "wa")),
            P(("blk", "wa")),
            P("blk"),
            P(("blk", "wa"), None),
        ),
        out_specs=(
            P(("blk", "wa"), None),
            P(("blk", "wa"), None),
            P(("blk", "wa"), None),
            P(("blk", "wa")),
        ),
        check_vma=False,
    )
```

profile of v0, /device:TPU:11, one launch (start us, length us, event | category | flops | bytes accessed | tf_op | source)
XLA Modules:
  0.0 1224.0 jit_solution(16427721719088083397)
XLA Ops:
  7.2 2.3 slice.162
  9.5 0.0 all-gather.5.cloned.1.call-start
  9.6 0.7 all-gather.5.cloned.1.call-update
  10.3 33.2 %all-gather.3.cloned.1.call-done = bf16[512,2048]{1,0:T(8,128)(2,1)} async-done(((bf16[256,2048]{1,0:T(8,128)(2,1)}), bf16[512,2048]{1,0:T(8,128)(2,1)}) %all-gather.3.cloned.1.call-update) | async-done | bytes 2097168 | tf_op jit(solution)/shard_map/all_gather | solution.py:30
  43.5 0.7 collective-permute-start.1
  44.2 1.1 collective-permute-start
  45.9 0.9 dynamic-update-slice.3
  46.8 84.7 %all-reduce = bf16[2048]{0:T(1024)(128)(2,1)S(1)} all-reduce(bf16[2048]{0:T(1024)(128)(2,1)S(1)} %dynamic-update-slice.3), channel_id=1, replica_groups=mesh['blk'=16,'wa'=2] {'blk','wa'}, use_global_device_ids=true, to_apply=%add | all-reduce | flops 2048 | bytes 8192
  131.4 0.7 iota_compare_fusion.16
  132.2 0.3 slice_reduce_fusion.15
  132.5 1.8 slice_reduce_fusion.31
  134.3 0.7 add_divide_fusion
  135.0 24.0 %fusion.64 = bf16[3200,2048]{1,0:T(8,128)(2,1)} fusion(bf16[512,2048]{1,0:T(8,128)(2,1)S(1)} %collective-permute-done.1, bf16[512,2048]{1,0:T(8,128)(2,1)} %collective-permute-done, bf16[512,2048]{1,0:T(8,128)(2,1)} %all-gather.3.cloned.1.call-done, bf16[1664,2048]{1,0:T(8,128)(2,1)} %param.9), kind=kLoop, calls=%fused_computation.45.clone.clone.clone.2 | loop fusion | flops 52428800 | bytes 26214400 | tf_op jit(solution)/shard_map/dot_general | solution.py:43
  159.0 102.4 %multiply_convert_fusion = bf16[1664,2048]{1,0:T(8,128)(2,1)} fusion(bf16[1664,2048]{1,0:T(8,128)(2,1)} %param.9, f32[1664]{0:T(1024)S(1)} %add_divide_fusion, s32[1664]{0:T(1024)S(1)} %get-tuple-element.30, s32[1664]{0:T(1024)S(1)} %get-tuple-element.31, s32[1664]{0:T(1024)S(1)} %get-tuple-element.17, s32[1664]{0:T(1024)S(1)} %get-tuple-element.18, ...), kind=kOutput, calls=%fused_computation.43 | convolution fusion | flops 22168207360 | bytes 26878464 | tf_op jit(solution)/shard_map/dot_general | solution.py:43
  261.5 31.6 %fusion.46 = (f32[2048]{0:T(1024)}, bf16[1664,2048]{1,0:T(8,128)(2,1)S(1)}, f32[1664,2048]{1,0:T(8,128)}) fusion(f32[2048]{0:T(1024)S(1)} %convert_element_type.97, bf16[1664,2048]{1,0:T(8,128)(2,1)} %param.15, f32[1664]{0:T(1024)S(1)} %fusion.44, bf16[1664,2048]{1,0:T(8,128)(2,1)} %multiply_convert_fusion, bf16[2048,2048]{1,0:T(8,128)(2,1)} %all-gather.5.cloned.1.call-done), kind=kOutput, calls=%fused_computation.101 | convolution fusion | flops 14047246336 | bytes 42490368 | tf_op jit(solution)/shard_map/dot_general | solution.py:47
  293.1 2.7 copy-done.2
  295.8 17.9 %fusion.41 = f32[1664,2048]{1,0:T(8,128)} fusion(bf16[2048,2048]{1,0:T(8,128)(2,1)S(1)} %copy-done.1, bf16[1664,2048]{1,0:T(8,128)(2,1)S(1)} %get-tuple-element.49), kind=kOutput, calls=%fused_computation.60 | convolution fusion | flops 13958643712 | bytes 28835840 | tf_op jit(solution)/shard_map/dot_general | solution.py:58
  313.7 10.6 fusion.66
  324.3 370.7 %fusion.30 = f32[3200,2048]{1,0:T(8,128)} fusion(s32[1664]{0:T(1024)S(1)} %get-tuple-element.30, s32[1664]{0:T(1024)S(1)} %get-tuple-element.31, s32[1664]{0:T(1024)S(1)} %get-tuple-element.17, s32[1664]{0:T(1024)S(1)} %get-tuple-element.18, s32[1664]{0:T(1024)S(1)} %get-tuple-element.19, s32[1664]{0:T(1024)S(1)} %get-tuple-element.20, ...), kind=kOutput, calls=%fused_computation.52 | convolution fusion | flops 131197747200 | bytes 39979008 | tf_op jit(solution)/shard_map/dot_general | solution.py:62
  695.0 4.1 fusion.48
  699.0 2.4 collective-permute-start.2
  701.4 0.3 collective-permute-start.3
  701.7 91.1 %collective-permute-done.2 = f32[512,2048]{1,0:T(8,128)S(1)} collective-permute-done((f32[512,2048]{1,0:T(8,128)S(1)}, f32[512,2048]{1,0:T(8,128)S(1)}, u32[]{:S(2)}, u32[]{:S(2)}) %collective-permute-start.2) | collective-permute-done | bytes 4194336 | tf_op jit(solution)/shard_map/ppermute | solution.py:12
  792.8 5.6 fusion.38
  798.4 0.0 reduce-scatter.5.cloned.1.call-start
  798.5 21.6 %fusion.39 = f32[2048,2048]{1,0:T(8,128)} fusion(bf16[1664,2048]{1,0:T(8,128)(2,1)} %multiply_convert_fusion, bf16[1664,2048]{1,0:T(8,128)(2,1)} %copy-done.2), kind=kOutput, calls=%fused_computation.58 | convolution fusion | flops 13958643712 | bytes 30408704 | tf_op jit(solution)/shard_map/dot_general | solution.py:55
  820.1 0.7 copy-done
  820.8 40.1 %all-reduce.1 = f32[2048]{0:T(1024)S(1)} all-reduce(f32[2048]{0:T(1024)S(1)} %copy-done), channel_id=4, replica_groups=mesh['blk'=16,'wa'=2] {'blk','wa'}, use_global_device_ids=true, to_apply=%region_3.0.clone | all-reduce | flops 2048 | bytes 16384
  860.9 0.6 dynamic-slice.8
  861.4 15.2 %slice_add_fusion = f32[1664,2048]{1,0:T(8,128)} fusion(f32[3200,2048]{1,0:T(8,128)} %fusion.30, f32[1664,2048]{1,0:T(8,128)} %fusion.41, f32[1664]{0:T(1024)S(1)} %add_divide_fusion), kind=kLoop, calls=%fused_computation.41 | loop fusion | flops 10223616 | bytes 40901120 | tf_op jit(solution)/shard_map/add | solution.py:78
  876.6 3.9 fusion.43
  880.5 336.5 %reduce-scatter.5.cloned.1.call-done = f32[64,2048]{1,0:T(8,128)} async-done(((f32[2048,2048]{1,0:T(8,128)}), f32[64,2048]{1,0:T(8,128)}) %reduce-scatter.5.cloned.1.call-update) | async-done | bytes 524304 | tf_op jit(solution)/shard_map/reduce_scatter | solution.py:81
  (17 shorter events, 0.2 us)
Async XLA Ops:
  7.2 36.3 %all-gather.3.cloned.1.call-start = ((), (), s32[]{:S(2)}) async-start(), calls=%async_computation.2 | async-start | bytes 3145728 | tf_op jit(solution)/shard_map/all_gather | solution.py:30
  9.5 251.9 %all-gather.5.cloned.1.call-start = ((), (), s32[]{:S(2)}) async-start(), calls=%async_computation.3 | async-start | bytes 8650752 | tf_op jit(solution)/shard_map/all_gather | solution.py:24
  10.3 866.3 %reduce-scatter.3.cloned.1.call-start = ((), (), s32[]{:S(2)}) async-start(), calls=%async_computation.4 | async-start | bytes 6291456 | tf_op jit(solution)/shard_map/reduce_scatter | solution.py:75
  43.5 91.5 %collective-permute-start.1 = (bf16[512,2048]{1,0:T(8,128)(2,1)}, bf16[512,2048]{1,0:T(8,128)(2,1)S(1)}, u32[]{:S(2)}, u32[]{:S(2)}) collective-permute-start(bf16[512,2048]{1,0:T(8,128)(2,1)} %all-gather.3.cloned.1.call-done), channel_id=1, source_target_pairs={{0,30},{2,0},{4,2},{6,4},{8,6},{10,8},{12,10},{14,12},{16,14},{18,... | collective-permute-start | bytes 6291464 | tf_op jit(solution)/shard_map/ppermute | solution.py:12
  44.2 90.8 %collective-permute-start = (bf16[512,2048]{1,0:T(8,128)(2,1)}, bf16[512,2048]{1,0:T(8,128)(2,1)}, u32[]{:S(2)}, u32[]{:S(2)}) collective-permute-start(bf16[512,2048]{1,0:T(8,128)(2,1)} %all-gather.3.cloned.1.call-done), channel_id=1, source_target_pairs={{0,2},{2,4},{4,6},{6,8},{8,10},{10,12},{12,14},{14,16},{16,18},{18... | collective-permute-start | bytes 6291464 | tf_op jit(solution)/shard_map/ppermute | solution.py:12
  261.4 34.4 %copy-start.1 = (bf16[2048,2048]{1,0:T(8,128)(2,1)S(1)}, bf16[2048,2048]{1,0:T(8,128)(2,1)}, u32[]{:S(2)}) copy-start(bf16[2048,2048]{1,0:T(8,128)(2,1)} %all-gather.5.cloned.1.call-done) | copy-start | bytes 25165828
  293.1 2.7 copy-start.2
  699.0 93.7 %collective-permute-start.2 = (f32[512,2048]{1,0:T(8,128)S(1)}, f32[512,2048]{1,0:T(8,128)S(1)}, u32[]{:S(2)}, u32[]{:S(2)}) collective-permute-start(f32[512,2048]{1,0:T(8,128)S(1)} %get-tuple-element.50), channel_id=1, source_target_pairs={{0,30},{2,0},{4,2},{6,4},{8,6},{10,8},{12,10},{14,12},{16,14},{18,... | collective-permute-start | bytes 12582920 | tf_op jit(solution)/shard_map/ppermute | solution.py:12
  701.4 91.4 %collective-permute-start.3 = (f32[512,2048]{1,0:T(8,128)S(1)}, f32[512,2048]{1,0:T(8,128)S(1)}, u32[]{:S(2)}, u32[]{:S(2)}) collective-permute-start(f32[512,2048]{1,0:T(8,128)S(1)} %get-tuple-element.51), channel_id=1, source_target_pairs={{0,2},{2,4},{4,6},{6,8},{8,10},{10,12},{12,14},{14,16},{16,18},{18... | collective-permute-start | bytes 12582920 | tf_op jit(solution)/shard_map/ppermute | solution.py:12
  798.4 418.6 %reduce-scatter.5.cloned.1.call-start = ((), (), s32[]{:S(2)}) async-start(), calls=%async_computation.5 | async-start | bytes 17301504 | tf_op jit(solution)/shard_map/reduce_scatter | solution.py:81
  820.1 0.7 copy-start
Sparse Core Ops, SparseCore 0:
  10.1 33.3 all-gather.2
  46.5 89.3 all-gather.4
  798.5 54.8 reduce-scatter.2
  856.2 360.7 reduce-scatter.4
where the time goes:
time: 1230 us; the launch traced here: 1220 us
  matrix products  544 us (44%)
  waiting for transfers between devices  462 us (38%)
  blocking collectives  125 us (10%)
  other arithmetic  60.7 us (5%)
  between operations  14.9 us (1%)
  local copies, waits for them, and re-layouts  13.3 us (1%)
    dot_general x1, matrix products, body(): lax.dot_general(counts, grad_scaled, (((0,), (0,)), ((), ())), precision=...  371 us
    reduce_scatter x1, waiting for transfers between devices, body(): lax.psum_scatter(weight_part, ('blk', 'wa'), scatter_dimension=0, tiled=T...  337 us
    unnamed x2, blocking collectives  125 us
    dot_general x1, matrix products, body(): gathered_sum = jnp.dot(adjacency, table, preferred_element_type=jnp.float32)  102 us
    ppermute x4, waiting for transfers between devices, shifted(): lax.ppermute(shard, axis, [(i, (i + by) % count) for i in range(count)])  91.1 us
    all_gather x1, waiting for transfers between devices, body(): own_pair = lax.all_gather(edge_rows, 'wa', axis=0, tiled=True)  33.2 us
    dot_general x1, matrix products, body(): jnp.dot(blended, matrix, preferred_element_type=jnp.float32)  31.6 us
  transfers between devices with their start and end apart: 8, of which 3 were waited for; matrix products, arithmetic and copies ran while one was open for 14% of the time, Pallas kernels for 0%

commit v1 on v0

v1 whole, which is shorter than its diff:
```python
import functools
import math

import jax
import jax.numpy as jnp
from jax import lax
from jax.experimental import pallas as pl
from jax.experimental.pallas import tpu as pltpu
from jax.sharding import PartitionSpec as P

FANOUT = 16
BOUND = 256
CMAX = 3016
TILE = 256
F32 = jnp.float32
BF16 = jnp.bfloat16
VMEM = 60 * 1024 * 1024
GELU_A = math.sqrt(2 / math.pi)
GELU_B = 0.044715


def params():
    return pltpu.CompilerParams(vmem_limit_bytes=VMEM)


def cost(flops, nbytes):
    return pl.CostEstimate(flops=int(flops), bytes_accessed=int(nbytes), transcendentals=0)


def dot(a, b, ca, cb):
    return lax.dot_general(a, b, (((ca,), (cb,)), ((), ())), preferred_element_type=F32)


def small(value):
    return value.astype(F32).astype(BF16)


def counts_kernel(index_ref, out_ref):
    base = pl.program_id(0) * TILE
    rows = small(lax.broadcasted_iota(jnp.int32, (TILE, 128), 0))
    lanes = lax.broadcasted_iota(jnp.int32, (FANOUT, 128), 1)
    zero, one, two = (jnp.array(v, BF16) for v in (0, 1, 2))
    for c in range(0, out_ref.shape[1], 128):
        entry = small(jnp.clip(index_ref[:, c : c + 128] - base, -1, TILE))
        own = small(jnp.clip(lanes + (c - base), -1, TILE))
        total = jnp.where(own[0:1, :] == rows, two, zero)
        for s in range(FANOUT):
            total = total + jnp.where(entry[s : s + 1, :] == rows, one, zero)
        out_ref[:, c : c + 128] = total


def counts(index, tiles):
    n = index.shape[1]
    return pl.pallas_call(
        counts_kernel,
        grid=(tiles,),
        in_specs=[pl.BlockSpec((FANOUT, n), lambda i: (0, 0))],
        out_specs=pl.BlockSpec((TILE, n), lambda i: (i, 0)),
        out_shape=jax.ShapeDtypeStruct((tiles * TILE, n), BF16),
        compiler_params=params(),
        cost_estimate=cost(0, tiles * TILE * n * 16),
        name="counts",
    )(index)


def gather_own_kernel(c_ref, t_ref, o_ref):
    o_ref[...] = dot(c_ref[...], t_ref[...], 0, 0)


def gather_own(adjacency, features, live):
    h = features.shape[1]
    return pl.pallas_call(
        gather_own_kernel,
        grid=(live // TILE,),
        in_specs=[pl.BlockSpec((live, TILE), lambda i: (0, i)), pl.BlockSpec((live, h), lambda i: (0, 0))],
        out_specs=pl.BlockSpec((TILE, h), lambda i: (i, 0)),
        out_shape=jax.ShapeDtypeStruct((live, h), F32),
        compiler_params=params(),
        cost_estimate=cost(2 * live * live * h, live * h * 6),
        name="gather_own",
    )(adjacency, features)


def gather_bound_kernel(c_ref, part_ref, inv_ref, *refs):
    o_ref = refs[-1]
    total = part_ref[...]
    for k, ref in enumerate(refs[:-1]):
        total = total + dot(c_ref[k * BOUND : (k + 1) * BOUND, :], ref[...], 0, 0)
    o_ref[...] = (total * inv_ref[...]).astype(BF16)


def gather_bound(adjacency, part, inverse, blocks):
    live, h = part.shape
    rest = adjacency.shape[0] - live
    return pl.pallas_call(
        gather_bound_kernel,
        grid=(live // TILE,),
        in_specs=[
            pl.BlockSpec((pl.Element(rest), pl.Element(TILE)), lambda i: (live, i * TILE)),
            pl.BlockSpec((TILE, h), lambda i: (i, 0)),
            pl.BlockSpec((TILE, 1), lambda i: (i, 0)),
        ]
        + [pl.BlockSpec((BOUND, h), lambda i: (0, 0))] * len(blocks),
        out_specs=pl.BlockSpec((TILE, h), lambda i: (i, 0)),
        out_shape=jax.ShapeDtypeStruct((live, h), BF16),
        compiler_params=params(),
        cost_estimate=cost(2 * live * rest * h, live * h * 6),
        name="gather_bound",
    )(adjacency, part, inverse, *blocks)


def layer_kernel(live_ref, m_ref, w_ref, b_ref, ct_ref, o_ref, gl_ref, gb_ref, *, tiles):
    i = pl.program_id(0)

    @pl.when(i == 0)
    def _():
        gb_ref[...] = jnp.zeros_like(gb_ref)

    @pl.when(i == tiles)
    def _():
        o_ref[...] = jnp.zeros_like(o_ref)

    @pl.when(i < tiles)
    def _():
        live = i * TILE + lax.broadcasted_iota(jnp.int32, (TILE, 256), 0) < live_ref[0]
        for j in range(0, w_ref.shape[1], 256):
            at = slice(j, j + 256)
            v = dot(m_ref[...], w_ref[:, at], 1, 0) + b_ref[:, at]
            square = v * v
            t = jnp.tanh(v * (GELU_A + (GELU_A * GELU_B) * square))
            half = 0.5 + 0.5 * t
            o_ref[:, at] = jnp.where(live, v * half, 0.0)
            slope = half + (0.5 * v) * (1 - t * t) * (GELU_A + (3 * GELU_A * GELU_B) * square)
            grad = jnp.where(live, ct_ref[:, at].astype(F32) * slope, 0.0)
            gl_ref[:, at] = grad.astype(BF16)
            gb_ref[:, at] += jnp.sum(grad.reshape(TILE // 8, 8, 256), axis=0)


def layer(live_count, mixed, matrix, offset, cotangent):
    live, h = mixed.shape
    nodes, n = cotangent.shape
    tiles = live // TILE

    def used(i, s):
        return (jnp.minimum(i, tiles - 1), 0)

    return pl.pallas_call(
        functools.partial(layer_kernel, tiles=tiles),
        grid_spec=pltpu.PrefetchScalarGridSpec(
            num_scalar_prefetch=1,
            grid=(tiles + 1,),
            in_specs=[
                pl.BlockSpec((TILE, h), used),
                pl.BlockSpec((h, n), lambda i, s: (0, 0)),
                pl.BlockSpec((1, n), lambda i, s: (0, 0)),
                pl.BlockSpec((TILE, n), used),
            ],
            out_specs=[
                pl.BlockSpec((TILE, n), lambda i, s: (i, 0)),
                pl.BlockSpec((TILE, n), used),
                pl.BlockSpec((8, n), lambda i, s: (0, 0)),
            ],
        ),
        out_shape=[
            jax.ShapeDtypeStruct((nodes, n), F32),
            jax.ShapeDtypeStruct((live, n), BF16),
            jax.ShapeDtypeStruct((8, n), F32),
        ],
        compiler_params=params(),
        cost_estimate=cost(2 * live * h * n, live * n * 20),
        name="layer",
    )(live_count, mixed, matrix, offset, cotangent)


def grad_weight_kernel(half_ref, m_ref, g_ref, o_ref):
    o_ref[...] = dot(m_ref[...], g_ref[...], 0, 0).astype(o_ref.dtype)


def grad_weight_half(half, mixed, grad_low, dtype):
    live, h = mixed.shape
    n = grad_low.shape[1] // 2
    return pl.pallas_call(
        grad_weight_kernel,
        grid_spec=pltpu.PrefetchScalarGridSpec(
            num_scalar_prefetch=1,
            grid=(h // TILE,),
            in_specs=[
                pl.BlockSpec((live, TILE), lambda i, s: (0, i)),
                pl.BlockSpec((live, n), lambda i, s: (0, s[0])),
            ],
            out_specs=pl.BlockSpec((TILE, n), lambda i, s: (i, 0)),
        ),
        out_shape=jax.ShapeDtypeStruct((h, n), dtype),
        compiler_params=params(),
        cost_estimate=cost(2 * live * h * n, live * h * 4),
        name="grad_weight",
    )(half, mixed, grad_low)


def grad_mixed_kernel(g_ref, w_ref, inv_ref, o_ref):
    o_ref[...] = (dot(g_ref[...], w_ref[...], 1, 1) * inv_ref[...]).astype(BF16)


def grad_mixed(grad_low, matrix, inverse):
    live, n = grad_low.shape
    h = matrix.shape[0]
    return pl.pallas_call(
        grad_mixed_kernel,
        grid=(live // TILE,),
        in_specs=[
            pl.BlockSpec((TILE, n), lambda i: (i, 0)),
            pl.BlockSpec((h, n), lambda i: (0, 0)),
            pl.BlockSpec((TILE, 1), lambda i: (i, 0)),
        ],
        out_specs=pl.BlockSpec((TILE, h), lambda i: (i, 0)),
        out_shape=jax.ShapeDtypeStruct((live, h), BF16),
        compiler_params=params(),
        cost_estimate=cost(2 * live * h * n, live * h * 4),
        name="grad_mixed",
    )(grad_low, matrix, inverse)


def scatter_bound_kernel(c_ref, g_ref, *outs):
    i = pl.program_id(0)
    part = dot(c_ref[...], g_ref[...], 1, 0).astype(BF16)
    for k, out in enumerate(outs):

        @pl.when(i == k)
        def _():
            out[...] = part


def scatter_bound(adjacency, grads):
    live, h = grads.shape
    blocks = (adjacency.shape[0] - live) // BOUND
    return pl.pallas_call(
        scatter_bound_kernel,
        grid=(blocks,),
        in_specs=[
            pl.BlockSpec((BOUND, live), lambda i: (i + live // BOUND, 0)),
            pl.BlockSpec((live, h), lambda i: (0, 0)),
        ],
        out_specs=[pl.BlockSpec((BOUND, h), lambda i: (0, 0))] * blocks,
        out_shape=[jax.ShapeDtypeStruct((BOUND, h), BF16)] * blocks,
        compiler_params=params(),
        cost_estimate=cost(2 * blocks * BOUND * live * h, live * h * 4),
        name="scatter_bound",
    )(adjacency, grads)


def scatter_own_kernel(c_ref, g_ref, o_ref, *, tiles):
    i = pl.program_id(0)

    @pl.when(i < tiles)
    def _():
        o_ref[...] = dot(c_ref[...], g_ref[...], 1, 0)

    @pl.when(i == tiles)
    def _():
        o_ref[...] = jnp.zeros_like(o_ref)


def scatter_own(adjacency, grads, nodes):
    live, h = grads.shape
    tiles = live // TILE
    return pl.pallas_call(
        functools.partial(scatter_own_kernel, tiles=tiles),
        grid=(tiles + 1,),
        in_specs=[
            pl.BlockSpec((TILE, live), lambda i: (jnp.minimum(i, tiles - 1), 0)),
            pl.BlockSpec((live, h), lambda i: (0, 0)),
        ],
        out_specs=pl.BlockSpec((TILE, h), lambda i: (i, 0)),
        out_shape=jax.ShapeDtypeStruct((nodes, h), F32),
        compiler_params=params(),
        cost_estimate=cost(2 * live * live * h, live * h * 6),
        name="scatter_own",
    )(adjacency, grads)


def add_returned_kernel(g_ref, *refs):
    total = g_ref[...]
    for ref in refs[:-1]:
        total = total + ref[...].astype(F32)
    refs[-1][...] = total


def add_returned(grads, returned):
    h = grads.shape[1]
    rows = pl.BlockSpec((64, h), lambda i: (i, 0))
    return pl.pallas_call(
        add_returned_kernel,
        grid=(BOUND // 64,),
        in_specs=[rows] * (1 + len(returned)),
        out_specs=rows,
        out_shape=jax.ShapeDtypeStruct(grads.shape, F32),
        input_output_aliases={0: 0},
        compiler_params=params(),
        cost_estimate=cost(0, BOUND * h * 14),
        name="add_returned",
    )(grads, *returned)


def body(features, weight, bias, neighbours, degrees, cluster_sizes, cotangent):
    axes = ("blk", "wa")
    n_blk, n_wa = lax.axis_size("blk"), lax.axis_size("wa")
    devices = n_blk * n_wa
    blk, wa = lax.axis_index("blk"), lax.axis_index("wa")
    core = blk % 2
    n_hi = n_blk // 4
    nodes, h = features.shape
    live = min(nodes, -(-(-(-CMAX // n_wa)) // TILE) * TILE)

    def permute(value, target):
        pairs = [(b * n_wa + w, target(b, w)) for b in range(n_blk) for w in range(n_wa)]
        return lax.ppermute(value, axes, [(s, b * n_wa + w) for s, (b, w) in pairs])

    def swap_wa(value):
        return permute(value, lambda b, w: (b, 1 - w))

    def swap_core(value):
        return permute(value, lambda b, w: (b ^ 1, w))

    def swap_outer(value):
        return permute(value, lambda b, w: ((b + (1 if b % 2 else -1)) % n_blk, w))

    def swap_lo(value):
        return permute(value, lambda b, w: (b ^ 2, w))

    def rotate_hi(value, k):
        return permute(value, lambda b, w: ((b + 4 * k) % n_blk, w))

    matrix = lax.all_gather(weight, axes, axis=0, tiled=True)
    leading = features[:BOUND]
    partner = swap_wa(leading)
    outer_same = swap_outer(leading)
    inner_same = swap_core(leading)
    inner_other = swap_core(partner)
    outer_other = swap_wa(outer_same)
    blocks = (partner, inner_same, inner_other, outer_same, outer_other)

    offset = bias
    stage, span = [("wa", n_wa)], 1
    for kind in range(1 + (n_blk - 1).bit_length()):
        if kind == 0:
            other, bit = swap_wa(offset), wa % 2
        else:
            step = 1 << (kind - 1)
            other = permute(offset, lambda b, w: (b ^ step, w))
            bit = (blk // step) % 2
        offset = jnp.where(bit == 0, jnp.concatenate([offset, other]), jnp.concatenate([other, offset]))
    offset = offset.astype(F32)[None, :]

    live_count = (cluster_sizes[0] - wa + n_wa - 1) // n_wa
    table = neighbours[:, :live]
    beyond = table - nodes
    segment, within = beyond // (n_wa * BOUND), beyond % (n_wa * BOUND)
    same = within // BOUND == wa
    row = within % BOUND
    side = jnp.where(same, 0, BOUND) + row
    inner = (segment == 2) == (core == 0)
    away = jnp.where(inner, live + BOUND, live + BOUND + n_wa * BOUND) + side
    home = jnp.where(same, row, live + row)
    index = jnp.where(table < nodes, table, jnp.where(segment == 0, home, away))
    valid = jnp.arange(FANOUT, dtype=jnp.int32)[:, None] < degrees[None, :live]
    index = jnp.where(valid, index, -1)
    inverse = (1.0 / (degrees[:live].astype(F32) + 1.0))[:, None]

    adjacency = counts(index, (live + (1 + 2 * n_wa) * BOUND) // TILE)
    part = gather_own(adjacency, features, live)
    mixed = gather_bound(adjacency, part, inverse, blocks)
    output, grad_low, bias_part = layer(live_count[None], mixed, matrix, offset, cotangent)

    mine = core[None].astype(jnp.int32)
    sent = swap_core(grad_weight_half(1 - mine, mixed, grad_low, BF16))
    kept = grad_weight_half(mine, mixed, grad_low, F32)
    grads = grad_mixed(grad_low, matrix, inverse)
    own_bound, inner_same_g, inner_other_g, outer_same_g, outer_other_g = scatter_bound(adjacency, grads)
    grad_features = scatter_own(adjacency, grads, nodes)

    def pick(value, axis, at):
        return lax.dynamic_index_in_dim(value, at, axis, keepdims=False)

    hi, lo = blk // 4, (blk // 2) % 2
    total = (kept + sent.astype(F32)).reshape(n_hi, 2, 2, n_wa, h // devices, h // 2)
    first, second = total[..., : h // 4], total[..., h // 4 :]
    first = pick(first, 3, wa) + swap_wa(pick(first, 3, 1 - wa).astype(BF16)).astype(F32)
    second = pick(second, 1, lo) + swap_lo(pick(second, 1, 1 - lo).astype(BF16)).astype(F32)
    first = pick(first, 1, lo) + swap_lo(pick(first, 1, 1 - lo).astype(BF16)).astype(F32)
    second = pick(second, 2, wa) + swap_wa(pick(second, 2, 1 - wa).astype(BF16)).astype(F32)
    rows = jnp.concatenate([first, second], axis=-1)
    summed = pick(rows, 0, hi)
    for k in range(1, n_hi):
        away = pick(rows, 0, (hi + k) % n_hi).astype(BF16)
        summed = summed + rotate_hi(away, k).astype(F32)
    mine_rows = pick(summed, 0, core)
    other_rows = swap_core(pick(summed, 0, 1 - core))
    grad_weight = jnp.where(
        core == 0,
        jnp.concatenate([mine_rows, other_rows], axis=1),
        jnp.concatenate([other_rows, mine_rows], axis=1),
    )

    bias_sum = jnp.sum(bias_part, axis=0)
    bias_sum = bias_sum + swap_wa(bias_sum)
    step = 1
    while step < n_blk:
        bias_sum = bias_sum + permute(bias_sum, lambda b, w: (b ^ step, w))
        step *= 2
    grad_bias = lax.dynamic_slice_in_dim(bias_sum, (blk * n_wa + wa) * (h // devices), h // devices)

    outer_back = (outer_same_g.astype(F32) + swap_wa(outer_other_g).astype(F32)).astype(BF16)
    own_back = (own_bound.astype(F32) + swap_core(inner_other_g).astype(F32)).astype(BF16)
    returned = (swap_core(inner_same_g), swap_wa(own_back), swap_outer(outer_back))
    grad_features = add_returned(grad_features, returned)
    return (output, grad_features, grad_weight, grad_bias)


def solution(mesh):
    return jax.shard_map(
        body,
        mesh=mesh,
        in_specs=(
            P(("blk", "wa"), None),
            P(("blk", "wa"), None),
            P(("blk", "wa")),
            P(None, ("blk", "wa")),
            P(("blk", "wa")),
            P("blk"),
            P(("blk", "wa"), None),
        ),
        out_specs=(
            P(("blk", "wa"), None),
            P(("blk", "wa"), None),
            P(("blk", "wa"), None),
            P(("blk", "wa")),
        ),
        check_vma=False,
    )
```

time: 1230 us -> 313 us (0.25)
  matrix products: 544 us -> 0 us
  waiting for transfers between devices: 462 us -> 89.2 us
  Pallas kernels: 0 us -> 157 us
  blocking collectives: 125 us -> 0 us
  other arithmetic: 60.7 us -> 15.3 us
  starting transfers between devices: 4.6 us -> 25.9 us
    dot_general x5 -> x0, matrix products: 544 us -> none  [the longest x1 371 us: body(): lax.dot_general(counts, grad_scaled, (((0,), (0,)), ((), ())), precision=...]
    reduce_scatter x2 -> x0, waiting for transfers between devices: 337 us -> none  [the longest x1 337 us: body(): lax.psum_scatter(weight_part, ('blk', 'wa'), scatter_dimension=0, tiled=T...]
    pallas_call x0 -> x10, Pallas kernels: none -> 157 us  [the longest x1 28.9 us: layer(): pl.pallas_call(functools.partial(layer_kernel, tiles=tiles), grid_spec=pl...]
    unnamed x2 -> x0, blocking collectives: 125 us -> none
    dot_general x2 -> x0, other arithmetic: 34.6 us -> none  [the longest x1 24 us: body(): gathered_sum = jnp.dot(adjacency, table, preferred_element_type=jnp.float32)]
    ppermute x4 -> x29, starting transfers between devices: 4.44 us -> 25.9 us  [permute(): return lax.ppermute(value, axes, [(s, b * n_wa + w) for s, (b, w) in pairs])]
    ppermute x4 -> x29, waiting for transfers between devices: 91.1 us -> 70 us  [permute(): return lax.ppermute(value, axes, [(s, b * n_wa + w) for s, (b, w) in pairs])]
    all_gather x2 -> x1, waiting for transfers between devices: 33.2 us -> 18.5 us  [body(): matrix = lax.all_gather(weight, axes, axis=0, tiled=True)]
  transfers between devices with their start and end apart: 8 -> 30, of which waited for: 3 -> 17; matrix products, arithmetic and copies ran while one was open for 14% -> 4% of each run, Pallas kernels for 0% -> 37%
where the time goes in v1:
time: 313 us; the launch traced here: 310 us
  Pallas kernels  157 us (50%)
  waiting for transfers between devices  89.2 us (28%)
  starting transfers between devices  25.9 us (8%)
  other arithmetic  15.3 us (5%)
  between operations  15 us (5%)
  local copies, waits for them, and re-layouts  8.13 us (3%)
    ppermute x29, waiting for transfers between devices, permute(): return lax.ppermute(value, axes, [(s, b * n_wa + w) for s, (b, w) in pairs])  70 us
    pallas_call x1, Pallas kernels, layer(): pl.pallas_call(functools.partial(layer_kernel, tiles=tiles), grid_spec=pl...  28.9 us
    ppermute x29, starting transfers between devices, permute(): return lax.ppermute(value, axes, [(s, b * n_wa + w) for s, (b, w) in pairs])  25.9 us
    pallas_call x2, Pallas kernels, grad_weight_half(): pl.pallas_call(grad_weight_kernel, grid_spec=pltpu.PrefetchScalarGridSpec...  25.1 us
    pallas_call x1, Pallas kernels, grad_mixed(): pl.pallas_call(grad_mixed_kernel, grid=(live // TILE,), in_specs=[pl.Bloc...  19.4 us
    all_gather x1, waiting for transfers between devices, body(): matrix = lax.all_gather(weight, axes, axis=0, tiled=True)  18.5 us
    pallas_call x1, Pallas kernels, counts(): pl.pallas_call(counts_kernel, grid=(tiles,), in_specs=[pl.BlockSpec((FANO...  17.4 us
    pallas_call x1, Pallas kernels, gather_bound(): pl.pallas_call(gather_bound_kernel, grid=(live // TILE,), in_specs=[pl.Bl...  15.7 us
  transfers between devices with their start and end apart: 30, of which 17 were waited for; matrix products, arithmetic and copies ran while one was open for 4% of the time, Pallas kernels for 37%

profile of v1, /device:TPU:11, one launch (start us, length us, event | category | flops | bytes accessed | tf_op | source)
XLA Modules:
  0.0 310.4 jit_solution(1005268890989809927)
XLA Ops:
  7.9 2.3 slice.18
  10.2 1.8 collective-permute-start.3
  13.5 1.8 fusion.21.index_ref
  15.2 17.4 %counts.1.c_ref = bf16[2816,1536]{1,0:T(8,128)(2,1)} custom-call(s32[16,1536]{1,0:T(8,128)} %fusion.21.index_ref), custom_call_target="tpu_custom_call" | custom-call | bytes 69206016 | tf_op jit(solution)/shard_map/counts/pallas_call | solution.py:54
  32.6 5.4 %collective-permute-done.3.refs_3_ = bf16[256,2048]{1,0:T(8,128)(2,1)S(1)} collective-permute-done((bf16[256,2048]{1,0:T(8,128)(2,1)}, bf16[256,2048]{1,0:T(8,128)(2,1)S(1)}, u32[]{:S(2)}, u32[]{:S(2)}) %collective-permute-start.3) | collective-permute-done | bytes 1048608 | tf_op jit(solution)/shard_map/ppermute | solution.py:316
  39.7 15.4 %gather_own.1.part_ref = f32[1536,2048]{1,0:T(8,128)} custom-call(bf16[2816,1536]{1,0:T(8,128)(2,1)} %counts.1.c_ref, bf16[1664,2048]{1,0:T(8,128)(2,1)} %t_ref.1), custom_call_target="tpu_custom_call" | custom-call | flops 9663676416 | bytes 18874368 | tf_op jit(solution)/shard_map/gather_own/pallas_call | solution.py:72
  57.0 2.3 collective-permute-done.7
  59.5 2.7 collective-permute-done.8
  62.1 2.4 collective-permute-start.9
  67.0 2.0 collective-permute-done.4.refs_4_
  69.0 15.7 %gather_bound.1.m_ref = bf16[1536,2048]{1,0:T(8,128)(2,1)} custom-call(bf16[2816,1536]{1,0:T(8,128)(2,1)} %counts.1.c_ref, f32[1536,2048]{1,0:T(8,128)} %gather_own.1.part_ref, f32[1536,1]{1,0:T(8,128)} %broadcast_in_dim.29.inv_ref, bf16[256,2048]{1,0:T(8,128)(2,1)} %copy-done.4, bf16[256,2048]{1,0:T(8,128)(2,1)} %copy-done.5, ...), custom_call_target="tpu_custom_call" | custom-call | flops 8053063680 | bytes 18874368 | tf_op jit(solution)/shard_map/gather_bound/pallas_call | solution.py:95
  84.8 18.5 %all-gather.2.cloned.1.call-done.w_ref = bf16[2048,2048]{1,0:T(8,128)(2,1)} async-done(((bf16[64,2048]{1,0:T(8,128)(2,1)}), bf16[2048,2048]{1,0:T(8,128)(2,1)}) %all-gather.2.cloned.1.call-update) | async-done | bytes 8388624 | tf_op jit(solution)/shard_map/all_gather | solution.py:333
  103.3 28.9 %layer.1 = (f32[1664,2048]{1,0:T(8,128)}, bf16[1536,2048]{1,0:T(8,128)(2,1)}, f32[8,2048]{1,0:T(8,128)}) custom-call(s32[1]{0:T(128)} %bitcast.1.live_ref, bf16[1536,2048]{1,0:T(8,128)(2,1)} %gather_bound.1.m_ref, bf16[2048,2048]{1,0:T(8,128)(2,1)} %all-gather.2.cloned.1.call-done.w_ref, f32[1,2048]{1,0:T(1,128)} %fusion.25.b_ref, bf16[1664,2048]{1,0:T(8,128)(2,1)} %ct_ref.1), custom_call_target="tpu_custom_call" | custom-call | flops 12884901888 | bytes 62914560 | tf_op jit(solution)/shard_map/layer/pallas_call | solution.py:147
  132.2 12.2 %grad_weight.3 = bf16[2048,1024]{1,0:T(8,128)(2,1)} custom-call(s32[1]{0:T(128)S(6)} %sub.58.half_ref, bf16[1536,2048]{1,0:T(8,128)(2,1)} %gather_bound.1.m_ref, bf16[1536,2048]{1,0:T(8,128)(2,1)} %get-tuple-element.13.g_ref), custom_call_target="tpu_custom_call" | custom-call | flops 6442450944 | bytes 12582912 | tf_op jit(solution)/shard_map/grad_weight/pallas_call | solution.py:182
  144.7 12.9 %grad_weight.2 = f32[2048,1024]{1,0:T(8,128)} custom-call(s32[1]{0:T(128)} %bitcast.2.half_ref, bf16[1536,2048]{1,0:T(8,128)(2,1)} %gather_bound.1.m_ref, bf16[1536,2048]{1,0:T(8,128)(2,1)} %get-tuple-element.13.g_ref), custom_call_target="tpu_custom_call" | custom-call | flops 6442450944 | bytes 12582912 | tf_op jit(solution)/shard_map/grad_weight/pallas_call | solution.py:182
  157.6 19.4 %grad_mixed.1.g_ref = bf16[1536,2048]{1,0:T(8,128)(2,1)} custom-call(bf16[1536,2048]{1,0:T(8,128)(2,1)} %get-tuple-element.13.g_ref, bf16[2048,2048]{1,0:T(8,128)(2,1)} %all-gather.2.cloned.1.call-done.w_ref, f32[1536,1]{1,0:T(8,128)} %broadcast_in_dim.29.inv_ref), custom_call_target="tpu_custom_call" | custom-call | flops 12884901888 | bytes 12582912 | tf_op jit(solution)/shard_map/grad_mixed/pallas_call | solution.py:207
  177.0 6.1 %convert_add_fusion = f32[2048,1024]{1,0:T(8,128)S(1)} fusion(f32[2048,1024]{1,0:T(8,128)} %grad_weight.2, bf16[2048,1024]{1,0:T(8,128)(2,1)} %collective-permute-done.15), kind=kLoop, calls=%fused_computation | loop fusion | flops 4194304 | bytes 20971520 | tf_op jit(solution)/shard_map/add | solution.py:385
  185.1 1.5 copy-done
  188.3 15.0 %scatter_bound.1 = (bf16[256,2048]{1,0:T(8,128)(2,1)}, bf16[256,2048]{1,0:T(8,128)(2,1)}, bf16[256,2048]{1,0:T(8,128)(2,1)}, bf16[256,2048]{1,0:T(8,128)(2,1)}, bf16[256,2048]{1,0:T(8,128)(2,1)}) custom-call(bf16[2816,1536]{1,0:T(8,128)(2,1)} %counts.1.c_ref, bf16[1536,2048]{1,0:T(8,128)(2,1)} %grad_mixed.1.g_ref), custom_call_target="tpu_custom_call" | custom-call | flops 8053063680 | bytes 12582912 | tf_op jit(solution)/shard_map/scatter_bound/pallas_call | solution.py:236
  205.1 4.5 %collective-permute-done.24 = f32[2048]{0:T(1024)S(1)} collective-permute-done((f32[2048]{0:T(1024)S(1)}, f32[2048]{0:T(1024)S(1)}, u32[]{:S(2)}, u32[]{:S(2)}) %collective-permute-start.24) | collective-permute-done | bytes 8224 | tf_op jit(solution)/shard_map/ppermute | solution.py:316
  211.7 2.2 collective-permute-done.26
  214.2 1.8 collective-permute-start.10
  217.9 2.2 fusion
  221.5 1.6 bitcast_add_fusion
  224.0 7.0 %collective-permute-done.17 = bf16[4,2,64,512]{3,2,1,0:T(8,128)(2,1)S(1)} collective-permute-done((bf16[4,2,64,512]{3,2,1,0:T(8,128)(2,1)S(1)}, bf16[4,2,64,512]{3,2,1,0:T(8,128)(2,1)S(1)}, u32[]{:S(2)}, u32[]{:S(2)}) %collective-permute-start.17) | collective-permute-done | bytes 524320 | tf_op jit(solution)/shard_map/ppermute | solution.py:316
  231.2 18.7 %collective-permute-done.19 = bf16[4,2,64,512]{3,2,1,0:T(8,128)(2,1)S(1)} collective-permute-done((bf16[4,2,64,512]{3,2,1,0:T(8,128)(2,1)S(1)}, bf16[4,2,64,512]{3,2,1,0:T(8,128)(2,1)S(1)}, u32[]{:S(2)}, u32[]{:S(2)}) %collective-permute-start.19) | collective-permute-done | bytes 524320 | tf_op jit(solution)/shard_map/ppermute | solution.py:316
  250.9 2.7 collective-permute-start.21
  255.8 14.7 %collective-permute-done.21 = bf16[2,64,1024]{2,1,0:T(8,128)(2,1)S(1)} collective-permute-done((bf16[2,64,1024]{2,1,0:T(8,128)(2,1)S(1)}, bf16[2,64,1024]{2,1,0:T(8,128)(2,1)S(1)}, u32[]{:S(2)}, u32[]{:S(2)}) %collective-permute-start.21) | collective-permute-done | bytes 262176 | tf_op jit(solution)/shard_map/ppermute | solution.py:316
  270.4 4.1 %collective-permute-start.14 = (bf16[256,2048]{1,0:T(8,128)(2,1)S(1)}, bf16[256,2048]{1,0:T(8,128)(2,1)}, u32[]{:S(2)}, u32[]{:S(2)}) collective-permute-start(bf16[256,2048]{1,0:T(8,128)(2,1)S(1)} %add_convert_fusion), channel_id=1, source_target_pairs={{0,30},{1,31},{2,4},{3,5},{4,2},{5,3},{6,8},{7,9},{8,6},{9,7},{10,... | collective-permute-start | bytes 3145736 | tf_op jit(solution)/shard_map/ppermute | solution.py:316
  277.4 15.6 %scatter_own.1.g_ref = f32[1664,2048]{1,0:T(8,128)} custom-call(bf16[2816,1536]{1,0:T(8,128)(2,1)} %counts.1.c_ref, bf16[1536,2048]{1,0:T(8,128)(2,1)} %grad_mixed.1.g_ref), custom_call_target="tpu_custom_call" | custom-call | flops 9663676416 | bytes 18874368 | tf_op jit(solution)/shard_map/scatter_own/pallas_call | solution.py:266
  293.5 4.8 %collective-permute-done.14.refs_2_ = bf16[256,2048]{1,0:T(8,128)(2,1)} collective-permute-done((bf16[256,2048]{1,0:T(8,128)(2,1)S(1)}, bf16[256,2048]{1,0:T(8,128)(2,1)}, u32[]{:S(2)}, u32[]{:S(2)}) %collective-permute-start.14) | collective-permute-done | bytes 1048608 | tf_op jit(solution)/shard_map/ppermute | solution.py:316
  298.3 4.4 %add_returned.1 = f32[1664,2048]{1,0:T(8,128)} custom-call(f32[1664,2048]{1,0:T(8,128)} %scatter_own.1.g_ref, bf16[256,2048]{1,0:T(8,128)(2,1)} %collective-permute-done.10.refs_0_, bf16[256,2048]{1,0:T(8,128)(2,1)} %copy-done.8, bf16[256,2048]{1,0:T(8,128)(2,1)} %collective-permute-done.14.refs_2_), custom_call_target="tpu_custom_call", output_to_operand_aliasing={{}: (0, {})} | custom-call | bytes 7340032 | tf_op jit(solution)/shard_map/add_returned/pallas_call | solution.py:291
  (96 shorter events, 27.5 us)
Async XLA Ops:
  7.2 96.1 %all-gather.2.cloned.1.call-start = ((), (), s32[]{:S(2)}) async-start(), calls=%async_computation | async-start | bytes 8650752 | tf_op jit(solution)/shard_map/all_gather | solution.py:333
  10.2 27.9 %collective-permute-start.3 = (bf16[256,2048]{1,0:T(8,128)(2,1)}, bf16[256,2048]{1,0:T(8,128)(2,1)S(1)}, u32[]{:S(2)}, u32[]{:S(2)}) collective-permute-start(bf16[256,2048]{1,0:T(8,128)(2,1)} %slice.18), channel_id=1, source_target_pairs={{0,30},{1,31},{2,4},{3,5},{4,2},{5,3},{6,8},{7,9},{8,6},{9,7},{10,... | collective-permute-start | bytes 3145736 | tf_op jit(solution)/shard_map/ppermute | solution.py:316
  12.0 27.1 %collective-permute-start = (bf16[256,2048]{1,0:T(8,128)(2,1)}, bf16[256,2048]{1,0:T(8,128)(2,1)S(1)}, u32[]{:S(2)}, u32[]{:S(2)}) collective-permute-start(bf16[256,2048]{1,0:T(8,128)(2,1)} %slice.18), channel_id=1, source_target_pairs={{0,1},{1,0},{2,3},{3,2},{4,5},{5,4},{6,7},{7,6},{8,9},{9,8},{10,11... | collective-permute-start | bytes 3145736 | tf_op jit(solution)/shard_map/ppermute | solution.py:316
  12.3 54.7 %collective-permute-start.1 = (bf16[256,2048]{1,0:T(8,128)(2,1)}, bf16[256,2048]{1,0:T(8,128)(2,1)S(1)}, u32[]{:S(2)}, u32[]{:S(2)}) collective-permute-start(bf16[256,2048]{1,0:T(8,128)(2,1)} %slice.18), channel_id=1, source_target_pairs={{0,2},{1,3},{2,0},{3,1},{4,6},{5,7},{6,4},{7,5},{8,10},{9,11},{10,... | collective-permute-start | bytes 3145736 | tf_op jit(solution)/shard_map/ppermute | solution.py:316
  12.3 42.8 %collective-permute-start.5 = (bf16[64]{0:T(256)(128)(2,1)}, bf16[64]{0:T(256)(128)(2,1)S(1)}, u32[]{:S(2)}, u32[]{:S(2)}) collective-permute-start(bf16[64]{0:T(256)(128)(2,1)} %param.9), channel_id=1, source_target_pairs={{0,1},{1,0},{2,3},{3,2},{4,5},{5,4},{6,7},{7,6},{8,9},{9,8},{10,11... | collective-permute-start | bytes 392 | tf_op jit(solution)/shard_map/ppermute | solution.py:316
  32.6 22.5 %copy-start.11 = (bf16[64]{0:T(256)(128)(2,1)S(1)}, bf16[64]{0:T(256)(128)(2,1)}, u32[]{:S(2)}) copy-start(bf16[64]{0:T(256)(128)(2,1)} %param.9) | copy-start | bytes 388
  38.1 30.9 %collective-permute-start.4 = (bf16[256,2048]{1,0:T(8,128)(2,1)S(1)}, bf16[256,2048]{1,0:T(8,128)(2,1)}, u32[]{:S(2)}, u32[]{:S(2)}) collective-permute-start(bf16[256,2048]{1,0:T(8,128)(2,1)S(1)} %collective-permute-done.3.refs_3_), channel_id=1, source_target_pairs={{0,1},{1,0},{2,3},{3,2},{4,5},{5,4},{6,7},{7,6},{8,9},{9,8},{10,11... | collective-permute-start | bytes 3145736 | tf_op jit(solution)/shard_map/ppermute | solution.py:316
  39.1 29.9 %collective-permute-start.2 = (bf16[256,2048]{1,0:T(8,128)(2,1)S(1)}, bf16[256,2048]{1,0:T(8,128)(2,1)}, u32[]{:S(2)}, u32[]{:S(2)}) collective-permute-start(bf16[256,2048]{1,0:T(8,128)(2,1)S(1)} %collective-permute-done.refs_0_), channel_id=1, source_target_pairs={{0,2},{1,3},{2,0},{3,1},{4,6},{5,7},{6,4},{7,5},{8,10},{9,11},{10,... | collective-permute-start | bytes 3145736 | tf_op jit(solution)/shard_map/ppermute | solution.py:316
  55.2 1.2 collective-permute-start.6
  56.4 2.9 collective-permute-start.7
  59.3 2.9 collective-permute-start.8
  62.1 4.2 %collective-permute-start.9 = (bf16[1024]{0:T(1024)(128)(2,1)S(1)}, bf16[1024]{0:T(1024)(128)(2,1)S(1)}, u32[]{:S(2)}, u32[]{:S(2)}) collective-permute-start(bf16[1024]{0:T(1024)(128)(2,1)S(1)} %maximum_select_fusion.1), channel_id=1, source_target_pairs={{0,16},{1,17},{2,18},{3,19},{4,20},{5,21},{6,22},{7,23},{8,24},{9,... | collective-permute-start | bytes 6152 | tf_op jit(solution)/shard_map/ppermute | solution.py:316
  144.4 32.6 %collective-permute-start.15 = (bf16[2048,1024]{1,0:T(8,128)(2,1)}, bf16[2048,1024]{1,0:T(8,128)(2,1)}, u32[]{:S(2)}, u32[]{:S(2)}) collective-permute-start(bf16[2048,1024]{1,0:T(8,128)(2,1)} %grad_weight.3), channel_id=1, source_target_pairs={{0,2},{1,3},{2,0},{3,1},{4,6},{5,7},{6,4},{7,5},{8,10},{9,11},{10,... | collective-permute-start | bytes 12582920 | tf_op jit(solution)/shard_map/ppermute | solution.py:316
  184.7 32.0 %collective-permute-start.16 = (bf16[4,2,2,64,512]{4,3,2,0,1:T(8,128)(2,1)S(1)}, bf16[4,2,2,64,512]{4,3,2,0,1:T(8,128)(2,1)}, u32[]{:S(2)}, u32[]{:S(2)}) collective-permute-start(bf16[4,2,2,64,512]{4,3,2,0,1:T(8,128)(2,1)S(1)} %fusion.2), channel_id=1, source_target_pairs={{0,1},{1,0},{2,3},{3,2},{4,5},{5,4},{6,7},{7,6},{8,9},{9,8},{10,11... | collective-permute-start | bytes 3145736 | tf_op jit(solution)/shard_map/ppermute | solution.py:316
  188.0 32.3 %collective-permute-start.18 = (bf16[4,2,2,64,512]{4,3,2,1,0:T(8,128)(2,1)S(1)}, bf16[4,2,2,64,512]{4,3,2,1,0:T(8,128)(2,1)}, u32[]{:S(2)}, u32[]{:S(2)}) collective-permute-start(bf16[4,2,2,64,512]{4,3,2,1,0:T(8,128)(2,1)S(1)} %fusion.1), channel_id=1, source_target_pairs={{0,4},{1,5},{2,6},{3,7},{4,0},{5,1},{6,2},{7,3},{8,12},{9,13},{10,... | collective-permute-start | bytes 3145736 | tf_op jit(solution)/shard_map/ppermute | solution.py:316
  203.3 19.9 %collective-permute-start.11 = (bf16[256,2048]{1,0:T(8,128)(2,1)}, bf16[256,2048]{1,0:T(8,128)(2,1)S(1)}, u32[]{:S(2)}, u32[]{:S(2)}) collective-permute-start(bf16[256,2048]{1,0:T(8,128)(2,1)} %get-tuple-element.16), channel_id=1, source_target_pairs={{0,2},{1,3},{2,0},{3,1},{4,6},{5,7},{6,4},{7,5},{8,10},{9,11},{10,... | collective-permute-start | bytes 3145736 | tf_op jit(solution)/shard_map/ppermute | solution.py:316
  203.8 5.8 %collective-permute-start.24 = (f32[2048]{0:T(1024)S(1)}, f32[2048]{0:T(1024)S(1)}, u32[]{:S(2)}, u32[]{:S(2)}) collective-permute-start(f32[2048]{0:T(1024)S(1)} %reduce_sum.9), channel_id=1, source_target_pairs={{0,1},{1,0},{2,3},{3,2},{4,5},{5,4},{6,7},{7,6},{8,9},{9,8},{10,11... | collective-permute-start | bytes 24584 | tf_op jit(solution)/shard_map/ppermute | solution.py:316
  209.6 1.8 collective-permute-start.25
  211.4 2.5 collective-permute-start.26
  213.9 2.5 collective-permute-start.27
  214.2 79.4 %collective-permute-start.10 = (bf16[256,2048]{1,0:T(8,128)(2,1)}, bf16[256,2048]{1,0:T(8,128)(2,1)}, u32[]{:S(2)}, u32[]{:S(2)}) collective-permute-start(bf16[256,2048]{1,0:T(8,128)(2,1)} %get-tuple-element.14), channel_id=1, source_target_pairs={{0,2},{1,3},{2,0},{3,1},{4,6},{5,7},{6,4},{7,5},{8,10},{9,11},{10,... | collective-permute-start | bytes 3145736 | tf_op jit(solution)/shard_map/ppermute | solution.py:316
  216.4 37.2 %collective-permute-start.13 = (bf16[256,2048]{1,0:T(8,128)(2,1)}, bf16[256,2048]{1,0:T(8,128)(2,1)S(1)}, u32[]{:S(2)}, u32[]{:S(2)}) collective-permute-start(bf16[256,2048]{1,0:T(8,128)(2,1)} %get-tuple-element.18), channel_id=1, source_target_pairs={{0,1},{1,0},{2,3},{3,2},{4,5},{5,4},{6,7},{7,6},{8,9},{9,8},{10,11... | collective-permute-start | bytes 3145736 | tf_op jit(solution)/shard_map/ppermute | solution.py:316
  216.7 76.2 %collective-permute-start.28 = (f32[2048]{0:T(1024)S(1)}, f32[2048]{0:T(1024)S(1)}, u32[]{:S(2)}, u32[]{:S(2)}) collective-permute-start(f32[2048]{0:T(1024)S(1)} %add.208), channel_id=1, source_target_pairs={{0,16},{1,17},{2,18},{3,19},{4,20},{5,21},{6,22},{7,23},{8,24},{9,... | collective-permute-start | bytes 24584 | tf_op jit(solution)/shard_map/ppermute | solution.py:316
  220.3 10.8 %collective-permute-start.17 = (bf16[4,2,64,512]{3,2,1,0:T(8,128)(2,1)S(1)}, bf16[4,2,64,512]{3,2,1,0:T(8,128)(2,1)S(1)}, u32[]{:S(2)}, u32[]{:S(2)}) collective-permute-start(bf16[4,2,64,512]{3,2,1,0:T(8,128)(2,1)S(1)} %fusion.3), channel_id=1, source_target_pairs={{0,4},{1,5},{2,6},{3,7},{4,0},{5,1},{6,2},{7,3},{8,12},{9,13},{10,... | collective-permute-start | bytes 1572872 | tf_op jit(solution)/shard_map/ppermute | solution.py:316
  223.2 26.7 %collective-permute-start.19 = (bf16[4,2,64,512]{3,2,1,0:T(8,128)(2,1)S(1)}, bf16[4,2,64,512]{3,2,1,0:T(8,128)(2,1)S(1)}, u32[]{:S(2)}, u32[]{:S(2)}) collective-permute-start(bf16[4,2,64,512]{3,2,1,0:T(8,128)(2,1)S(1)} %fusion.4), channel_id=1, source_target_pairs={{0,1},{1,0},{2,3},{3,2},{4,5},{5,4},{6,7},{7,6},{8,9},{9,8},{10,11... | collective-permute-start | bytes 1572872 | tf_op jit(solution)/shard_map/ppermute | solution.py:316
  224.0 29.6 %copy-start.6 = (bf16[256,2048]{1,0:T(8,128)(2,1)S(1)}, bf16[256,2048]{1,0:T(8,128)(2,1)}, u32[]{:S(2)}) copy-start(bf16[256,2048]{1,0:T(8,128)(2,1)} %get-tuple-element.17) | copy-start | bytes 3145732
  250.2 5.3 %collective-permute-start.20 = (bf16[2,64,1024]{2,1,0:T(8,128)(2,1)S(1)}, bf16[2,64,1024]{2,1,0:T(8,128)(2,1)S(1)}, u32[]{:S(2)}, u32[]{:S(2)}) collective-permute-start(bf16[2,64,1024]{2,1,0:T(8,128)(2,1)S(1)} %get-tuple-element.22), channel_id=1, source_target_pairs={{0,8},{1,9},{2,10},{3,11},{4,12},{5,13},{6,14},{7,15},{8,16},{9,17... | collective-permute-start | bytes 786440 | tf_op jit(solution)/shard_map/ppermute | solution.py:316
  250.9 19.5 %collective-permute-start.21 = (bf16[2,64,1024]{2,1,0:T(8,128)(2,1)S(1)}, bf16[2,64,1024]{2,1,0:T(8,128)(2,1)S(1)}, u32[]{:S(2)}, u32[]{:S(2)}) collective-permute-start(bf16[2,64,1024]{2,1,0:T(8,128)(2,1)S(1)} %get-tuple-element.23), channel_id=1, source_target_pairs={{0,16},{1,17},{2,18},{3,19},{4,20},{5,21},{6,22},{7,23},{8,24},{9,... | collective-permute-start | bytes 786440 | tf_op jit(solution)/shard_map/ppermute | solution.py:316
  253.6 22.2 %collective-permute-start.22 = (bf16[2,64,1024]{2,1,0:T(8,128)(2,1)S(1)}, bf16[2,64,1024]{2,1,0:T(8,128)(2,1)S(1)}, u32[]{:S(2)}, u32[]{:S(2)}) collective-permute-start(bf16[2,64,1024]{2,1,0:T(8,128)(2,1)S(1)} %get-tuple-element.24), channel_id=1, source_target_pairs={{0,24},{1,25},{2,26},{3,27},{4,28},{5,29},{6,30},{7,31},{8,0},{9,1... | collective-permute-start | bytes 786440 | tf_op jit(solution)/shard_map/ppermute | solution.py:316
  255.5 38.1 %collective-permute-start.12 = (bf16[256,2048]{1,0:T(8,128)(2,1)S(1)}, bf16[256,2048]{1,0:T(8,128)(2,1)S(1)}, u32[]{:S(2)}, u32[]{:S(2)}) collective-permute-start(bf16[256,2048]{1,0:T(8,128)(2,1)S(1)} %add_convert_fusion.1), channel_id=1, source_target_pairs={{0,1},{1,0},{2,3},{3,2},{4,5},{5,4},{6,7},{7,6},{8,9},{9,8},{10,11... | collective-permute-start | bytes 3145736 | tf_op jit(solution)/shard_map/ppermute | solution.py:316
  270.4 27.9 %collective-permute-start.14 = (bf16[256,2048]{1,0:T(8,128)(2,1)S(1)}, bf16[256,2048]{1,0:T(8,128)(2,1)}, u32[]{:S(2)}, u32[]{:S(2)}) collective-permute-start(bf16[256,2048]{1,0:T(8,128)(2,1)S(1)} %add_convert_fusion), channel_id=1, source_target_pairs={{0,30},{1,31},{2,4},{3,5},{4,2},{5,3},{6,8},{7,9},{8,6},{9,7},{10,... | collective-permute-start | bytes 3145736 | tf_op jit(solution)/shard_map/ppermute | solution.py:316
  276.0 26.7 %collective-permute-start.23 = (f32[64,1024]{1,0:T(8,128)S(1)}, f32[64,1024]{1,0:T(8,128)S(1)}, u32[]{:S(2)}, u32[]{:S(2)}) collective-permute-start(f32[64,1024]{1,0:T(8,128)S(1)} %get-tuple-element.26), channel_id=1, source_target_pairs={{0,2},{1,3},{2,0},{3,1},{4,6},{5,7},{6,4},{7,5},{8,10},{9,11},{10,... | collective-permute-start | bytes 786440 | tf_op jit(solution)/shard_map/ppermute | solution.py:316
  (10 other events, 94.3 us)
Sparse Core Ops, SparseCore 0:
  11.0 92.2 all-gather.1

commit v2 on v1

v2 whole, which is shorter than its diff:
```python
import functools
import math

import jax
import jax.numpy as jnp
from jax import lax
from jax.experimental import pallas as pl
from jax.experimental.pallas import tpu as pltpu
from jax.sharding import PartitionSpec as P

FANOUT = 16
BOUND = 256
CMAX = 3016
TILE = 256
F32 = jnp.float32
BF16 = jnp.bfloat16
VMEM = 60 * 1024 * 1024
GELU_A = math.sqrt(2 / math.pi)
GELU_B = 0.044715


ANY = pl.BlockSpec(memory_space=pl.ANY)
SMEM = pl.BlockSpec(memory_space=pltpu.SMEM)
WHOLE = pl.BlockSpec(memory_space=pltpu.VMEM)
SPARE = 16
TOKEN = jax.ShapeDtypeStruct((8, 128), F32)


def params():
    return pltpu.CompilerParams(vmem_limit_bytes=VMEM)


def tie_kernel(*refs):
    pass


def tie(values, after):
    n = len(values)
    return pl.pallas_call(
        tie_kernel,
        in_specs=[ANY] * (n + len(after)),
        out_specs=[ANY] * n,
        out_shape=[jax.ShapeDtypeStruct(v.shape, v.dtype) for v in values],
        input_output_aliases={k: k for k in range(n)},
        name="tie",
    )(*values, *after)


def resident(shape):
    return pl.BlockSpec(shape, lambda *_: (0,) * len(shape), pipeline_mode=pl.Buffered(1))


def cost(flops, nbytes):
    return pl.CostEstimate(flops=int(flops) // 16, bytes_accessed=int(nbytes) // 16, transcendentals=0)


def dot(a, b, ca, cb):
    return lax.dot_general(a, b, (((ca,), (cb,)), ((), ())), preferred_element_type=F32)


def small(value):
    return value.astype(F32).astype(BF16)


def counts_kernel(index_ref, out_ref):
    base = pl.program_id(0) * TILE
    rows = small(lax.broadcasted_iota(jnp.int32, (TILE, 128), 0))
    lanes = lax.broadcasted_iota(jnp.int32, (FANOUT, 128), 1)
    zero, one, two = (jnp.array(v, BF16) for v in (0, 1, 2))
    for c in range(0, out_ref.shape[1], 128):
        entry = small(jnp.clip(index_ref[:, c : c + 128] - base, -1, TILE))
        own = small(jnp.clip(lanes + (c - base), -1, TILE))
        total = jnp.where(own[0:1, :] == rows, two, zero)
        for s in range(FANOUT):
            total = total + jnp.where(entry[s : s + 1, :] == rows, one, zero)
        out_ref[:, c : c + 128] = total


def counts(index, tiles):
    n = index.shape[1]
    return pl.pallas_call(
        counts_kernel,
        grid=(tiles,),
        in_specs=[pl.BlockSpec((FANOUT, n), lambda i: (0, 0))],
        out_specs=pl.BlockSpec((TILE, n), lambda i: (i, 0)),
        out_shape=jax.ShapeDtypeStruct((tiles * TILE, n), BF16),
        compiler_params=params(),
        cost_estimate=cost(0, tiles * TILE * n * 16),
        name="counts",
    )(index)


def gather_own_kernel(c_ref, t_ref, o_ref):
    o_ref[...] = dot(c_ref[...], t_ref[...], 0, 0)


def gather_own(adjacency, features, live):
    h = features.shape[1]
    return pl.pallas_call(
        gather_own_kernel,
        grid=(live // TILE,),
        in_specs=[pl.BlockSpec((live, TILE), lambda i: (0, i)), resident((live, h))],
        out_specs=pl.BlockSpec((TILE, h), lambda i: (i, 0)),
        out_shape=jax.ShapeDtypeStruct((live, h), F32),
        compiler_params=params(),
        cost_estimate=cost(2 * live * live * h, live * h * 6),
        name="gather_own",
    )(adjacency, features)


def gather_bound_kernel(c_ref, part_ref, inv_ref, *refs):
    o_ref = refs[-1]
    total = part_ref[...]
    for k, ref in enumerate(refs[:-1]):
        total = total + dot(c_ref[k * BOUND : (k + 1) * BOUND, :], ref[...], 0, 0)
    o_ref[...] = (total * inv_ref[...]).astype(BF16)


def gather_bound(adjacency, part, inverse, blocks):
    live, h = part.shape
    rest = adjacency.shape[0] - live
    return pl.pallas_call(
        gather_bound_kernel,
        grid=(live // TILE,),
        in_specs=[
            pl.BlockSpec((pl.Element(rest), pl.Element(TILE)), lambda i: (live, i * TILE)),
            pl.BlockSpec((TILE, h), lambda i: (i, 0)),
            pl.BlockSpec((TILE, 1), lambda i: (i, 0)),
        ]
        + [resident((BOUND, h))] * len(blocks),
        out_specs=pl.BlockSpec((TILE, h), lambda i: (i, 0)),
        out_shape=jax.ShapeDtypeStruct((live, h), BF16),
        compiler_params=params(),
        cost_estimate=cost(2 * live * rest * h, live * h * 6),
        name="gather_bound",
    )(adjacency, part, inverse, *blocks)


def layer_kernel(at_ref, m_ref, w, ct_ref, inv_ref, o_ref, agl_ref, own_ref, gb_ref, sent_ref, b, m_all, gl_all, gb, *, tiles):
    i = pl.program_id(0)
    h = m_ref.shape[1]
    n = h // 2
    mine = pl.ds(pl.multiple_of(at_ref[1] * n, n), n)
    other = pl.ds(pl.multiple_of((1 - at_ref[1]) * n, n), n)

    @pl.when(i == 0)
    def _():
        b[...] = w[:, h:].astype(F32).T[:8, :]
        gb[...] = jnp.zeros_like(gb)

    @pl.when(i < tiles)
    def _():
        base = pl.multiple_of(i * TILE, TILE)
        rows = pl.ds(base, TILE)
        mixed = m_ref[...]
        m_all[rows, :] = mixed
        live = base + lax.broadcasted_iota(jnp.int32, (TILE, 256), 0) < at_ref[0]
        inverse = inv_ref[...]
        for j in range(0, h, 256):
            at = slice(j, j + 256)
            v = dot(mixed, w[:, at], 1, 0) + b[0:1, at]
            square = v * v
            t = jnp.tanh(v * (GELU_A + (GELU_A * GELU_B) * square))
            half = 0.5 + 0.5 * t
            active = v * half
            o_ref[:, at] = jnp.where(live, active, 0.0)
            slope = half + (active - active * half) * (2 * GELU_A + (6 * GELU_A * GELU_B) * square)
            grad = jnp.where(live, ct_ref[:, at].astype(F32) * slope, 0.0)
            gl_all[rows, at] = grad.astype(BF16)
            agl_ref[:, at] = (grad * inverse).astype(BF16)
            gb[:, at] += jnp.sum(grad.reshape(TILE // 8, 8, 256), axis=0)
        own_ref[...] = gl_all[rows, mine]

    @pl.when(i == tiles)
    def _():
        o_ref[...] = jnp.zeros_like(o_ref)

    @pl.when((i > tiles) & (i <= tiles + h // TILE))
    def _():
        at = pl.ds(pl.multiple_of((i - tiles - 1) * TILE, TILE), TILE)
        sent_ref[...] = dot(m_all[:, at], gl_all[:, other], 0, 0).astype(BF16)

    @pl.when(i > tiles + h // TILE)
    def _():
        gb_ref[...] = jnp.broadcast_to(jnp.sum(gb[:, mine], axis=0, keepdims=True), gb_ref.shape)
        sent_ref[:SPARE, :] = jnp.broadcast_to(jnp.sum(gb[:, other], axis=0, keepdims=True), (SPARE, n)).astype(BF16)


def layer(at, mixed, weight, cotangent, inverse):
    live, h = mixed.shape
    nodes, n = cotangent.shape[0], h // 2
    tiles, blocks = live // TILE, h // TILE

    def row(i, s):
        return (jnp.minimum(i, tiles - 1), 0)

    return pl.pallas_call(
        functools.partial(layer_kernel, tiles=tiles),
        grid_spec=pltpu.PrefetchScalarGridSpec(
            num_scalar_prefetch=1,
            grid=(tiles + 1 + blocks + 1,),
            in_specs=[
                pl.BlockSpec((TILE, h), row),
                resident(weight.shape),
                pl.BlockSpec((TILE, h), row),
                pl.BlockSpec((TILE, 1), row),
            ],
            out_specs=[
                pl.BlockSpec((TILE, h), lambda i, s: (jnp.minimum(i, tiles), 0)),
                pl.BlockSpec((TILE, h), row),
                pl.BlockSpec((TILE, n), row),
                resident((8, n)),
                pl.BlockSpec((TILE, n), lambda i, s: (jnp.maximum(i - tiles - 1, 0), 0)),
            ],
            scratch_shapes=[
                pltpu.VMEM((8, h), F32),
                pltpu.VMEM((live, h), BF16),
                pltpu.VMEM((live, h), BF16),
                pltpu.VMEM((8, h), F32),
            ],
        ),
        out_shape=[
            jax.ShapeDtypeStruct((nodes, h), F32),
            jax.ShapeDtypeStruct((live, h), BF16),
            jax.ShapeDtypeStruct((live, n), BF16),
            jax.ShapeDtypeStruct((8, n), F32),
            jax.ShapeDtypeStruct((h + SPARE, n), BF16),
        ],
        compiler_params=params(),
        cost_estimate=cost(3 * live * h * h, live * h * 12),
        name="layer",
    )(at, mixed, weight, cotangent, inverse)


def halves(at_ref, value, rows):
    parts = [value[k * rows : (k + 1) * rows] for k in range(4)]
    even, odd = jnp.concatenate([parts[0], parts[2]]), jnp.concatenate([parts[1], parts[3]])
    first = at_ref[4] == 0
    return jnp.where(first, even, odd), jnp.where(first, odd, even)


def spare_rows(row, n):
    rows = lax.broadcasted_iota(jnp.int32, (SPARE, n), 0)
    return jnp.where(rows == 0, row[:, :n], jnp.where(rows == 1, row[:, n:], 0.0)).astype(BF16)


def from_spare(rows):
    return jnp.concatenate([rows[0:1, :], rows[1:2, :]], axis=1).astype(F32)


def grad_weight_kernel(at_ref, m_ref, g_ref, came_ref, cb_ref, gb_ref, _, a_own, a_sent, b_own, b_sent, gb_out, *, rows):
    t = pl.program_id(0)
    last = pl.num_programs(0) - 1
    n = g_ref.shape[1] // 2
    groups = TILE // (4 * rows)

    @pl.when(t < last)
    def _():
        part = dot(m_ref[...], g_ref[...], 0, 0) + came_ref[...].astype(F32)
        for g in range(groups):
            value = part[g * 4 * rows : (g + 1) * 4 * rows]
            mine, other = halves(at_ref, value[:, :n], rows)
            at = slice(g * 2 * rows, (g + 1) * 2 * rows)
            a_own[at, :] = mine
            a_sent[at, :] = other.astype(BF16)
            here = (t * groups + g) % 2 == at_ref[2]
            at = slice(g // 2 * 4 * rows, (g // 2 + 1) * 4 * rows)

            @pl.when(here)
            def _():
                b_own[at, :] = value[:, n:]

            @pl.when(jnp.logical_not(here))
            def _():
                b_sent[at, :] = value[:, n:].astype(BF16)

    @pl.when(t == last)
    def _():
        total = gb_ref[0:1, :] + cb_ref[0:1, :].astype(F32)
        gb_out[...] = jnp.broadcast_to(total, gb_out.shape)
        a_sent[:SPARE, :] = spare_rows(total, n)


def grad_weight_share(at, mixed, low, came, bias, rows, after):
    live, h = mixed.shape
    n = low.shape[1]
    blocks = h // TILE
    single = TILE == 4 * rows
    b_rows = TILE if single else TILE // 2

    def tile(t):
        return jnp.minimum(t, blocks - 1)

    def plane(t, s):
        return (tile(t) // 2 if single else tile(t), 0)

    return pl.pallas_call(
        functools.partial(grad_weight_kernel, rows=rows),
        grid_spec=pltpu.PrefetchScalarGridSpec(
            num_scalar_prefetch=1,
            grid=(blocks + 1,),
            in_specs=[
                pl.BlockSpec((live, TILE), lambda t, s: (0, tile(t))),
                resident((live, n)),
                pl.BlockSpec((TILE, n), lambda t, s: (tile(t), 0)),
                pl.BlockSpec((SPARE, n), lambda t, s: (h // SPARE, 0)),
                resident((8, n)),
                ANY,
            ],
            out_specs=[
                pl.BlockSpec((TILE // 2, n // 2), lambda t, s: (tile(t), 0)),
                pl.BlockSpec((TILE // 2, n // 2), lambda t, s: (t, 0)),
                pl.BlockSpec((b_rows, n // 2), plane),
                pl.BlockSpec((b_rows, n // 2), plane),
                resident((8, n)),
            ],
        ),
        out_shape=[
            jax.ShapeDtypeStruct((h // 2, n // 2), F32),
            jax.ShapeDtypeStruct((h // 2 + SPARE, n // 2), BF16),
            jax.ShapeDtypeStruct((h // 2, n // 2), F32),
            jax.ShapeDtypeStruct((h // 2, n // 2), BF16),
            jax.ShapeDtypeStruct((8, n), F32),
        ],
        compiler_params=params(),
        cost_estimate=cost(2 * live * h * n, live * h * 3),
        name="grad_weight",
    )(at, mixed, low, came, came, bias, after)


def fold_kernel(at_ref, a_ref, a_came, b_ref, b_came, gb_ref, _, a_own, a_sent, b_own, b_sent, gb_out, *, rows):
    lo, two = at_ref[2], 2 * rows
    n = a_ref.shape[1]
    planes = a_ref.shape[0] // (2 * two)
    for z in range(planes):
        out = slice(z * two, (z + 1) * two)
        near = pl.ds(pl.multiple_of((2 * z + lo) * two, two), two)
        far = pl.ds(pl.multiple_of((2 * z + 1 - lo) * two, two), two)
        a_own[out, :] = a_ref[near, :] + a_came[near, :].astype(F32)
        a_sent[out, :] = (a_ref[far, :] + a_came[far, :].astype(F32)).astype(BF16)
        at = slice(z * 2 * two, (z + 1) * 2 * two)
        mine, other = halves(at_ref, b_ref[at, :] + b_came[at, :].astype(F32), rows)
        b_own[out, :] = mine
        b_sent[out, :] = other.astype(BF16)
    total = gb_ref[0:1, :] + from_spare(a_came[a_ref.shape[0] :, :])
    gb_out[...] = jnp.broadcast_to(total, gb_out.shape)
    a_sent[planes * two :, :] = spare_rows(total, n)


def fold(at, a_own, a_came, b_own, b_came, bias, rows, after):
    count, n = b_own.shape[0] // 2, b_own.shape[1]
    return pl.pallas_call(
        functools.partial(fold_kernel, rows=rows),
        in_specs=[SMEM] + [WHOLE] * 5 + [ANY],
        out_specs=[WHOLE] * 5,
        out_shape=[
            jax.ShapeDtypeStruct((count, n), F32),
            jax.ShapeDtypeStruct((count + SPARE, n), BF16),
            jax.ShapeDtypeStruct((count, n), F32),
            jax.ShapeDtypeStruct((count, n), BF16),
            jax.ShapeDtypeStruct(bias.shape, F32),
        ],
        compiler_params=params(),
        cost_estimate=cost(0, b_own.size * 9),
        name="fold",
    )(at, a_own, a_came, b_own, b_came, bias, after)


def part_kernel(at_ref, a_ref, a_came, b_ref, b_came, gb_ref, *refs, rows, planes):
    gb_out, own, *sent = refs[-1 - planes :]
    two = 2 * rows
    n = a_ref.shape[1]
    total = gb_ref[0:1, :] + from_spare(a_came[a_ref.shape[0] :, :])
    gb_out[...] = jnp.broadcast_to(total, gb_out.shape)
    for k in range(planes):
        at = pl.ds(pl.multiple_of(lax.rem(at_ref[3] + k, planes) * two, two), two)
        out = own if k == 0 else sent[k - 1]
        out[:two, :n] = (a_ref[at, :] + a_came[at, :].astype(F32)).astype(out.dtype)
        out[:two, n:] = (b_ref[at, :] + b_came[at, :].astype(F32)).astype(out.dtype)
        if k:
            out[two:, :] = jnp.broadcast_to(total, (SPARE, 2 * n)).astype(BF16)


def part_planes(at, a_own, a_came, b_own, b_came, bias, rows, planes, after):
    n = a_own.shape[1]
    return pl.pallas_call(
        functools.partial(part_kernel, rows=rows, planes=planes),
        in_specs=[SMEM] + [WHOLE] * 5 + [ANY] * len(after),
        out_specs=[WHOLE] * (1 + planes),
        out_shape=[jax.ShapeDtypeStruct(bias.shape, F32), jax.ShapeDtypeStruct((2 * rows, 2 * n), F32)]
        + [jax.ShapeDtypeStruct((2 * rows + SPARE, 2 * n), BF16)] * (planes - 1),
        compiler_params=params(),
        cost_estimate=cost(0, a_own.size * 18),
        name="part_planes",
    )(at, a_own, a_came, b_own, b_came, bias, *after)


def finish_kernel(at_ref, gb_ref, own, *refs, rows):
    came, mine_ref, other_ref = refs[:-2], refs[-2], refs[-1]
    total, bias = own[...], gb_ref[0:1, :]
    for ref in came:
        total = total + ref[: 2 * rows, :].astype(F32)
        bias = bias + ref[2 * rows : 2 * rows + 1, :].astype(F32)
    first = at_ref[1] == 0
    low, high = total[:rows], total[rows:]
    bias = jnp.broadcast_to(bias, (8, bias.shape[1]))
    mine_ref[:rows, :], other_ref[:rows, :] = jnp.where(first, low, high), jnp.where(first, high, low)
    mine_ref[rows:, :], other_ref[rows:, :] = bias, bias


def finish(at, bias, own, came, rows):
    shape = jax.ShapeDtypeStruct((rows + 8, own.shape[1]), F32)
    return pl.pallas_call(
        functools.partial(finish_kernel, rows=rows),
        in_specs=[SMEM] + [WHOLE] * (2 + len(came)),
        out_specs=[WHOLE] * 2,
        out_shape=[shape] * 2,
        compiler_params=params(),
        cost_estimate=cost(0, own.size * 8),
        name="finish",
    )(at, bias, own, *came)


def scatter_bound_kernel(c_ref, g_ref, *refs):
    outs, part, sem = refs[:-2], refs[-2], refs[-1]
    i = pl.program_id(0)
    part[i] = dot(c_ref[...], g_ref[...], 1, 0).astype(BF16)
    copies = [pltpu.make_async_copy(part.at[k], out, sem.at[k]) for k, out in enumerate(outs)]
    for k, copy in enumerate(copies):

        @pl.when(i == k)
        def _():
            copy.start()

    @pl.when(i == len(outs) - 1)
    def _():
        for copy in copies:
            copy.wait()


def scatter_bound(adjacency, grads):
    live, h = grads.shape
    blocks = (adjacency.shape[0] - live) // BOUND
    return pl.pallas_call(
        scatter_bound_kernel,
        grid=(blocks,),
        in_specs=[pl.BlockSpec((BOUND, live), lambda i: (i + live // BOUND, 0)), resident((live, h))],
        out_specs=[ANY] * blocks,
        out_shape=[jax.ShapeDtypeStruct((BOUND, h), BF16)] * blocks,
        scratch_shapes=[pltpu.VMEM((blocks, BOUND, h), BF16), pltpu.SemaphoreType.DMA((blocks,))],
        compiler_params=params(),
        cost_estimate=cost(2 * blocks * BOUND * live * h, live * h * 4),
        name="scatter_bound",
    )(adjacency, grads)


def grad_rows_kernel(c_ref, g_ref, w_hbm, *refs, low, tiles):
    o_ref, lead_ref, w, sem = refs[-4:]
    i = pl.program_id(0)
    copy = pltpu.make_async_copy(w_hbm.at[:, pl.ds(0, w.shape[1])], w, sem)

    @pl.when(i == 0)
    def _():
        copy.start()

    if low:

        @pl.when(i == 0)
        def _():
            copy.wait()

    @pl.when(low + i < tiles)
    def _():
        total = dot(c_ref[...], g_ref[...], 1, 0)
        if low == 0:

            @pl.when(i == 0)
            def _():
                lead_ref[...] = total
                copy.wait()

        @pl.when(low + i > 0)
        def _():
            o_ref[...] = dot(total.astype(BF16), w[...], 1, 1)

    if low:
        lead_ref[...] = jnp.zeros_like(lead_ref)

    @pl.when(low + i == tiles)
    def _():
        o_ref[...] = jnp.zeros_like(o_ref)


def grad_rows(adjacency, grads, weight, nodes, low, high, before, after):
    live, h = grads.shape
    tiles = live // TILE
    extra = [] if before is None else [before]
    return pl.pallas_call(
        functools.partial(grad_rows_kernel, low=low, tiles=tiles),
        grid=(high - low,),
        in_specs=[
            pl.BlockSpec((TILE, live), lambda i: (jnp.minimum(low + i, tiles - 1), 0)),
            resident((live, h)),
            ANY,
        ]
        + [ANY] * (len(extra) + len(after)),
        out_specs=[pl.BlockSpec((TILE, h), lambda i: (low + i, 0)), resident((8, 128) if low else (TILE, h))],
        out_shape=[jax.ShapeDtypeStruct((nodes, h), F32), TOKEN if low else jax.ShapeDtypeStruct((TILE, h), F32)],
        scratch_shapes=[pltpu.VMEM((h, h), BF16), pltpu.SemaphoreType.DMA],
        input_output_aliases={3: 0} if extra else {},
        compiler_params=params(),
        cost_estimate=cost((2 * live + 2 * h) * (high - low) * TILE * h, live * h * 8),
        name="grad_rows",
    )(adjacency, grads, weight, *extra, *after)


def back_kernel(a_ref, b_ref, c_ref, d_ref, _, o_ref, p_ref):
    o_ref[...] = (a_ref[...].astype(F32) + b_ref[...].astype(F32)).astype(BF16)
    p_ref[...] = (c_ref[...].astype(F32) + d_ref[...].astype(F32)).astype(BF16)


def back(a, b, c, d, after):
    block = pl.BlockSpec((64, a.shape[1]), lambda i: (i, 0))
    return pl.pallas_call(
        back_kernel,
        grid=(a.shape[0] // 64,),
        in_specs=[block] * 4 + [ANY],
        out_specs=[block] * 2,
        out_shape=[jax.ShapeDtypeStruct(a.shape, BF16)] * 2,
        compiler_params=params(),
        cost_estimate=cost(0, a.size * 12),
        name="back",
    )(a, b, c, d, after)


def grad_lead_kernel(lead_ref, *refs):
    came, (w_ref, _, o_ref, total) = refs[:3], refs[3:]

    @pl.when(pl.program_id(0) == 0)
    def _():
        value = lead_ref[...]
        for ref in came:
            value = value + ref[...].astype(F32)
        total[...] = value.astype(BF16)

    o_ref[...] = dot(total[...], w_ref[...], 1, 1)


def grad_lead(lead, came, weight, grads):
    rows, h = lead.shape
    return pl.pallas_call(
        grad_lead_kernel,
        grid=(4,),
        in_specs=[resident((rows, h))] * 4 + [pl.BlockSpec((h // 4, h), lambda i: (i, 0)), ANY],
        out_specs=pl.BlockSpec((rows, h // 4), lambda i: (0, i)),
        out_shape=jax.ShapeDtypeStruct(grads.shape, F32),
        scratch_shapes=[pltpu.VMEM((rows, h), BF16)],
        input_output_aliases={5: 0},
        compiler_params=params(),
        cost_estimate=cost(2 * rows * h * h, h * h * 2),
        name="grad_lead",
    )(lead, *came, weight, grads)


def body(features, weight, bias, neighbours, degrees, cluster_sizes, cotangent):
    axes = ("blk", "wa")
    n_blk, n_wa = lax.axis_size("blk"), lax.axis_size("wa")
    devices, n_hi = n_blk * n_wa, n_blk // 4
    blk, wa = lax.axis_index("blk"), lax.axis_index("wa")
    core, lo, hi = blk % 2, (blk // 2) % 2, blk // 4
    nodes, h = features.shape
    share, n = h // devices, h // 2
    live = min(nodes, -(-(-(-CMAX // n_wa)) // TILE) * TILE)

    def permute(value, target):
        pairs = [(b * n_wa + w, target(b, w)) for b in range(n_blk) for w in range(n_wa)]
        return lax.ppermute(value, axes, [(s, b * n_wa + w) for s, (b, w) in pairs])

    def swap_wa(value):
        return permute(value, lambda b, w: (b, 1 - w))

    def swap_core(value):
        return permute(value, lambda b, w: (b ^ 1, w))

    def swap_outer(value):
        return permute(value, lambda b, w: ((b + (1 if b % 2 else -1)) % n_blk, w))

    def swap_lo(value):
        return permute(value, lambda b, w: (b ^ 2, w))

    def rotate_hi(value, k):
        return permute(value, lambda b, w: ((b + 4 * k) % n_blk, w))

    sheet = jnp.concatenate([weight, jnp.broadcast_to(bias[:, None], (share, 128))], axis=1)
    sheet = lax.all_gather(sheet, axes, axis=0, tiled=True)

    leading = features[:BOUND]
    partner = swap_wa(leading)
    outer_same = swap_outer(leading)
    inner_same = swap_core(leading)
    live_count = (cluster_sizes[0] - wa + n_wa - 1) // n_wa
    table = neighbours[:, :live]
    beyond = table - nodes
    segment, within = beyond // (n_wa * BOUND), beyond % (n_wa * BOUND)
    same = within // BOUND == wa
    row = within % BOUND
    side = jnp.where(same, 0, BOUND) + row
    inner = (segment == 2) == (core == 0)
    away = jnp.where(inner, live + BOUND, live + BOUND + n_wa * BOUND) + side
    home = jnp.where(same, row, live + row)
    index = jnp.where(table < nodes, table, jnp.where(segment == 0, home, away))
    valid = jnp.arange(FANOUT, dtype=jnp.int32)[:, None] < degrees[None, :live]
    index = jnp.where(valid, index, -1)
    inverse = (1.0 / (degrees[:live].astype(F32) + 1.0))[:, None]
    at = jnp.stack([live_count, core, lo, hi, wa]).astype(jnp.int32)

    adjacency = counts(index, (live + (1 + 2 * n_wa) * BOUND) // TILE)
    partner, outer_same, inner_same = tie([partner, outer_same, inner_same], [adjacency])
    inner_other = swap_core(partner)
    outer_other = swap_wa(outer_same)
    blocks = (partner, inner_same, inner_other, outer_same, outer_other)
    part = gather_own(adjacency, features, live)
    mixed = gather_bound(adjacency, part, inverse, blocks)
    output, grads, own_low, bias_sum, sent = layer(at, mixed, sheet, cotangent, inverse)
    came = swap_core(sent)

    own_bound, inner_same_g, inner_other_g, outer_same_g, outer_other_g = scatter_bound(adjacency, grads)
    outer_came, own_came, inner_came = swap_wa(outer_other_g), swap_core(inner_other_g), swap_core(inner_same_g)

    a, a_sent, b, b_sent, bias_sum = grad_weight_share(at, mixed, own_low, came, bias_sum, share, own_bound)
    a_came, b_came = swap_wa(a_sent), swap_lo(b_sent)
    split, tiles = live // TILE // 2, -(-nodes // TILE)
    grad_features, lead = grad_rows(adjacency, grads, sheet, nodes, 0, split, None, [bias_sum])
    outer_back, own_back = back(outer_same_g, outer_came, own_bound, own_came, lead)
    returned = (inner_came, swap_wa(own_back), swap_outer(outer_back))
    a, a_sent, b, b_sent, bias_sum = fold(at, a, a_came, b, b_came, bias_sum, share, own_back)
    a_came, b_came = swap_lo(a_sent), swap_wa(b_sent)
    grad_features, token = grad_rows(adjacency, grads, sheet, nodes, split, tiles, grad_features, [bias_sum])
    bias_sum, own, *rest = part_planes(
        at, a, a_came, b, b_came, bias_sum, share, n_hi, [token, returned[1]]
    )
    rest = [rotate_hi(value, k + 1) for k, value in enumerate(rest)]
    grad_features = grad_lead(lead, returned, sheet, grad_features)
    mine, other = finish(at, bias_sum, own, rest, share)
    other = swap_core(other)
    pair = jnp.where(core == 0, jnp.concatenate([mine, other], axis=1), jnp.concatenate([other, mine], axis=1))
    grad_weight = pair[:share]
    grad_bias = lax.dynamic_slice_in_dim(pair[share], (blk * n_wa + wa) * share, share)
    return (output, grad_features, grad_weight, grad_bias)


def solution(mesh):
    return jax.shard_map(
        body,
        mesh=mesh,
        in_specs=(
            P(("blk", "wa"), None),
            P(("blk", "wa"), None),
            P(("blk", "wa")),
            P(None, ("blk", "wa")),
            P(("blk", "wa")),
            P("blk"),
            P(("blk", "wa"), None),
        ),
        out_specs=(
            P(("blk", "wa"), None),
            P(("blk", "wa"), None),
            P(("blk", "wa"), None),
            P(("blk", "wa")),
        ),
        check_vma=False,
    )
```

time: 313 us -> 298 us (0.952)
  Pallas kernels: 157 us -> 178 us
  waiting for transfers between devices: 89.2 us -> 73.1 us
  starting transfers between devices: 25.9 us -> 13.5 us
  other arithmetic: 15.3 us -> 3.49 us
  local copies, waits for them, and re-layouts: 8.13 us -> 14.3 us
    ppermute x29 -> x19, starting transfers between devices: 25.9 us -> 13.4 us  [permute(): return lax.ppermute(value, axes, [(s, b * n_wa + w) for s, (b, w) in pairs])]
    ppermute x29 -> x19, waiting for transfers between devices: 70 us -> 57.6 us  [permute(): return lax.ppermute(value, axes, [(s, b * n_wa + w) for s, (b, w) in pairs])]
    add x11 -> x0, other arithmetic: 11.1 us -> none  [the longest x1 6.11 us: body(): kept + sent.astype(F32)]
    pallas_call x5 -> x9, Pallas kernels: 64.5 us -> 75.5 us  [the longest x2 37.6 us: grad_rows(): pl.pallas_call(functools.partial(grad_rows_kernel, low=low, tiles=tiles),...]
    pallas_call x1, Pallas kernels: 28.9 us -> 39 us  [layer(): pl.pallas_call(functools.partial(layer_kernel, tiles=tiles), grid_spec=pl...]
    unnamed x24 -> x34, local copies, waits for them, and re-layouts: 2.72 us -> 8.04 us
  transfers between devices with their start and end apart: 30 -> 20, of which waited for: 17 -> 9; matrix products, arithmetic and copies ran while one was open for 4% -> 2% of each run, Pallas kernels for 37% -> 47%
where the time goes in v2:
time: 298 us; the launch traced here: 297 us
  Pallas kernels  178 us (60%)
  waiting for transfers between devices  73.1 us (25%)
  between operations  14.9 us (5%)
  local copies, waits for them, and re-layouts  14.3 us (5%)
  starting transfers between devices  13.5 us (5%)
  other arithmetic  3.49 us (1%)
    ppermute x19, waiting for transfers between devices, permute(): return lax.ppermute(value, axes, [(s, b * n_wa + w) for s, (b, w) in pairs])  57.6 us
    pallas_call x1, Pallas kernels, layer(): pl.pallas_call(functools.partial(layer_kernel, tiles=tiles), grid_spec=pl...  39 us
    pallas_call x2, Pallas kernels, grad_rows(): pl.pallas_call(functools.partial(grad_rows_kernel, low=low, tiles=tiles),...  37.6 us
    pallas_call x1, Pallas kernels, counts(): pl.pallas_call(counts_kernel, grid=(tiles,), in_specs=[pl.BlockSpec((FANO...  17.3 us
    pallas_call x1, Pallas kernels, gather_bound(): pl.pallas_call(gather_bound_kernel, grid=(live // TILE,), in_specs=[pl.Bl...  16.9 us
    pallas_call x1, Pallas kernels, gather_own(): pl.pallas_call(gather_own_kernel, grid=(live // TILE,), in_specs=[pl.Bloc...  15.6 us
    all_gather x1, waiting for transfers between devices, body(): sheet = lax.all_gather(sheet, axes, axis=0, tiled=True)  15.5 us
    pallas_call x1, Pallas kernels, grad_weight_share(): pl.pallas_call(functools.partial(grad_weight_kernel, rows=rows), grid_spe...  14.9 us
  transfers between devices with their start and end apart: 20, of which 9 were waited for; matrix products, arithmetic and copies ran while one was open for 2% of the time, Pallas kernels for 47%

profile of v2, /device:TPU:11, one launch (start us, length us, event | category | flops | bytes accessed | tf_op | source)
XLA Modules:
  0.0 296.8 jit_solution(13233317835207995393)
XLA Ops:
  7.9 1.7 pad_maximum_fusion
  9.6 2.3 slice.18
  12.6 1.1 collective-permute-start.1
  14.0 1.8 fusion.2.index_ref
  15.8 17.3 %counts.1.c_ref.refs_3_ = bf16[2816,1536]{1,0:T(8,128)(2,1)} custom-call(s32[16,1536]{1,0:T(8,128)} %fusion.2.index_ref), custom_call_target="tpu_custom_call" | custom-call | bytes 4325376 | tf_op jit(solution)/shard_map/counts/pallas_call | solution.py:81
  33.1 7.5 %collective-permute-done.1.refs_1_ = bf16[256,2048]{1,0:T(8,128)(2,1)S(1)} collective-permute-done((bf16[256,2048]{1,0:T(8,128)(2,1)}, bf16[256,2048]{1,0:T(8,128)(2,1)S(1)}, u32[]{:S(2)}, u32[]{:S(2)}) %collective-permute-start.1) | collective-permute-done | bytes 1048608 | tf_op jit(solution)/shard_map/ppermute | solution.py:577
  43.5 1.1 broadcast_in_dim.27.inv_ref
  45.3 15.6 %gather_own.1.part_ref = f32[1536,2048]{1,0:T(8,128)} custom-call(bf16[2816,1536]{1,0:T(8,128)(2,1)} %counts.1.c_ref.refs_3_, bf16[1664,2048]{1,0:T(8,128)(2,1)} %t_ref.1), custom_call_target="tpu_custom_call" | custom-call | flops 603979776 | bytes 1179648 | tf_op jit(solution)/shard_map/gather_own/pallas_call | solution.py:99
  60.9 13.9 %collective-permute-done.4.refs_4_ = bf16[256,2048]{1,0:T(8,128)(2,1)S(1)} collective-permute-done((bf16[256,2048]{1,0:T(8,128)(2,1)}, bf16[256,2048]{1,0:T(8,128)(2,1)S(1)}, u32[]{:S(2)}, u32[]{:S(2)}) %collective-permute-start.4) | collective-permute-done | bytes 1048608 | tf_op jit(solution)/shard_map/ppermute | solution.py:577
  75.9 16.9 %gather_bound.1.m_ref = bf16[1536,2048]{1,0:T(8,128)(2,1)} custom-call(bf16[2816,1536]{1,0:T(8,128)(2,1)} %counts.1.c_ref.refs_3_, f32[1536,2048]{1,0:T(8,128)} %gather_own.1.part_ref, f32[1536,1]{1,0:T(8,128)} %broadcast_in_dim.27.inv_ref, bf16[256,2048]{1,0:T(8,128)(2,1)} %get-tuple-element.40.refs_0_, bf16[256,2048]{1,0:T(8,128)(2,1)} %get-tuple-element.41.refs_1_, ...), custom_call_target="tpu_custom_call" | custom-call | flops 503316480 | bytes 1179648 | tf_op jit(solution)/shard_map/gather_bound/pallas_call | solution.py:122
  92.8 15.5 %all-gather.2.cloned.1.call-done.w.w_hbm.refs_3_ = bf16[2048,2176]{1,0:T(8,128)(2,1)} async-done(((bf16[64,2176]{1,0:T(8,128)(2,1)}), bf16[2048,2176]{1,0:T(8,128)(2,1)}) %all-gather.2.cloned.1.call-update) | async-done | bytes 8912912 | tf_op jit(solution)/shard_map/all_gather | solution.py:595
  108.3 39.0 %layer.1 = (f32[1664,2048]{1,0:T(8,128)}, bf16[1536,2048]{1,0:T(8,128)(2,1)}, bf16[1536,1024]{1,0:T(8,128)(2,1)}, f32[8,1024]{1,0:T(8,128)}, bf16[2064,1024]{1,0:T(8,128)(2,1)}) custom-call(s32[5]{0:T(128)} %stack.23.at_ref, bf16[1536,2048]{1,0:T(8,128)(2,1)} %gather_bound.1.m_ref, bf16[2048,2176]{1,0:T(8,128)(2,1)} %all-gather.2.cloned.1.call-done.w.w_hbm.refs_3_, ...), custom_call_target="tpu_custom_call" | custom-call | flops 1207959552 | bytes 2359296 | tf_op jit(solution)/shard_map/layer/pallas_call | solution.py:197
  147.6 13.1 %scatter_bound.1 = (bf16[256,2048]{1,0:T(8,128)(2,1)}, bf16[256,2048]{1,0:T(8,128)(2,1)}, bf16[256,2048]{1,0:T(8,128)(2,1)}, bf16[256,2048]{1,0:T(8,128)(2,1)}, bf16[256,2048]{1,0:T(8,128)(2,1)}) custom-call(bf16[2816,1536]{1,0:T(8,128)(2,1)} %counts.1.c_ref.refs_3_, bf16[1536,2048]{1,0:T(8,128)(2,1)} %get-tuple-element.44.g_ref), custom_call_target="tpu_custom_call" | custom-call | flops 503316480 | bytes 786432 | tf_op jit(solution)/shard_map/scatter_bound/pallas_call | solution.py:444
  161.8 14.9 %grad_weight.1 = (f32[1024,512]{1,0:T(8,128)}, bf16[1040,512]{1,0:T(8,128)(2,1)}, f32[1024,512]{1,0:T(8,128)}, bf16[1024,512]{1,0:T(8,128)(2,1)}, f32[8,1024]{1,0:T(8,128)}) custom-call(s32[5]{0:T(128)} %stack.23.at_ref, bf16[1536,2048]{1,0:T(8,128)(2,1)} %gather_bound.1.m_ref, bf16[1536,1024]{1,0:T(8,128)(2,1)} %get-tuple-element.45.g_ref, ...), custom_call_target="tpu_custom_call" | custom-call | flops 402653184 | bytes 589824 | tf_op jit(solution)/shard_map/grad_weight/pallas_call | solution.py:297
  176.7 1.1 collective-permute-start.11
  178.2 16.9 %grad_rows.2 = (f32[1664,2048]{1,0:T(8,128)}, f32[256,2048]{1,0:T(8,128)}) custom-call(bf16[2816,1536]{1,0:T(8,128)(2,1)} %counts.1.c_ref.refs_3_, bf16[1536,2048]{1,0:T(8,128)(2,1)} %get-tuple-element.44.g_ref, bf16[2048,2176]{1,0:T(8,128)(2,1)} %all-gather.2.cloned.1.call-done.w.w_hbm.refs_3_, f32[8,1024]{1,0:T(8,128)} %get-tuple-element.49.refs_0_.gb_ref), custom_call_target="tpu_custom_call" | custom-call | flops 704643072 | bytes 1572864 | tf_op jit(solution)/shard_map/grad_rows/pallas_call | solution.py:498
  196.5 4.2 %back.1 = (bf16[256,2048]{1,0:T(8,128)(2,1)}, bf16[256,2048]{1,0:T(8,128)(2,1)}) custom-call(bf16[256,2048]{1,0:T(8,128)(2,1)} %get-tuple-element.52.a_ref, bf16[256,2048]{1,0:T(8,128)(2,1)} %copy-done.9, bf16[256,2048]{1,0:T(8,128)(2,1)} %get-tuple-element.48._.c_ref, bf16[256,2048]{1,0:T(8,128)(2,1)} %copy-done.10, f32[256,2048]{1,0:T(8,128)} %get-tuple-element.50._.lead_ref), custom_call_target="tpu_custom_call" | custom-call | bytes 393216 | tf_op jit(solution)/shard_map/back/pallas_call | solution.py:524
  200.6 1.2 collective-permute-start.9
  202.5 5.8 %collective-permute-done.11.a_came = bf16[1040,512]{1,0:T(8,128)(2,1)S(1)} collective-permute-done((bf16[1040,512]{1,0:T(8,128)(2,1)}, bf16[1040,512]{1,0:T(8,128)(2,1)S(1)}, u32[]{:S(2)}, u32[]{:S(2)}) %collective-permute-start.11) | collective-permute-done | bytes 1064992 | tf_op jit(solution)/shard_map/ppermute | solution.py:577
  208.3 1.0 copy-done.4
  209.3 4.9 %fold.1 = (f32[512,512]{1,0:T(8,128)}, bf16[528,512]{1,0:T(8,128)(2,1)}, f32[512,512]{1,0:T(8,128)}, bf16[512,512]{1,0:T(8,128)(2,1)}, f32[8,1024]{1,0:T(8,128)}) custom-call(s32[5]{0:T(128)} %stack.23.at_ref, f32[1024,512]{1,0:T(8,128)} %get-tuple-element.58.a_ref, bf16[1040,512]{1,0:T(8,128)(2,1)} %copy-done.4, f32[1024,512]{1,0:T(8,128)} %get-tuple-element.60.b_ref, ...), custom_call_target="tpu_custom_call" | custom-call | bytes 294912 | tf_op jit(solution)/shard_map/fold/pallas_call | solution.py:352
  214.7 1.2 collective-permute-start.14
  215.9 2.3 collective-permute-start.6
  218.4 20.7 %grad_rows.3 = (f32[1664,2048]{1,0:T(8,128)}, f32[8,128]{1,0:T(8,128)}) custom-call(bf16[2816,1536]{1,0:T(8,128)(2,1)} %counts.1.c_ref.refs_3_, bf16[1536,2048]{1,0:T(8,128)(2,1)} %get-tuple-element.44.g_ref, bf16[2048,2176]{1,0:T(8,128)(2,1)} %all-gather.2.cloned.1.call-done.w.w_hbm.refs_3_, ...), custom_call_target="tpu_custom_call", output_to_operand_aliasing={{0}: (3, {})} | custom-call | flops 939524096 | bytes 1572864 | tf_op jit(solution)/shard_map/grad_rows/pallas_call | solution.py:498
  239.1 3.0 %collective-permute-done.14.b_came = bf16[512,512]{1,0:T(8,128)(2,1)} collective-permute-done((bf16[512,512]{1,0:T(8,128)(2,1)}, bf16[512,512]{1,0:T(8,128)(2,1)}, u32[]{:S(2)}, u32[]{:S(2)}) %collective-permute-start.14) | collective-permute-done | bytes 524320 | tf_op jit(solution)/shard_map/ppermute | solution.py:577
  242.9 3.1 %part_planes.1 = (f32[8,1024]{1,0:T(8,128)}, f32[128,1024]{1,0:T(8,128)}, bf16[144,1024]{1,0:T(8,128)(2,1)}, bf16[144,1024]{1,0:T(8,128)(2,1)}, bf16[144,1024]{1,0:T(8,128)(2,1)}) custom-call(s32[5]{0:T(128)} %stack.23.at_ref, f32[512,512]{1,0:T(8,128)} %get-tuple-element.64.a_ref, bf16[528,512]{1,0:T(8,128)(2,1)} %copy-done.11, ...), custom_call_target="tpu_custom_call" | custom-call | bytes 294912 | tf_op jit(solution)/shard_map/part_planes/pallas_call | solution.py:386
  246.8 1.6 collective-permute-start.16
  248.4 5.3 %collective-permute-done.15.refs_0_ = bf16[144,1024]{1,0:T(8,128)(2,1)S(1)} collective-permute-done((bf16[144,1024]{1,0:T(8,128)(2,1)}, bf16[144,1024]{1,0:T(8,128)(2,1)S(1)}, u32[]{:S(2)}, u32[]{:S(2)}) %collective-permute-start.15) | collective-permute-done | bytes 294944 | tf_op jit(solution)/shard_map/ppermute | solution.py:577
  253.7 17.6 %collective-permute-done.16.refs_1_ = bf16[144,1024]{1,0:T(8,128)(2,1)S(1)} collective-permute-done((bf16[144,1024]{1,0:T(8,128)(2,1)}, bf16[144,1024]{1,0:T(8,128)(2,1)S(1)}, u32[]{:S(2)}, u32[]{:S(2)}) %collective-permute-start.16) | collective-permute-done | bytes 294944 | tf_op jit(solution)/shard_map/ppermute | solution.py:577
  271.3 3.8 %collective-permute-done.17.refs_2_ = bf16[144,1024]{1,0:T(8,128)(2,1)S(1)} collective-permute-done((bf16[144,1024]{1,0:T(8,128)(2,1)}, bf16[144,1024]{1,0:T(8,128)(2,1)S(1)}, u32[]{:S(2)}, u32[]{:S(2)}) %collective-permute-start.17) | collective-permute-done | bytes 294944 | tf_op jit(solution)/shard_map/ppermute | solution.py:577
  275.8 2.3 finish.1
  279.9 8.6 %grad_lead.1 = f32[1664,2048]{1,0:T(8,128)} custom-call(f32[256,2048]{1,0:T(8,128)} %get-tuple-element.50._.lead_ref, bf16[256,2048]{1,0:T(8,128)(2,1)} %copy-done.7, bf16[256,2048]{1,0:T(8,128)(2,1)} %copy-done, bf16[256,2048]{1,0:T(8,128)(2,1)} %copy-done.8, ...), custom_call_target="tpu_custom_call", output_to_operand_aliasing={{}: (5, {})} | custom-call | flops 134217728 | bytes 524288 | tf_op jit(solution)/shard_map/grad_lead/pallas_call | solution.py:551
  (68 shorter events, 15.7 us)
Async XLA Ops:
  7.2 101.1 %all-gather.2.cloned.1.call-start = ((), (), s32[]{:S(2)}) async-start(), calls=%async_computation | async-start | bytes 9191424 | tf_op jit(solution)/shard_map/all_gather | solution.py:595
  12.0 21.2 %collective-permute-start.2 = (bf16[256,2048]{1,0:T(8,128)(2,1)}, bf16[256,2048]{1,0:T(8,128)(2,1)S(1)}, u32[]{:S(2)}, u32[]{:S(2)}) collective-permute-start(bf16[256,2048]{1,0:T(8,128)(2,1)} %slice.18), channel_id=1, source_target_pairs={{0,2},{1,3},{2,0},{3,1},{4,6},{5,7},{6,4},{7,5},{8,10},{9,11},{10,... | collective-permute-start | bytes 3145736 | tf_op jit(solution)/shard_map/ppermute | solution.py:577
  12.6 28.0 %collective-permute-start.1 = (bf16[256,2048]{1,0:T(8,128)(2,1)}, bf16[256,2048]{1,0:T(8,128)(2,1)S(1)}, u32[]{:S(2)}, u32[]{:S(2)}) collective-permute-start(bf16[256,2048]{1,0:T(8,128)(2,1)} %slice.18), channel_id=1, source_target_pairs={{0,30},{1,31},{2,4},{3,5},{4,2},{5,3},{6,8},{7,9},{8,6},{9,7},{10,... | collective-permute-start | bytes 3145736 | tf_op jit(solution)/shard_map/ppermute | solution.py:577
  13.8 26.8 %collective-permute-start = (bf16[256,2048]{1,0:T(8,128)(2,1)}, bf16[256,2048]{1,0:T(8,128)(2,1)S(1)}, u32[]{:S(2)}, u32[]{:S(2)}) collective-permute-start(bf16[256,2048]{1,0:T(8,128)(2,1)} %slice.18), channel_id=1, source_target_pairs={{0,1},{1,0},{2,3},{3,2},{4,5},{5,4},{6,7},{7,6},{8,9},{9,8},{10,11... | collective-permute-start | bytes 3145736 | tf_op jit(solution)/shard_map/ppermute | solution.py:577
  33.1 10.4 %copy-start.16 = (s32[1664]{0:T(1024)S(1)}, s32[1664]{0:T(1024)}, u32[]{:S(2)}) copy-start(s32[1664]{0:T(1024)} %param.11) | copy-start | bytes 19972
  33.1 7.5 %copy-start.1 = (bf16[256,2048]{1,0:T(8,128)(2,1)}, bf16[256,2048]{1,0:T(8,128)(2,1)S(1)}, u32[]{:S(2)}) copy-start(bf16[256,2048]{1,0:T(8,128)(2,1)S(1)} %collective-permute-done.2.refs_2_) | copy-start | bytes 3145732
  42.5 18.4 %collective-permute-start.3 = (bf16[256,2048]{1,0:T(8,128)(2,1)}, bf16[256,2048]{1,0:T(8,128)(2,1)S(1)}, u32[]{:S(2)}, u32[]{:S(2)}) collective-permute-start(bf16[256,2048]{1,0:T(8,128)(2,1)} %get-tuple-element.40.refs_0_), channel_id=1, source_target_pairs={{0,2},{1,3},{2,0},{3,1},{4,6},{5,7},{6,4},{7,5},{8,10},{9,11},{10,... | collective-permute-start | bytes 3145736 | tf_op jit(solution)/shard_map/ppermute | solution.py:577
  42.5 32.3 %collective-permute-start.4 = (bf16[256,2048]{1,0:T(8,128)(2,1)}, bf16[256,2048]{1,0:T(8,128)(2,1)S(1)}, u32[]{:S(2)}, u32[]{:S(2)}) collective-permute-start(bf16[256,2048]{1,0:T(8,128)(2,1)} %get-tuple-element.42.refs_3_), channel_id=1, source_target_pairs={{0,1},{1,0},{2,3},{3,2},{4,5},{5,4},{6,7},{7,6},{8,9},{9,8},{10,11... | collective-permute-start | bytes 3145736 | tf_op jit(solution)/shard_map/ppermute | solution.py:577
  60.9 13.9 %copy-start.5 = (bf16[256,2048]{1,0:T(8,128)(2,1)}, bf16[256,2048]{1,0:T(8,128)(2,1)S(1)}, u32[]{:S(2)}) copy-start(bf16[256,2048]{1,0:T(8,128)(2,1)S(1)} %collective-permute-done.3.refs_2_) | copy-start | bytes 3145732
  74.9 1.0 copy-start.6
  147.3 14.5 %collective-permute-start.5 = (bf16[2064,1024]{1,0:T(8,128)(2,1)}, bf16[2064,1024]{1,0:T(8,128)(2,1)}, u32[]{:S(2)}, u32[]{:S(2)}) collective-permute-start(bf16[2064,1024]{1,0:T(8,128)(2,1)} %get-tuple-element.46), channel_id=1, source_target_pairs={{0,2},{1,3},{2,0},{3,1},{4,6},{5,7},{6,4},{7,5},{8,10},{9,11},{10,... | collective-permute-start | bytes 12681224 | tf_op jit(solution)/shard_map/ppermute | solution.py:577
  160.7 34.4 %collective-permute-start.7 = (bf16[256,2048]{1,0:T(8,128)(2,1)}, bf16[256,2048]{1,0:T(8,128)(2,1)S(1)}, u32[]{:S(2)}, u32[]{:S(2)}) collective-permute-start(bf16[256,2048]{1,0:T(8,128)(2,1)} %get-tuple-element.53), channel_id=1, source_target_pairs={{0,1},{1,0},{2,3},{3,2},{4,5},{5,4},{6,7},{7,6},{8,9},{9,8},{10,11... | collective-permute-start | bytes 3145736 | tf_op jit(solution)/shard_map/ppermute | solution.py:577
  161.3 33.9 %collective-permute-start.8 = (bf16[256,2048]{1,0:T(8,128)(2,1)}, bf16[256,2048]{1,0:T(8,128)(2,1)S(1)}, u32[]{:S(2)}, u32[]{:S(2)}) collective-permute-start(bf16[256,2048]{1,0:T(8,128)(2,1)} %get-tuple-element.54), channel_id=1, source_target_pairs={{0,2},{1,3},{2,0},{3,1},{4,6},{5,7},{6,4},{7,5},{8,10},{9,11},{10,... | collective-permute-start | bytes 3145736 | tf_op jit(solution)/shard_map/ppermute | solution.py:577
  176.7 31.6 %collective-permute-start.11 = (bf16[1040,512]{1,0:T(8,128)(2,1)}, bf16[1040,512]{1,0:T(8,128)(2,1)S(1)}, u32[]{:S(2)}, u32[]{:S(2)}) collective-permute-start(bf16[1040,512]{1,0:T(8,128)(2,1)} %get-tuple-element.59), channel_id=1, source_target_pairs={{0,1},{1,0},{2,3},{3,2},{4,5},{5,4},{6,7},{7,6},{8,9},{9,8},{10,11... | collective-permute-start | bytes 3194888 | tf_op jit(solution)/shard_map/ppermute | solution.py:577
  177.7 24.8 %collective-permute-start.12 = (bf16[1024,512]{1,0:T(8,128)(2,1)}, bf16[1024,512]{1,0:T(8,128)(2,1)}, u32[]{:S(2)}, u32[]{:S(2)}) collective-permute-start(bf16[1024,512]{1,0:T(8,128)(2,1)} %get-tuple-element.61), channel_id=1, source_target_pairs={{0,4},{1,5},{2,6},{3,7},{4,0},{5,1},{6,2},{7,3},{8,12},{9,13},{10,... | collective-permute-start | bytes 3145736 | tf_op jit(solution)/shard_map/ppermute | solution.py:577
  195.2 1.0 copy-start.9
  195.2 1.3 copy-start.10
  200.6 38.4 %collective-permute-start.9 = (bf16[256,2048]{1,0:T(8,128)(2,1)}, bf16[256,2048]{1,0:T(8,128)(2,1)S(1)}, u32[]{:S(2)}, u32[]{:S(2)}) collective-permute-start(bf16[256,2048]{1,0:T(8,128)(2,1)} %get-tuple-element.55._), channel_id=1, source_target_pairs={{0,1},{1,0},{2,3},{3,2},{4,5},{5,4},{6,7},{7,6},{8,9},{9,8},{10,11... | collective-permute-start | bytes 3145736 | tf_op jit(solution)/shard_map/ppermute | solution.py:577
  208.3 1.0 copy-start.4
  214.2 27.9 %collective-permute-start.13 = (bf16[528,512]{1,0:T(8,128)(2,1)}, bf16[528,512]{1,0:T(8,128)(2,1)S(1)}, u32[]{:S(2)}, u32[]{:S(2)}) collective-permute-start(bf16[528,512]{1,0:T(8,128)(2,1)} %get-tuple-element.65), channel_id=1, source_target_pairs={{0,4},{1,5},{2,6},{3,7},{4,0},{5,1},{6,2},{7,3},{8,12},{9,13},{10,... | collective-permute-start | bytes 1622024 | tf_op jit(solution)/shard_map/ppermute | solution.py:577
  214.7 27.4 %collective-permute-start.14 = (bf16[512,512]{1,0:T(8,128)(2,1)}, bf16[512,512]{1,0:T(8,128)(2,1)}, u32[]{:S(2)}, u32[]{:S(2)}) collective-permute-start(bf16[512,512]{1,0:T(8,128)(2,1)} %get-tuple-element.67), channel_id=1, source_target_pairs={{0,1},{1,0},{2,3},{3,2},{4,5},{5,4},{6,7},{7,6},{8,9},{9,8},{10,11... | collective-permute-start | bytes 1572872 | tf_op jit(solution)/shard_map/ppermute | solution.py:577
  215.9 62.6 %collective-permute-start.6 = (bf16[256,2048]{1,0:T(8,128)(2,1)}, bf16[256,2048]{1,0:T(8,128)(2,1)S(1)}, u32[]{:S(2)}, u32[]{:S(2)}) collective-permute-start(bf16[256,2048]{1,0:T(8,128)(2,1)} %get-tuple-element.51), channel_id=1, source_target_pairs={{0,2},{1,3},{2,0},{3,1},{4,6},{5,7},{6,4},{7,5},{8,10},{9,11},{10,... | collective-permute-start | bytes 3145736 | tf_op jit(solution)/shard_map/ppermute | solution.py:577
  218.2 60.4 %collective-permute-start.10 = (bf16[256,2048]{1,0:T(8,128)(2,1)}, bf16[256,2048]{1,0:T(8,128)(2,1)S(1)}, u32[]{:S(2)}, u32[]{:S(2)}) collective-permute-start(bf16[256,2048]{1,0:T(8,128)(2,1)} %get-tuple-element.56), channel_id=1, source_target_pairs={{0,30},{1,31},{2,4},{3,5},{4,2},{5,3},{6,8},{7,9},{8,6},{9,7},{10,... | collective-permute-start | bytes 3145736 | tf_op jit(solution)/shard_map/ppermute | solution.py:577
  239.1 3.1 %copy-start = (bf16[256,2048]{1,0:T(8,128)(2,1)}, bf16[256,2048]{1,0:T(8,128)(2,1)S(1)}, u32[]{:S(2)}) copy-start(bf16[256,2048]{1,0:T(8,128)(2,1)S(1)} %collective-permute-done.9.refs_1_) | copy-start | bytes 3145732
  246.0 7.6 %collective-permute-start.15 = (bf16[144,1024]{1,0:T(8,128)(2,1)}, bf16[144,1024]{1,0:T(8,128)(2,1)S(1)}, u32[]{:S(2)}, u32[]{:S(2)}) collective-permute-start(bf16[144,1024]{1,0:T(8,128)(2,1)} %get-tuple-element.71), channel_id=1, source_target_pairs={{0,8},{1,9},{2,10},{3,11},{4,12},{5,13},{6,14},{7,15},{8,16},{9,17... | collective-permute-start | bytes 884744 | tf_op jit(solution)/shard_map/ppermute | solution.py:577
  246.8 24.5 %collective-permute-start.16 = (bf16[144,1024]{1,0:T(8,128)(2,1)}, bf16[144,1024]{1,0:T(8,128)(2,1)S(1)}, u32[]{:S(2)}, u32[]{:S(2)}) collective-permute-start(bf16[144,1024]{1,0:T(8,128)(2,1)} %get-tuple-element.72), channel_id=1, source_target_pairs={{0,16},{1,17},{2,18},{3,19},{4,20},{5,21},{6,22},{7,23},{8,24},{9,... | collective-permute-start | bytes 884744 | tf_op jit(solution)/shard_map/ppermute | solution.py:577
  248.4 26.7 %collective-permute-start.17 = (bf16[144,1024]{1,0:T(8,128)(2,1)}, bf16[144,1024]{1,0:T(8,128)(2,1)S(1)}, u32[]{:S(2)}, u32[]{:S(2)}) collective-permute-start(bf16[144,1024]{1,0:T(8,128)(2,1)} %get-tuple-element.73), channel_id=1, source_target_pairs={{0,24},{1,25},{2,26},{3,27},{4,28},{5,29},{6,30},{7,31},{8,0},{9,1... | collective-permute-start | bytes 884744 | tf_op jit(solution)/shard_map/ppermute | solution.py:577
  253.7 21.4 %copy-start.13 = (bf16[144,1024]{1,0:T(8,128)(2,1)}, bf16[144,1024]{1,0:T(8,128)(2,1)S(1)}, u32[]{:S(2)}) copy-start(bf16[144,1024]{1,0:T(8,128)(2,1)S(1)} %collective-permute-done.15.refs_0_) | copy-start | bytes 884740
  271.3 3.8 %copy-start.14 = (bf16[144,1024]{1,0:T(8,128)(2,1)}, bf16[144,1024]{1,0:T(8,128)(2,1)S(1)}, u32[]{:S(2)}) copy-start(bf16[144,1024]{1,0:T(8,128)(2,1)S(1)} %collective-permute-done.16.refs_1_) | copy-start | bytes 884740
  278.1 10.4 %collective-permute-start.18 = (f32[72,1024]{1,0:T(8,128)}, f32[72,1024]{1,0:T(8,128)S(1)}, u32[]{:S(2)}, u32[]{:S(2)}) collective-permute-start(f32[72,1024]{1,0:T(8,128)} %get-tuple-element.75), channel_id=1, source_target_pairs={{0,2},{1,3},{2,0},{3,1},{4,6},{5,7},{6,4},{7,5},{8,10},{9,11},{10,... | collective-permute-start | bytes 884744 | tf_op jit(solution)/shard_map/ppermute | solution.py:577
  278.6 1.3 copy-start.8
  279.9 8.6 %copy-start.12 = (f32[72,1024]{1,0:T(8,128)S(1)}, f32[72,1024]{1,0:T(8,128)}, u32[]{:S(2)}) copy-start(f32[72,1024]{1,0:T(8,128)} %get-tuple-element.74) | copy-start | bytes 884740
  (5 other events, 4.4 us)
Sparse Core Ops, SparseCore 0:
  11.5 96.7 all-gather.1

commit v3 on v2

--- a/solution.py
+++ b/solution.py
@@ -14,7 +14,7 @@
 TILE = 256
 F32 = jnp.float32
 BF16 = jnp.bfloat16
-VMEM = 60 * 1024 * 1024
+MIB = 1024 * 1024
 GELU_A = math.sqrt(2 / math.pi)
 GELU_B = 0.044715
 
@@ -26,8 +26,8 @@
 TOKEN = jax.ShapeDtypeStruct((8, 128), F32)
 
 
-def params():
-    return pltpu.CompilerParams(vmem_limit_bytes=VMEM)
+def params(mib):
+    return pltpu.CompilerParams(vmem_limit_bytes=mib * MIB)
 
 
 def tie_kernel(*refs):
@@ -42,6 +42,7 @@
         out_specs=[ANY] * n,
         out_shape=[jax.ShapeDtypeStruct(v.shape, v.dtype) for v in values],
         input_output_aliases={k: k for k in range(n)},
+        compiler_params=params(4),
         name="tie",
     )(*values, *after)
 
@@ -84,76 +85,91 @@
         in_specs=[pl.BlockSpec((FANOUT, n), lambda i: (0, 0))],
         out_specs=pl.BlockSpec((TILE, n), lambda i: (i, 0)),
         out_shape=jax.ShapeDtypeStruct((tiles * TILE, n), BF16),
-        compiler_params=params(),
+        compiler_params=params(12),
         cost_estimate=cost(0, tiles * TILE * n * 16),
         name="counts",
     )(index)
 
 
-def gather_own_kernel(c_ref, t_ref, o_ref):
-    o_ref[...] = dot(c_ref[...], t_ref[...], 0, 0)
-
-
-def gather_own(adjacency, features, live):
+def gather_kernel(c_ref, t_ref, *refs):
+    o_ref = refs[-1]
+    live = t_ref.shape[0]
+    total = dot(c_ref[:live, :], t_ref[...], 0, 0)
+    for k, ref in enumerate(refs[:-1]):
+        at = live + k * BOUND
+        total = total + dot(c_ref[at : at + BOUND, :], ref[...], 0, 0)
+    o_ref[...] = total
+
+
+def gather(adjacency, features, blocks, live):
     h = features.shape[1]
-    return pl.pallas_call(
-        gather_own_kernel,
+    rows = live + len(blocks) * BOUND
+    return pl.pallas_call(
+        gather_kernel,
         grid=(live // TILE,),
-        in_specs=[pl.BlockSpec((live, TILE), lambda i: (0, i)), resident((live, h))],
+        in_specs=[pl.BlockSpec((rows, TILE), lambda i: (0, i)), resident((live, h))] + [resident((BOUND, h))] * len(blocks),
         out_specs=pl.BlockSpec((TILE, h), lambda i: (i, 0)),
         out_shape=jax.ShapeDtypeStruct((live, h), F32),
-        compiler_params=params(),
-        cost_estimate=cost(2 * live * live * h, live * h * 6),
-        name="gather_own",
-    )(adjacency, features)
-
-
-def gather_bound_kernel(c_ref, part_ref, inv_ref, *refs):
-    o_ref = refs[-1]
-    total = part_ref[...]
-    for k, ref in enumerate(refs[:-1]):
-        total = total + dot(c_ref[k * BOUND : (k + 1) * BOUND, :], ref[...], 0, 0)
-    o_ref[...] = (total * inv_ref[...]).astype(BF16)
-
-
-def gather_bound(adjacency, part, inverse, blocks):
-    live, h = part.shape
-    rest = adjacency.shape[0] - live
-    return pl.pallas_call(
-        gather_bound_kernel,
-        grid=(live // TILE,),
-        in_specs=[
-            pl.BlockSpec((pl.Element(rest), pl.Element(TILE)), lambda i: (live, i * TILE)),
-            pl.BlockSpec((TILE, h), lambda i: (i, 0)),
-            pl.BlockSpec((TILE, 1), lambda i: (i, 0)),
-        ]
-        + [resident((BOUND, h))] * len(blocks),
-        out_specs=pl.BlockSpec((TILE, h), lambda i: (i, 0)),
-        out_shape=jax.ShapeDtypeStruct((live, h), BF16),
-        compiler_params=params(),
-        cost_estimate=cost(2 * live * rest * h, live * h * 6),
-        name="gather_bound",
-    )(adjacency, part, inverse, *blocks)
-
-
-def layer_kernel(at_ref, m_ref, w, ct_ref, inv_ref, o_ref, agl_ref, own_ref, gb_ref, sent_ref, b, m_all, gl_all, gb, *, tiles):
+        compiler_params=params(26),
+        cost_estimate=cost(2 * live * rows * h, live * h * 6),
+        name="gather",
+    )(adjacency, features, *blocks)
+
+
+def fetch(pieces, planes, target, sem, at_ref):
+    core, lo, hi, wa = (at_ref[j] for j in range(1, 5))
+    rows = pieces[0].shape[0] // planes
+    copies = []
+    for n, piece in enumerate(pieces):
+        for k in range(planes):
+            chip = lax.rem(hi - k + planes, planes) * 2 + (1 - lo if n // 2 % 2 else lo)
+            owner = (chip * 2 + (1 - core if n // 4 else core)) * 2 + (1 - wa if n % 2 else wa)
+            copies.append(
+                pltpu.make_async_copy(
+                    piece.at[pl.ds(k * rows, rows), :],
+                    target.at[pl.ds(pl.multiple_of(owner * rows, rows), rows), :],
+                    sem.at[n, k],
+                )
+            )
+    return copies
+
+
+def layer_kernel(at_ref, part_ref, c_ref, last_ref, inv_ref, ct_ref, *refs, tiles, planes):
+    pieces, refs = refs[:8], refs[8:]
+    o_ref, agl_ref, own_ref, m_ref, w_ref, gb_ref, sent_ref, w, b, m_all, gl_all, gb, sem, sem_out = refs
     i = pl.program_id(0)
     h = m_ref.shape[1]
     n = h // 2
+    copies = fetch(pieces, planes, w, sem, at_ref)
+    copy_out = pltpu.make_async_copy(w.at[:, pl.ds(0, h)], w_ref, sem_out)
     mine = pl.ds(pl.multiple_of(at_ref[1] * n, n), n)
     other = pl.ds(pl.multiple_of((1 - at_ref[1]) * n, n), n)
 
     @pl.when(i == 0)
     def _():
+        for copy in copies:
+            copy.start()
+        gb[...] = jnp.zeros_like(gb)
+
+    @pl.when(i < tiles)
+    def _():
+        total = part_ref[...] + dot(c_ref[...], last_ref[...], 0, 0)
+        mixed = (total * inv_ref[...]).astype(BF16)
+        m_ref[...] = mixed
+        m_all[pl.ds(pl.multiple_of(i * TILE, TILE), TILE), :] = mixed
+
+    @pl.when(i == 0)
+    def _():
+        for copy in copies:
+            copy.wait()
+        copy_out.start()
         b[...] = w[:, h:].astype(F32).T[:8, :]
-        gb[...] = jnp.zeros_like(gb)
 
     @pl.when(i < tiles)
     def _():
         base = pl.multiple_of(i * TILE, TILE)
         rows = pl.ds(base, TILE)
-        mixed = m_ref[...]
-        m_all[rows, :] = mixed
+        mixed = m_all[rows, :]
         live = base + lax.broadcasted_iota(jnp.int32, (TILE, 256), 0) < at_ref[0]
         inverse = inv_ref[...]
         for j in range(0, h, 256):
@@ -182,54 +198,65 @@
 
     @pl.when(i > tiles + h // TILE)
     def _():
+        copy_out.wait()
         gb_ref[...] = jnp.broadcast_to(jnp.sum(gb[:, mine], axis=0, keepdims=True), gb_ref.shape)
         sent_ref[:SPARE, :] = jnp.broadcast_to(jnp.sum(gb[:, other], axis=0, keepdims=True), (SPARE, n)).astype(BF16)
 
 
-def layer(at, mixed, weight, cotangent, inverse):
-    live, h = mixed.shape
+def layer(at, part, adjacency, last, inverse, cotangent, pieces, planes):
+    live, h = part.shape
     nodes, n = cotangent.shape[0], h // 2
     tiles, blocks = live // TILE, h // TILE
+    below = adjacency.shape[0] // BOUND - 1
 
     def row(i, s):
         return (jnp.minimum(i, tiles - 1), 0)
 
     return pl.pallas_call(
-        functools.partial(layer_kernel, tiles=tiles),
+        functools.partial(layer_kernel, tiles=tiles, planes=planes),
         grid_spec=pltpu.PrefetchScalarGridSpec(
             num_scalar_prefetch=1,
             grid=(tiles + 1 + blocks + 1,),
             in_specs=[
                 pl.BlockSpec((TILE, h), row),
-                resident(weight.shape),
+                pl.BlockSpec((BOUND, TILE), lambda i, s: (below, jnp.minimum(i, tiles - 1))),
+                resident(last.shape),
+                pl.BlockSpec((TILE, 1), row),
                 pl.BlockSpec((TILE, h), row),
-                pl.BlockSpec((TILE, 1), row),
-            ],
+            ]
+            + [ANY] * len(pieces),
             out_specs=[
                 pl.BlockSpec((TILE, h), lambda i, s: (jnp.minimum(i, tiles), 0)),
                 pl.BlockSpec((TILE, h), row),
                 pl.BlockSpec((TILE, n), row),
+                pl.BlockSpec((TILE, h), row),
+                ANY,
                 resident((8, n)),
                 pl.BlockSpec((TILE, n), lambda i, s: (jnp.maximum(i - tiles - 1, 0), 0)),
             ],
             scratch_shapes=[
+                pltpu.VMEM((h, pieces[0].shape[1]), BF16),
                 pltpu.VMEM((8, h), F32),
                 pltpu.VMEM((live, h), BF16),
                 pltpu.VMEM((live, h), BF16),
                 pltpu.VMEM((8, h), F32),
+                pltpu.SemaphoreType.DMA((len(pieces), planes)),
+                pltpu.SemaphoreType.DMA,
             ],
         ),
         out_shape=[
             jax.ShapeDtypeStruct((nodes, h), F32),
             jax.ShapeDtypeStruct((live, h), BF16),
             jax.ShapeDtypeStruct((live, n), BF16),
+            jax.ShapeDtypeStruct((live, h), BF16),
+            jax.ShapeDtypeStruct((h, h), BF16),
             jax.ShapeDtypeStruct((8, n), F32),
             jax.ShapeDtypeStruct((h + SPARE, n), BF16),
         ],
-        compiler_params=params(),
+        compiler_params=params(46),
         cost_estimate=cost(3 * live * h * h, live * h * 12),
         name="layer",
-    )(at, mixed, weight, cotangent, inverse)
+    )(at, part, adjacency, last, inverse, cotangent, *pieces)
 
 
 def halves(at_ref, value, rows):
@@ -322,7 +349,7 @@
             jax.ShapeDtypeStruct((h // 2, n // 2), BF16),
             jax.ShapeDtypeStruct((8, n), F32),
         ],
-        compiler_params=params(),
+        compiler_params=params(18),
         cost_estimate=cost(2 * live * h * n, live * h * 3),
         name="grad_weight",
     )(at, mixed, low, came, came, bias, after)
@@ -360,7 +387,7 @@
             jax.ShapeDtypeStruct((count, n), BF16),
             jax.ShapeDtypeStruct(bias.shape, F32),
         ],
-        compiler_params=params(),
+        compiler_params=params(22),
         cost_estimate=cost(0, b_own.size * 9),
         name="fold",
     )(at, a_own, a_came, b_own, b_came, bias, after)
@@ -389,14 +416,14 @@
         out_specs=[WHOLE] * (1 + planes),
         out_shape=[jax.ShapeDtypeStruct(bias.shape, F32), jax.ShapeDtypeStruct((2 * rows, 2 * n), F32)]
         + [jax.ShapeDtypeStruct((2 * rows + SPARE, 2 * n), BF16)] * (planes - 1),
-        compiler_params=params(),
+        compiler_params=params(14),
         cost_estimate=cost(0, a_own.size * 18),
         name="part_planes",
     )(at, a_own, a_came, b_own, b_came, bias, *after)
 
 
 def finish_kernel(at_ref, gb_ref, own, *refs, rows):
-    came, mine_ref, other_ref = refs[:-2], refs[-2], refs[-1]
+    came, mine_ref, other_ref = refs[:-3], refs[-2], refs[-1]
     total, bias = own[...], gb_ref[0:1, :]
     for ref in came:
         total = total + ref[: 2 * rows, :].astype(F32)
@@ -408,21 +435,21 @@
     mine_ref[rows:, :], other_ref[rows:, :] = bias, bias
 
 
-def finish(at, bias, own, came, rows):
+def finish(at, bias, own, came, rows, after):
     shape = jax.ShapeDtypeStruct((rows + 8, own.shape[1]), F32)
     return pl.pallas_call(
         functools.partial(finish_kernel, rows=rows),
-        in_specs=[SMEM] + [WHOLE] * (2 + len(came)),
+        in_specs=[SMEM] + [WHOLE] * (2 + len(came)) + [ANY],
         out_specs=[WHOLE] * 2,
         out_shape=[shape] * 2,
-        compiler_params=params(),
+        compiler_params=params(10),
         cost_estimate=cost(0, own.size * 8),
         name="finish",
-    )(at, bias, own, *came)
-
-
-def scatter_bound_kernel(c_ref, g_ref, *refs):
-    outs, part, sem = refs[:-2], refs[-2], refs[-1]
+    )(at, bias, own, *came, after)
+
+
+def scatter_bound_kernel(c_ref, g_ref, *refs, count):
+    *outs, part, sem = refs[len(refs) - 2 - count :]
     i = pl.program_id(0)
     part[i] = dot(c_ref[...], g_ref[...], 1, 0).astype(BF16)
     copies = [pltpu.make_async_copy(part.at[k], out, sem.at[k]) for k, out in enumerate(outs)]
@@ -438,20 +465,21 @@
             copy.wait()
 
 
-def scatter_bound(adjacency, grads):
+def scatter_bound(adjacency, grads, low, high, after):
     live, h = grads.shape
-    blocks = (adjacency.shape[0] - live) // BOUND
-    return pl.pallas_call(
-        scatter_bound_kernel,
+    blocks = high - low
+    return pl.pallas_call(
+        functools.partial(scatter_bound_kernel, count=blocks),
         grid=(blocks,),
-        in_specs=[pl.BlockSpec((BOUND, live), lambda i: (i + live // BOUND, 0)), resident((live, h))],
+        in_specs=[pl.BlockSpec((BOUND, live), lambda i: (i + low + live // BOUND, 0)), resident((live, h))]
+        + [ANY] * len(after),
         out_specs=[ANY] * blocks,
         out_shape=[jax.ShapeDtypeStruct((BOUND, h), BF16)] * blocks,
         scratch_shapes=[pltpu.VMEM((blocks, BOUND, h), BF16), pltpu.SemaphoreType.DMA((blocks,))],
-        compiler_params=params(),
+        compiler_params=params(22),
         cost_estimate=cost(2 * blocks * BOUND * live * h, live * h * 4),
         name="scatter_bound",
-    )(adjacency, grads)
+    )(adjacency, grads, *after)
 
 
 def grad_rows_kernel(c_ref, g_ref, w_hbm, *refs, low, tiles):
@@ -508,7 +536,7 @@
         out_shape=[jax.ShapeDtypeStruct((nodes, h), F32), TOKEN if low else jax.ShapeDtypeStruct((TILE, h), F32)],
         scratch_shapes=[pltpu.VMEM((h, h), BF16), pltpu.SemaphoreType.DMA],
         input_output_aliases={3: 0} if extra else {},
-        compiler_params=params(),
+        compiler_params=params(30),
         cost_estimate=cost((2 * live + 2 * h) * (high - low) * TILE * h, live * h * 8),
         name="grad_rows",
     )(adjacency, grads, weight, *extra, *after)
@@ -527,14 +555,14 @@
         in_specs=[block] * 4 + [ANY],
         out_specs=[block] * 2,
         out_shape=[jax.ShapeDtypeStruct(a.shape, BF16)] * 2,
-        compiler_params=params(),
+        compiler_params=params(10),
         cost_estimate=cost(0, a.size * 12),
         name="back",
     )(a, b, c, d, after)
 
 
 def grad_lead_kernel(lead_ref, *refs):
-    came, (w_ref, _, o_ref, total) = refs[:3], refs[3:]
+    came, (w_ref, _, o_ref, token_ref, total) = refs[:3], refs[3:]
 
     @pl.when(pl.program_id(0) == 0)
     def _():
@@ -542,6 +570,7 @@
         for ref in came:
             value = value + ref[...].astype(F32)
         total[...] = value.astype(BF16)
+        token_ref[...] = jnp.zeros_like(token_ref)
 
     o_ref[...] = dot(total[...], w_ref[...], 1, 1)
 
@@ -552,11 +581,11 @@
         grad_lead_kernel,
         grid=(4,),
         in_specs=[resident((rows, h))] * 4 + [pl.BlockSpec((h // 4, h), lambda i: (i, 0)), ANY],
-        out_specs=pl.BlockSpec((rows, h // 4), lambda i: (0, i)),
-        out_shape=jax.ShapeDtypeStruct(grads.shape, F32),
+        out_specs=[pl.BlockSpec((rows, h // 4), lambda i: (0, i)), resident((8, 128))],
+        out_shape=[jax.ShapeDtypeStruct(grads.shape, F32), TOKEN],
         scratch_shapes=[pltpu.VMEM((rows, h), BF16)],
         input_output_aliases={5: 0},
-        compiler_params=params(),
+        compiler_params=params(20),
         cost_estimate=cost(2 * rows * h * h, h * h * 2),
         name="grad_lead",
     )(lead, *came, weight, grads)
@@ -591,13 +620,13 @@
     def rotate_hi(value, k):
         return permute(value, lambda b, w: ((b + 4 * k) % n_blk, w))
 
-    sheet = jnp.concatenate([weight, jnp.broadcast_to(bias[:, None], (share, 128))], axis=1)
-    sheet = lax.all_gather(sheet, axes, axis=0, tiled=True)
-
     leading = features[:BOUND]
     partner = swap_wa(leading)
     outer_same = swap_outer(leading)
-    inner_same = swap_core(leading)
+
+    sheet = jnp.concatenate([weight, jnp.broadcast_to(bias[:, None], (share, 128))], axis=1)
+    planes = [rotate_hi(sheet, k) for k in range(1, n_hi)]
+
     live_count = (cluster_sizes[0] - wa + n_wa - 1) // n_wa
     table = neighbours[:, :live]
     beyond = table - nodes
@@ -615,33 +644,41 @@
     at = jnp.stack([live_count, core, lo, hi, wa]).astype(jnp.int32)
 
     adjacency = counts(index, (live + (1 + 2 * n_wa) * BOUND) // TILE)
-    partner, outer_same, inner_same = tie([partner, outer_same, inner_same], [adjacency])
-    inner_other = swap_core(partner)
+    partner, *planes = tie([partner, *planes], [adjacency])
+    sheet = jnp.concatenate([sheet, *planes])
+    half_sheet, row_sheet = swap_wa(sheet), swap_lo(sheet)
+    inner_same, inner_other = swap_core(leading), swap_core(partner)
+    part = gather(adjacency, features, (partner, inner_same, inner_other, outer_same), live)
+    half_sheet, row_sheet, outer_same = tie([half_sheet, row_sheet, outer_same], [part])
     outer_other = swap_wa(outer_same)
-    blocks = (partner, inner_same, inner_other, outer_same, outer_other)
-    part = gather_own(adjacency, features, live)
-    mixed = gather_bound(adjacency, part, inverse, blocks)
-    output, grads, own_low, bias_sum, sent = layer(at, mixed, sheet, cotangent, inverse)
+    both_sheet, outer_other = tie([swap_lo(half_sheet), outer_other], [])
+    pieces = [sheet, half_sheet, row_sheet, both_sheet]
+    pieces = pieces + [swap_core(value) for value in pieces]
+    output, grads, own_low, mixed, matrix, bias_sum, sent = layer(
+        at, part, adjacency, outer_other, inverse, cotangent, pieces, n_hi
+    )
     came = swap_core(sent)
 
-    own_bound, inner_same_g, inner_other_g, outer_same_g, outer_other_g = scatter_bound(adjacency, grads)
-    outer_came, own_came, inner_came = swap_wa(outer_other_g), swap_core(inner_other_g), swap_core(inner_same_g)
-
-    a, a_sent, b, b_sent, bias_sum = grad_weight_share(at, mixed, own_low, came, bias_sum, share, own_bound)
+    (outer_other_g,) = scatter_bound(adjacency, grads, 4, 5, [])
+    outer_came = swap_wa(outer_other_g)
+
+    a, a_sent, b, b_sent, bias_sum = grad_weight_share(at, mixed, own_low, came, bias_sum, share, outer_other_g)
     a_came, b_came = swap_wa(a_sent), swap_lo(b_sent)
+    own_bound, inner_same_g, inner_other_g, outer_same_g = scatter_bound(adjacency, grads, 0, 4, [bias_sum])
+    own_came, inner_came = swap_core(inner_other_g), swap_core(inner_same_g)
     split, tiles = live // TILE // 2, -(-nodes // TILE)
-    grad_features, lead = grad_rows(adjacency, grads, sheet, nodes, 0, split, None, [bias_sum])
+    grad_features, lead = grad_rows(adjacency, grads, matrix, nodes, 0, split, None, [own_bound])
     outer_back, own_back = back(outer_same_g, outer_came, own_bound, own_came, lead)
     returned = (inner_came, swap_wa(own_back), swap_outer(outer_back))
     a, a_sent, b, b_sent, bias_sum = fold(at, a, a_came, b, b_came, bias_sum, share, own_back)
     a_came, b_came = swap_lo(a_sent), swap_wa(b_sent)
-    grad_features, token = grad_rows(adjacency, grads, sheet, nodes, split, tiles, grad_features, [bias_sum])
+    grad_features, token = grad_rows(adjacency, grads, matrix, nodes, split, tiles, grad_features, [bias_sum])
     bias_sum, own, *rest = part_planes(
         at, a, a_came, b, b_came, bias_sum, share, n_hi, [token, returned[1]]
     )
     rest = [rotate_hi(value, k + 1) for k, value in enumerate(rest)]
-    grad_features = grad_lead(lead, returned, sheet, grad_features)
-    mine, other = finish(at, bias_sum, own, rest, share)
+    grad_features, token = grad_lead(lead, returned, matrix, grad_features)
+    mine, other = finish(at, bias_sum, own, rest, share, token)
     other = swap_core(other)
     pair = jnp.where(core == 0, jnp.concatenate([mine, other], axis=1), jnp.concatenate([other, mine], axis=1))
     grad_weight = pair[:share]

time: 298 us -> 278 us (0.933)
  Pallas kernels: 178 us -> 143 us
  starting transfers between devices: 13.5 us -> 30.3 us
  between operations: 14.9 us -> 1.61 us
  local copies, waits for them, and re-layouts: 14.3 us -> 27.2 us
  other arithmetic: 3.49 us -> 0.4 us
    ppermute x19 -> x29, starting transfers between devices: 13.4 us -> 30.3 us  [permute(): return lax.ppermute(value, axes, [(s, b * n_wa + w) for s, (b, w) in pairs])]
    ppermute x19 -> x29, waiting for transfers between devices: 57.6 us -> 74 us  [permute(): return lax.ppermute(value, axes, [(s, b * n_wa + w) for s, (b, w) in pairs])]
    all_gather x1 -> x0, waiting for transfers between devices: 15.5 us -> none  [body(): sheet = lax.all_gather(sheet, axes, axis=0, tiled=True)]
    unnamed x34 -> x54, local copies, waits for them, and re-layouts: 8.04 us -> 21.4 us
    pallas_call x4, Pallas kernels: 84.7 us -> 74.4 us  [the longest x1 44.2 us: layer(): pl.pallas_call(functools.partial(layer_kernel, tiles=tiles, planes=planes...]
    pallas_call x2, Pallas kernels: 37.6 us -> 28.4 us  [grad_rows(): pl.pallas_call(functools.partial(grad_rows_kernel, low=low, tiles=tiles),...]
    pallas_call x1, Pallas kernels: 14.9 us -> 11.4 us  [grad_weight_share(): pl.pallas_call(functools.partial(grad_weight_kernel, rows=rows), grid_spe...]
    pallas_call x1, Pallas kernels: 8.58 us -> 5.52 us  [grad_lead(): pl.pallas_call(grad_lead_kernel, grid=(4,), in_specs=[resident((rows, h))...]
  transfers between devices with their start and end apart: 20 -> 29, of which waited for: 9 -> 14; matrix products, arithmetic and copies ran while one was open for 2% -> 1% of each run, Pallas kernels for 47% -> 35%
where the time goes in v3:
time: 278 us; the launch traced here: 276 us
  Pallas kernels  143 us (51%)
  waiting for transfers between devices  74 us (27%)
  starting transfers between devices  30.3 us (11%)
  local copies, waits for them, and re-layouts  27.2 us (10%)
    ppermute x29, waiting for transfers between devices, permute(): return lax.ppermute(value, axes, [(s, b * n_wa + w) for s, (b, w) in pairs])  74 us
    pallas_call x1, Pallas kernels, layer(): pl.pallas_call(functools.partial(layer_kernel, tiles=tiles, planes=planes...  44.2 us
    ppermute x29, starting transfers between devices, permute(): return lax.ppermute(value, axes, [(s, b * n_wa + w) for s, (b, w) in pairs])  30.3 us
    pallas_call x2, Pallas kernels, grad_rows(): pl.pallas_call(functools.partial(grad_rows_kernel, low=low, tiles=tiles),...  28.4 us
    unnamed x54, local copies, waits for them, and re-layouts  21.4 us
    pallas_call x1, Pallas kernels, gather(): pl.pallas_call(gather_kernel, grid=(live // TILE,), in_specs=[pl.BlockSpe...  20.4 us
    pallas_call x1, Pallas kernels, counts(): pl.pallas_call(counts_kernel, grid=(tiles,), in_specs=[pl.BlockSpec((FANO...  15.5 us
    pallas_call x1, Pallas kernels, grad_weight_share(): pl.pallas_call(functools.partial(grad_weight_kernel, rows=rows), grid_spe...  11.4 us
  transfers between devices with their start and end apart: 29, of which 14 were waited for; matrix products, arithmetic and copies ran while one was open for 1% of the time, Pallas kernels for 35%

profile of v3, /device:TPU:11, one launch (start us, length us, event | category | flops | bytes accessed | tf_op | source)
XLA Modules:
  0.0 276.1 jit_solution(12228119494520884995)
XLA Ops:
  0.7 2.4 slice.18
  4.1 2.5 collective-permute-start.2
  6.6 2.2 collective-permute-start.1
  8.8 2.9 %collective-permute-start.6 = (bf16[256,2048]{1,0:T(8,128)(2,1)}, bf16[256,2048]{1,0:T(8,128)(2,1)}, u32[]{:S(2)}, u32[]{:S(2)}) collective-permute-start(bf16[256,2048]{1,0:T(8,128)(2,1)} %slice.18), channel_id=1, source_target_pairs={{0,30},{1,31},{2,4},{3,5},{4,2},{5,3},{6,8},{7,9},{8,6},{9,7},{10,... | collective-permute-start | bytes 3145736 | tf_op jit(solution)/shard_map/ppermute | solution.py:606
  11.9 15.5 %counts.1.refs_4_.c_ref = bf16[2816,1536]{1,0:T(8,128)(2,1)S(1)} custom-call(s32[16,1536]{1,0:T(8,128)S(1)} %fusion.2.index_ref), custom_call_target="tpu_custom_call" | custom-call | bytes 4325376 | tf_op jit(solution)/shard_map/counts/pallas_call | solution.py:82
  27.5 13.8 %collective-permute-done.1.refs_1_ = bf16[64,2176]{1,0:T(8,128)(2,1)S(1)} collective-permute-done((bf16[64,2176]{1,0:T(8,128)(2,1)S(1)}, bf16[64,2176]{1,0:T(8,128)(2,1)S(1)}, u32[]{:S(2)}, u32[]{:S(2)}) %collective-permute-start.1) | collective-permute-done | bytes 278560 | tf_op jit(solution)/shard_map/ppermute | solution.py:606
  44.9 20.4 %gather.1.refs_3_.part_ref = f32[1536,2048]{1,0:T(8,128)} custom-call(bf16[2816,1536]{1,0:T(8,128)(2,1)S(1)} %counts.1.refs_4_.c_ref, bf16[1664,2048]{1,0:T(8,128)(2,1)S(1)} %bitcast.19, bf16[256,2048]{1,0:T(8,128)(2,1)S(1)} %get-tuple-element.49.refs_0_, bf16[256,2048]{1,0:T(8,128)(2,1)S(1)} %collective-permute-done.4.refs_1_, ...), custom_call_target="tpu_custom_call" | custom-call | flops 1006632960 | bytes 1179648 | tf_op jit(solution)/shard_map/gather/pallas_call | solution.py:107
  65.3 3.8 %collective-permute-done.8.refs_1_ = bf16[256,2176]{1,0:T(8,128)(2,1)} collective-permute-done((bf16[256,2176]{1,0:T(8,128)(2,1)S(1)}, bf16[256,2176]{1,0:T(8,128)(2,1)}, u32[]{:S(2)}, u32[]{:S(2)}) %collective-permute-start.8) | collective-permute-done | bytes 1114144 | tf_op jit(solution)/shard_map/ppermute | solution.py:606
  69.2 4.6 %copy-done.1 = f32[1536,2048]{1,0:T(8,128)S(1)} copy-done((f32[1536,2048]{1,0:T(8,128)S(1)}, f32[1536,2048]{1,0:T(8,128)}, u32[]{:S(2)}) %copy-start.1) | copy-done | bytes 12582936
  76.0 1.7 collective-permute-start.11
  78.2 20.1 %collective-permute-done.10.refs_1_ = bf16[256,2048]{1,0:T(8,128)(2,1)S(1)} collective-permute-done((bf16[256,2048]{1,0:T(8,128)(2,1)}, bf16[256,2048]{1,0:T(8,128)(2,1)S(1)}, u32[]{:S(2)}, u32[]{:S(2)}) %collective-permute-start.10) | collective-permute-done | bytes 1048608 | tf_op jit(solution)/shard_map/ppermute | solution.py:606
  100.2 1.7 collective-permute-start.14
  107.1 44.2 %layer.1 = (f32[1664,2048]{1,0:T(8,128)}, bf16[1536,2048]{1,0:T(8,128)(2,1)}, bf16[1536,1024]{1,0:T(8,128)(2,1)}, bf16[1536,2048]{1,0:T(8,128)(2,1)}, bf16[2048,...) custom-call(s32[5]{0:T(128)S(1)} %stack.23.at_ref, f32[1536,2048]{1,0:T(8,128)} %gather.1.refs_3_.part_ref, ...), custom_call_target="tpu_custom_call" | custom-call | flops 1207959552 | bytes 2359296 | tf_op jit(solution)/shard_map/layer/pallas_call | solution.py:215
  151.8 2.8 %copy-done.2 = bf16[1536,2048]{1,0:T(8,128)(2,1)S(1)} copy-done((bf16[1536,2048]{1,0:T(8,128)(2,1)S(1)}, bf16[1536,2048]{1,0:T(8,128)(2,1)}, u32[]{:S(2)}) %copy-start.2) | copy-done | bytes 6291480
  154.6 2.0 scatter_bound.2._
  158.8 2.8 %copy-done.5 = bf16[1536,2048]{1,0:T(8,128)(2,1)S(1)} copy-done((bf16[1536,2048]{1,0:T(8,128)(2,1)S(1)}, bf16[1536,2048]{1,0:T(8,128)(2,1)}, u32[]{:S(2)}) %copy-start.5) | copy-done | bytes 6291480
  161.6 11.4 %grad_weight.1 = (f32[1024,512]{1,0:T(8,128)S(1)}, bf16[1040,512]{1,0:T(8,128)(2,1)}, f32[1024,512]{1,0:T(8,128)S(1)}, bf16[1024,512]{1,0:T(8,128)(2,1)}, f32[8,1024]{1,0:T(8,128)S(1)}) custom-call(s32[5]{0:T(128)S(1)} %stack.23.at_ref, bf16[1536,2048]{1,0:T(8,128)(2,1)S(1)} %copy-done.5, bf16[1536,1024]{1,0:T(8,128)(2,1)S(1)} %copy-done.8, ...), custom_call_target="tpu_custom_call" | custom-call | flops 402653184 | bytes 589824 | tf_op jit(solution)/shard_map/grad_weight/pallas_call | solution.py:324
  173.1 1.4 copy-done.10
  174.5 7.8 %scatter_bound.3 = (bf16[256,2048]{1,0:T(8,128)(2,1)S(1)}, bf16[256,2048]{1,0:T(8,128)(2,1)}, bf16[256,2048]{1,0:T(8,128)(2,1)}, bf16[256,2048]{1,0:T(8,128)(2,1)S(1)}) custom-call(bf16[2816,1536]{1,0:T(8,128)(2,1)S(1)} %bitcast.11, bf16[1536,2048]{1,0:T(8,128)(2,1)S(1)} %bitcast.15, f32[8,1024]{1,0:T(8,128)S(1)} %get-tuple-element.65.refs_0_.gb_ref), custom_call_target="tpu_custom_call" | custom-call | flops 402653184 | bytes 786432 | tf_op jit(solution)/shard_map/scatter_bound/pallas_call | solution.py:471
  185.0 3.4 %copy-done.4 = bf16[2048,2048]{1,0:T(8,128)(2,1)S(1)} copy-done((bf16[2048,2048]{1,0:T(8,128)(2,1)S(1)}, bf16[2048,2048]{1,0:T(8,128)(2,1)}, u32[]{:S(2)}) %copy-start.4) | copy-done | bytes 8388632
  188.4 13.4 %grad_rows.2 = (f32[1664,2048]{1,0:T(8,128)}, f32[256,2048]{1,0:T(8,128)S(1)}) custom-call(bf16[2816,1536]{1,0:T(8,128)(2,1)} %copy-done, bf16[1536,2048]{1,0:T(8,128)(2,1)S(1)} %bitcast.17, bf16[2048,2048]{1,0:T(8,128)(2,1)S(1)} %copy-done.4, bf16[256,2048]{1,0:T(8,128)(2,1)S(1)} %get-tuple-element.66.refs_0_.c_ref), custom_call_target="tpu_custom_call" | custom-call | flops 704643072 | bytes 1572864 | tf_op jit(solution)/shard_map/grad_rows/pallas_call | solution.py:526
  201.9 3.6 %back.1 = (bf16[256,2048]{1,0:T(8,128)(2,1)}, bf16[256,2048]{1,0:T(8,128)(2,1)S(1)}) custom-call(bf16[256,2048]{1,0:T(8,128)(2,1)S(1)} %get-tuple-element.69.a_ref, bf16[256,2048]{1,0:T(8,128)(2,1)} %collective-permute-done.17.b_ref, bf16[256,2048]{1,0:T(8,128)(2,1)S(1)} %get-tuple-element.66.refs_0_.c_ref, ...), custom_call_target="tpu_custom_call" | custom-call | bytes 393216 | tf_op jit(solution)/shard_map/back/pallas_call | solution.py:552
  207.1 1.4 collective-permute-done.22.b_came
  208.5 2.4 fold.1
  210.9 1.6 collective-permute-start.23
  213.7 2.8 %copy-done.3 = bf16[1536,2048]{1,0:T(8,128)(2,1)S(1)} copy-done((bf16[1536,2048]{1,0:T(8,128)(2,1)S(1)}, bf16[1536,2048]{1,0:T(8,128)(2,1)}, u32[]{:S(2)}) %copy-start.3) | copy-done | bytes 6291480
  216.5 14.9 %grad_rows.3 = (f32[1664,2048]{1,0:T(8,128)}, f32[8,128]{1,0:T(8,128)S(1)}) custom-call(bf16[2816,1536]{1,0:T(8,128)(2,1)S(1)} %bitcast.13, bf16[1536,2048]{1,0:T(8,128)(2,1)S(1)} %copy-done.3, bf16[2048,2048]{1,0:T(8,128)(2,1)S(1)} %copy-done.4, f32[1664,2048]{1,0:T(8,128)} %get-tuple-element.73.refs_0_, ...), custom_call_target="tpu_custom_call", output_to_operand_aliasing={{0}: (3, {})} | custom-call | flops 939524096 | bytes 1572864 | tf_op jit(solution)/shard_map/grad_rows/pallas_call | solution.py:526
  231.4 9.8 %collective-permute-done.24.b_came = bf16[512,512]{1,0:T(8,128)(2,1)S(1)} collective-permute-done((bf16[512,512]{1,0:T(8,128)(2,1)}, bf16[512,512]{1,0:T(8,128)(2,1)S(1)}, u32[]{:S(2)}, u32[]{:S(2)}) %collective-permute-start.24) | collective-permute-done | bytes 524320 | tf_op jit(solution)/shard_map/ppermute | solution.py:606
  243.0 2.2 collective-permute-start.25
  246.5 5.5 %grad_lead.1 = (f32[1664,2048]{1,0:T(8,128)}, f32[8,128]{1,0:T(8,128)S(1)}) custom-call(f32[256,2048]{1,0:T(8,128)S(1)} %get-tuple-element.67._.lead_ref, bf16[256,2048]{1,0:T(8,128)(2,1)S(1)} %collective-permute-done.16.refs_0_, bf16[256,2048]{1,0:T(8,128)(2,1)S(1)} %collective-permute-done.19.refs_1_, ...), custom_call_target="tpu_custom_call", output_to_operand_aliasing={{0}: (5, {})} | custom-call | flops 134217728 | bytes 524288 | tf_op jit(solution)/shard_map/grad_lead/pallas_call | solution.py:580
  252.0 16.2 %collective-permute-done.26.refs_1_ = bf16[144,1024]{1,0:T(8,128)(2,1)S(1)} collective-permute-done((bf16[144,1024]{1,0:T(8,128)(2,1)S(1)}, bf16[144,1024]{1,0:T(8,128)(2,1)S(1)}, u32[]{:S(2)}, u32[]{:S(2)}) %collective-permute-start.26) | collective-permute-done | bytes 294944 | tf_op jit(solution)/shard_map/ppermute | solution.py:606
  268.2 3.1 %collective-permute-done.27.refs_2_ = bf16[144,1024]{1,0:T(8,128)(2,1)S(1)} collective-permute-done((bf16[144,1024]{1,0:T(8,128)(2,1)S(1)}, bf16[144,1024]{1,0:T(8,128)(2,1)S(1)}, u32[]{:S(2)}, u32[]{:S(2)}) %collective-permute-start.27) | collective-permute-done | bytes 294944 | tf_op jit(solution)/shard_map/ppermute | solution.py:606
  (113 shorter events, 30.3 us)
Async XLA Ops:
  3.0 38.3 %collective-permute-start = (bf16[256,2048]{1,0:T(8,128)(2,1)}, bf16[256,2048]{1,0:T(8,128)(2,1)S(1)}, u32[]{:S(2)}, u32[]{:S(2)}) collective-permute-start(bf16[256,2048]{1,0:T(8,128)(2,1)} %slice.18), channel_id=1, source_target_pairs={{0,1},{1,0},{2,3},{3,2},{4,5},{5,4},{6,7},{7,6},{8,9},{9,8},{10,11... | collective-permute-start | bytes 3145736 | tf_op jit(solution)/shard_map/ppermute | solution.py:606
  4.0 23.4 %collective-permute-start.3 = (bf16[64,2176]{1,0:T(8,128)(2,1)S(1)}, bf16[64,2176]{1,0:T(8,128)(2,1)S(1)}, u32[]{:S(2)}, u32[]{:S(2)}) collective-permute-start(bf16[64,2176]{1,0:T(8,128)(2,1)S(1)} %pad_maximum_fusion.1), channel_id=1, source_target_pairs={{0,24},{1,25},{2,26},{3,27},{4,28},{5,29},{6,30},{7,31},{8,0},{9,1... | collective-permute-start | bytes 835592 | tf_op jit(solution)/shard_map/ppermute | solution.py:606
  4.1 23.4 %collective-permute-start.2 = (bf16[64,2176]{1,0:T(8,128)(2,1)S(1)}, bf16[64,2176]{1,0:T(8,128)(2,1)S(1)}, u32[]{:S(2)}, u32[]{:S(2)}) collective-permute-start(bf16[64,2176]{1,0:T(8,128)(2,1)S(1)} %pad_maximum_fusion.1), channel_id=1, source_target_pairs={{0,16},{1,17},{2,18},{3,19},{4,20},{5,21},{6,22},{7,23},{8,24},{9,... | collective-permute-start | bytes 835592 | tf_op jit(solution)/shard_map/ppermute | solution.py:606
  6.6 34.8 %collective-permute-start.1 = (bf16[64,2176]{1,0:T(8,128)(2,1)S(1)}, bf16[64,2176]{1,0:T(8,128)(2,1)S(1)}, u32[]{:S(2)}, u32[]{:S(2)}) collective-permute-start(bf16[64,2176]{1,0:T(8,128)(2,1)S(1)} %pad_maximum_fusion.1), channel_id=1, source_target_pairs={{0,8},{1,9},{2,10},{3,11},{4,12},{5,13},{6,14},{7,15},{8,16},{9,17... | collective-permute-start | bytes 835592 | tf_op jit(solution)/shard_map/ppermute | solution.py:606
  8.8 35.3 %collective-permute-start.6 = (bf16[256,2048]{1,0:T(8,128)(2,1)}, bf16[256,2048]{1,0:T(8,128)(2,1)}, u32[]{:S(2)}, u32[]{:S(2)}) collective-permute-start(bf16[256,2048]{1,0:T(8,128)(2,1)} %slice.18), channel_id=1, source_target_pairs={{0,30},{1,31},{2,4},{3,5},{4,2},{5,3},{6,8},{7,9},{8,6},{9,7},{10,... | collective-permute-start | bytes 3145736 | tf_op jit(solution)/shard_map/ppermute | solution.py:606
  27.4 16.6 %collective-permute-start.4 = (bf16[256,2048]{1,0:T(8,128)(2,1)}, bf16[256,2048]{1,0:T(8,128)(2,1)S(1)}, u32[]{:S(2)}, u32[]{:S(2)}) collective-permute-start(bf16[256,2048]{1,0:T(8,128)(2,1)} %slice.18), channel_id=1, source_target_pairs={{0,2},{1,3},{2,0},{3,1},{4,6},{5,7},{6,4},{7,5},{8,10},{9,11},{10,... | collective-permute-start | bytes 3145736 | tf_op jit(solution)/shard_map/ppermute | solution.py:606
  41.3 3.6 %collective-permute-start.5 = (bf16[256,2048]{1,0:T(8,128)(2,1)S(1)}, bf16[256,2048]{1,0:T(8,128)(2,1)S(1)}, u32[]{:S(2)}, u32[]{:S(2)}) collective-permute-start(bf16[256,2048]{1,0:T(8,128)(2,1)S(1)} %get-tuple-element.49.refs_0_), channel_id=1, source_target_pairs={{0,2},{1,3},{2,0},{3,1},{4,6},{5,7},{6,4},{7,5},{8,10},{9,11},{10,... | collective-permute-start | bytes 3145736 | tf_op jit(solution)/shard_map/ppermute | solution.py:606
  42.7 26.4 %collective-permute-start.8 = (bf16[256,2176]{1,0:T(8,128)(2,1)S(1)}, bf16[256,2176]{1,0:T(8,128)(2,1)}, u32[]{:S(2)}, u32[]{:S(2)}) collective-permute-start(bf16[256,2176]{1,0:T(8,128)(2,1)S(1)} %pad_maximum_fusion.refs_0_), channel_id=1, source_target_pairs={{0,4},{1,5},{2,6},{3,7},{4,0},{5,1},{6,2},{7,3},{8,12},{9,13},{10,... | collective-permute-start | bytes 3342344 | tf_op jit(solution)/shard_map/ppermute | solution.py:606
  42.8 26.4 %collective-permute-start.7 = (bf16[256,2176]{1,0:T(8,128)(2,1)S(1)}, bf16[256,2176]{1,0:T(8,128)(2,1)}, u32[]{:S(2)}, u32[]{:S(2)}) collective-permute-start(bf16[256,2176]{1,0:T(8,128)(2,1)S(1)} %pad_maximum_fusion.refs_0_), channel_id=1, source_target_pairs={{0,1},{1,0},{2,3},{3,2},{4,5},{5,4},{6,7},{7,6},{8,9},{9,8},{10,11... | collective-permute-start | bytes 3342344 | tf_op jit(solution)/shard_map/ppermute | solution.py:606
  73.7 25.5 %collective-permute-start.9 = (bf16[256,2176]{1,0:T(8,128)(2,1)}, bf16[256,2176]{1,0:T(8,128)(2,1)S(1)}, u32[]{:S(2)}, u32[]{:S(2)}) collective-permute-start(bf16[256,2176]{1,0:T(8,128)(2,1)} %get-tuple-element.53.refs_1_), channel_id=1, source_target_pairs={{0,4},{1,5},{2,6},{3,7},{4,0},{5,1},{6,2},{7,3},{8,12},{9,13},{10,... | collective-permute-start | bytes 3342344 | tf_op jit(solution)/shard_map/ppermute | solution.py:606
  74.8 23.5 %collective-permute-start.10 = (bf16[256,2048]{1,0:T(8,128)(2,1)}, bf16[256,2048]{1,0:T(8,128)(2,1)S(1)}, u32[]{:S(2)}, u32[]{:S(2)}) collective-permute-start(bf16[256,2048]{1,0:T(8,128)(2,1)} %get-tuple-element.54), channel_id=1, source_target_pairs={{0,1},{1,0},{2,3},{3,2},{4,5},{5,4},{6,7},{7,6},{8,9},{9,8},{10,11... | collective-permute-start | bytes 3145736 | tf_op jit(solution)/shard_map/ppermute | solution.py:606
  76.0 27.8 %collective-permute-start.11 = (bf16[256,2176]{1,0:T(8,128)(2,1)S(1)}, bf16[256,2176]{1,0:T(8,128)(2,1)}, u32[]{:S(2)}, u32[]{:S(2)}) collective-permute-start(bf16[256,2176]{1,0:T(8,128)(2,1)S(1)} %pad_maximum_fusion.refs_0_), channel_id=1, source_target_pairs={{0,2},{1,3},{2,0},{3,1},{4,6},{5,7},{6,4},{7,5},{8,10},{9,11},{10,... | collective-permute-start | bytes 3342344 | tf_op jit(solution)/shard_map/ppermute | solution.py:606
  77.7 26.2 %collective-permute-start.12 = (bf16[256,2176]{1,0:T(8,128)(2,1)}, bf16[256,2176]{1,0:T(8,128)(2,1)}, u32[]{:S(2)}, u32[]{:S(2)}) collective-permute-start(bf16[256,2176]{1,0:T(8,128)(2,1)} %get-tuple-element.53.refs_1_), channel_id=1, source_target_pairs={{0,2},{1,3},{2,0},{3,1},{4,6},{5,7},{6,4},{7,5},{8,10},{9,11},{10,... | collective-permute-start | bytes 3342344 | tf_op jit(solution)/shard_map/ppermute | solution.py:606
  77.7 26.2 %collective-permute-start.13 = (bf16[256,2176]{1,0:T(8,128)(2,1)}, bf16[256,2176]{1,0:T(8,128)(2,1)}, u32[]{:S(2)}, u32[]{:S(2)}) collective-permute-start(bf16[256,2176]{1,0:T(8,128)(2,1)} %get-tuple-element.56.refs_2_), channel_id=1, source_target_pairs={{0,2},{1,3},{2,0},{3,1},{4,6},{5,7},{6,4},{7,5},{8,10},{9,11},{10,... | collective-permute-start | bytes 3342344 | tf_op jit(solution)/shard_map/ppermute | solution.py:606
  100.2 4.2 %collective-permute-start.14 = (bf16[256,2176]{1,0:T(8,128)(2,1)S(1)}, bf16[256,2176]{1,0:T(8,128)(2,1)}, u32[]{:S(2)}, u32[]{:S(2)}) collective-permute-start(bf16[256,2176]{1,0:T(8,128)(2,1)S(1)} %get-tuple-element.57.refs_3_), channel_id=1, source_target_pairs={{0,2},{1,3},{2,0},{3,1},{4,6},{5,7},{6,4},{7,5},{8,10},{9,11},{10,... | collective-permute-start | bytes 3342344 | tf_op jit(solution)/shard_map/ppermute | solution.py:606
  104.4 47.4 %slice-start = ((s8[8650752]{0:T(1024)(128)(4,1)}), s8[4194304]{0:T(1024)(128)(4,1)S(1)}, s32[]{:S(2)}) async-start(s8[8650752]{0:T(1024)(128)(4,1)} %bitcast.10), calls=%async_computation | async-start | bytes 8388608
  107.1 44.7 %slice-start.1 = ((s8[8650752]{0:T(1024)(128)(4,1)}), s8[4194304]{0:T(1024)(128)(4,1)S(1)}, s32[]{:S(2)}) async-start(s8[8650752]{0:T(1024)(128)(4,1)} %bitcast.10), calls=%async_computation.1 | async-start | bytes 8388608
  107.1 44.7 %slice-start.2 = ((s8[8650752]{0:T(1024)(128)(4,1)}), s8[262144]{0:T(1024)(128)(4,1)S(1)}, s32[]{:S(2)}) async-start(s8[8650752]{0:T(1024)(128)(4,1)} %bitcast.10), calls=%async_computation.2 | async-start | bytes 524288
  151.3 7.5 %collective-permute-start.15 = (bf16[2064,1024]{1,0:T(8,128)(2,1)}, bf16[2064,1024]{1,0:T(8,128)(2,1)S(1)}, u32[]{:S(2)}, u32[]{:S(2)}) collective-permute-start(bf16[2064,1024]{1,0:T(8,128)(2,1)} %get-tuple-element.63), channel_id=1, source_target_pairs={{0,2},{1,3},{2,0},{3,1},{4,6},{5,7},{6,4},{7,5},{8,10},{9,11},{10,... | collective-permute-start | bytes 12681224 | tf_op jit(solution)/shard_map/ppermute | solution.py:606
  156.6 45.3 %collective-permute-start.17 = (bf16[256,2048]{1,0:T(8,128)(2,1)S(1)}, bf16[256,2048]{1,0:T(8,128)(2,1)}, u32[]{:S(2)}, u32[]{:S(2)}) collective-permute-start(bf16[256,2048]{1,0:T(8,128)(2,1)S(1)} %scatter_bound.2._), channel_id=1, source_target_pairs={{0,1},{1,0},{2,3},{3,2},{4,5},{5,4},{6,7},{7,6},{8,9},{9,8},{10,11... | collective-permute-start | bytes 3145736 | tf_op jit(solution)/shard_map/ppermute | solution.py:606
  182.3 19.6 %collective-permute-start.18 = (bf16[256,2048]{1,0:T(8,128)(2,1)}, bf16[256,2048]{1,0:T(8,128)(2,1)S(1)}, u32[]{:S(2)}, u32[]{:S(2)}) collective-permute-start(bf16[256,2048]{1,0:T(8,128)(2,1)} %get-tuple-element.70), channel_id=1, source_target_pairs={{0,2},{1,3},{2,0},{3,1},{4,6},{5,7},{6,4},{7,5},{8,10},{9,11},{10,... | collective-permute-start | bytes 3145736 | tf_op jit(solution)/shard_map/ppermute | solution.py:606
  182.7 25.8 %collective-permute-start.21 = (bf16[1040,512]{1,0:T(8,128)(2,1)}, bf16[1040,512]{1,0:T(8,128)(2,1)S(1)}, u32[]{:S(2)}, u32[]{:S(2)}) collective-permute-start(bf16[1040,512]{1,0:T(8,128)(2,1)} %get-tuple-element.75), channel_id=1, source_target_pairs={{0,1},{1,0},{2,3},{3,2},{4,5},{5,4},{6,7},{7,6},{8,9},{9,8},{10,11... | collective-permute-start | bytes 3194888 | tf_op jit(solution)/shard_map/ppermute | solution.py:606
  183.9 24.6 %collective-permute-start.22 = (bf16[1024,512]{1,0:T(8,128)(2,1)}, bf16[1024,512]{1,0:T(8,128)(2,1)}, u32[]{:S(2)}, u32[]{:S(2)}) collective-permute-start(bf16[1024,512]{1,0:T(8,128)(2,1)} %get-tuple-element.77), channel_id=1, source_target_pairs={{0,4},{1,5},{2,6},{3,7},{4,0},{5,1},{6,2},{7,3},{8,12},{9,13},{10,... | collective-permute-start | bytes 3145736 | tf_op jit(solution)/shard_map/ppermute | solution.py:606
  205.6 36.7 %collective-permute-start.19 = (bf16[256,2048]{1,0:T(8,128)(2,1)S(1)}, bf16[256,2048]{1,0:T(8,128)(2,1)S(1)}, u32[]{:S(2)}, u32[]{:S(2)}) collective-permute-start(bf16[256,2048]{1,0:T(8,128)(2,1)S(1)} %get-tuple-element.71._), channel_id=1, source_target_pairs={{0,1},{1,0},{2,3},{3,2},{4,5},{5,4},{6,7},{7,6},{8,9},{9,8},{10,11... | collective-permute-start | bytes 3145736 | tf_op jit(solution)/shard_map/ppermute | solution.py:606
  205.8 40.7 %collective-permute-start.16 = (bf16[256,2048]{1,0:T(8,128)(2,1)}, bf16[256,2048]{1,0:T(8,128)(2,1)S(1)}, u32[]{:S(2)}, u32[]{:S(2)}) collective-permute-start(bf16[256,2048]{1,0:T(8,128)(2,1)} %get-tuple-element.68), channel_id=1, source_target_pairs={{0,2},{1,3},{2,0},{3,1},{4,6},{5,7},{6,4},{7,5},{8,10},{9,11},{10,... | collective-permute-start | bytes 3145736 | tf_op jit(solution)/shard_map/ppermute | solution.py:606
  206.8 39.7 %collective-permute-start.20 = (bf16[256,2048]{1,0:T(8,128)(2,1)}, bf16[256,2048]{1,0:T(8,128)(2,1)}, u32[]{:S(2)}, u32[]{:S(2)}) collective-permute-start(bf16[256,2048]{1,0:T(8,128)(2,1)} %get-tuple-element.72), channel_id=1, source_target_pairs={{0,30},{1,31},{2,4},{3,5},{4,2},{5,3},{6,8},{7,9},{8,6},{9,7},{10,... | collective-permute-start | bytes 3145736 | tf_op jit(solution)/shard_map/ppermute | solution.py:606
  210.9 31.4 %collective-permute-start.23 = (bf16[528,512]{1,0:T(8,128)(2,1)S(1)}, bf16[528,512]{1,0:T(8,128)(2,1)S(1)}, u32[]{:S(2)}, u32[]{:S(2)}) collective-permute-start(bf16[528,512]{1,0:T(8,128)(2,1)S(1)} %get-tuple-element.82), channel_id=1, source_target_pairs={{0,4},{1,5},{2,6},{3,7},{4,0},{5,1},{6,2},{7,3},{8,12},{9,13},{10,... | collective-permute-start | bytes 1622024 | tf_op jit(solution)/shard_map/ppermute | solution.py:606
  212.5 28.7 %collective-permute-start.24 = (bf16[512,512]{1,0:T(8,128)(2,1)}, bf16[512,512]{1,0:T(8,128)(2,1)S(1)}, u32[]{:S(2)}, u32[]{:S(2)}) collective-permute-start(bf16[512,512]{1,0:T(8,128)(2,1)} %get-tuple-element.84), channel_id=1, source_target_pairs={{0,1},{1,0},{2,3},{3,2},{4,5},{5,4},{6,7},{7,6},{8,9},{9,8},{10,11... | collective-permute-start | bytes 1572872 | tf_op jit(solution)/shard_map/ppermute | solution.py:606
  243.0 9.0 %collective-permute-start.25 = (bf16[144,1024]{1,0:T(8,128)(2,1)S(1)}, bf16[144,1024]{1,0:T(8,128)(2,1)S(1)}, u32[]{:S(2)}, u32[]{:S(2)}) collective-permute-start(bf16[144,1024]{1,0:T(8,128)(2,1)S(1)} %get-tuple-element.88), channel_id=1, source_target_pairs={{0,8},{1,9},{2,10},{3,11},{4,12},{5,13},{6,14},{7,15},{8,16},{9,17... | collective-permute-start | bytes 884744 | tf_op jit(solution)/shard_map/ppermute | solution.py:606
  245.2 23.0 %collective-permute-start.26 = (bf16[144,1024]{1,0:T(8,128)(2,1)S(1)}, bf16[144,1024]{1,0:T(8,128)(2,1)S(1)}, u32[]{:S(2)}, u32[]{:S(2)}) collective-permute-start(bf16[144,1024]{1,0:T(8,128)(2,1)S(1)} %get-tuple-element.89), channel_id=1, source_target_pairs={{0,16},{1,17},{2,18},{3,19},{4,20},{5,21},{6,22},{7,23},{8,24},{9,... | collective-permute-start | bytes 884744 | tf_op jit(solution)/shard_map/ppermute | solution.py:606
  246.5 24.9 %collective-permute-start.27 = (bf16[144,1024]{1,0:T(8,128)(2,1)S(1)}, bf16[144,1024]{1,0:T(8,128)(2,1)S(1)}, u32[]{:S(2)}, u32[]{:S(2)}) collective-permute-start(bf16[144,1024]{1,0:T(8,128)(2,1)S(1)} %get-tuple-element.90), channel_id=1, source_target_pairs={{0,24},{1,25},{2,26},{3,27},{4,28},{5,29},{6,30},{7,31},{8,0},{9,1... | collective-permute-start | bytes 884744 | tf_op jit(solution)/shard_map/ppermute | solution.py:606
  272.1 2.6 collective-permute-start.28
  (24 other events, 241.8 us)

commit v4 on v3

--- a/solution.py
+++ b/solution.py
@@ -28,6 +28,10 @@
 
 def params(mib):
     return pltpu.CompilerParams(vmem_limit_bytes=mib * MIB)
+
+
+def far(value):
+    return pltpu.with_memory_space_constraint(value, pltpu.HBM)
 
 
 def tie_kernel(*refs):
@@ -91,29 +95,31 @@
     )(index)
 
 
-def gather_kernel(c_ref, t_ref, *refs):
+def gather_kernel(c_ref, t_ref, *refs, count):
     o_ref = refs[-1]
     live = t_ref.shape[0]
     total = dot(c_ref[:live, :], t_ref[...], 0, 0)
-    for k, ref in enumerate(refs[:-1]):
+    for k, ref in enumerate(refs[:count]):
         at = live + k * BOUND
         total = total + dot(c_ref[at : at + BOUND, :], ref[...], 0, 0)
     o_ref[...] = total
 
 
-def gather(adjacency, features, blocks, live):
+def gather(adjacency, features, blocks, live, after):
     h = features.shape[1]
     rows = live + len(blocks) * BOUND
     return pl.pallas_call(
-        gather_kernel,
+        functools.partial(gather_kernel, count=len(blocks)),
         grid=(live // TILE,),
-        in_specs=[pl.BlockSpec((rows, TILE), lambda i: (0, i)), resident((live, h))] + [resident((BOUND, h))] * len(blocks),
+        in_specs=[pl.BlockSpec((rows, TILE), lambda i: (0, i)), resident((live, h))]
+        + [resident((BOUND, h))] * len(blocks)
+        + [ANY] * len(after),
         out_specs=pl.BlockSpec((TILE, h), lambda i: (i, 0)),
         out_shape=jax.ShapeDtypeStruct((live, h), F32),
         compiler_params=params(26),
         cost_estimate=cost(2 * live * rows * h, live * h * 6),
         name="gather",
-    )(adjacency, features, *blocks)
+    )(far(adjacency), far(features), *blocks, *after)
 
 
 def fetch(pieces, planes, target, sem, at_ref):
@@ -126,7 +132,7 @@
             owner = (chip * 2 + (1 - core if n // 4 else core)) * 2 + (1 - wa if n % 2 else wa)
             copies.append(
                 pltpu.make_async_copy(
-                    piece.at[pl.ds(k * rows, rows), :],
+                    piece.at[pl.ds(k * rows, rows), pl.ds(0, target.shape[1])],
                     target.at[pl.ds(pl.multiple_of(owner * rows, rows), rows), :],
                     sem.at[n, k],
                 )
@@ -134,14 +140,13 @@
     return copies
 
 
-def layer_kernel(at_ref, part_ref, c_ref, last_ref, inv_ref, ct_ref, *refs, tiles, planes):
+def layer_kernel(at_ref, part_ref, c_ref, cl_ref, last_ref, inv_ref, ct_ref, *refs, tiles, planes):
     pieces, refs = refs[:8], refs[8:]
-    o_ref, agl_ref, own_ref, m_ref, w_ref, gb_ref, sent_ref, w, b, m_all, gl_all, gb, sem, sem_out = refs
+    o_ref, agl_ref, gb_ref, kept_ref, sent_ref, far_ref, w, b, m_all, gl_all, gb, sem = refs
     i = pl.program_id(0)
-    h = m_ref.shape[1]
+    h = part_ref.shape[1]
     n = h // 2
     copies = fetch(pieces, planes, w, sem, at_ref)
-    copy_out = pltpu.make_async_copy(w.at[:, pl.ds(0, h)], w_ref, sem_out)
     mine = pl.ds(pl.multiple_of(at_ref[1] * n, n), n)
     other = pl.ds(pl.multiple_of((1 - at_ref[1]) * n, n), n)
 
@@ -154,15 +159,12 @@
     @pl.when(i < tiles)
     def _():
         total = part_ref[...] + dot(c_ref[...], last_ref[...], 0, 0)
-        mixed = (total * inv_ref[...]).astype(BF16)
-        m_ref[...] = mixed
-        m_all[pl.ds(pl.multiple_of(i * TILE, TILE), TILE), :] = mixed
+        m_all[pl.ds(pl.multiple_of(i * TILE, TILE), TILE), :] = (total * inv_ref[...]).astype(BF16)
 
     @pl.when(i == 0)
     def _():
         for copy in copies:
             copy.wait()
-        copy_out.start()
         b[...] = w[:, h:].astype(F32).T[:8, :]
 
     @pl.when(i < tiles)
@@ -176,29 +178,27 @@
             at = slice(j, j + 256)
             v = dot(mixed, w[:, at], 1, 0) + b[0:1, at]
             square = v * v
-            t = jnp.tanh(v * (GELU_A + (GELU_A * GELU_B) * square))
-            half = 0.5 + 0.5 * t
-            active = v * half
-            o_ref[:, at] = jnp.where(live, active, 0.0)
-            slope = half + (active - active * half) * (2 * GELU_A + (6 * GELU_A * GELU_B) * square)
-            grad = jnp.where(live, ct_ref[:, at].astype(F32) * slope, 0.0)
+            half = jnp.where(live, 0.5 + 0.5 * jnp.tanh(v * (GELU_A + (GELU_A * GELU_B) * square)), 0.0)
+            o_ref[:, at] = v * half
+            slope = half + (half - half * half) * (v * (2 * GELU_A + (6 * GELU_A * GELU_B) * square))
+            grad = ct_ref[:, at].astype(F32) * slope
             gl_all[rows, at] = grad.astype(BF16)
-            agl_ref[:, at] = (grad * inverse).astype(BF16)
+            agl_ref[rows, at] = (grad * inverse).astype(BF16)
             gb[:, at] += jnp.sum(grad.reshape(TILE // 8, 8, 256), axis=0)
-        own_ref[...] = gl_all[rows, mine]
 
     @pl.when(i == tiles)
     def _():
         o_ref[...] = jnp.zeros_like(o_ref)
+        far_ref[...] = dot(cl_ref[...], agl_ref[...], 1, 0).astype(BF16)
 
     @pl.when((i > tiles) & (i <= tiles + h // TILE))
     def _():
         at = pl.ds(pl.multiple_of((i - tiles - 1) * TILE, TILE), TILE)
+        kept_ref[...] = dot(m_all[:, at], gl_all[:, mine], 0, 0).astype(BF16)
         sent_ref[...] = dot(m_all[:, at], gl_all[:, other], 0, 0).astype(BF16)
 
     @pl.when(i > tiles + h // TILE)
     def _():
-        copy_out.wait()
         gb_ref[...] = jnp.broadcast_to(jnp.sum(gb[:, mine], axis=0, keepdims=True), gb_ref.shape)
         sent_ref[:SPARE, :] = jnp.broadcast_to(jnp.sum(gb[:, other], axis=0, keepdims=True), (SPARE, n)).astype(BF16)
 
@@ -220,6 +220,7 @@
             in_specs=[
                 pl.BlockSpec((TILE, h), row),
                 pl.BlockSpec((BOUND, TILE), lambda i, s: (below, jnp.minimum(i, tiles - 1))),
+                pl.BlockSpec((BOUND, live), lambda i, s: (below, 0), pipeline_mode=pl.Buffered(1)),
                 resident(last.shape),
                 pl.BlockSpec((TILE, 1), row),
                 pl.BlockSpec((TILE, h), row),
@@ -227,12 +228,11 @@
             + [ANY] * len(pieces),
             out_specs=[
                 pl.BlockSpec((TILE, h), lambda i, s: (jnp.minimum(i, tiles), 0)),
-                pl.BlockSpec((TILE, h), row),
-                pl.BlockSpec((TILE, n), row),
-                pl.BlockSpec((TILE, h), row),
-                ANY,
+                WHOLE,
                 resident((8, n)),
+                pl.BlockSpec((TILE, n), lambda i, s: (jnp.clip(i - tiles - 1, 0, blocks - 1), 0)),
                 pl.BlockSpec((TILE, n), lambda i, s: (jnp.maximum(i - tiles - 1, 0), 0)),
+                resident((BOUND, h)),
             ],
             scratch_shapes=[
                 pltpu.VMEM((h, pieces[0].shape[1]), BF16),
@@ -241,22 +241,20 @@
                 pltpu.VMEM((live, h), BF16),
                 pltpu.VMEM((8, h), F32),
                 pltpu.SemaphoreType.DMA((len(pieces), planes)),
-                pltpu.SemaphoreType.DMA,
             ],
         ),
         out_shape=[
             jax.ShapeDtypeStruct((nodes, h), F32),
-            jax.ShapeDtypeStruct((live, h), BF16),
-            jax.ShapeDtypeStruct((live, n), BF16),
-            jax.ShapeDtypeStruct((live, h), BF16),
-            jax.ShapeDtypeStruct((h, h), BF16),
+            pltpu.VMEM((live, h), BF16),
             jax.ShapeDtypeStruct((8, n), F32),
-            jax.ShapeDtypeStruct((h + SPARE, n), BF16),
+            jax.ShapeDtypeStruct((h, n), BF16),
+            pltpu.HBM((h + SPARE, n), BF16),
+            pltpu.HBM((BOUND, h), BF16),
         ],
         compiler_params=params(46),
         cost_estimate=cost(3 * live * h * h, live * h * 12),
         name="layer",
-    )(at, part, adjacency, last, inverse, cotangent, *pieces)
+    )(at, far(part), far(adjacency), far(adjacency), last, inverse, far(cotangent), *pieces)
 
 
 def halves(at_ref, value, rows):
@@ -275,21 +273,21 @@
     return jnp.concatenate([rows[0:1, :], rows[1:2, :]], axis=1).astype(F32)
 
 
-def grad_weight_kernel(at_ref, m_ref, g_ref, came_ref, cb_ref, gb_ref, _, a_own, a_sent, b_own, b_sent, gb_out, *, rows):
+def share_kernel(at_ref, kept_ref, came_ref, cb_ref, gb_ref, _, a_own, a_sent, b_own, b_sent, gb_out, *, rows):
     t = pl.program_id(0)
     last = pl.num_programs(0) - 1
-    n = g_ref.shape[1] // 2
+    n = kept_ref.shape[1] // 2
     groups = TILE // (4 * rows)
 
     @pl.when(t < last)
     def _():
-        part = dot(m_ref[...], g_ref[...], 0, 0) + came_ref[...].astype(F32)
+        part = kept_ref[...].astype(F32) + came_ref[...].astype(F32)
         for g in range(groups):
-            value = part[g * 4 * rows : (g + 1) * 4 * rows]
+            value = part[g * 4 * rows : (g + 1) * 4 * rows].astype(BF16)
             mine, other = halves(at_ref, value[:, :n], rows)
             at = slice(g * 2 * rows, (g + 1) * 2 * rows)
             a_own[at, :] = mine
-            a_sent[at, :] = other.astype(BF16)
+            a_sent[at, :] = other
             here = (t * groups + g) % 2 == at_ref[2]
             at = slice(g // 2 * 4 * rows, (g // 2 + 1) * 4 * rows)
 
@@ -299,7 +297,7 @@
 
             @pl.when(jnp.logical_not(here))
             def _():
-                b_sent[at, :] = value[:, n:].astype(BF16)
+                b_sent[at, :] = value[:, n:]
 
     @pl.when(t == last)
     def _():
@@ -308,9 +306,8 @@
         a_sent[:SPARE, :] = spare_rows(total, n)
 
 
-def grad_weight_share(at, mixed, low, came, bias, rows, after):
-    live, h = mixed.shape
-    n = low.shape[1]
+def share_rows(at, kept, came, bias, rows, after):
+    h, n = kept.shape
     blocks = h // TILE
     single = TILE == 4 * rows
     b_rows = TILE if single else TILE // 2
@@ -322,13 +319,12 @@
         return (tile(t) // 2 if single else tile(t), 0)
 
     return pl.pallas_call(
-        functools.partial(grad_weight_kernel, rows=rows),
+        functools.partial(share_kernel, rows=rows),
         grid_spec=pltpu.PrefetchScalarGridSpec(
             num_scalar_prefetch=1,
             grid=(blocks + 1,),
             in_specs=[
-                pl.BlockSpec((live, TILE), lambda t, s: (0, tile(t))),
-                resident((live, n)),
+                pl.BlockSpec((TILE, n), lambda t, s: (tile(t), 0)),
                 pl.BlockSpec((TILE, n), lambda t, s: (tile(t), 0)),
                 pl.BlockSpec((SPARE, n), lambda t, s: (h // SPARE, 0)),
                 resident((8, n)),
@@ -343,16 +339,16 @@
             ],
         ),
         out_shape=[
-            jax.ShapeDtypeStruct((h // 2, n // 2), F32),
-            jax.ShapeDtypeStruct((h // 2 + SPARE, n // 2), BF16),
-            jax.ShapeDtypeStruct((h // 2, n // 2), F32),
-            jax.ShapeDtypeStruct((h // 2, n // 2), BF16),
+            pltpu.HBM((h // 2, n // 2), BF16),
+            pltpu.HBM((h // 2 + SPARE, n // 2), BF16),
+            pltpu.HBM((h // 2, n // 2), BF16),
+            pltpu.HBM((h // 2, n // 2), BF16),
             jax.ShapeDtypeStruct((8, n), F32),
         ],
-        compiler_params=params(18),
-        cost_estimate=cost(2 * live * h * n, live * h * 3),
-        name="grad_weight",
-    )(at, mixed, low, came, came, bias, after)
+        compiler_params=params(10),
+        cost_estimate=cost(0, h * n * 8),
+        name="share",
+    )(at, kept, came, came, bias, after)
 
 
 def fold_kernel(at_ref, a_ref, a_came, b_ref, b_came, gb_ref, _, a_own, a_sent, b_own, b_sent, gb_out, *, rows):
@@ -363,10 +359,10 @@
         out = slice(z * two, (z + 1) * two)
         near = pl.ds(pl.multiple_of((2 * z + lo) * two, two), two)
         far = pl.ds(pl.multiple_of((2 * z + 1 - lo) * two, two), two)
-        a_own[out, :] = a_ref[near, :] + a_came[near, :].astype(F32)
-        a_sent[out, :] = (a_ref[far, :] + a_came[far, :].astype(F32)).astype(BF16)
+        a_own[out, :] = a_ref[near, :].astype(F32) + a_came[near, :].astype(F32)
+        a_sent[out, :] = (a_ref[far, :].astype(F32) + a_came[far, :].astype(F32)).astype(BF16)
         at = slice(z * 2 * two, (z + 1) * 2 * two)
-        mine, other = halves(at_ref, b_ref[at, :] + b_came[at, :].astype(F32), rows)
+        mine, other = halves(at_ref, b_ref[at, :].astype(F32) + b_came[at, :].astype(F32), rows)
         b_own[out, :] = mine
         b_sent[out, :] = other.astype(BF16)
     total = gb_ref[0:1, :] + from_spare(a_came[a_ref.shape[0] :, :])
@@ -390,7 +386,7 @@
         compiler_params=params(22),
         cost_estimate=cost(0, b_own.size * 9),
         name="fold",
-    )(at, a_own, a_came, b_own, b_came, bias, after)
+    )(at, far(a_own), far(a_came), far(b_own), far(b_came), bias, after)
 
 
 def part_kernel(at_ref, a_ref, a_came, b_ref, b_came, gb_ref, *refs, rows, planes):
@@ -465,81 +461,97 @@
             copy.wait()
 
 
-def scatter_bound(adjacency, grads, low, high, after):
+def scatter_bound(adjacency, grads):
     live, h = grads.shape
-    blocks = high - low
+    blocks = (adjacency.shape[0] - live) // BOUND - 1
     return pl.pallas_call(
         functools.partial(scatter_bound_kernel, count=blocks),
         grid=(blocks,),
-        in_specs=[pl.BlockSpec((BOUND, live), lambda i: (i + low + live // BOUND, 0)), resident((live, h))]
-        + [ANY] * len(after),
+        in_specs=[pl.BlockSpec((BOUND, live), lambda i: (i + live // BOUND, 0)), resident((live, h))],
         out_specs=[ANY] * blocks,
-        out_shape=[jax.ShapeDtypeStruct((BOUND, h), BF16)] * blocks,
+        out_shape=[pltpu.HBM((BOUND, h), BF16)] * blocks,
         scratch_shapes=[pltpu.VMEM((blocks, BOUND, h), BF16), pltpu.SemaphoreType.DMA((blocks,))],
         compiler_params=params(22),
         cost_estimate=cost(2 * blocks * BOUND * live * h, live * h * 4),
         name="scatter_bound",
-    )(adjacency, grads, *after)
-
-
-def grad_rows_kernel(c_ref, g_ref, w_hbm, *refs, low, tiles):
-    o_ref, lead_ref, w, sem = refs[-4:]
+    )(adjacency, grads)
+
+
+def grad_rows_kernel(at_ref, c_ref, g_ref, *refs, low, tiles, planes):
+    w, sem, sem_out = refs[-3:]
     i = pl.program_id(0)
-    copy = pltpu.make_async_copy(w_hbm.at[:, pl.ds(0, w.shape[1])], w, sem)
+    if low:
+        o_ref, lead_ref = refs[-5:-3]
+        copies = [pltpu.make_async_copy(refs[0], w, sem_out)]
+    else:
+        o_ref, lead_ref, w_ref = refs[-6:-3]
+        copies = fetch(refs[:8], planes, w, sem, at_ref)
+        copy_out = pltpu.make_async_copy(w, w_ref, sem_out)
 
     @pl.when(i == 0)
     def _():
-        copy.start()
-
-    if low:
+        for copy in copies:
+            copy.start()
+
+    @pl.when(low + i < tiles)
+    def _():
+        total = dot(c_ref[...], g_ref[...], 1, 0)
 
         @pl.when(i == 0)
         def _():
-            copy.wait()
-
-    @pl.when(low + i < tiles)
-    def _():
-        total = dot(c_ref[...], g_ref[...], 1, 0)
-        if low == 0:
-
-            @pl.when(i == 0)
-            def _():
-                lead_ref[...] = total
+            lead_ref[...] = total if low == 0 else jnp.zeros_like(lead_ref)
+            for copy in copies:
                 copy.wait()
+            if low == 0:
+                copy_out.start()
 
         @pl.when(low + i > 0)
         def _():
             o_ref[...] = dot(total.astype(BF16), w[...], 1, 1)
 
-    if low:
-        lead_ref[...] = jnp.zeros_like(lead_ref)
-
     @pl.when(low + i == tiles)
     def _():
         o_ref[...] = jnp.zeros_like(o_ref)
 
-
-def grad_rows(adjacency, grads, weight, nodes, low, high, before, after):
+    if low == 0:
+
+        @pl.when(i == pl.num_programs(0) - 1)
+        def _():
+            copy_out.wait()
+
+
+def grad_rows(at, adjacency, grads, weight, nodes, low, high, planes, before, after):
     live, h = grads.shape
     tiles = live // TILE
     extra = [] if before is None else [before]
-    return pl.pallas_call(
-        functools.partial(grad_rows_kernel, low=low, tiles=tiles),
-        grid=(high - low,),
-        in_specs=[
-            pl.BlockSpec((TILE, live), lambda i: (jnp.minimum(low + i, tiles - 1), 0)),
-            resident((live, h)),
-            ANY,
-        ]
-        + [ANY] * (len(extra) + len(after)),
-        out_specs=[pl.BlockSpec((TILE, h), lambda i: (low + i, 0)), resident((8, 128) if low else (TILE, h))],
-        out_shape=[jax.ShapeDtypeStruct((nodes, h), F32), TOKEN if low else jax.ShapeDtypeStruct((TILE, h), F32)],
-        scratch_shapes=[pltpu.VMEM((h, h), BF16), pltpu.SemaphoreType.DMA],
-        input_output_aliases={3: 0} if extra else {},
+    outs = [jax.ShapeDtypeStruct((nodes, h), F32), TOKEN if low else jax.ShapeDtypeStruct((TILE, h), F32)]
+    out_specs = [pl.BlockSpec((TILE, h), lambda i, s: (low + i, 0)), resident((8, 128) if low else (TILE, h))]
+    if low == 0:
+        outs += [jax.ShapeDtypeStruct((h, h), BF16)]
+        out_specs += [ANY]
+    return pl.pallas_call(
+        functools.partial(grad_rows_kernel, low=low, tiles=tiles, planes=planes),
+        grid_spec=pltpu.PrefetchScalarGridSpec(
+            num_scalar_prefetch=1,
+            grid=(high - low,),
+            in_specs=[
+                pl.BlockSpec((TILE, live), lambda i, s: (jnp.minimum(low + i, tiles - 1), 0)),
+                resident((live, h)),
+            ]
+            + [ANY] * (len(weight) + len(extra) + len(after)),
+            out_specs=out_specs,
+            scratch_shapes=[
+                pltpu.VMEM((h, h), BF16),
+                pltpu.SemaphoreType.DMA((len(weight), planes)),
+                pltpu.SemaphoreType.DMA,
+            ],
+        ),
+        out_shape=outs,
+        input_output_aliases={3 + len(weight): 0} if extra else {},
         compiler_params=params(30),
         cost_estimate=cost((2 * live + 2 * h) * (high - low) * TILE * h, live * h * 8),
         name="grad_rows",
-    )(adjacency, grads, weight, *extra, *after)
+    )(at, adjacency, grads, *weight, *extra, *after)
 
 
 def back_kernel(a_ref, b_ref, c_ref, d_ref, _, o_ref, p_ref):
@@ -558,7 +570,7 @@
         compiler_params=params(10),
         cost_estimate=cost(0, a.size * 12),
         name="back",
-    )(a, b, c, d, after)
+    )(far(a), far(b), far(c), far(d), after)
 
 
 def grad_lead_kernel(lead_ref, *refs):
@@ -648,34 +660,37 @@
     sheet = jnp.concatenate([sheet, *planes])
     half_sheet, row_sheet = swap_wa(sheet), swap_lo(sheet)
     inner_same, inner_other = swap_core(leading), swap_core(partner)
-    part = gather(adjacency, features, (partner, inner_same, inner_other, outer_same), live)
+    part = gather(adjacency, features, (partner, inner_same, inner_other, outer_same), live, [inverse, at])
     half_sheet, row_sheet, outer_same = tie([half_sheet, row_sheet, outer_same], [part])
     outer_other = swap_wa(outer_same)
     both_sheet, outer_other = tie([swap_lo(half_sheet), outer_other], [])
     pieces = [sheet, half_sheet, row_sheet, both_sheet]
     pieces = pieces + [swap_core(value) for value in pieces]
-    output, grads, own_low, mixed, matrix, bias_sum, sent = layer(
+    output, grads, bias_sum, kept, sent, outer_other_g = layer(
         at, part, adjacency, outer_other, inverse, cotangent, pieces, n_hi
     )
     came = swap_core(sent)
 
-    (outer_other_g,) = scatter_bound(adjacency, grads, 4, 5, [])
     outer_came = swap_wa(outer_other_g)
-
-    a, a_sent, b, b_sent, bias_sum = grad_weight_share(at, mixed, own_low, came, bias_sum, share, outer_other_g)
+    own_bound, inner_same_g, inner_other_g, outer_same_g = scatter_bound(adjacency, grads)
+    own_came, inner_came = swap_core(inner_other_g), swap_core(inner_same_g)
+
+    a, a_sent, b, b_sent, bias_sum = share_rows(at, kept, came, bias_sum, share, own_bound)
     a_came, b_came = swap_wa(a_sent), swap_lo(b_sent)
-    own_bound, inner_same_g, inner_other_g, outer_same_g = scatter_bound(adjacency, grads, 0, 4, [bias_sum])
-    own_came, inner_came = swap_core(inner_other_g), swap_core(inner_same_g)
     split, tiles = live // TILE // 2, -(-nodes // TILE)
-    grad_features, lead = grad_rows(adjacency, grads, matrix, nodes, 0, split, None, [own_bound])
+    grad_features, lead, matrix = grad_rows(at, adjacency, grads, pieces, nodes, 0, split, n_hi, None, [bias_sum, outer_came])
     outer_back, own_back = back(outer_same_g, outer_came, own_bound, own_came, lead)
-    returned = (inner_came, swap_wa(own_back), swap_outer(outer_back))
+    outer_back = swap_outer(outer_back)
     a, a_sent, b, b_sent, bias_sum = fold(at, a, a_came, b, b_came, bias_sum, share, own_back)
     a_came, b_came = swap_lo(a_sent), swap_wa(b_sent)
-    grad_features, token = grad_rows(adjacency, grads, matrix, nodes, split, tiles, grad_features, [bias_sum])
+    grad_features, token = grad_rows(
+        at, adjacency, grads, [matrix], nodes, split, tiles, n_hi, grad_features, [bias_sum]
+    )
     bias_sum, own, *rest = part_planes(
-        at, a, a_came, b, b_came, bias_sum, share, n_hi, [token, returned[1]]
+        at, a, a_came, b, b_came, bias_sum, share, n_hi, [token]
     )
+    (own_back,) = tie([own_back], [own])
+    returned = (inner_came, outer_back, swap_wa(own_back))
     rest = [rotate_hi(value, k + 1) for k, value in enumerate(rest)]
     grad_features, token = grad_lead(lead, returned, matrix, grad_features)
     mine, other = finish(at, bias_sum, own, rest, share, token)

time: 278 us -> 271 us (0.975)
  local copies, waits for them, and re-layouts: 27.2 us -> 17.7 us
  Pallas kernels: 143 us -> 147 us
    unnamed x54 -> x80, local copies, waits for them, and re-layouts: 21.4 us -> 12.9 us
    pallas_call x1, Pallas kernels: 44.2 us -> 52.4 us  [layer(): pl.pallas_call(functools.partial(layer_kernel, tiles=tiles, planes=planes...]
    pallas_call x2 -> x1, Pallas kernels: 9.79 us -> 8.43 us  [scatter_bound(): pl.pallas_call(functools.partial(scatter_bound_kernel, count=blocks), gri...]
  transfers between devices with their start and end apart: 29 -> 29, of which waited for: 14 -> 14; matrix products, arithmetic and copies ran while one was open for 1% -> 1% of each run, Pallas kernels for 35% -> 34%
where the time goes in v4:
time: 271 us; the launch traced here: 268 us
  Pallas kernels  147 us (54%)
  waiting for transfers between devices  72.9 us (27%)
  starting transfers between devices  28.9 us (11%)
  local copies, waits for them, and re-layouts  17.7 us (7%)
    ppermute x29, waiting for transfers between devices, permute(): return lax.ppermute(value, axes, [(s, b * n_wa + w) for s, (b, w) in pairs])  72.9 us
    pallas_call x1, Pallas kernels, layer(): pl.pallas_call(functools.partial(layer_kernel, tiles=tiles, planes=planes...  52.4 us
    pallas_call x2, Pallas kernels, grad_rows(): pl.pallas_call(functools.partial(grad_rows_kernel, low=low, tiles=tiles,...  30.8 us
    ppermute x29, starting transfers between devices, permute(): return lax.ppermute(value, axes, [(s, b * n_wa + w) for s, (b, w) in pairs])  28.9 us
    pallas_call x1, Pallas kernels, gather(): pl.pallas_call(functools.partial(gather_kernel, count=len(blocks)), grid=...  21.8 us
    pallas_call x1, Pallas kernels, counts(): pl.pallas_call(counts_kernel, grid=(tiles,), in_specs=[pl.BlockSpec((FANO...  15.5 us
    unnamed x80, local copies, waits for them, and re-layouts  12.9 us
    pallas_call x1, Pallas kernels, scatter_bound(): pl.pallas_call(functools.partial(scatter_bound_kernel, count=blocks), gri...  8.43 us
  transfers between devices with their start and end apart: 29, of which 14 were waited for; matrix products, arithmetic and copies ran while one was open for 1% of the time, Pallas kernels for 34%

profile of v4, /device:TPU:11, one launch (start us, length us, event | category | flops | bytes accessed | tf_op | source)
XLA Modules:
  0.0 268.5 jit_solution(9214593149544910346)
XLA Ops:
  0.7 2.4 slice.18
  4.1 2.5 collective-permute-start.2
  6.6 2.2 collective-permute-start.1
  8.8 2.9 %collective-permute-start.6 = (bf16[256,2048]{1,0:T(8,128)(2,1)}, bf16[256,2048]{1,0:T(8,128)(2,1)}, u32[]{:S(2)}, u32[]{:S(2)}) collective-permute-start(bf16[256,2048]{1,0:T(8,128)(2,1)} %slice.18), channel_id=1, source_target_pairs={{0,30},{1,31},{2,4},{3,5},{4,2},{5,3},{6,8},{7,9},{8,6},{9,7},{10,... | collective-permute-start | bytes 3145736 | tf_op jit(solution)/shard_map/ppermute | solution.py:618
  11.9 15.5 %counts.1.refs_4_.c_ref.cl_ref = bf16[2816,1536]{1,0:T(8,128)(2,1)S(1)} custom-call(s32[16,1536]{1,0:T(8,128)S(1)} %fusion.2.index_ref), custom_call_target="tpu_custom_call" | custom-call | bytes 4325376 | tf_op jit(solution)/shard_map/counts/pallas_call | solution.py:86
  27.5 13.8 %collective-permute-done.1.refs_1_ = bf16[64,2176]{1,0:T(8,128)(2,1)S(1)} collective-permute-done((bf16[64,2176]{1,0:T(8,128)(2,1)S(1)}, bf16[64,2176]{1,0:T(8,128)(2,1)S(1)}, u32[]{:S(2)}, u32[]{:S(2)}) %collective-permute-start.1) | collective-permute-done | bytes 278560 | tf_op jit(solution)/shard_map/ppermute | solution.py:618
  45.3 21.8 %gather.1.refs_3_.part_ref = f32[1536,2048]{1,0:T(8,128)S(1)} custom-call(bf16[2816,1536]{1,0:T(8,128)(2,1)} %copy-done, bf16[1664,2048]{1,0:T(8,128)(2,1)} %t_ref.1, bf16[256,2048]{1,0:T(8,128)(2,1)} %get-tuple-element.49.refs_0_, bf16[256,2048]{1,0:T(8,128)(2,1)} %collective-permute-done.4.refs_1_, bf16[256,2048]{1,0:T(8,128)(2,1)} %collective-permute-done.5.refs_2_, ...), custom_call_target="tpu_custom_call" | custom-call | flops 1006632960 | bytes 1179648 | tf_op jit(solution)/shard_map/gather/pallas_call | solution.py:111
  67.1 2.0 collective-permute-done.8.refs_1_
  69.2 2.7 copy-done.1
  71.8 1.3 collective-permute-start.9
  75.0 22.1 %collective-permute-done.10.refs_1_ = bf16[256,2048]{1,0:T(8,128)(2,1)S(1)} collective-permute-done((bf16[256,2048]{1,0:T(8,128)(2,1)}, bf16[256,2048]{1,0:T(8,128)(2,1)S(1)}, u32[]{:S(2)}, u32[]{:S(2)}) %collective-permute-start.10) | collective-permute-done | bytes 1048608 | tf_op jit(solution)/shard_map/ppermute | solution.py:618
  100.0 2.3 collective-permute-done.14.refs_7_
  103.4 1.4 copy-done.19
  104.8 52.4 %layer.1 = (f32[1664,2048]{1,0:T(8,128)}, bf16[1536,2048]{1,0:T(8,128)(2,1)S(1)}, f32[8,1024]{1,0:T(8,128)S(1)}, bf16[2048,1024]{1,0:T(8,128)(2,1)}, bf16[2064,1...) custom-call(s32[5]{0:T(128)S(1)} %stack.23.refs_5_.at_ref, f32[1536,2048]{1,0:T(8,128)} %copy-done.1, ...), custom_call_target="tpu_custom_call" | custom-call | flops 1207959552 | bytes 2359296 | tf_op jit(solution)/shard_map/layer/pallas_call | solution.py:215
  158.9 8.4 %scatter_bound.1 = (bf16[256,2048]{1,0:T(8,128)(2,1)}, bf16[256,2048]{1,0:T(8,128)(2,1)}, bf16[256,2048]{1,0:T(8,128)(2,1)}, bf16[256,2048]{1,0:T(8,128)(2,1)}) custom-call(bf16[2816,1536]{1,0:T(8,128)(2,1)S(1)} %bitcast.11, bf16[1536,2048]{1,0:T(8,128)(2,1)S(1)} %get-tuple-element.59.g_ref), custom_call_target="tpu_custom_call" | custom-call | flops 402653184 | bytes 786432 | tf_op jit(solution)/shard_map/scatter_bound/pallas_call | solution.py:467
  167.4 1.4 copy-done.21
  168.8 5.4 %share.1 = (bf16[1024,512]{1,0:T(8,128)(2,1)}, bf16[1040,512]{1,0:T(8,128)(2,1)}, bf16[1024,512]{1,0:T(8,128)(2,1)}, bf16[1024,512]{1,0:T(8,128)(2,1)}, f32[8,1024]{1,0:T(8,128)S(1)}) custom-call(s32[5]{0:T(128)S(1)} %stack.23.refs_5_.at_ref, bf16[2048,1024]{1,0:T(8,128)(2,1)S(1)} %copy-done.20, ...), custom_call_target="tpu_custom_call" | custom-call | bytes 1048576 | tf_op jit(solution)/shard_map/share/pallas_call | solution.py:321
  175.1 1.3 collective-permute-start.21
  176.4 6.0 %collective-permute-done.16.refs_9_.b_ref = bf16[256,2048]{1,0:T(8,128)(2,1)S(1)} collective-permute-done((bf16[256,2048]{1,0:T(8,128)(2,1)}, bf16[256,2048]{1,0:T(8,128)(2,1)S(1)}, u32[]{:S(2)}, u32[]{:S(2)}) %collective-permute-start.16) | collective-permute-done | bytes 1048608 | tf_op jit(solution)/shard_map/ppermute | solution.py:618
  182.6 15.3 %grad_rows.2 = (f32[1664,2048]{1,0:T(8,128)}, f32[256,2048]{1,0:T(8,128)S(1)}, bf16[2048,2048]{1,0:T(8,128)(2,1)}) custom-call(s32[5]{0:T(128)S(1)} %stack.23.refs_5_.at_ref, bf16[2816,1536]{1,0:T(8,128)(2,1)} %copy-done, bf16[1536,2048]{1,0:T(8,128)(2,1)S(1)} %bitcast.15, bf16[256,2176]{1,0:T(8,128)(2,1)S(1)} %copy-done.5, ...), custom_call_target="tpu_custom_call" | custom-call | flops 704643072 | bytes 1572864 | tf_op jit(solution)/shard_map/grad_rows/pallas_call | solution.py:532
  198.9 3.7 %back.1 = (bf16[256,2048]{1,0:T(8,128)(2,1)S(1)}, bf16[256,2048]{1,0:T(8,128)(2,1)S(1)}) custom-call(bf16[256,2048]{1,0:T(8,128)(2,1)} %get-tuple-element.68.a_ref, bf16[256,2048]{1,0:T(8,128)(2,1)} %copy-done.22, bf16[256,2048]{1,0:T(8,128)(2,1)} %get-tuple-element.63._.c_ref, bf16[256,2048]{1,0:T(8,128)(2,1)} %copy-done.26, ...), custom_call_target="tpu_custom_call" | custom-call | bytes 393216 | tf_op jit(solution)/shard_map/back/pallas_call | solution.py:564
  202.6 2.6 collective-permute-done.20.a_came
  206.3 2.8 %fold.1 = (f32[512,512]{1,0:T(8,128)S(1)}, bf16[528,512]{1,0:T(8,128)(2,1)S(1)}, f32[512,512]{1,0:T(8,128)S(1)}, bf16[512,512]{1,0:T(8,128)(2,1)S(1)}, f32[8,1024]{1,0:T(8,128)S(1)}) custom-call(s32[5]{0:T(128)S(1)} %stack.23.refs_5_.at_ref, bf16[1024,512]{1,0:T(8,128)(2,1)} %get-tuple-element.72.a_ref, bf16[1040,512]{1,0:T(8,128)(2,1)} %copy-done.23, ...), custom_call_target="tpu_custom_call" | custom-call | bytes 294912 | tf_op jit(solution)/shard_map/fold/pallas_call | solution.py:375
  209.2 1.5 collective-permute-start.22
  210.8 1.5 collective-permute-start.17
  213.4 3.4 %copy-done.3 = bf16[2048,2048]{1,0:T(8,128)(2,1)S(1)} copy-done((bf16[2048,2048]{1,0:T(8,128)(2,1)S(1)}, bf16[2048,2048]{1,0:T(8,128)(2,1)}, u32[]{:S(2)}) %copy-start.3) | copy-done | bytes 8388632
  216.8 15.5 %grad_rows.3 = (f32[1664,2048]{1,0:T(8,128)}, f32[8,128]{1,0:T(8,128)S(1)}) custom-call(s32[5]{0:T(128)S(1)} %stack.23.refs_5_.at_ref, bf16[2816,1536]{1,0:T(8,128)(2,1)S(1)} %bitcast.13, bf16[1536,2048]{1,0:T(8,128)(2,1)S(1)} %bitcast.17, bf16[2048,2048]{1,0:T(8,128)(2,1)S(1)} %copy-done.3, ...), custom_call_target="tpu_custom_call", output_to_operand_aliasing={{0}: (4, {})} | custom-call | flops 939524096 | bytes 1572864 | tf_op jit(solution)/shard_map/grad_rows/pallas_call | solution.py:532
  235.4 2.2 collective-permute-start.25
  238.8 7.2 %collective-permute-done.19.refs_1_ = bf16[256,2048]{1,0:T(8,128)(2,1)S(1)} collective-permute-done((bf16[256,2048]{1,0:T(8,128)(2,1)S(1)}, bf16[256,2048]{1,0:T(8,128)(2,1)S(1)}, u32[]{:S(2)}, u32[]{:S(2)}) %collective-permute-start.19) | collective-permute-done | bytes 1048608 | tf_op jit(solution)/shard_map/ppermute | solution.py:618
  246.0 10.3 %collective-permute-done.24.refs_2_ = bf16[256,2048]{1,0:T(8,128)(2,1)S(1)} collective-permute-done((bf16[256,2048]{1,0:T(8,128)(2,1)S(1)}, bf16[256,2048]{1,0:T(8,128)(2,1)S(1)}, u32[]{:S(2)}, u32[]{:S(2)}) %collective-permute-start.24) | collective-permute-done | bytes 1048608 | tf_op jit(solution)/shard_map/ppermute | solution.py:618
  256.3 4.3 %grad_lead.1 = (f32[1664,2048]{1,0:T(8,128)}, f32[8,128]{1,0:T(8,128)S(1)}) custom-call(f32[256,2048]{1,0:T(8,128)S(1)} %get-tuple-element.66._.lead_ref, bf16[256,2048]{1,0:T(8,128)(2,1)S(1)} %collective-permute-done.17.refs_0_, bf16[256,2048]{1,0:T(8,128)(2,1)S(1)} %collective-permute-done.19.refs_1_, ...), custom_call_target="tpu_custom_call", output_to_operand_aliasing={{0}: (5, {})} | custom-call | flops 134217728 | bytes 524288 | tf_op jit(solution)/shard_map/grad_lead/pallas_call | solution.py:592
  260.7 3.3 %collective-permute-done.27.refs_2_ = bf16[144,1024]{1,0:T(8,128)(2,1)S(1)} collective-permute-done((bf16[144,1024]{1,0:T(8,128)(2,1)S(1)}, bf16[144,1024]{1,0:T(8,128)(2,1)S(1)}, u32[]{:S(2)}, u32[]{:S(2)}) %collective-permute-start.27) | collective-permute-done | bytes 294944 | tf_op jit(solution)/shard_map/ppermute | solution.py:618
  (138 shorter events, 25.1 us)
Async XLA Ops:
  3.0 38.3 %collective-permute-start = (bf16[256,2048]{1,0:T(8,128)(2,1)}, bf16[256,2048]{1,0:T(8,128)(2,1)}, u32[]{:S(2)}, u32[]{:S(2)}) collective-permute-start(bf16[256,2048]{1,0:T(8,128)(2,1)} %slice.18), channel_id=1, source_target_pairs={{0,1},{1,0},{2,3},{3,2},{4,5},{5,4},{6,7},{7,6},{8,9},{9,8},{10,11... | collective-permute-start | bytes 3145736 | tf_op jit(solution)/shard_map/ppermute | solution.py:618
  4.0 23.4 %collective-permute-start.3 = (bf16[64,2176]{1,0:T(8,128)(2,1)S(1)}, bf16[64,2176]{1,0:T(8,128)(2,1)S(1)}, u32[]{:S(2)}, u32[]{:S(2)}) collective-permute-start(bf16[64,2176]{1,0:T(8,128)(2,1)S(1)} %pad_maximum_fusion.1), channel_id=1, source_target_pairs={{0,24},{1,25},{2,26},{3,27},{4,28},{5,29},{6,30},{7,31},{8,0},{9,1... | collective-permute-start | bytes 835592 | tf_op jit(solution)/shard_map/ppermute | solution.py:618
  4.1 23.4 %collective-permute-start.2 = (bf16[64,2176]{1,0:T(8,128)(2,1)S(1)}, bf16[64,2176]{1,0:T(8,128)(2,1)S(1)}, u32[]{:S(2)}, u32[]{:S(2)}) collective-permute-start(bf16[64,2176]{1,0:T(8,128)(2,1)S(1)} %pad_maximum_fusion.1), channel_id=1, source_target_pairs={{0,16},{1,17},{2,18},{3,19},{4,20},{5,21},{6,22},{7,23},{8,24},{9,... | collective-permute-start | bytes 835592 | tf_op jit(solution)/shard_map/ppermute | solution.py:618
  6.6 34.8 %collective-permute-start.1 = (bf16[64,2176]{1,0:T(8,128)(2,1)S(1)}, bf16[64,2176]{1,0:T(8,128)(2,1)S(1)}, u32[]{:S(2)}, u32[]{:S(2)}) collective-permute-start(bf16[64,2176]{1,0:T(8,128)(2,1)S(1)} %pad_maximum_fusion.1), channel_id=1, source_target_pairs={{0,8},{1,9},{2,10},{3,11},{4,12},{5,13},{6,14},{7,15},{8,16},{9,17... | collective-permute-start | bytes 835592 | tf_op jit(solution)/shard_map/ppermute | solution.py:618
  8.8 36.4 %collective-permute-start.6 = (bf16[256,2048]{1,0:T(8,128)(2,1)}, bf16[256,2048]{1,0:T(8,128)(2,1)}, u32[]{:S(2)}, u32[]{:S(2)}) collective-permute-start(bf16[256,2048]{1,0:T(8,128)(2,1)} %slice.18), channel_id=1, source_target_pairs={{0,30},{1,31},{2,4},{3,5},{4,2},{5,3},{6,8},{7,9},{8,6},{9,7},{10,... | collective-permute-start | bytes 3145736 | tf_op jit(solution)/shard_map/ppermute | solution.py:618
  27.4 17.7 %collective-permute-start.4 = (bf16[256,2048]{1,0:T(8,128)(2,1)}, bf16[256,2048]{1,0:T(8,128)(2,1)}, u32[]{:S(2)}, u32[]{:S(2)}) collective-permute-start(bf16[256,2048]{1,0:T(8,128)(2,1)} %slice.18), channel_id=1, source_target_pairs={{0,2},{1,3},{2,0},{3,1},{4,6},{5,7},{6,4},{7,5},{8,10},{9,11},{10,... | collective-permute-start | bytes 3145736 | tf_op jit(solution)/shard_map/ppermute | solution.py:618
  41.3 3.9 %collective-permute-start.5 = (bf16[256,2048]{1,0:T(8,128)(2,1)}, bf16[256,2048]{1,0:T(8,128)(2,1)}, u32[]{:S(2)}, u32[]{:S(2)}) collective-permute-start(bf16[256,2048]{1,0:T(8,128)(2,1)} %get-tuple-element.49.refs_0_), channel_id=1, source_target_pairs={{0,2},{1,3},{2,0},{3,1},{4,6},{5,7},{6,4},{7,5},{8,10},{9,11},{10,... | collective-permute-start | bytes 3145736 | tf_op jit(solution)/shard_map/ppermute | solution.py:618
  42.7 26.4 %collective-permute-start.8 = (bf16[256,2176]{1,0:T(8,128)(2,1)S(1)}, bf16[256,2176]{1,0:T(8,128)(2,1)S(1)}, u32[]{:S(2)}, u32[]{:S(2)}) collective-permute-start(bf16[256,2176]{1,0:T(8,128)(2,1)S(1)} %pad_maximum_fusion.refs_0_), channel_id=1, source_target_pairs={{0,4},{1,5},{2,6},{3,7},{4,0},{5,1},{6,2},{7,3},{8,12},{9,13},{10,... | collective-permute-start | bytes 3342344 | tf_op jit(solution)/shard_map/ppermute | solution.py:618
  42.8 26.4 %collective-permute-start.7 = (bf16[256,2176]{1,0:T(8,128)(2,1)S(1)}, bf16[256,2176]{1,0:T(8,128)(2,1)}, u32[]{:S(2)}, u32[]{:S(2)}) collective-permute-start(bf16[256,2176]{1,0:T(8,128)(2,1)S(1)} %pad_maximum_fusion.refs_0_), channel_id=1, source_target_pairs={{0,1},{1,0},{2,3},{3,2},{4,5},{5,4},{6,7},{7,6},{8,9},{9,8},{10,11... | collective-permute-start | bytes 3342344 | tf_op jit(solution)/shard_map/ppermute | solution.py:618
  71.8 26.0 %collective-permute-start.9 = (bf16[256,2176]{1,0:T(8,128)(2,1)}, bf16[256,2176]{1,0:T(8,128)(2,1)S(1)}, u32[]{:S(2)}, u32[]{:S(2)}) collective-permute-start(bf16[256,2176]{1,0:T(8,128)(2,1)} %get-tuple-element.53.refs_1_), channel_id=1, source_target_pairs={{0,4},{1,5},{2,6},{3,7},{4,0},{5,1},{6,2},{7,3},{8,12},{9,13},{10,... | collective-permute-start | bytes 3342344 | tf_op jit(solution)/shard_map/ppermute | solution.py:618
  73.1 24.0 %collective-permute-start.10 = (bf16[256,2048]{1,0:T(8,128)(2,1)}, bf16[256,2048]{1,0:T(8,128)(2,1)S(1)}, u32[]{:S(2)}, u32[]{:S(2)}) collective-permute-start(bf16[256,2048]{1,0:T(8,128)(2,1)} %get-tuple-element.54), channel_id=1, source_target_pairs={{0,1},{1,0},{2,3},{3,2},{4,5},{5,4},{6,7},{7,6},{8,9},{9,8},{10,11... | collective-permute-start | bytes 3145736 | tf_op jit(solution)/shard_map/ppermute | solution.py:618
  73.4 26.6 %collective-permute-start.11 = (bf16[256,2176]{1,0:T(8,128)(2,1)S(1)}, bf16[256,2176]{1,0:T(8,128)(2,1)S(1)}, u32[]{:S(2)}, u32[]{:S(2)}) collective-permute-start(bf16[256,2176]{1,0:T(8,128)(2,1)S(1)} %pad_maximum_fusion.refs_0_), channel_id=1, source_target_pairs={{0,2},{1,3},{2,0},{3,1},{4,6},{5,7},{6,4},{7,5},{8,10},{9,11},{10,... | collective-permute-start | bytes 3342344 | tf_op jit(solution)/shard_map/ppermute | solution.py:618
  74.5 25.5 %collective-permute-start.12 = (bf16[256,2176]{1,0:T(8,128)(2,1)}, bf16[256,2176]{1,0:T(8,128)(2,1)S(1)}, u32[]{:S(2)}, u32[]{:S(2)}) collective-permute-start(bf16[256,2176]{1,0:T(8,128)(2,1)} %get-tuple-element.53.refs_1_), channel_id=1, source_target_pairs={{0,2},{1,3},{2,0},{3,1},{4,6},{5,7},{6,4},{7,5},{8,10},{9,11},{10,... | collective-permute-start | bytes 3342344 | tf_op jit(solution)/shard_map/ppermute | solution.py:618
  74.5 25.5 %collective-permute-start.13 = (bf16[256,2176]{1,0:T(8,128)(2,1)S(1)}, bf16[256,2176]{1,0:T(8,128)(2,1)S(1)}, u32[]{:S(2)}, u32[]{:S(2)}) collective-permute-start(bf16[256,2176]{1,0:T(8,128)(2,1)S(1)} %get-tuple-element.56.refs_2_), channel_id=1, source_target_pairs={{0,2},{1,3},{2,0},{3,1},{4,6},{5,7},{6,4},{7,5},{8,10},{9,11},{10,... | collective-permute-start | bytes 3342344 | tf_op jit(solution)/shard_map/ppermute | solution.py:618
  98.8 3.6 %collective-permute-start.14 = (bf16[256,2176]{1,0:T(8,128)(2,1)S(1)}, bf16[256,2176]{1,0:T(8,128)(2,1)S(1)}, u32[]{:S(2)}, u32[]{:S(2)}) collective-permute-start(bf16[256,2176]{1,0:T(8,128)(2,1)S(1)} %get-tuple-element.57.refs_3_), channel_id=1, source_target_pairs={{0,2},{1,3},{2,0},{3,1},{4,6},{5,7},{6,4},{7,5},{8,10},{9,11},{10,... | collective-permute-start | bytes 3342344 | tf_op jit(solution)/shard_map/ppermute | solution.py:618
  103.4 55.5 %slice-start = ((s8[8650752]{0:T(1024)(128)(4,1)}), s8[4194304]{0:T(1024)(128)(4,1)S(1)}, s32[]{:S(2)}) async-start(s8[8650752]{0:T(1024)(128)(4,1)} %bitcast.10), calls=%async_computation | async-start | bytes 8388608
  104.8 54.1 %slice-start.1 = ((s8[8650752]{0:T(1024)(128)(4,1)}), s8[4194304]{0:T(1024)(128)(4,1)S(1)}, s32[]{:S(2)}) async-start(s8[8650752]{0:T(1024)(128)(4,1)} %bitcast.10), calls=%async_computation.1 | async-start | bytes 8388608
  104.8 54.1 %slice-start.2 = ((s8[8650752]{0:T(1024)(128)(4,1)}), s8[262144]{0:T(1024)(128)(4,1)S(1)}, s32[]{:S(2)}) async-start(s8[8650752]{0:T(1024)(128)(4,1)} %bitcast.10), calls=%async_computation.2 | async-start | bytes 524288
  157.2 10.2 %collective-permute-start.15 = (bf16[2064,1024]{1,0:T(8,128)(2,1)}, bf16[2064,1024]{1,0:T(8,128)(2,1)S(1)}, u32[]{:S(2)}, u32[]{:S(2)}) collective-permute-start(bf16[2064,1024]{1,0:T(8,128)(2,1)} %get-tuple-element.61), channel_id=1, source_target_pairs={{0,2},{1,3},{2,0},{3,1},{4,6},{5,7},{6,4},{7,5},{8,10},{9,11},{10,... | collective-permute-start | bytes 12681224 | tf_op jit(solution)/shard_map/ppermute | solution.py:618
  157.6 24.8 %collective-permute-start.16 = (bf16[256,2048]{1,0:T(8,128)(2,1)}, bf16[256,2048]{1,0:T(8,128)(2,1)S(1)}, u32[]{:S(2)}, u32[]{:S(2)}) collective-permute-start(bf16[256,2048]{1,0:T(8,128)(2,1)} %get-tuple-element.65), channel_id=1, source_target_pairs={{0,1},{1,0},{2,3},{3,2},{4,5},{5,4},{6,7},{7,6},{8,9},{9,8},{10,11... | collective-permute-start | bytes 3145736 | tf_op jit(solution)/shard_map/ppermute | solution.py:618
  174.2 31.1 %collective-permute-start.20 = (bf16[1040,512]{1,0:T(8,128)(2,1)}, bf16[1040,512]{1,0:T(8,128)(2,1)S(1)}, u32[]{:S(2)}, u32[]{:S(2)}) collective-permute-start(bf16[1040,512]{1,0:T(8,128)(2,1)} %get-tuple-element.73), channel_id=1, source_target_pairs={{0,1},{1,0},{2,3},{3,2},{4,5},{5,4},{6,7},{7,6},{8,9},{9,8},{10,11... | collective-permute-start | bytes 3194888 | tf_op jit(solution)/shard_map/ppermute | solution.py:618
  174.4 23.5 %collective-permute-start.18 = (bf16[256,2048]{1,0:T(8,128)(2,1)}, bf16[256,2048]{1,0:T(8,128)(2,1)S(1)}, u32[]{:S(2)}, u32[]{:S(2)}) collective-permute-start(bf16[256,2048]{1,0:T(8,128)(2,1)} %get-tuple-element.69), channel_id=1, source_target_pairs={{0,2},{1,3},{2,0},{3,1},{4,6},{5,7},{6,4},{7,5},{8,10},{9,11},{10,... | collective-permute-start | bytes 3145736 | tf_op jit(solution)/shard_map/ppermute | solution.py:618
  175.1 27.5 %collective-permute-start.21 = (bf16[1024,512]{1,0:T(8,128)(2,1)}, bf16[1024,512]{1,0:T(8,128)(2,1)S(1)}, u32[]{:S(2)}, u32[]{:S(2)}) collective-permute-start(bf16[1024,512]{1,0:T(8,128)(2,1)} %get-tuple-element.75), channel_id=1, source_target_pairs={{0,4},{1,5},{2,6},{3,7},{4,0},{5,1},{6,2},{7,3},{8,12},{9,13},{10,... | collective-permute-start | bytes 3145736 | tf_op jit(solution)/shard_map/ppermute | solution.py:618
  209.2 24.2 %collective-permute-start.22 = (bf16[528,512]{1,0:T(8,128)(2,1)S(1)}, bf16[528,512]{1,0:T(8,128)(2,1)S(1)}, u32[]{:S(2)}, u32[]{:S(2)}) collective-permute-start(bf16[528,512]{1,0:T(8,128)(2,1)S(1)} %get-tuple-element.77), channel_id=1, source_target_pairs={{0,4},{1,5},{2,6},{3,7},{4,0},{5,1},{6,2},{7,3},{8,12},{9,13},{10,... | collective-permute-start | bytes 1622024 | tf_op jit(solution)/shard_map/ppermute | solution.py:618
  210.7 21.6 %collective-permute-start.23 = (bf16[512,512]{1,0:T(8,128)(2,1)S(1)}, bf16[512,512]{1,0:T(8,128)(2,1)S(1)}, u32[]{:S(2)}, u32[]{:S(2)}) collective-permute-start(bf16[512,512]{1,0:T(8,128)(2,1)S(1)} %get-tuple-element.79), channel_id=1, source_target_pairs={{0,1},{1,0},{2,3},{3,2},{4,5},{5,4},{6,7},{7,6},{8,9},{9,8},{10,11... | collective-permute-start | bytes 1572872 | tf_op jit(solution)/shard_map/ppermute | solution.py:618
  210.8 27.7 %collective-permute-start.17 = (bf16[256,2048]{1,0:T(8,128)(2,1)S(1)}, bf16[256,2048]{1,0:T(8,128)(2,1)S(1)}, u32[]{:S(2)}, u32[]{:S(2)}) collective-permute-start(bf16[256,2048]{1,0:T(8,128)(2,1)S(1)} %copy-done.29), channel_id=1, source_target_pairs={{0,2},{1,3},{2,0},{3,1},{4,6},{5,7},{6,4},{7,5},{8,10},{9,11},{10,... | collective-permute-start | bytes 3145736 | tf_op jit(solution)/shard_map/ppermute | solution.py:618
  212.3 33.7 %collective-permute-start.19 = (bf16[256,2048]{1,0:T(8,128)(2,1)S(1)}, bf16[256,2048]{1,0:T(8,128)(2,1)S(1)}, u32[]{:S(2)}, u32[]{:S(2)}) collective-permute-start(bf16[256,2048]{1,0:T(8,128)(2,1)S(1)} %get-tuple-element.70), channel_id=1, source_target_pairs={{0,30},{1,31},{2,4},{3,5},{4,2},{5,3},{6,8},{7,9},{8,6},{9,7},{10,... | collective-permute-start | bytes 3145736 | tf_op jit(solution)/shard_map/ppermute | solution.py:618
  234.1 22.2 %collective-permute-start.24 = (bf16[256,2048]{1,0:T(8,128)(2,1)S(1)}, bf16[256,2048]{1,0:T(8,128)(2,1)S(1)}, u32[]{:S(2)}, u32[]{:S(2)}) collective-permute-start(bf16[256,2048]{1,0:T(8,128)(2,1)S(1)} %tie.7), channel_id=1, source_target_pairs={{0,1},{1,0},{2,3},{3,2},{4,5},{5,4},{6,7},{7,6},{8,9},{9,8},{10,11... | collective-permute-start | bytes 3145736 | tf_op jit(solution)/shard_map/ppermute | solution.py:618
  235.4 25.3 %collective-permute-start.25 = (bf16[144,1024]{1,0:T(8,128)(2,1)S(1)}, bf16[144,1024]{1,0:T(8,128)(2,1)S(1)}, u32[]{:S(2)}, u32[]{:S(2)}) collective-permute-start(bf16[144,1024]{1,0:T(8,128)(2,1)S(1)} %get-tuple-element.88), channel_id=1, source_target_pairs={{0,8},{1,9},{2,10},{3,11},{4,12},{5,13},{6,14},{7,15},{8,16},{9,17... | collective-permute-start | bytes 884744 | tf_op jit(solution)/shard_map/ppermute | solution.py:618
  237.6 23.1 %collective-permute-start.26 = (bf16[144,1024]{1,0:T(8,128)(2,1)S(1)}, bf16[144,1024]{1,0:T(8,128)(2,1)S(1)}, u32[]{:S(2)}, u32[]{:S(2)}) collective-permute-start(bf16[144,1024]{1,0:T(8,128)(2,1)S(1)} %get-tuple-element.89), channel_id=1, source_target_pairs={{0,16},{1,17},{2,18},{3,19},{4,20},{5,21},{6,22},{7,23},{8,24},{9,... | collective-permute-start | bytes 884744 | tf_op jit(solution)/shard_map/ppermute | solution.py:618
  238.5 25.4 %collective-permute-start.27 = (bf16[144,1024]{1,0:T(8,128)(2,1)S(1)}, bf16[144,1024]{1,0:T(8,128)(2,1)S(1)}, u32[]{:S(2)}, u32[]{:S(2)}) collective-permute-start(bf16[144,1024]{1,0:T(8,128)(2,1)S(1)} %get-tuple-element.90), channel_id=1, source_target_pairs={{0,24},{1,25},{2,26},{3,27},{4,28},{5,29},{6,30},{7,31},{8,0},{9,1... | collective-permute-start | bytes 884744 | tf_op jit(solution)/shard_map/ppermute | solution.py:618
  264.7 2.3 collective-permute-start.28
  (37 other events, 424.6 us)

commit v5 on v4

--- a/solution.py
+++ b/solution.py
@@ -23,11 +23,16 @@
 SMEM = pl.BlockSpec(memory_space=pltpu.SMEM)
 WHOLE = pl.BlockSpec(memory_space=pltpu.VMEM)
 SPARE = 16
+FIRST = 4
 TOKEN = jax.ShapeDtypeStruct((8, 128), F32)
 
 
 def params(mib):
     return pltpu.CompilerParams(vmem_limit_bytes=mib * MIB)
+
+
+def held(value):
+    return pltpu.with_memory_space_constraint(value, pltpu.VMEM)
 
 
 def far(value):
@@ -67,7 +72,8 @@
     return value.astype(F32).astype(BF16)
 
 
-def counts_kernel(index_ref, out_ref):
+def counts_kernel(index_ref, *refs):
+    out_ref = refs[-1]
     base = pl.program_id(0) * TILE
     rows = small(lax.broadcasted_iota(jnp.int32, (TILE, 128), 0))
     lanes = lax.broadcasted_iota(jnp.int32, (FANOUT, 128), 1)
@@ -81,18 +87,18 @@
         out_ref[:, c : c + 128] = total
 
 
-def counts(index, tiles):
+def counts(index, tiles, after):
     n = index.shape[1]
     return pl.pallas_call(
         counts_kernel,
         grid=(tiles,),
-        in_specs=[pl.BlockSpec((FANOUT, n), lambda i: (0, 0))],
+        in_specs=[pl.BlockSpec((FANOUT, n), lambda i: (0, 0))] + [ANY] * len(after),
         out_specs=pl.BlockSpec((TILE, n), lambda i: (i, 0)),
-        out_shape=jax.ShapeDtypeStruct((tiles * TILE, n), BF16),
+        out_shape=pltpu.HBM((tiles * TILE, n), BF16),
         compiler_params=params(12),
         cost_estimate=cost(0, tiles * TILE * n * 16),
         name="counts",
-    )(index)
+    )(index, *after)
 
 
 def gather_kernel(c_ref, t_ref, *refs, count):
@@ -115,7 +121,7 @@
         + [resident((BOUND, h))] * len(blocks)
         + [ANY] * len(after),
         out_specs=pl.BlockSpec((TILE, h), lambda i: (i, 0)),
-        out_shape=jax.ShapeDtypeStruct((live, h), F32),
+        out_shape=pltpu.HBM((live, h), F32),
         compiler_params=params(26),
         cost_estimate=cost(2 * live * rows * h, live * h * 6),
         name="gather",
@@ -142,13 +148,10 @@
 
 def layer_kernel(at_ref, part_ref, c_ref, cl_ref, last_ref, inv_ref, ct_ref, *refs, tiles, planes):
     pieces, refs = refs[:8], refs[8:]
-    o_ref, agl_ref, gb_ref, kept_ref, sent_ref, far_ref, w, b, m_all, gl_all, gb, sem = refs
+    o_ref, agl_ref, m_all, gl_all, gb, far_ref, w, b, sem = refs
     i = pl.program_id(0)
     h = part_ref.shape[1]
-    n = h // 2
     copies = fetch(pieces, planes, w, sem, at_ref)
-    mine = pl.ds(pl.multiple_of(at_ref[1] * n, n), n)
-    other = pl.ds(pl.multiple_of((1 - at_ref[1]) * n, n), n)
 
     @pl.when(i == 0)
     def _():
@@ -191,22 +194,54 @@
         o_ref[...] = jnp.zeros_like(o_ref)
         far_ref[...] = dot(cl_ref[...], agl_ref[...], 1, 0).astype(BF16)
 
-    @pl.when((i > tiles) & (i <= tiles + h // TILE))
-    def _():
-        at = pl.ds(pl.multiple_of((i - tiles - 1) * TILE, TILE), TILE)
-        kept_ref[...] = dot(m_all[:, at], gl_all[:, mine], 0, 0).astype(BF16)
-        sent_ref[...] = dot(m_all[:, at], gl_all[:, other], 0, 0).astype(BF16)
-
-    @pl.when(i > tiles + h // TILE)
-    def _():
-        gb_ref[...] = jnp.broadcast_to(jnp.sum(gb[:, mine], axis=0, keepdims=True), gb_ref.shape)
-        sent_ref[:SPARE, :] = jnp.broadcast_to(jnp.sum(gb[:, other], axis=0, keepdims=True), (SPARE, n)).astype(BF16)
+
+def weight_kernel(at_ref, m_all, gl_all, gb, *refs, mine):
+    out_ref, gb_ref = refs[-2:]
+    i = pl.program_id(0)
+    blocks = m_all.shape[1] // TILE
+    n = out_ref.shape[1]
+    core = at_ref[1] if mine else 1 - at_ref[1]
+    columns = pl.ds(pl.multiple_of(core * n, n), n)
+
+    @pl.when(i < blocks)
+    def _():
+        at = pl.ds(pl.multiple_of(i * TILE, TILE), TILE)
+        out_ref[...] = dot(m_all[:, at], gl_all[:, columns], 0, 0).astype(BF16)
+
+    @pl.when(i == blocks)
+    def _():
+        total = jnp.sum(gb[:, columns], axis=0, keepdims=True)
+        gb_ref[...] = jnp.broadcast_to(total, gb_ref.shape)
+        if not mine:
+            out_ref[:SPARE, :] = jnp.broadcast_to(total, (SPARE, n)).astype(BF16)
+
+
+def weight_share(at, mixed, low, bias, mine, after):
+    live, h = mixed.shape
+    n, blocks = h // 2, h // TILE
+    rows = h if mine else h + SPARE
+    return pl.pallas_call(
+        functools.partial(weight_kernel, mine=mine),
+        grid_spec=pltpu.PrefetchScalarGridSpec(
+            num_scalar_prefetch=1,
+            grid=(blocks + 1,),
+            in_specs=[WHOLE, WHOLE, resident((8, h))] + [ANY] * len(after),
+            out_specs=[
+                pl.BlockSpec((TILE, n), lambda i, s: (jnp.minimum(i, -(-rows // TILE) - 1), 0)),
+                resident((8, n)),
+            ],
+        ),
+        out_shape=[(pltpu.VMEM if mine else pltpu.HBM)((rows, n), BF16), jax.ShapeDtypeStruct((8, n), F32)],
+        compiler_params=params(12),
+        cost_estimate=cost(live * h * h, live * h * 4),
+        name="weight_share",
+    )(at, held(mixed), held(low), bias, *after)
 
 
 def layer(at, part, adjacency, last, inverse, cotangent, pieces, planes):
     live, h = part.shape
-    nodes, n = cotangent.shape[0], h // 2
-    tiles, blocks = live // TILE, h // TILE
+    nodes = cotangent.shape[0]
+    tiles = live // TILE
     below = adjacency.shape[0] // BOUND - 1
 
     def row(i, s):
@@ -216,7 +251,7 @@
         functools.partial(layer_kernel, tiles=tiles, planes=planes),
         grid_spec=pltpu.PrefetchScalarGridSpec(
             num_scalar_prefetch=1,
-            grid=(tiles + 1 + blocks + 1,),
+            grid=(tiles + 1,),
             in_specs=[
                 pl.BlockSpec((TILE, h), row),
                 pl.BlockSpec((BOUND, TILE), lambda i, s: (below, jnp.minimum(i, tiles - 1))),
@@ -227,18 +262,15 @@
             ]
             + [ANY] * len(pieces),
             out_specs=[
-                pl.BlockSpec((TILE, h), lambda i, s: (jnp.minimum(i, tiles), 0)),
+                pl.BlockSpec((TILE, h), lambda i, s: (i, 0)),
                 WHOLE,
-                resident((8, n)),
-                pl.BlockSpec((TILE, n), lambda i, s: (jnp.clip(i - tiles - 1, 0, blocks - 1), 0)),
-                pl.BlockSpec((TILE, n), lambda i, s: (jnp.maximum(i - tiles - 1, 0), 0)),
+                WHOLE,
+                WHOLE,
+                resident((8, h)),
                 resident((BOUND, h)),
             ],
             scratch_shapes=[
                 pltpu.VMEM((h, pieces[0].shape[1]), BF16),
-                pltpu.VMEM((8, h), F32),
-                pltpu.VMEM((live, h), BF16),
-                pltpu.VMEM((live, h), BF16),
                 pltpu.VMEM((8, h), F32),
                 pltpu.SemaphoreType.DMA((len(pieces), planes)),
             ],
@@ -246,12 +278,12 @@
         out_shape=[
             jax.ShapeDtypeStruct((nodes, h), F32),
             pltpu.VMEM((live, h), BF16),
-            jax.ShapeDtypeStruct((8, n), F32),
-            jax.ShapeDtypeStruct((h, n), BF16),
-            pltpu.HBM((h + SPARE, n), BF16),
+            pltpu.VMEM((live, h), BF16),
+            pltpu.VMEM((live, h), BF16),
+            jax.ShapeDtypeStruct((8, h), F32),
             pltpu.HBM((BOUND, h), BF16),
         ],
-        compiler_params=params(46),
+        compiler_params=params(24),
         cost_estimate=cost(3 * live * h * h, live * h * 12),
         name="layer",
     )(at, far(part), far(adjacency), far(adjacency), last, inverse, far(cotangent), *pieces)
@@ -265,18 +297,24 @@
 
 
 def spare_rows(row, n):
-    rows = lax.broadcasted_iota(jnp.int32, (SPARE, n), 0)
-    return jnp.where(rows == 0, row[:, :n], jnp.where(rows == 1, row[:, n:], 0.0)).astype(BF16)
-
-
-def from_spare(rows):
-    return jnp.concatenate([rows[0:1, :], rows[1:2, :]], axis=1).astype(F32)
-
-
-def share_kernel(at_ref, kept_ref, came_ref, cb_ref, gb_ref, _, a_own, a_sent, b_own, b_sent, gb_out, *, rows):
+    count = -(-row.shape[1] // n)
+    row = jnp.concatenate([row, jnp.zeros((1, count * n - row.shape[1]), F32)], axis=1) if count * n > row.shape[1] else row
+    at = lax.broadcasted_iota(jnp.int32, (SPARE, n), 0)
+    rows = jnp.zeros((SPARE, n), F32)
+    for k in range(count):
+        rows = jnp.where(at == k, row[:, k * n : (k + 1) * n], rows)
+    return rows.astype(BF16)
+
+
+def from_spare(rows, total):
+    n = rows.shape[1]
+    return jnp.concatenate([rows[k : k + 1, :] for k in range(-(-total // n))], axis=1)[:, :total].astype(F32)
+
+
+def share_kernel(at_ref, kept_ref, came_ref, cb_ref, gb_ref, a_own, a_sent, b_own, b_sent, gb_out, *, rows):
     t = pl.program_id(0)
     last = pl.num_programs(0) - 1
-    n = kept_ref.shape[1] // 2
+    n = a_own.shape[1]
     groups = TILE // (4 * rows)
 
     @pl.when(t < last)
@@ -304,10 +342,13 @@
         total = gb_ref[0:1, :] + cb_ref[0:1, :].astype(F32)
         gb_out[...] = jnp.broadcast_to(total, gb_out.shape)
         a_sent[:SPARE, :] = spare_rows(total, n)
-
-
-def share_rows(at, kept, came, bias, rows, after):
+        b_sent[:SPARE, :] = jnp.zeros((SPARE, b_sent.shape[1]), BF16)
+
+
+def share_rows(at, kept, came, bias, rows):
     h, n = kept.shape
+    n_a = n * FIRST // 8
+    n_b = n - n_a
     blocks = h // TILE
     single = TILE == 4 * rows
     b_rows = TILE if single else TILE // 2
@@ -328,27 +369,26 @@
                 pl.BlockSpec((TILE, n), lambda t, s: (tile(t), 0)),
                 pl.BlockSpec((SPARE, n), lambda t, s: (h // SPARE, 0)),
                 resident((8, n)),
-                ANY,
             ],
             out_specs=[
-                pl.BlockSpec((TILE // 2, n // 2), lambda t, s: (tile(t), 0)),
-                pl.BlockSpec((TILE // 2, n // 2), lambda t, s: (t, 0)),
-                pl.BlockSpec((b_rows, n // 2), plane),
-                pl.BlockSpec((b_rows, n // 2), plane),
+                pl.BlockSpec((TILE // 2, n_a), lambda t, s: (tile(t), 0)),
+                pl.BlockSpec((TILE // 2, n_a), lambda t, s: (t, 0)),
+                pl.BlockSpec((b_rows, n_b), plane),
+                pl.BlockSpec((b_rows, n_b), lambda t, s: (t // 2 if single else t, 0)),
                 resident((8, n)),
             ],
         ),
         out_shape=[
-            pltpu.HBM((h // 2, n // 2), BF16),
-            pltpu.HBM((h // 2 + SPARE, n // 2), BF16),
-            pltpu.HBM((h // 2, n // 2), BF16),
-            pltpu.HBM((h // 2, n // 2), BF16),
+            pltpu.HBM((h // 2, n_a), BF16),
+            pltpu.HBM((h // 2 + SPARE, n_a), BF16),
+            pltpu.HBM((h // 2, n_b), BF16),
+            pltpu.HBM((h // 2 + SPARE, n_b), BF16),
             jax.ShapeDtypeStruct((8, n), F32),
         ],
         compiler_params=params(10),
         cost_estimate=cost(0, h * n * 8),
         name="share",
-    )(at, kept, came, came, bias, after)
+    )(at, kept, came, came, bias)
 
 
 def fold_kernel(at_ref, a_ref, a_came, b_ref, b_came, gb_ref, _, a_own, a_sent, b_own, b_sent, gb_out, *, rows):
@@ -365,35 +405,35 @@
         mine, other = halves(at_ref, b_ref[at, :].astype(F32) + b_came[at, :].astype(F32), rows)
         b_own[out, :] = mine
         b_sent[out, :] = other.astype(BF16)
-    total = gb_ref[0:1, :] + from_spare(a_came[a_ref.shape[0] :, :])
+    total = gb_ref[0:1, :] + from_spare(a_came[a_ref.shape[0] :, :], gb_ref.shape[1])
     gb_out[...] = jnp.broadcast_to(total, gb_out.shape)
     a_sent[planes * two :, :] = spare_rows(total, n)
 
 
 def fold(at, a_own, a_came, b_own, b_came, bias, rows, after):
-    count, n = b_own.shape[0] // 2, b_own.shape[1]
+    count, n_a, n_b = b_own.shape[0] // 2, a_own.shape[1], b_own.shape[1]
     return pl.pallas_call(
         functools.partial(fold_kernel, rows=rows),
         in_specs=[SMEM] + [WHOLE] * 5 + [ANY],
         out_specs=[WHOLE] * 5,
         out_shape=[
-            jax.ShapeDtypeStruct((count, n), F32),
-            jax.ShapeDtypeStruct((count + SPARE, n), BF16),
-            jax.ShapeDtypeStruct((count, n), F32),
-            jax.ShapeDtypeStruct((count, n), BF16),
+            jax.ShapeDtypeStruct((count, n_a), F32),
+            jax.ShapeDtypeStruct((count + SPARE, n_a), BF16),
+            jax.ShapeDtypeStruct((count, n_b), F32),
+            jax.ShapeDtypeStruct((count, n_b), BF16),
             jax.ShapeDtypeStruct(bias.shape, F32),
         ],
         compiler_params=params(22),
         cost_estimate=cost(0, b_own.size * 9),
         name="fold",
-    )(at, far(a_own), far(a_came), far(b_own), far(b_came), bias, after)
+    )(at, far(a_own), a_came, far(b_own), b_came, bias, after)
 
 
 def part_kernel(at_ref, a_ref, a_came, b_ref, b_came, gb_ref, *refs, rows, planes):
     gb_out, own, *sent = refs[-1 - planes :]
     two = 2 * rows
     n = a_ref.shape[1]
-    total = gb_ref[0:1, :] + from_spare(a_came[a_ref.shape[0] :, :])
+    total = gb_ref[0:1, :] + from_spare(a_came[a_ref.shape[0] :, :], gb_ref.shape[1])
     gb_out[...] = jnp.broadcast_to(total, gb_out.shape)
     for k in range(planes):
         at = pl.ds(pl.multiple_of(lax.rem(at_ref[3] + k, planes) * two, two), two)
@@ -401,17 +441,17 @@
         out[:two, :n] = (a_ref[at, :] + a_came[at, :].astype(F32)).astype(out.dtype)
         out[:two, n:] = (b_ref[at, :] + b_came[at, :].astype(F32)).astype(out.dtype)
         if k:
-            out[two:, :] = jnp.broadcast_to(total, (SPARE, 2 * n)).astype(BF16)
+            out[two:, :] = jnp.broadcast_to(total, (SPARE, total.shape[1])).astype(BF16)
 
 
 def part_planes(at, a_own, a_came, b_own, b_came, bias, rows, planes, after):
-    n = a_own.shape[1]
+    n = a_own.shape[1] + b_own.shape[1]
     return pl.pallas_call(
         functools.partial(part_kernel, rows=rows, planes=planes),
         in_specs=[SMEM] + [WHOLE] * 5 + [ANY] * len(after),
         out_specs=[WHOLE] * (1 + planes),
-        out_shape=[jax.ShapeDtypeStruct(bias.shape, F32), jax.ShapeDtypeStruct((2 * rows, 2 * n), F32)]
-        + [jax.ShapeDtypeStruct((2 * rows + SPARE, 2 * n), BF16)] * (planes - 1),
+        out_shape=[jax.ShapeDtypeStruct(bias.shape, F32), jax.ShapeDtypeStruct((2 * rows, n), F32)]
+        + [jax.ShapeDtypeStruct((2 * rows + SPARE, n), BF16)] * (planes - 1),
         compiler_params=params(14),
         cost_estimate=cost(0, a_own.size * 18),
         name="part_planes",
@@ -461,20 +501,20 @@
             copy.wait()
 
 
-def scatter_bound(adjacency, grads):
+def scatter_bound(adjacency, grads, after):
     live, h = grads.shape
     blocks = (adjacency.shape[0] - live) // BOUND - 1
     return pl.pallas_call(
         functools.partial(scatter_bound_kernel, count=blocks),
         grid=(blocks,),
-        in_specs=[pl.BlockSpec((BOUND, live), lambda i: (i + live // BOUND, 0)), resident((live, h))],
+        in_specs=[pl.BlockSpec((BOUND, live), lambda i: (i + live // BOUND, 0)), resident((live, h))] + [ANY] * len(after),
         out_specs=[ANY] * blocks,
         out_shape=[pltpu.HBM((BOUND, h), BF16)] * blocks,
         scratch_shapes=[pltpu.VMEM((blocks, BOUND, h), BF16), pltpu.SemaphoreType.DMA((blocks,))],
         compiler_params=params(22),
         cost_estimate=cost(2 * blocks * BOUND * live * h, live * h * 4),
         name="scatter_bound",
-    )(adjacency, grads)
+    )(far(adjacency), grads, *after)
 
 
 def grad_rows_kernel(at_ref, c_ref, g_ref, *refs, low, tiles, planes):
@@ -551,7 +591,7 @@
         compiler_params=params(30),
         cost_estimate=cost((2 * live + 2 * h) * (high - low) * TILE * h, live * h * 8),
         name="grad_rows",
-    )(at, adjacency, grads, *weight, *extra, *after)
+    )(at, far(adjacency), grads, *weight, *extra, *after)
 
 
 def back_kernel(a_ref, b_ref, c_ref, d_ref, _, o_ref, p_ref):
@@ -570,7 +610,7 @@
         compiler_params=params(10),
         cost_estimate=cost(0, a.size * 12),
         name="back",
-    )(far(a), far(b), far(c), far(d), after)
+    )(far(a), b, far(c), d, after)
 
 
 def grad_lead_kernel(lead_ref, *refs):
@@ -655,30 +695,32 @@
     inverse = (1.0 / (degrees[:live].astype(F32) + 1.0))[:, None]
     at = jnp.stack([live_count, core, lo, hi, wa]).astype(jnp.int32)
 
-    adjacency = counts(index, (live + (1 + 2 * n_wa) * BOUND) // TILE)
-    partner, *planes = tie([partner, *planes], [adjacency])
+    adjacency = counts(index, (live + (1 + 2 * n_wa) * BOUND) // TILE, [inverse, at])
+    partner, *planes = tie([partner, *planes], [far(adjacency)])
     sheet = jnp.concatenate([sheet, *planes])
     half_sheet, row_sheet = swap_wa(sheet), swap_lo(sheet)
     inner_same, inner_other = swap_core(leading), swap_core(partner)
     part = gather(adjacency, features, (partner, inner_same, inner_other, outer_same), live, [inverse, at])
-    half_sheet, row_sheet, outer_same = tie([half_sheet, row_sheet, outer_same], [part])
+    half_sheet, row_sheet, outer_same = tie([half_sheet, row_sheet, outer_same], [far(part)])
     outer_other = swap_wa(outer_same)
     both_sheet, outer_other = tie([swap_lo(half_sheet), outer_other], [])
     pieces = [sheet, half_sheet, row_sheet, both_sheet]
     pieces = pieces + [swap_core(value) for value in pieces]
-    output, grads, bias_sum, kept, sent, outer_other_g = layer(
+    output, grads, mixed, low, bias_sum, outer_other_g = layer(
         at, part, adjacency, outer_other, inverse, cotangent, pieces, n_hi
     )
+    sent, token = weight_share(at, mixed, low, bias_sum, False, [])
     came = swap_core(sent)
+    kept, bias_sum = weight_share(at, mixed, low, bias_sum, True, [token])
+
+    a, a_sent, b, b_sent, bias_sum = share_rows(at, kept, came, bias_sum, share)
+    a_came, b_came = swap_wa(a_sent), swap_lo(b_sent)
 
     outer_came = swap_wa(outer_other_g)
-    own_bound, inner_same_g, inner_other_g, outer_same_g = scatter_bound(adjacency, grads)
+    own_bound, inner_same_g, inner_other_g, outer_same_g = scatter_bound(adjacency, grads, [bias_sum])
     own_came, inner_came = swap_core(inner_other_g), swap_core(inner_same_g)
-
-    a, a_sent, b, b_sent, bias_sum = share_rows(at, kept, came, bias_sum, share, own_bound)
-    a_came, b_came = swap_wa(a_sent), swap_lo(b_sent)
     split, tiles = live // TILE // 2, -(-nodes // TILE)
-    grad_features, lead, matrix = grad_rows(at, adjacency, grads, pieces, nodes, 0, split, n_hi, None, [bias_sum, outer_came])
+    grad_features, lead, matrix = grad_rows(at, adjacency, grads, pieces, nodes, 0, split, n_hi, None, [far(own_bound), outer_came])
     outer_back, own_back = back(outer_same_g, outer_came, own_bound, own_came, lead)
     outer_back = swap_outer(outer_back)
     a, a_sent, b, b_sent, bias_sum = fold(at, a, a_came, b, b_came, bias_sum, share, own_back)

time: 271 us -> 255 us (0.941)
  local copies, waits for them, and re-layouts: 17.7 us -> 4.86 us
  waiting for transfers between devices: 72.9 us -> 64.1 us
    pallas_call x1, Pallas kernels: 52.4 us -> 32.7 us  [layer(): pl.pallas_call(functools.partial(layer_kernel, tiles=tiles, planes=planes...]
    pallas_call x0 -> x2, Pallas kernels: none -> 19 us  [weight_share(): pl.pallas_call(functools.partial(weight_kernel, mine=mine), grid_spec=plt...]
    unnamed x80 -> x12, local copies, waits for them, and re-layouts: 12.9 us -> 0.03 us
    ppermute x29, waiting for transfers between devices: 72.9 us -> 64.1 us  [permute(): return lax.ppermute(value, axes, [(s, b * n_wa + w) for s, (b, w) in pairs])]
  transfers between devices with their start and end apart: 29 -> 29, of which waited for: 14 -> 12; matrix products, arithmetic and copies ran while one was open for 1% -> 2% of each run, Pallas kernels for 34% -> 40%
where the time goes in v5:
time: 255 us; the launch traced here: 252 us
  Pallas kernels  148 us (58%)
  waiting for transfers between devices  64.1 us (25%)
  starting transfers between devices  31.2 us (12%)
  local copies, waits for them, and re-layouts  4.86 us (2%)
  other arithmetic  2.95 us (1%)
    ppermute x29, waiting for transfers between devices, permute(): return lax.ppermute(value, axes, [(s, b * n_wa + w) for s, (b, w) in pairs])  64.1 us
    pallas_call x1, Pallas kernels, layer(): pl.pallas_call(functools.partial(layer_kernel, tiles=tiles, planes=planes...  32.7 us
    ppermute x29, starting transfers between devices, permute(): return lax.ppermute(value, axes, [(s, b * n_wa + w) for s, (b, w) in pairs])  31.2 us
    pallas_call x2, Pallas kernels, grad_rows(): pl.pallas_call(functools.partial(grad_rows_kernel, low=low, tiles=tiles,...  31.2 us
    pallas_call x1, Pallas kernels, gather(): pl.pallas_call(functools.partial(gather_kernel, count=len(blocks)), grid=...  22 us
    pallas_call x2, Pallas kernels, weight_share(): pl.pallas_call(functools.partial(weight_kernel, mine=mine), grid_spec=plt...  19 us
    pallas_call x1, Pallas kernels, counts(): pl.pallas_call(counts_kernel, grid=(tiles,), in_specs=[pl.BlockSpec((FANO...  16.5 us
    pallas_call x1, Pallas kernels, scatter_bound(): pl.pallas_call(functools.partial(scatter_bound_kernel, count=blocks), gri...  9.78 us
  transfers between devices with their start and end apart: 29, of which 12 were waited for; matrix products, arithmetic and copies ran while one was open for 2% of the time, Pallas kernels for 40%

profile of v5, /device:TPU:11, one launch (start us, length us, event | category | flops | bytes accessed | tf_op | source)
XLA Modules:
  0.0 252.3 jit_solution(5480934936323100121)
XLA Ops:
  0.7 2.3 slice.18
  4.7 2.5 collective-permute-start.2
  7.2 2.2 collective-permute-start.1
  9.4 2.9 %collective-permute-start.6 = (bf16[256,2048]{1,0:T(8,128)(2,1)}, bf16[256,2048]{1,0:T(8,128)(2,1)S(1)}, u32[]{:S(2)}, u32[]{:S(2)}) collective-permute-start(bf16[256,2048]{1,0:T(8,128)(2,1)} %slice.18), channel_id=1, source_target_pairs={{0,30},{1,31},{2,4},{3,5},{4,2},{5,3},{6,8},{7,9},{8,6},{9,7},{10,... | collective-permute-start | bytes 3145736 | tf_op jit(solution)/shard_map/ppermute | solution.py:658
  14.5 16.5 %counts.1.refs_4_.c_ref.cl_ref = bf16[2816,1536]{1,0:T(8,128)(2,1)} custom-call(s32[16,1536]{1,0:T(8,128)S(1)} %fusion.2.index_ref, f32[1536,1]{1,0:T(8,128)S(1)} %broadcast_in_dim.27.refs_0_.refs_4_.inv_ref, s32[5]{0:T(128)S(1)} %stack.23.refs_1_.refs_5_.at_ref), custom_call_target="tpu_custom_call" | custom-call | bytes 4325376 | tf_op jit(solution)/shard_map/counts/pallas_call | solution.py:92
  31.0 11.3 %collective-permute-done.1.refs_1_ = bf16[64,2176]{1,0:T(8,128)(2,1)} collective-permute-done((bf16[64,2176]{1,0:T(8,128)(2,1)}, bf16[64,2176]{1,0:T(8,128)(2,1)}, u32[]{:S(2)}, u32[]{:S(2)}) %collective-permute-start.1) | collective-permute-done | bytes 278560 | tf_op jit(solution)/shard_map/ppermute | solution.py:658
  42.3 1.3 collective-permute-start.5
  46.0 22.0 %gather.1.refs_3_.part_ref = f32[1536,2048]{1,0:T(8,128)} custom-call(bf16[2816,1536]{1,0:T(8,128)(2,1)} %counts.1.refs_4_.c_ref.cl_ref, bf16[1664,2048]{1,0:T(8,128)(2,1)} %t_ref.1, bf16[256,2048]{1,0:T(8,128)(2,1)S(1)} %get-tuple-element.53.refs_0_, bf16[256,2048]{1,0:T(8,128)(2,1)S(1)} %collective-permute-done.4.refs_1_, ...), custom_call_target="tpu_custom_call" | custom-call | flops 1006632960 | bytes 1179648 | tf_op jit(solution)/shard_map/gather/pallas_call | solution.py:117
  68.0 2.9 %collective-permute-done.8.refs_1_ = bf16[256,2176]{1,0:T(8,128)(2,1)S(1)} collective-permute-done((bf16[256,2176]{1,0:T(8,128)(2,1)S(1)}, bf16[256,2176]{1,0:T(8,128)(2,1)S(1)}, u32[]{:S(2)}, u32[]{:S(2)}) %collective-permute-start.8) | collective-permute-done | bytes 1114144 | tf_op jit(solution)/shard_map/ppermute | solution.py:658
  73.2 1.7 collective-permute-start.11
  75.4 19.9 %collective-permute-done.10.refs_1_ = bf16[256,2048]{1,0:T(8,128)(2,1)S(1)} collective-permute-done((bf16[256,2048]{1,0:T(8,128)(2,1)S(1)}, bf16[256,2048]{1,0:T(8,128)(2,1)S(1)}, u32[]{:S(2)}, u32[]{:S(2)}) %collective-permute-start.10) | collective-permute-done | bytes 1048608 | tf_op jit(solution)/shard_map/ppermute | solution.py:658
  96.3 1.7 collective-permute-start.14
  98.0 2.4 collective-permute-done.14.refs_7_
  100.3 32.7 %layer.1 = (f32[1664,2048]{1,0:T(8,128)}, bf16[1536,2048]{1,0:T(8,128)(2,1)S(1)}, bf16[1536,2048]{1,0:T(8,128)(2,1)S(1)}, bf16[1536,2048]{1,0:T(8,128)(2,1)S(1)}...) custom-call(s32[5]{0:T(128)S(1)} %stack.23.refs_1_.refs_5_.at_ref, f32[1536,2048]{1,0:T(8,128)} %gather.1.refs_3_.part_ref, ...), custom_call_target="tpu_custom_call" | custom-call | flops 1207959552 | bytes 2359296 | tf_op jit(solution)/shard_map/layer/pallas_call | solution.py:250
  133.0 9.8 %weight_share.2 = (bf16[2064,1024]{1,0:T(8,128)(2,1)}, f32[8,1024]{1,0:T(8,128)S(1)}) custom-call(s32[5]{0:T(128)S(1)} %stack.23.refs_1_.refs_5_.at_ref, bf16[1536,2048]{1,0:T(8,128)(2,1)S(1)} %get-tuple-element.64.m_all, bf16[1536,2048]{1,0:T(8,128)(2,1)S(1)} %get-tuple-element.65.gl_all, f32[8,2048]{1,0:T(8,128)S(1)} %get-tuple-element.66.gb), custom_call_target="tpu_custom_call" | custom-call | flops 402653184 | bytes 786432 | tf_op jit(solution)/shard_map/weight_share/pallas_call | solution.py:223
  144.5 9.2 %weight_share.3 = (bf16[2048,1024]{1,0:T(8,128)(2,1)S(1)}, f32[8,1024]{1,0:T(8,128)S(1)}) custom-call(s32[5]{0:T(128)S(1)} %stack.23.refs_1_.refs_5_.at_ref, bf16[1536,2048]{1,0:T(8,128)(2,1)S(1)} %get-tuple-element.64.m_all, bf16[1536,2048]{1,0:T(8,128)(2,1)S(1)} %get-tuple-element.65.gl_all, f32[8,2048]{1,0:T(8,128)S(1)} %get-tuple-element.66.gb, ...), custom_call_target="tpu_custom_call" | custom-call | flops 402653184 | bytes 786432 | tf_op jit(solution)/shard_map/weight_share/pallas_call | solution.py:223
  153.7 5.5 %share.1 = (bf16[1024,512]{1,0:T(8,128)(2,1)}, bf16[1040,512]{1,0:T(8,128)(2,1)}, bf16[1024,512]{1,0:T(8,128)(2,1)}, bf16[1040,512]{1,0:T(8,128)(2,1)}, f32[8,1024]{1,0:T(8,128)S(1)}) custom-call(s32[5]{0:T(128)S(1)} %stack.23.refs_1_.refs_5_.at_ref, bf16[2048,1024]{1,0:T(8,128)(2,1)S(1)} %get-tuple-element.68.kept_ref, ...), custom_call_target="tpu_custom_call" | custom-call | bytes 1048576 | tf_op jit(solution)/shard_map/share/pallas_call | solution.py:362
  160.5 9.8 %scatter_bound.1 = (bf16[256,2048]{1,0:T(8,128)(2,1)}, bf16[256,2048]{1,0:T(8,128)(2,1)}, bf16[256,2048]{1,0:T(8,128)(2,1)}, bf16[256,2048]{1,0:T(8,128)(2,1)}) custom-call(bf16[2816,1536]{1,0:T(8,128)(2,1)} %counts.1.refs_4_.c_ref.cl_ref, bf16[1536,2048]{1,0:T(8,128)(2,1)S(1)} %get-tuple-element.63.g_ref, f32[8,1024]{1,0:T(8,128)S(1)} %get-tuple-element.71.refs_0_.gb_ref), custom_call_target="tpu_custom_call" | custom-call | flops 402653184 | bytes 786432 | tf_op jit(solution)/shard_map/scatter_bound/pallas_call | solution.py:507
  171.3 14.5 %grad_rows.2 = (f32[1664,2048]{1,0:T(8,128)}, f32[256,2048]{1,0:T(8,128)S(1)}, bf16[2048,2048]{1,0:T(8,128)(2,1)}) custom-call(s32[5]{0:T(128)S(1)} %stack.23.refs_1_.refs_5_.at_ref, bf16[2816,1536]{1,0:T(8,128)(2,1)} %counts.1.refs_4_.c_ref.cl_ref, bf16[1536,2048]{1,0:T(8,128)(2,1)S(1)} %get-tuple-element.63.g_ref, ...), custom_call_target="tpu_custom_call" | custom-call | flops 704643072 | bytes 1572864 | tf_op jit(solution)/shard_map/grad_rows/pallas_call | solution.py:572
  185.9 3.0 %back.1 = (bf16[256,2048]{1,0:T(8,128)(2,1)S(1)}, bf16[256,2048]{1,0:T(8,128)(2,1)S(1)}) custom-call(bf16[256,2048]{1,0:T(8,128)(2,1)} %get-tuple-element.76.a_ref, bf16[256,2048]{1,0:T(8,128)(2,1)S(1)} %collective-permute-done.16.refs_9_.b_ref, bf16[256,2048]{1,0:T(8,128)(2,1)} %get-tuple-element.72.refs_8_.c_ref, ...), custom_call_target="tpu_custom_call" | custom-call | bytes 393216 | tf_op jit(solution)/shard_map/back/pallas_call | solution.py:604
  188.9 1.9 collective-permute-done.20.a_came
  190.7 2.2 fold.1
  195.3 1.5 collective-permute-start.17
  197.1 16.7 %grad_rows.3 = (f32[1664,2048]{1,0:T(8,128)}, f32[8,128]{1,0:T(8,128)S(1)}) custom-call(s32[5]{0:T(128)S(1)} %stack.23.refs_1_.refs_5_.at_ref, bf16[2816,1536]{1,0:T(8,128)(2,1)} %counts.1.refs_4_.c_ref.cl_ref, bf16[1536,2048]{1,0:T(8,128)(2,1)S(1)} %get-tuple-element.63.g_ref, bf16[2048,2048]{1,0:T(8,128)(2,1)S(1)} %copy-done, ...), custom_call_target="tpu_custom_call", output_to_operand_aliasing={{0}: (4, {})} | custom-call | flops 939524096 | bytes 1572864 | tf_op jit(solution)/shard_map/grad_rows/pallas_call | solution.py:572
  213.8 3.3 %collective-permute-done.22.a_came = bf16[528,512]{1,0:T(8,128)(2,1)S(1)} collective-permute-done((bf16[528,512]{1,0:T(8,128)(2,1)S(1)}, bf16[528,512]{1,0:T(8,128)(2,1)S(1)}, u32[]{:S(2)}, u32[]{:S(2)}) %collective-permute-start.22) | collective-permute-done | bytes 540704 | tf_op jit(solution)/shard_map/ppermute | solution.py:658
  219.1 2.2 collective-permute-start.25
  221.3 1.5 collective-permute-start.26
  222.8 7.0 %collective-permute-done.19.refs_1_ = bf16[256,2048]{1,0:T(8,128)(2,1)S(1)} collective-permute-done((bf16[256,2048]{1,0:T(8,128)(2,1)S(1)}, bf16[256,2048]{1,0:T(8,128)(2,1)S(1)}, u32[]{:S(2)}, u32[]{:S(2)}) %collective-permute-start.19) | collective-permute-done | bytes 1048608 | tf_op jit(solution)/shard_map/ppermute | solution.py:658
  229.8 10.6 %collective-permute-done.24.refs_2_ = bf16[256,2048]{1,0:T(8,128)(2,1)S(1)} collective-permute-done((bf16[256,2048]{1,0:T(8,128)(2,1)S(1)}, bf16[256,2048]{1,0:T(8,128)(2,1)S(1)}, u32[]{:S(2)}, u32[]{:S(2)}) %collective-permute-start.24) | collective-permute-done | bytes 1048608 | tf_op jit(solution)/shard_map/ppermute | solution.py:658
  240.4 4.3 %grad_lead.1 = (f32[1664,2048]{1,0:T(8,128)}, f32[8,128]{1,0:T(8,128)S(1)}) custom-call(f32[256,2048]{1,0:T(8,128)S(1)} %get-tuple-element.74._.lead_ref, bf16[256,2048]{1,0:T(8,128)(2,1)S(1)} %collective-permute-done.17.refs_0_, bf16[256,2048]{1,0:T(8,128)(2,1)S(1)} %collective-permute-done.19.refs_1_, ...), custom_call_target="tpu_custom_call", output_to_operand_aliasing={{0}: (5, {})} | custom-call | flops 134217728 | bytes 524288 | tf_op jit(solution)/shard_map/grad_lead/pallas_call | solution.py:632
  244.7 2.7 %collective-permute-done.27.refs_2_ = bf16[144,1024]{1,0:T(8,128)(2,1)S(1)} collective-permute-done((bf16[144,1024]{1,0:T(8,128)(2,1)S(1)}, bf16[144,1024]{1,0:T(8,128)(2,1)S(1)}, u32[]{:S(2)}, u32[]{:S(2)}) %collective-permute-start.27) | collective-permute-done | bytes 294944 | tf_op jit(solution)/shard_map/ppermute | solution.py:658
  248.1 1.5 collective-permute-start.28
  (68 shorter events, 21.4 us)
Async XLA Ops:
  0.6 12.4 %copy-start.3 = (s32[1664]{0:T(1024)S(1)}, s32[1664]{0:T(1024)}, u32[]{:S(2)}) copy-start(s32[1664]{0:T(1024)} %param.11) | copy-start | bytes 19972
  3.0 39.3 %collective-permute-start = (bf16[256,2048]{1,0:T(8,128)(2,1)}, bf16[256,2048]{1,0:T(8,128)(2,1)S(1)}, u32[]{:S(2)}, u32[]{:S(2)}) collective-permute-start(bf16[256,2048]{1,0:T(8,128)(2,1)} %slice.18), channel_id=1, source_target_pairs={{0,1},{1,0},{2,3},{3,2},{4,5},{5,4},{6,7},{7,6},{8,9},{9,8},{10,11... | collective-permute-start | bytes 3145736 | tf_op jit(solution)/shard_map/ppermute | solution.py:658
  4.7 26.3 %collective-permute-start.3 = (bf16[64,2176]{1,0:T(8,128)(2,1)}, bf16[64,2176]{1,0:T(8,128)(2,1)S(1)}, u32[]{:S(2)}, u32[]{:S(2)}) collective-permute-start(bf16[64,2176]{1,0:T(8,128)(2,1)} %pad_maximum_fusion.1), channel_id=1, source_target_pairs={{0,24},{1,25},{2,26},{3,27},{4,28},{5,29},{6,30},{7,31},{8,0},{9,1... | collective-permute-start | bytes 835592 | tf_op jit(solution)/shard_map/ppermute | solution.py:658
  4.7 26.3 %collective-permute-start.2 = (bf16[64,2176]{1,0:T(8,128)(2,1)}, bf16[64,2176]{1,0:T(8,128)(2,1)S(1)}, u32[]{:S(2)}, u32[]{:S(2)}) collective-permute-start(bf16[64,2176]{1,0:T(8,128)(2,1)} %pad_maximum_fusion.1), channel_id=1, source_target_pairs={{0,16},{1,17},{2,18},{3,19},{4,20},{5,21},{6,22},{7,23},{8,24},{9,... | collective-permute-start | bytes 835592 | tf_op jit(solution)/shard_map/ppermute | solution.py:658
  7.2 35.1 %collective-permute-start.1 = (bf16[64,2176]{1,0:T(8,128)(2,1)}, bf16[64,2176]{1,0:T(8,128)(2,1)}, u32[]{:S(2)}, u32[]{:S(2)}) collective-permute-start(bf16[64,2176]{1,0:T(8,128)(2,1)} %pad_maximum_fusion.1), channel_id=1, source_target_pairs={{0,8},{1,9},{2,10},{3,11},{4,12},{5,13},{6,14},{7,15},{8,16},{9,17... | collective-permute-start | bytes 835592 | tf_op jit(solution)/shard_map/ppermute | solution.py:658
  9.4 36.6 %collective-permute-start.6 = (bf16[256,2048]{1,0:T(8,128)(2,1)}, bf16[256,2048]{1,0:T(8,128)(2,1)S(1)}, u32[]{:S(2)}, u32[]{:S(2)}) collective-permute-start(bf16[256,2048]{1,0:T(8,128)(2,1)} %slice.18), channel_id=1, source_target_pairs={{0,30},{1,31},{2,4},{3,5},{4,2},{5,3},{6,8},{7,9},{8,6},{9,7},{10,... | collective-permute-start | bytes 3145736 | tf_op jit(solution)/shard_map/ppermute | solution.py:658
  31.0 12.6 %copy-start.2 = (bf16[64,2048]{1,0:T(8,128)(2,1)S(1)}, bf16[64,2048]{1,0:T(8,128)(2,1)}, u32[]{:S(2)}) copy-start(bf16[64,2048]{1,0:T(8,128)(2,1)} %param.8) | copy-start | bytes 786436
  31.0 15.0 %collective-permute-start.4 = (bf16[256,2048]{1,0:T(8,128)(2,1)}, bf16[256,2048]{1,0:T(8,128)(2,1)S(1)}, u32[]{:S(2)}, u32[]{:S(2)}) collective-permute-start(bf16[256,2048]{1,0:T(8,128)(2,1)} %slice.18), channel_id=1, source_target_pairs={{0,2},{1,3},{2,0},{3,1},{4,6},{5,7},{6,4},{7,5},{8,10},{9,11},{10,... | collective-permute-start | bytes 3145736 | tf_op jit(solution)/shard_map/ppermute | solution.py:658
  42.3 3.7 %collective-permute-start.5 = (bf16[256,2048]{1,0:T(8,128)(2,1)S(1)}, bf16[256,2048]{1,0:T(8,128)(2,1)S(1)}, u32[]{:S(2)}, u32[]{:S(2)}) collective-permute-start(bf16[256,2048]{1,0:T(8,128)(2,1)S(1)} %get-tuple-element.53.refs_0_), channel_id=1, source_target_pairs={{0,2},{1,3},{2,0},{3,1},{4,6},{5,7},{6,4},{7,5},{8,10},{9,11},{10,... | collective-permute-start | bytes 3145736 | tf_op jit(solution)/shard_map/ppermute | solution.py:658
  44.6 26.3 %collective-permute-start.8 = (bf16[256,2176]{1,0:T(8,128)(2,1)S(1)}, bf16[256,2176]{1,0:T(8,128)(2,1)S(1)}, u32[]{:S(2)}, u32[]{:S(2)}) collective-permute-start(bf16[256,2176]{1,0:T(8,128)(2,1)S(1)} %pad_maximum_fusion.refs_0_), channel_id=1, source_target_pairs={{0,4},{1,5},{2,6},{3,7},{4,0},{5,1},{6,2},{7,3},{8,12},{9,13},{10,... | collective-permute-start | bytes 3342344 | tf_op jit(solution)/shard_map/ppermute | solution.py:658
  44.7 26.3 %collective-permute-start.7 = (bf16[256,2176]{1,0:T(8,128)(2,1)S(1)}, bf16[256,2176]{1,0:T(8,128)(2,1)S(1)}, u32[]{:S(2)}, u32[]{:S(2)}) collective-permute-start(bf16[256,2176]{1,0:T(8,128)(2,1)S(1)} %pad_maximum_fusion.refs_0_), channel_id=1, source_target_pairs={{0,1},{1,0},{2,3},{3,2},{4,5},{5,4},{6,7},{7,6},{8,9},{9,8},{10,11... | collective-permute-start | bytes 3342344 | tf_op jit(solution)/shard_map/ppermute | solution.py:658
  71.0 25.3 %collective-permute-start.9 = (bf16[256,2176]{1,0:T(8,128)(2,1)S(1)}, bf16[256,2176]{1,0:T(8,128)(2,1)S(1)}, u32[]{:S(2)}, u32[]{:S(2)}) collective-permute-start(bf16[256,2176]{1,0:T(8,128)(2,1)S(1)} %get-tuple-element.57.refs_1_), channel_id=1, source_target_pairs={{0,4},{1,5},{2,6},{3,7},{4,0},{5,1},{6,2},{7,3},{8,12},{9,13},{10,... | collective-permute-start | bytes 3342344 | tf_op jit(solution)/shard_map/ppermute | solution.py:658
  72.0 23.3 %collective-permute-start.10 = (bf16[256,2048]{1,0:T(8,128)(2,1)S(1)}, bf16[256,2048]{1,0:T(8,128)(2,1)S(1)}, u32[]{:S(2)}, u32[]{:S(2)}) collective-permute-start(bf16[256,2048]{1,0:T(8,128)(2,1)S(1)} %get-tuple-element.58), channel_id=1, source_target_pairs={{0,1},{1,0},{2,3},{3,2},{4,5},{5,4},{6,7},{7,6},{8,9},{9,8},{10,11... | collective-permute-start | bytes 3145736 | tf_op jit(solution)/shard_map/ppermute | solution.py:658
  73.2 24.7 %collective-permute-start.11 = (bf16[256,2176]{1,0:T(8,128)(2,1)S(1)}, bf16[256,2176]{1,0:T(8,128)(2,1)S(1)}, u32[]{:S(2)}, u32[]{:S(2)}) collective-permute-start(bf16[256,2176]{1,0:T(8,128)(2,1)S(1)} %pad_maximum_fusion.refs_0_), channel_id=1, source_target_pairs={{0,2},{1,3},{2,0},{3,1},{4,6},{5,7},{6,4},{7,5},{8,10},{9,11},{10,... | collective-permute-start | bytes 3342344 | tf_op jit(solution)/shard_map/ppermute | solution.py:658
  74.9 23.0 %collective-permute-start.12 = (bf16[256,2176]{1,0:T(8,128)(2,1)S(1)}, bf16[256,2176]{1,0:T(8,128)(2,1)S(1)}, u32[]{:S(2)}, u32[]{:S(2)}) collective-permute-start(bf16[256,2176]{1,0:T(8,128)(2,1)S(1)} %get-tuple-element.57.refs_1_), channel_id=1, source_target_pairs={{0,2},{1,3},{2,0},{3,1},{4,6},{5,7},{6,4},{7,5},{8,10},{9,11},{10,... | collective-permute-start | bytes 3342344 | tf_op jit(solution)/shard_map/ppermute | solution.py:658
  74.9 23.0 %collective-permute-start.13 = (bf16[256,2176]{1,0:T(8,128)(2,1)S(1)}, bf16[256,2176]{1,0:T(8,128)(2,1)S(1)}, u32[]{:S(2)}, u32[]{:S(2)}) collective-permute-start(bf16[256,2176]{1,0:T(8,128)(2,1)S(1)} %get-tuple-element.60.refs_2_), channel_id=1, source_target_pairs={{0,2},{1,3},{2,0},{3,1},{4,6},{5,7},{6,4},{7,5},{8,10},{9,11},{10,... | collective-permute-start | bytes 3342344 | tf_op jit(solution)/shard_map/ppermute | solution.py:658
  96.3 4.1 %collective-permute-start.14 = (bf16[256,2176]{1,0:T(8,128)(2,1)S(1)}, bf16[256,2176]{1,0:T(8,128)(2,1)S(1)}, u32[]{:S(2)}, u32[]{:S(2)}) collective-permute-start(bf16[256,2176]{1,0:T(8,128)(2,1)S(1)} %get-tuple-element.61.refs_3_), channel_id=1, source_target_pairs={{0,2},{1,3},{2,0},{3,1},{4,6},{5,7},{6,4},{7,5},{8,10},{9,11},{10,... | collective-permute-start | bytes 3342344 | tf_op jit(solution)/shard_map/ppermute | solution.py:658
  142.9 10.8 %collective-permute-start.15 = (bf16[2064,1024]{1,0:T(8,128)(2,1)}, bf16[2064,1024]{1,0:T(8,128)(2,1)S(1)}, u32[]{:S(2)}, u32[]{:S(2)}) collective-permute-start(bf16[2064,1024]{1,0:T(8,128)(2,1)} %get-tuple-element.69), channel_id=1, source_target_pairs={{0,2},{1,3},{2,0},{3,1},{4,6},{5,7},{6,4},{7,5},{8,10},{9,11},{10,... | collective-permute-start | bytes 12681224 | tf_op jit(solution)/shard_map/ppermute | solution.py:658
  143.3 28.1 %collective-permute-start.16 = (bf16[256,2048]{1,0:T(8,128)(2,1)S(1)}, bf16[256,2048]{1,0:T(8,128)(2,1)S(1)}, u32[]{:S(2)}, u32[]{:S(2)}) collective-permute-start(bf16[256,2048]{1,0:T(8,128)(2,1)S(1)} %copy-done.5), channel_id=1, source_target_pairs={{0,1},{1,0},{2,3},{3,2},{4,5},{5,4},{6,7},{7,6},{8,9},{9,8},{10,11... | collective-permute-start | bytes 3145736 | tf_op jit(solution)/shard_map/ppermute | solution.py:658
  159.1 31.6 %collective-permute-start.20 = (bf16[1040,512]{1,0:T(8,128)(2,1)}, bf16[1040,512]{1,0:T(8,128)(2,1)S(1)}, u32[]{:S(2)}, u32[]{:S(2)}) collective-permute-start(bf16[1040,512]{1,0:T(8,128)(2,1)} %get-tuple-element.81), channel_id=1, source_target_pairs={{0,1},{1,0},{2,3},{3,2},{4,5},{5,4},{6,7},{7,6},{8,9},{9,8},{10,11... | collective-permute-start | bytes 3194888 | tf_op jit(solution)/shard_map/ppermute | solution.py:658
  159.4 31.3 %collective-permute-start.21 = (bf16[1040,512]{1,0:T(8,128)(2,1)}, bf16[1040,512]{1,0:T(8,128)(2,1)S(1)}, u32[]{:S(2)}, u32[]{:S(2)}) collective-permute-start(bf16[1040,512]{1,0:T(8,128)(2,1)} %get-tuple-element.83), channel_id=1, source_target_pairs={{0,4},{1,5},{2,6},{3,7},{4,0},{5,1},{6,2},{7,3},{8,12},{9,13},{10,... | collective-permute-start | bytes 3194888 | tf_op jit(solution)/shard_map/ppermute | solution.py:658
  170.3 15.6 %collective-permute-start.18 = (bf16[256,2048]{1,0:T(8,128)(2,1)}, bf16[256,2048]{1,0:T(8,128)(2,1)S(1)}, u32[]{:S(2)}, u32[]{:S(2)}) collective-permute-start(bf16[256,2048]{1,0:T(8,128)(2,1)} %get-tuple-element.77), channel_id=1, source_target_pairs={{0,2},{1,3},{2,0},{3,1},{4,6},{5,7},{6,4},{7,5},{8,10},{9,11},{10,... | collective-permute-start | bytes 3145736 | tf_op jit(solution)/shard_map/ppermute | solution.py:658
  185.9 11.2 %copy-start = (bf16[2048,2048]{1,0:T(8,128)(2,1)S(1)}, bf16[2048,2048]{1,0:T(8,128)(2,1)}, u32[]{:S(2)}) copy-start(bf16[2048,2048]{1,0:T(8,128)(2,1)} %get-tuple-element.89.refs_0_.refs_3_) | copy-start | bytes 25165828
  193.0 24.1 %collective-permute-start.22 = (bf16[528,512]{1,0:T(8,128)(2,1)S(1)}, bf16[528,512]{1,0:T(8,128)(2,1)S(1)}, u32[]{:S(2)}, u32[]{:S(2)}) collective-permute-start(bf16[528,512]{1,0:T(8,128)(2,1)S(1)} %get-tuple-element.85), channel_id=1, source_target_pairs={{0,4},{1,5},{2,6},{3,7},{4,0},{5,1},{6,2},{7,3},{8,12},{9,13},{10,... | collective-permute-start | bytes 1622024 | tf_op jit(solution)/shard_map/ppermute | solution.py:658
  194.1 19.7 %collective-permute-start.23 = (bf16[512,512]{1,0:T(8,128)(2,1)S(1)}, bf16[512,512]{1,0:T(8,128)(2,1)S(1)}, u32[]{:S(2)}, u32[]{:S(2)}) collective-permute-start(bf16[512,512]{1,0:T(8,128)(2,1)S(1)} %get-tuple-element.87), channel_id=1, source_target_pairs={{0,1},{1,0},{2,3},{3,2},{4,5},{5,4},{6,7},{7,6},{8,9},{9,8},{10,11... | collective-permute-start | bytes 1572872 | tf_op jit(solution)/shard_map/ppermute | solution.py:658
  195.3 27.5 %collective-permute-start.17 = (bf16[256,2048]{1,0:T(8,128)(2,1)S(1)}, bf16[256,2048]{1,0:T(8,128)(2,1)S(1)}, u32[]{:S(2)}, u32[]{:S(2)}) collective-permute-start(bf16[256,2048]{1,0:T(8,128)(2,1)S(1)} %copy-done.4), channel_id=1, source_target_pairs={{0,2},{1,3},{2,0},{3,1},{4,6},{5,7},{6,4},{7,5},{8,10},{9,11},{10,... | collective-permute-start | bytes 3145736 | tf_op jit(solution)/shard_map/ppermute | solution.py:658
  196.8 33.0 %collective-permute-start.19 = (bf16[256,2048]{1,0:T(8,128)(2,1)S(1)}, bf16[256,2048]{1,0:T(8,128)(2,1)S(1)}, u32[]{:S(2)}, u32[]{:S(2)}) collective-permute-start(bf16[256,2048]{1,0:T(8,128)(2,1)S(1)} %get-tuple-element.78), channel_id=1, source_target_pairs={{0,30},{1,31},{2,4},{3,5},{4,2},{5,3},{6,8},{7,9},{8,6},{9,7},{10,... | collective-permute-start | bytes 3145736 | tf_op jit(solution)/shard_map/ppermute | solution.py:658
  217.8 22.5 %collective-permute-start.24 = (bf16[256,2048]{1,0:T(8,128)(2,1)S(1)}, bf16[256,2048]{1,0:T(8,128)(2,1)S(1)}, u32[]{:S(2)}, u32[]{:S(2)}) collective-permute-start(bf16[256,2048]{1,0:T(8,128)(2,1)S(1)} %tie.7), channel_id=1, source_target_pairs={{0,1},{1,0},{2,3},{3,2},{4,5},{5,4},{6,7},{7,6},{8,9},{9,8},{10,11... | collective-permute-start | bytes 3145736 | tf_op jit(solution)/shard_map/ppermute | solution.py:658
  219.1 25.6 %collective-permute-start.25 = (bf16[144,1024]{1,0:T(8,128)(2,1)S(1)}, bf16[144,1024]{1,0:T(8,128)(2,1)S(1)}, u32[]{:S(2)}, u32[]{:S(2)}) collective-permute-start(bf16[144,1024]{1,0:T(8,128)(2,1)S(1)} %get-tuple-element.96), channel_id=1, source_target_pairs={{0,8},{1,9},{2,10},{3,11},{4,12},{5,13},{6,14},{7,15},{8,16},{9,17... | collective-permute-start | bytes 884744 | tf_op jit(solution)/shard_map/ppermute | solution.py:658
  221.3 23.4 %collective-permute-start.26 = (bf16[144,1024]{1,0:T(8,128)(2,1)S(1)}, bf16[144,1024]{1,0:T(8,128)(2,1)S(1)}, u32[]{:S(2)}, u32[]{:S(2)}) collective-permute-start(bf16[144,1024]{1,0:T(8,128)(2,1)S(1)} %get-tuple-element.97), channel_id=1, source_target_pairs={{0,16},{1,17},{2,18},{3,19},{4,20},{5,21},{6,22},{7,23},{8,24},{9,... | collective-permute-start | bytes 884744 | tf_op jit(solution)/shard_map/ppermute | solution.py:658
  222.8 24.6 %collective-permute-start.27 = (bf16[144,1024]{1,0:T(8,128)(2,1)S(1)}, bf16[144,1024]{1,0:T(8,128)(2,1)S(1)}, u32[]{:S(2)}, u32[]{:S(2)}) collective-permute-start(bf16[144,1024]{1,0:T(8,128)(2,1)S(1)} %get-tuple-element.98), channel_id=1, source_target_pairs={{0,24},{1,25},{2,26},{3,27},{4,28},{5,29},{6,30},{7,31},{8,0},{9,1... | collective-permute-start | bytes 884744 | tf_op jit(solution)/shard_map/ppermute | solution.py:658
  248.1 2.7 %collective-permute-start.28 = (f32[72,1024]{1,0:T(8,128)S(1)}, f32[72,1024]{1,0:T(8,128)S(1)}, u32[]{:S(2)}, u32[]{:S(2)}) collective-permute-start(f32[72,1024]{1,0:T(8,128)S(1)} %get-tuple-element.101), channel_id=1, source_target_pairs={{0,2},{1,3},{2,0},{3,1},{4,6},{5,7},{6,4},{7,5},{8,10},{9,11},{10,... | collective-permute-start | bytes 884744 | tf_op jit(solution)/shard_map/ppermute | solution.py:658
  (3 other events, 18.1 us)

commit v6 on v5

--- a/solution.py
+++ b/solution.py
@@ -12,6 +12,7 @@
 BOUND = 256
 CMAX = 3016
 TILE = 256
+WIDE = 512
 F32 = jnp.float32
 BF16 = jnp.bfloat16
 MIB = 1024 * 1024
@@ -128,30 +129,54 @@
     )(far(adjacency), far(features), *blocks, *after)
 
 
-def fetch(pieces, planes, target, sem, at_ref):
+def fetch(pieces, numbers, planes, target, sem, at_ref):
     core, lo, hi, wa = (at_ref[j] for j in range(1, 5))
-    rows = pieces[0].shape[0] // planes
+    rows = target.shape[0] // (8 * planes)
     copies = []
-    for n, piece in enumerate(pieces):
-        for k in range(planes):
-            chip = lax.rem(hi - k + planes, planes) * 2 + (1 - lo if n // 2 % 2 else lo)
+    for m, ((n, first), piece) in enumerate(zip(numbers, pieces)):
+        for k in range(piece.shape[0] // rows):
+            chip = lax.rem(hi - first - k + planes, planes) * 2 + (1 - lo if n // 2 % 2 else lo)
             owner = (chip * 2 + (1 - core if n // 4 else core)) * 2 + (1 - wa if n % 2 else wa)
             copies.append(
                 pltpu.make_async_copy(
-                    piece.at[pl.ds(k * rows, rows), pl.ds(0, target.shape[1])],
+                    piece.at[pl.ds(k * rows, rows), :],
                     target.at[pl.ds(pl.multiple_of(owner * rows, rows), rows), :],
-                    sem.at[n, k],
+                    sem.at[m, k],
                 )
             )
     return copies
 
 
-def layer_kernel(at_ref, part_ref, c_ref, cl_ref, last_ref, inv_ref, ct_ref, *refs, tiles, planes):
-    pieces, refs = refs[:8], refs[8:]
+def place_kernel(at_ref, *refs, numbers, planes):
+    target, sem = refs[-2:]
+    copies = fetch(refs[: len(numbers)], numbers, planes, target, sem, at_ref)
+    for copy in copies:
+        copy.start()
+    for copy in copies:
+        copy.wait()
+
+
+def place(at, pieces, numbers, planes):
+    h, n = 8 * pieces[0].shape[0], pieces[0].shape[1]
+    return pl.pallas_call(
+        functools.partial(place_kernel, numbers=numbers, planes=planes),
+        in_specs=[SMEM] + [ANY] * len(pieces),
+        out_specs=WHOLE,
+        out_shape=pltpu.VMEM((h, n), BF16),
+        scratch_shapes=[pltpu.SemaphoreType.DMA((len(pieces), planes))],
+        compiler_params=params(4),
+        cost_estimate=cost(0, h * n),
+        name="place",
+    )(at, *pieces)
+
+
+def layer_kernel(at_ref, part_ref, c_ref, d_ref, cl_ref, same_ref, last_ref, inv_ref, ct_ref, *refs, tiles, numbers, planes):
+    count = len(numbers)
+    pieces, refs = refs[:count], refs[count + 1 :]
     o_ref, agl_ref, m_all, gl_all, gb, far_ref, w, b, sem = refs
     i = pl.program_id(0)
     h = part_ref.shape[1]
-    copies = fetch(pieces, planes, w, sem, at_ref)
+    copies = fetch(pieces, numbers, planes, w, sem, at_ref)
 
     @pl.when(i == 0)
     def _():
@@ -161,7 +186,7 @@
 
     @pl.when(i < tiles)
     def _():
-        total = part_ref[...] + dot(c_ref[...], last_ref[...], 0, 0)
+        total = part_ref[...] + dot(c_ref[...], same_ref[...], 0, 0) + dot(d_ref[...], last_ref[...], 0, 0)
         m_all[pl.ds(pl.multiple_of(i * TILE, TILE), TILE), :] = (total * inv_ref[...]).astype(BF16)
 
     @pl.when(i == 0)
@@ -198,14 +223,14 @@
 def weight_kernel(at_ref, m_all, gl_all, gb, *refs, mine):
     out_ref, gb_ref = refs[-2:]
     i = pl.program_id(0)
-    blocks = m_all.shape[1] // TILE
+    blocks = m_all.shape[1] // WIDE
     n = out_ref.shape[1]
     core = at_ref[1] if mine else 1 - at_ref[1]
     columns = pl.ds(pl.multiple_of(core * n, n), n)
 
     @pl.when(i < blocks)
     def _():
-        at = pl.ds(pl.multiple_of(i * TILE, TILE), TILE)
+        at = pl.ds(pl.multiple_of(i * WIDE, WIDE), WIDE)
         out_ref[...] = dot(m_all[:, at], gl_all[:, columns], 0, 0).astype(BF16)
 
     @pl.when(i == blocks)
@@ -218,7 +243,7 @@
 
 def weight_share(at, mixed, low, bias, mine, after):
     live, h = mixed.shape
-    n, blocks = h // 2, h // TILE
+    n, blocks = h // 2, h // WIDE
     rows = h if mine else h + SPARE
     return pl.pallas_call(
         functools.partial(weight_kernel, mine=mine),
@@ -227,7 +252,7 @@
             grid=(blocks + 1,),
             in_specs=[WHOLE, WHOLE, resident((8, h))] + [ANY] * len(after),
             out_specs=[
-                pl.BlockSpec((TILE, n), lambda i, s: (jnp.minimum(i, -(-rows // TILE) - 1), 0)),
+                pl.BlockSpec((WIDE, n), lambda i, s: (jnp.minimum(i, -(-rows // WIDE) - 1), 0)),
                 resident((8, n)),
             ],
         ),
@@ -238,7 +263,7 @@
     )(at, held(mixed), held(low), bias, *after)
 
 
-def layer(at, part, adjacency, last, inverse, cotangent, pieces, planes):
+def layer(at, part, adjacency, same, last, inverse, cotangent, pieces, numbers, weight, planes):
     live, h = part.shape
     nodes = cotangent.shape[0]
     tiles = live // TILE
@@ -248,19 +273,22 @@
         return (jnp.minimum(i, tiles - 1), 0)
 
     return pl.pallas_call(
-        functools.partial(layer_kernel, tiles=tiles, planes=planes),
+        functools.partial(layer_kernel, tiles=tiles, numbers=numbers, planes=planes),
         grid_spec=pltpu.PrefetchScalarGridSpec(
             num_scalar_prefetch=1,
             grid=(tiles + 1,),
             in_specs=[
                 pl.BlockSpec((TILE, h), row),
+                pl.BlockSpec((BOUND, TILE), lambda i, s: (below - 1, jnp.minimum(i, tiles - 1))),
                 pl.BlockSpec((BOUND, TILE), lambda i, s: (below, jnp.minimum(i, tiles - 1))),
                 pl.BlockSpec((BOUND, live), lambda i, s: (below, 0), pipeline_mode=pl.Buffered(1)),
+                resident(same.shape),
                 resident(last.shape),
                 pl.BlockSpec((TILE, 1), row),
                 pl.BlockSpec((TILE, h), row),
             ]
-            + [ANY] * len(pieces),
+            + [ANY] * len(pieces)
+            + [WHOLE],
             out_specs=[
                 pl.BlockSpec((TILE, h), lambda i, s: (i, 0)),
                 WHOLE,
@@ -268,9 +296,9 @@
                 WHOLE,
                 resident((8, h)),
                 resident((BOUND, h)),
+                WHOLE,
             ],
             scratch_shapes=[
-                pltpu.VMEM((h, pieces[0].shape[1]), BF16),
                 pltpu.VMEM((8, h), F32),
                 pltpu.SemaphoreType.DMA((len(pieces), planes)),
             ],
@@ -282,11 +310,13 @@
             pltpu.VMEM((live, h), BF16),
             jax.ShapeDtypeStruct((8, h), F32),
             pltpu.HBM((BOUND, h), BF16),
+            pltpu.VMEM(weight.shape, BF16),
         ],
-        compiler_params=params(24),
+        input_output_aliases={9 + len(pieces): 6},
+        compiler_params=params(16),
         cost_estimate=cost(3 * live * h * h, live * h * 12),
         name="layer",
-    )(at, far(part), far(adjacency), far(adjacency), last, inverse, far(cotangent), *pieces)
+    )(at, far(part), far(adjacency), far(adjacency), far(adjacency), same, last, inverse, far(cotangent), *pieces, held(weight))
 
 
 def halves(at_ref, value, rows):
@@ -315,7 +345,7 @@
     t = pl.program_id(0)
     last = pl.num_programs(0) - 1
     n = a_own.shape[1]
-    groups = TILE // (4 * rows)
+    groups = WIDE // (4 * rows)
 
     @pl.when(t < last)
     def _():
@@ -349,15 +379,14 @@
     h, n = kept.shape
     n_a = n * FIRST // 8
     n_b = n - n_a
-    blocks = h // TILE
-    single = TILE == 4 * rows
-    b_rows = TILE if single else TILE // 2
+    blocks = h // WIDE
+    b_rows = WIDE // 2
 
     def tile(t):
         return jnp.minimum(t, blocks - 1)
 
     def plane(t, s):
-        return (tile(t) // 2 if single else tile(t), 0)
+        return (tile(t), 0)
 
     return pl.pallas_call(
         functools.partial(share_kernel, rows=rows),
@@ -365,16 +394,16 @@
             num_scalar_prefetch=1,
             grid=(blocks + 1,),
             in_specs=[
-                pl.BlockSpec((TILE, n), lambda t, s: (tile(t), 0)),
-                pl.BlockSpec((TILE, n), lambda t, s: (tile(t), 0)),
+                pl.BlockSpec((WIDE, n), lambda t, s: (tile(t), 0)),
+                pl.BlockSpec((WIDE, n), lambda t, s: (tile(t), 0)),
                 pl.BlockSpec((SPARE, n), lambda t, s: (h // SPARE, 0)),
                 resident((8, n)),
             ],
             out_specs=[
-                pl.BlockSpec((TILE // 2, n_a), lambda t, s: (tile(t), 0)),
-                pl.BlockSpec((TILE // 2, n_a), lambda t, s: (t, 0)),
+                pl.BlockSpec((WIDE // 2, n_a), lambda t, s: (tile(t), 0)),
+                pl.BlockSpec((WIDE // 2, n_a), lambda t, s: (t, 0)),
                 pl.BlockSpec((b_rows, n_b), plane),
-                pl.BlockSpec((b_rows, n_b), lambda t, s: (t // 2 if single else t, 0)),
+                pl.BlockSpec((b_rows, n_b), lambda t, s: (t, 0)),
                 resident((8, n)),
             ],
         ),
@@ -517,21 +546,14 @@
     )(far(adjacency), grads, *after)
 
 
-def grad_rows_kernel(at_ref, c_ref, g_ref, *refs, low, tiles, planes):
-    w, sem, sem_out = refs[-3:]
+def grad_rows_kernel(c_ref, g_ref, *refs, low, tiles):
+    o_ref, lead_ref, w, sem = refs[-4:]
     i = pl.program_id(0)
-    if low:
-        o_ref, lead_ref = refs[-5:-3]
-        copies = [pltpu.make_async_copy(refs[0], w, sem_out)]
-    else:
-        o_ref, lead_ref, w_ref = refs[-6:-3]
-        copies = fetch(refs[:8], planes, w, sem, at_ref)
-        copy_out = pltpu.make_async_copy(w, w_ref, sem_out)
+    copy = pltpu.make_async_copy(refs[0].at[:, pl.ds(0, w.shape[1])], w, sem)
 
     @pl.when(i == 0)
     def _():
-        for copy in copies:
-            copy.start()
+        copy.start()
 
     @pl.when(low + i < tiles)
     def _():
@@ -540,10 +562,7 @@
         @pl.when(i == 0)
         def _():
             lead_ref[...] = total if low == 0 else jnp.zeros_like(lead_ref)
-            for copy in copies:
-                copy.wait()
-            if low == 0:
-                copy_out.start()
+            copy.wait()
 
         @pl.when(low + i > 0)
         def _():
@@ -553,45 +572,30 @@
     def _():
         o_ref[...] = jnp.zeros_like(o_ref)
 
-    if low == 0:
-
-        @pl.when(i == pl.num_programs(0) - 1)
-        def _():
-            copy_out.wait()
-
-
-def grad_rows(at, adjacency, grads, weight, nodes, low, high, planes, before, after):
+
+def grad_rows(adjacency, grads, weight, nodes, low, high, before, after):
     live, h = grads.shape
     tiles = live // TILE
     extra = [] if before is None else [before]
     outs = [jax.ShapeDtypeStruct((nodes, h), F32), TOKEN if low else jax.ShapeDtypeStruct((TILE, h), F32)]
-    out_specs = [pl.BlockSpec((TILE, h), lambda i, s: (low + i, 0)), resident((8, 128) if low else (TILE, h))]
-    if low == 0:
-        outs += [jax.ShapeDtypeStruct((h, h), BF16)]
-        out_specs += [ANY]
-    return pl.pallas_call(
-        functools.partial(grad_rows_kernel, low=low, tiles=tiles, planes=planes),
-        grid_spec=pltpu.PrefetchScalarGridSpec(
-            num_scalar_prefetch=1,
-            grid=(high - low,),
-            in_specs=[
-                pl.BlockSpec((TILE, live), lambda i, s: (jnp.minimum(low + i, tiles - 1), 0)),
-                resident((live, h)),
-            ]
-            + [ANY] * (len(weight) + len(extra) + len(after)),
-            out_specs=out_specs,
-            scratch_shapes=[
-                pltpu.VMEM((h, h), BF16),
-                pltpu.SemaphoreType.DMA((len(weight), planes)),
-                pltpu.SemaphoreType.DMA,
-            ],
-        ),
+    out_specs = [pl.BlockSpec((TILE, h), lambda i: (low + i, 0)), resident((8, 128) if low else (TILE, h))]
+    return pl.pallas_call(
+        functools.partial(grad_rows_kernel, low=low, tiles=tiles),
+        grid=(high - low,),
+        in_specs=[
+            pl.BlockSpec((TILE, live), lambda i: (jnp.minimum(low + i, tiles - 1), 0)),
+            resident((live, h)),
+            ANY,
+        ]
+        + [ANY] * (len(extra) + len(after)),
+        out_specs=out_specs,
+        scratch_shapes=[pltpu.VMEM((h, h), BF16), pltpu.SemaphoreType.DMA],
         out_shape=outs,
-        input_output_aliases={3 + len(weight): 0} if extra else {},
+        input_output_aliases={3: 0} if extra else {},
         compiler_params=params(30),
         cost_estimate=cost((2 * live + 2 * h) * (high - low) * TILE * h, live * h * 8),
         name="grad_rows",
-    )(at, far(adjacency), grads, *weight, *extra, *after)
+    )(far(adjacency), grads, far(weight), *extra, *after)
 
 
 def back_kernel(a_ref, b_ref, c_ref, d_ref, _, o_ref, p_ref):
@@ -663,8 +667,10 @@
     def swap_core(value):
         return permute(value, lambda b, w: (b ^ 1, w))
 
-    def swap_outer(value):
-        return permute(value, lambda b, w: ((b + (1 if b % 2 else -1)) % n_blk, w))
+    def swap_outer(value, parity=None):
+        pairs = [(b, (b + (1 if b % 2 else -1)) % n_blk) for b in range(n_blk)]
+        chosen = [(b, t) for b, t in pairs if parity is None or (b if b % 2 else t) // 2 % 2 == parity]
+        return lax.ppermute(value, axes, [(b * n_wa + w, t * n_wa + w) for b, t in chosen for w in range(n_wa)])
 
     def swap_lo(value):
         return permute(value, lambda b, w: (b ^ 2, w))
@@ -674,7 +680,7 @@
 
     leading = features[:BOUND]
     partner = swap_wa(leading)
-    outer_same = swap_outer(leading)
+    row_same = swap_outer(leading, 0)
 
     sheet = jnp.concatenate([weight, jnp.broadcast_to(bias[:, None], (share, 128))], axis=1)
     planes = [rotate_hi(sheet, k) for k in range(1, n_hi)]
@@ -696,18 +702,33 @@
     at = jnp.stack([live_count, core, lo, hi, wa]).astype(jnp.int32)
 
     adjacency = counts(index, (live + (1 + 2 * n_wa) * BOUND) // TILE, [inverse, at])
-    partner, *planes = tie([partner, *planes], [far(adjacency)])
+    partner, late_leading, *planes = tie([partner, leading, *planes], [far(adjacency)])
     sheet = jnp.concatenate([sheet, *planes])
     half_sheet, row_sheet = swap_wa(sheet), swap_lo(sheet)
-    inner_same, inner_other = swap_core(leading), swap_core(partner)
-    part = gather(adjacency, features, (partner, inner_same, inner_other, outer_same), live, [inverse, at])
-    half_sheet, row_sheet, outer_same = tie([half_sheet, row_sheet, outer_same], [far(part)])
+    inner_same, inner_other = swap_core(late_leading), swap_core(partner)
+    plane_same = swap_outer(late_leading, 1)
+    part = gather(adjacency, features, (partner, inner_same, inner_other), live, [])
+    half_sheet, row_same, plane_same = tie([half_sheet, row_same, plane_same], [far(part)])
+    outer_same = jnp.where((blk // 2 % 2 == 0) == (core == 1), row_same, plane_same)
     outer_other = swap_wa(outer_same)
-    both_sheet, outer_other = tie([swap_lo(half_sheet), outer_other], [])
-    pieces = [sheet, half_sheet, row_sheet, both_sheet]
+    cut = n_hi * 3 // 4
+    row_tail, outer_other = tie([row_sheet[cut * share :], outer_other], [])
+    late = list(tie([swap_lo(half_sheet[: cut * share]), swap_wa(row_tail)], []))
+    pieces = [sheet, half_sheet, row_sheet]
     pieces = pieces + [swap_core(value) for value in pieces]
-    output, grads, mixed, low, bias_sum, outer_other_g = layer(
-        at, part, adjacency, outer_other, inverse, cotangent, pieces, n_hi
+    matrix = place(at, pieces, [(k, 0) for k in (0, 1, 2, 4, 5, 6)], n_hi)
+    output, grads, mixed, low, bias_sum, outer_other_g, matrix = layer(
+        at,
+        part,
+        adjacency,
+        outer_same,
+        outer_other,
+        inverse,
+        cotangent,
+        late + [swap_core(value) for value in late],
+        [(3, 0), (3, cut), (7, 0), (7, cut)],
+        matrix,
+        n_hi,
     )
     sent, token = weight_share(at, mixed, low, bias_sum, False, [])
     came = swap_core(sent)
@@ -720,13 +741,13 @@
     own_bound, inner_same_g, inner_other_g, outer_same_g = scatter_bound(adjacency, grads, [bias_sum])
     own_came, inner_came = swap_core(inner_other_g), swap_core(inner_same_g)
     split, tiles = live // TILE // 2, -(-nodes // TILE)
-    grad_features, lead, matrix = grad_rows(at, adjacency, grads, pieces, nodes, 0, split, n_hi, None, [far(own_bound), outer_came])
+    grad_features, lead = grad_rows(adjacency, grads, matrix, nodes, 0, split, None, [far(own_bound)])
     outer_back, own_back = back(outer_same_g, outer_came, own_bound, own_came, lead)
     outer_back = swap_outer(outer_back)
     a, a_sent, b, b_sent, bias_sum = fold(at, a, a_came, b, b_came, bias_sum, share, own_back)
     a_came, b_came = swap_lo(a_sent), swap_wa(b_sent)
     grad_features, token = grad_rows(
-        at, adjacency, grads, [matrix], nodes, split, tiles, n_hi, grad_features, [bias_sum]
+        adjacency, grads, matrix, nodes, split, tiles, grad_features, [bias_sum]
     )
     bias_sum, own, *rest = part_planes(
         at, a, a_came, b, b_came, bias_sum, share, n_hi, [token]

time: 255 us -> 253 us (level)
    ppermute x0 -> x3, waiting for transfers between devices: none -> 9.08 us  [swap_outer(): lax.ppermute(value, axes, [(b * n_wa + w, t * n_wa + w) for b, t in chose...]
    ppermute x29, starting transfers between devices: 31.2 us -> 23.2 us  [permute(): return lax.ppermute(value, axes, [(s, b * n_wa + w) for s, (b, w) in pairs])]
    ppermute x29, waiting for transfers between devices: 64.1 us -> 56.2 us  [permute(): return lax.ppermute(value, axes, [(s, b * n_wa + w) for s, (b, w) in pairs])]
    ppermute x0 -> x3, starting transfers between devices: none -> 6.89 us  [swap_outer(): lax.ppermute(value, axes, [(b * n_wa + w, t * n_wa + w) for b, t in chose...]
    pallas_call x3 -> x4, Pallas kernels: 63.9 us -> 66.8 us  [the longest x1 32.9 us: layer(): pl.pallas_call(functools.partial(layer_kernel, tiles=tiles, numbers=numbe...]
  transfers between devices with their start and end apart: 29 -> 32, of which waited for: 12 -> 11; matrix products, arithmetic and copies ran while one was open for 2% -> 1% of each run, Pallas kernels for 40% -> 40%
where the time goes in v6:
time: 253 us; the launch traced here: 252 us
  Pallas kernels  146 us (58%)
  waiting for transfers between devices  65.3 us (26%)
  starting transfers between devices  30.1 us (12%)
  local copies, waits for them, and re-layouts  6.69 us (3%)
    ppermute x29, waiting for transfers between devices, permute(): return lax.ppermute(value, axes, [(s, b * n_wa + w) for s, (b, w) in pairs])  56.2 us
    pallas_call x1, Pallas kernels, layer(): pl.pallas_call(functools.partial(layer_kernel, tiles=tiles, numbers=numbe...  32.9 us
    pallas_call x2, Pallas kernels, grad_rows(): pl.pallas_call(functools.partial(grad_rows_kernel, low=low, tiles=tiles),...  32 us
    ppermute x29, starting transfers between devices, permute(): return lax.ppermute(value, axes, [(s, b * n_wa + w) for s, (b, w) in pairs])  23.2 us
    pallas_call x1, Pallas kernels, gather(): pl.pallas_call(functools.partial(gather_kernel, count=len(blocks)), grid=...  21.2 us
    pallas_call x2, Pallas kernels, weight_share(): pl.pallas_call(functools.partial(weight_kernel, mine=mine), grid_spec=plt...  16.9 us
    pallas_call x1, Pallas kernels, counts(): pl.pallas_call(counts_kernel, grid=(tiles,), in_specs=[pl.BlockSpec((FANO...  16.5 us
    pallas_call x1, Pallas kernels, scatter_bound(): pl.pallas_call(functools.partial(scatter_bound_kernel, count=blocks), gri...  9.35 us
  transfers between devices with their start and end apart: 32, of which 11 were waited for; matrix products, arithmetic and copies ran while one was open for 1% of the time, Pallas kernels for 40%

profile of v6, /device:TPU:11, one launch (start us, length us, event | category | flops | bytes accessed | tf_op | source)
XLA Modules:
  0.0 251.7 jit_solution(9134524809590155895)
XLA Ops:
  0.7 2.4 slice.24.refs_1_
  3.0 3.7 %collective-permute-start.7 = (bf16[256,2048]{1,0:T(8,128)(2,1)}, bf16[256,2048]{1,0:T(8,128)(2,1)S(1)}, u32[]{:S(2)}, u32[]{:S(2)}) collective-permute-start(bf16[256,2048]{1,0:T(8,128)(2,1)} %slice.24.refs_1_), channel_id=1, source_target_pairs={{2,4},{3,5},{4,2},{5,3},{10,12},{11,13},{12,10},{13,11},{18,20},{1... | collective-permute-start | bytes 3145736 | tf_op jit(solution)/shard_map/ppermute | solution.py:673
  8.0 2.3 collective-permute-start.2
  10.3 2.2 collective-permute-start.1
  13.8 16.5 %counts.1.refs_5_.c_ref.d_ref.cl_ref = bf16[2816,1536]{1,0:T(8,128)(2,1)} custom-call(s32[16,1536]{1,0:T(8,128)S(1)} %fusion.2.index_ref, f32[1536,1]{1,0:T(8,128)S(1)} %broadcast_in_dim.27.refs_0_.inv_ref, s32[5]{0:T(128)S(1)} %stack.23.refs_1_.at_ref), custom_call_target="tpu_custom_call" | custom-call | bytes 4325376 | tf_op jit(solution)/shard_map/counts/pallas_call | solution.py:93
  30.3 3.2 %collective-permute-done.1.refs_2_ = bf16[64,2176]{1,0:T(8,128)(2,1)S(1)} collective-permute-done((bf16[64,2176]{1,0:T(8,128)(2,1)S(1)}, bf16[64,2176]{1,0:T(8,128)(2,1)S(1)}, u32[]{:S(2)}, u32[]{:S(2)}) %collective-permute-start.1) | collective-permute-done | bytes 278560 | tf_op jit(solution)/shard_map/ppermute | solution.py:662
  38.1 1.6 collective-permute-start.8
  39.7 3.9 %collective-permute-start.9 = (bf16[256,2176]{1,0:T(8,128)(2,1)S(1)}, bf16[256,2176]{1,0:T(8,128)(2,1)S(1)}, u32[]{:S(2)}, u32[]{:S(2)}) collective-permute-start(bf16[256,2176]{1,0:T(8,128)(2,1)S(1)} %pad_maximum_fusion.refs_0_), channel_id=1, source_target_pairs={{0,4},{1,5},{2,6},{3,7},{4,0},{5,1},{6,2},{7,3},{8,12},{9,13},{10,... | collective-permute-start | bytes 3342344 | tf_op jit(solution)/shard_map/ppermute | solution.py:662
  43.6 21.2 %gather.1.refs_3_.part_ref = f32[1536,2048]{1,0:T(8,128)} custom-call(bf16[2816,1536]{1,0:T(8,128)(2,1)} %counts.1.refs_5_.c_ref.d_ref.cl_ref, bf16[1664,2048]{1,0:T(8,128)(2,1)} %t_ref.1, bf16[256,2048]{1,0:T(8,128)(2,1)} %get-tuple-element.56.refs_0_, bf16[256,2048]{1,0:T(8,128)(2,1)} %collective-permute-done.4.refs_1_, ...), custom_call_target="tpu_custom_call" | custom-call | flops 905969664 | bytes 1179648 | tf_op jit(solution)/shard_map/gather/pallas_call | solution.py:118
  67.2 11.9 %collective-permute-done.9.refs_2_ = bf16[256,2176]{1,0:T(8,128)(2,1)S(1)} collective-permute-done((bf16[256,2176]{1,0:T(8,128)(2,1)S(1)}, bf16[256,2176]{1,0:T(8,128)(2,1)S(1)}, u32[]{:S(2)}, u32[]{:S(2)}) %collective-permute-start.9) | collective-permute-done | bytes 1114144 | tf_op jit(solution)/shard_map/ppermute | solution.py:662
  79.2 10.3 %collective-permute-done.10.refs_1_ = bf16[256,2048]{1,0:T(8,128)(2,1)S(1)} collective-permute-done((bf16[256,2048]{1,0:T(8,128)(2,1)S(1)}, bf16[256,2048]{1,0:T(8,128)(2,1)S(1)}, u32[]{:S(2)}, u32[]{:S(2)}) %collective-permute-start.10) | collective-permute-done | bytes 1048608 | tf_op jit(solution)/shard_map/ppermute | solution.py:662
  89.6 7.3 %collective-permute-done.11.refs_0_ = bf16[192,2176]{1,0:T(8,128)(2,1)S(1)} collective-permute-done((bf16[192,2176]{1,0:T(8,128)(2,1)S(1)}, bf16[192,2176]{1,0:T(8,128)(2,1)S(1)}, u32[]{:S(2)}, u32[]{:S(2)}) %collective-permute-start.11) | collective-permute-done | bytes 835616 | tf_op jit(solution)/shard_map/ppermute | solution.py:662
  96.8 1.8 collective-permute-start.13
  98.7 1.9 place.1.refs_4_
  101.0 32.9 %layer.1 = (f32[1664,2048]{1,0:T(8,128)}, bf16[1536,2048]{1,0:T(8,128)(2,1)S(1)}, bf16[1536,2048]{1,0:T(8,128)(2,1)S(1)}, bf16[1536,2048]{1,0:T(8,128)(2,1)S(1)}...) custom-call(s32[5]{0:T(128)S(1)} %stack.23.refs_1_.at_ref, ...), custom_call_target="tpu_custom_call", output_to_operand_aliasing={{6}: (13, {})} | custom-call | flops 1207959552 | bytes 2359296 | tf_op jit(solution)/shard_map/layer/pallas_call | solution.py:275
  133.9 9.0 %weight_share.2 = (bf16[2064,1024]{1,0:T(8,128)(2,1)}, f32[8,1024]{1,0:T(8,128)S(1)}) custom-call(s32[5]{0:T(128)S(1)} %stack.23.refs_1_.at_ref, bf16[1536,2048]{1,0:T(8,128)(2,1)S(1)} %get-tuple-element.71.m_all, bf16[1536,2048]{1,0:T(8,128)(2,1)S(1)} %get-tuple-element.72.gl_all, f32[8,2048]{1,0:T(8,128)S(1)} %get-tuple-element.73.gb), custom_call_target="tpu_custom_call" | custom-call | flops 402653184 | bytes 786432 | tf_op jit(solution)/shard_map/weight_share/pallas_call | solution.py:248
  143.3 8.0 %weight_share.3 = (bf16[2048,1024]{1,0:T(8,128)(2,1)S(1)}, f32[8,1024]{1,0:T(8,128)S(1)}) custom-call(s32[5]{0:T(128)S(1)} %stack.23.refs_1_.at_ref, bf16[1536,2048]{1,0:T(8,128)(2,1)S(1)} %get-tuple-element.71.m_all, bf16[1536,2048]{1,0:T(8,128)(2,1)S(1)} %get-tuple-element.72.gl_all, f32[8,2048]{1,0:T(8,128)S(1)} %get-tuple-element.73.gb, ...), custom_call_target="tpu_custom_call" | custom-call | flops 402653184 | bytes 786432 | tf_op jit(solution)/shard_map/weight_share/pallas_call | solution.py:248
  151.2 4.7 %share.1 = (bf16[1024,512]{1,0:T(8,128)(2,1)}, bf16[1040,512]{1,0:T(8,128)(2,1)}, bf16[1024,512]{1,0:T(8,128)(2,1)}, bf16[1040,512]{1,0:T(8,128)(2,1)}, f32[8,1024]{1,0:T(8,128)S(1)}) custom-call(s32[5]{0:T(128)S(1)} %stack.23.refs_1_.at_ref, bf16[2048,1024]{1,0:T(8,128)(2,1)S(1)} %get-tuple-element.75.kept_ref, ...), custom_call_target="tpu_custom_call" | custom-call | bytes 1048576 | tf_op jit(solution)/shard_map/share/pallas_call | solution.py:391
  156.0 1.5 collective-permute-start.23
  157.4 9.4 %scatter_bound.1 = (bf16[256,2048]{1,0:T(8,128)(2,1)}, bf16[256,2048]{1,0:T(8,128)(2,1)}, bf16[256,2048]{1,0:T(8,128)(2,1)}, bf16[256,2048]{1,0:T(8,128)(2,1)}) custom-call(bf16[2816,1536]{1,0:T(8,128)(2,1)} %counts.1.refs_5_.c_ref.d_ref.cl_ref, bf16[1536,2048]{1,0:T(8,128)(2,1)S(1)} %get-tuple-element.69.g_ref, f32[8,1024]{1,0:T(8,128)S(1)} %get-tuple-element.78.refs_0_.gb_ref), custom_call_target="tpu_custom_call" | custom-call | flops 402653184 | bytes 786432 | tf_op jit(solution)/shard_map/scatter_bound/pallas_call | solution.py:536
  167.6 14.3 %grad_rows.2 = (f32[1664,2048]{1,0:T(8,128)}, f32[256,2048]{1,0:T(8,128)S(1)}) custom-call(bf16[2816,1536]{1,0:T(8,128)(2,1)} %counts.1.refs_5_.c_ref.d_ref.cl_ref, bf16[1536,2048]{1,0:T(8,128)(2,1)S(1)} %get-tuple-element.69.g_ref, bf16[2048,2176]{1,0:T(8,128)(2,1)} %copy-done, bf16[256,2048]{1,0:T(8,128)(2,1)} %get-tuple-element.79.refs_1_.c_ref), custom_call_target="tpu_custom_call" | custom-call | flops 704643072 | bytes 1572864 | tf_op jit(solution)/shard_map/grad_rows/pallas_call | solution.py:582
  181.8 2.5 %back.1 = (bf16[256,2048]{1,0:T(8,128)(2,1)S(1)}, bf16[256,2048]{1,0:T(8,128)(2,1)S(1)}) custom-call(bf16[256,2048]{1,0:T(8,128)(2,1)} %get-tuple-element.82.a_ref, bf16[256,2048]{1,0:T(8,128)(2,1)S(1)} %collective-permute-done.20.b_ref, bf16[256,2048]{1,0:T(8,128)(2,1)} %get-tuple-element.79.refs_1_.c_ref, ...), custom_call_target="tpu_custom_call" | custom-call | bytes 393216 | tf_op jit(solution)/shard_map/back/pallas_call | solution.py:608
  184.4 6.3 %collective-permute-done.23.a_came = bf16[1040,512]{1,0:T(8,128)(2,1)S(1)} collective-permute-done((bf16[1040,512]{1,0:T(8,128)(2,1)}, bf16[1040,512]{1,0:T(8,128)(2,1)S(1)}, u32[]{:S(2)}, u32[]{:S(2)}) %collective-permute-start.23) | collective-permute-done | bytes 1064992 | tf_op jit(solution)/shard_map/ppermute | solution.py:662
  190.7 2.2 fold.1
  194.3 1.6 collective-permute-start.22
  195.8 17.8 %grad_rows.3 = (f32[1664,2048]{1,0:T(8,128)}, f32[8,128]{1,0:T(8,128)S(1)}) custom-call(bf16[2816,1536]{1,0:T(8,128)(2,1)} %counts.1.refs_5_.c_ref.d_ref.cl_ref, bf16[1536,2048]{1,0:T(8,128)(2,1)S(1)} %get-tuple-element.69.g_ref, bf16[2048,2176]{1,0:T(8,128)(2,1)} %copy-done, ...), custom_call_target="tpu_custom_call", output_to_operand_aliasing={{0}: (3, {})} | custom-call | flops 939524096 | bytes 1572864 | tf_op jit(solution)/shard_map/grad_rows/pallas_call | solution.py:582
  213.6 3.4 %collective-permute-done.25.a_came = bf16[528,512]{1,0:T(8,128)(2,1)S(1)} collective-permute-done((bf16[528,512]{1,0:T(8,128)(2,1)S(1)}, bf16[528,512]{1,0:T(8,128)(2,1)S(1)}, u32[]{:S(2)}, u32[]{:S(2)}) %collective-permute-start.25) | collective-permute-done | bytes 540704 | tf_op jit(solution)/shard_map/ppermute | solution.py:662
  218.4 1.9 collective-permute-start.29
  220.6 9.1 %collective-permute-done.22.refs_1_ = bf16[256,2048]{1,0:T(8,128)(2,1)S(1)} collective-permute-done((bf16[256,2048]{1,0:T(8,128)(2,1)S(1)}, bf16[256,2048]{1,0:T(8,128)(2,1)S(1)}, u32[]{:S(2)}, u32[]{:S(2)}) %collective-permute-start.22) | collective-permute-done | bytes 1048608 | tf_op jit(solution)/shard_map/ppermute | solution.py:673
  229.7 10.9 %collective-permute-done.27.refs_2_ = bf16[256,2048]{1,0:T(8,128)(2,1)S(1)} collective-permute-done((bf16[256,2048]{1,0:T(8,128)(2,1)S(1)}, bf16[256,2048]{1,0:T(8,128)(2,1)S(1)}, u32[]{:S(2)}, u32[]{:S(2)}) %collective-permute-start.27) | collective-permute-done | bytes 1048608 | tf_op jit(solution)/shard_map/ppermute | solution.py:662
  240.6 4.9 %grad_lead.1 = (f32[1664,2048]{1,0:T(8,128)}, f32[8,128]{1,0:T(8,128)S(1)}) custom-call(f32[256,2048]{1,0:T(8,128)S(1)} %get-tuple-element.80._.lead_ref, bf16[256,2048]{1,0:T(8,128)(2,1)S(1)} %collective-permute-done.19.refs_0_, bf16[256,2048]{1,0:T(8,128)(2,1)S(1)} %collective-permute-done.22.refs_1_, ...), custom_call_target="tpu_custom_call", output_to_operand_aliasing={{0}: (5, {})} | custom-call | flops 134217728 | bytes 524288 | tf_op jit(solution)/shard_map/grad_lead/pallas_call | solution.py:636
  247.5 1.5 collective-permute-start.31
  (94 shorter events, 18.3 us)
Async XLA Ops:
  3.0 30.5 %collective-permute-start.7 = (bf16[256,2048]{1,0:T(8,128)(2,1)}, bf16[256,2048]{1,0:T(8,128)(2,1)S(1)}, u32[]{:S(2)}, u32[]{:S(2)}) collective-permute-start(bf16[256,2048]{1,0:T(8,128)(2,1)} %slice.24.refs_1_), channel_id=1, source_target_pairs={{2,4},{3,5},{4,2},{5,3},{10,12},{11,13},{12,10},{13,11},{18,20},{1... | collective-permute-start | bytes 3145736 | tf_op jit(solution)/shard_map/ppermute | solution.py:673
  6.7 26.8 %collective-permute-start = (bf16[256,2048]{1,0:T(8,128)(2,1)}, bf16[256,2048]{1,0:T(8,128)(2,1)}, u32[]{:S(2)}, u32[]{:S(2)}) collective-permute-start(bf16[256,2048]{1,0:T(8,128)(2,1)} %slice.24.refs_1_), channel_id=1, source_target_pairs={{0,1},{1,0},{2,3},{3,2},{4,5},{5,4},{6,7},{7,6},{8,9},{9,8},{10,11... | collective-permute-start | bytes 3145736 | tf_op jit(solution)/shard_map/ppermute | solution.py:662
  7.8 22.5 %collective-permute-start.3 = (bf16[64,2176]{1,0:T(8,128)(2,1)S(1)}, bf16[64,2176]{1,0:T(8,128)(2,1)S(1)}, u32[]{:S(2)}, u32[]{:S(2)}) collective-permute-start(bf16[64,2176]{1,0:T(8,128)(2,1)S(1)} %pad_maximum_fusion.1), channel_id=1, source_target_pairs={{0,24},{1,25},{2,26},{3,27},{4,28},{5,29},{6,30},{7,31},{8,0},{9,1... | collective-permute-start | bytes 835592 | tf_op jit(solution)/shard_map/ppermute | solution.py:662
  8.0 22.3 %collective-permute-start.2 = (bf16[64,2176]{1,0:T(8,128)(2,1)S(1)}, bf16[64,2176]{1,0:T(8,128)(2,1)S(1)}, u32[]{:S(2)}, u32[]{:S(2)}) collective-permute-start(bf16[64,2176]{1,0:T(8,128)(2,1)S(1)} %pad_maximum_fusion.1), channel_id=1, source_target_pairs={{0,16},{1,17},{2,18},{3,19},{4,20},{5,21},{6,22},{7,23},{8,24},{9,... | collective-permute-start | bytes 835592 | tf_op jit(solution)/shard_map/ppermute | solution.py:662
  10.3 23.1 %collective-permute-start.1 = (bf16[64,2176]{1,0:T(8,128)(2,1)S(1)}, bf16[64,2176]{1,0:T(8,128)(2,1)S(1)}, u32[]{:S(2)}, u32[]{:S(2)}) collective-permute-start(bf16[64,2176]{1,0:T(8,128)(2,1)S(1)} %pad_maximum_fusion.1), channel_id=1, source_target_pairs={{0,8},{1,9},{2,10},{3,11},{4,12},{5,13},{6,14},{7,15},{8,16},{9,17... | collective-permute-start | bytes 835592 | tf_op jit(solution)/shard_map/ppermute | solution.py:662
  35.2 8.4 %collective-permute-start.5 = (bf16[256,2048]{1,0:T(8,128)(2,1)}, bf16[256,2048]{1,0:T(8,128)(2,1)}, u32[]{:S(2)}, u32[]{:S(2)}) collective-permute-start(bf16[256,2048]{1,0:T(8,128)(2,1)} %get-tuple-element.56.refs_0_), channel_id=1, source_target_pairs={{0,2},{1,3},{2,0},{3,1},{4,6},{5,7},{6,4},{7,5},{8,10},{9,11},{10,... | collective-permute-start | bytes 3145736 | tf_op jit(solution)/shard_map/ppermute | solution.py:662
  35.2 8.4 %collective-permute-start.4 = (bf16[256,2048]{1,0:T(8,128)(2,1)}, bf16[256,2048]{1,0:T(8,128)(2,1)}, u32[]{:S(2)}, u32[]{:S(2)}) collective-permute-start(bf16[256,2048]{1,0:T(8,128)(2,1)} %get-tuple-element.57), channel_id=1, source_target_pairs={{0,2},{1,3},{2,0},{3,1},{4,6},{5,7},{6,4},{7,5},{8,10},{9,11},{10,... | collective-permute-start | bytes 3145736 | tf_op jit(solution)/shard_map/ppermute | solution.py:662
  36.8 28.0 %collective-permute-start.6 = (bf16[256,2176]{1,0:T(8,128)(2,1)S(1)}, bf16[256,2176]{1,0:T(8,128)(2,1)S(1)}, u32[]{:S(2)}, u32[]{:S(2)}) collective-permute-start(bf16[256,2176]{1,0:T(8,128)(2,1)S(1)} %pad_maximum_fusion.refs_0_), channel_id=1, source_target_pairs={{0,1},{1,0},{2,3},{3,2},{4,5},{5,4},{6,7},{7,6},{8,9},{9,8},{10,11... | collective-permute-start | bytes 3342344 | tf_op jit(solution)/shard_map/ppermute | solution.py:662
  38.1 26.7 %collective-permute-start.8 = (bf16[256,2048]{1,0:T(8,128)(2,1)}, bf16[256,2048]{1,0:T(8,128)(2,1)}, u32[]{:S(2)}, u32[]{:S(2)}) collective-permute-start(bf16[256,2048]{1,0:T(8,128)(2,1)} %get-tuple-element.57), channel_id=1, source_target_pairs={{0,30},{1,31},{6,8},{7,9},{8,6},{9,7},{14,16},{15,17},{16,14},{17,... | collective-permute-start | bytes 3145736 | tf_op jit(solution)/shard_map/ppermute | solution.py:673
  39.7 39.4 %collective-permute-start.9 = (bf16[256,2176]{1,0:T(8,128)(2,1)S(1)}, bf16[256,2176]{1,0:T(8,128)(2,1)S(1)}, u32[]{:S(2)}, u32[]{:S(2)}) collective-permute-start(bf16[256,2176]{1,0:T(8,128)(2,1)S(1)} %pad_maximum_fusion.refs_0_), channel_id=1, source_target_pairs={{0,4},{1,5},{2,6},{3,7},{4,0},{5,1},{6,2},{7,3},{8,12},{9,13},{10,... | collective-permute-start | bytes 3342344 | tf_op jit(solution)/shard_map/ppermute | solution.py:662
  65.0 24.6 %collective-permute-start.10 = (bf16[256,2048]{1,0:T(8,128)(2,1)S(1)}, bf16[256,2048]{1,0:T(8,128)(2,1)S(1)}, u32[]{:S(2)}, u32[]{:S(2)}) collective-permute-start(bf16[256,2048]{1,0:T(8,128)(2,1)S(1)} %broadcast_select_fusion.same_ref), channel_id=1, source_target_pairs={{0,1},{1,0},{2,3},{3,2},{4,5},{5,4},{6,7},{7,6},{8,9},{9,8},{10,11... | collective-permute-start | bytes 3145736 | tf_op jit(solution)/shard_map/ppermute | solution.py:662
  65.3 31.5 %collective-permute-start.11 = (bf16[192,2176]{1,0:T(8,128)(2,1)S(1)}, bf16[192,2176]{1,0:T(8,128)(2,1)S(1)}, u32[]{:S(2)}, u32[]{:S(2)}) collective-permute-start(bf16[192,2176]{1,0:T(8,128)(2,1)S(1)} %slice.26), channel_id=1, source_target_pairs={{0,4},{1,5},{2,6},{3,7},{4,0},{5,1},{6,2},{7,3},{8,12},{9,13},{10,... | collective-permute-start | bytes 2506760 | tf_op jit(solution)/shard_map/ppermute | solution.py:662
  66.7 31.9 %collective-permute-start.15 = (bf16[256,2176]{1,0:T(8,128)(2,1)S(1)}, bf16[256,2176]{1,0:T(8,128)(2,1)S(1)}, u32[]{:S(2)}, u32[]{:S(2)}) collective-permute-start(bf16[256,2176]{1,0:T(8,128)(2,1)S(1)} %pad_maximum_fusion.refs_0_), channel_id=1, source_target_pairs={{0,2},{1,3},{2,0},{3,1},{4,6},{5,7},{6,4},{7,5},{8,10},{9,11},{10,... | collective-permute-start | bytes 3342344 | tf_op jit(solution)/shard_map/ppermute | solution.py:662
  66.9 31.7 %collective-permute-start.16 = (bf16[256,2176]{1,0:T(8,128)(2,1)S(1)}, bf16[256,2176]{1,0:T(8,128)(2,1)S(1)}, u32[]{:S(2)}, u32[]{:S(2)}) collective-permute-start(bf16[256,2176]{1,0:T(8,128)(2,1)S(1)} %get-tuple-element.64.refs_1_), channel_id=1, source_target_pairs={{0,2},{1,3},{2,0},{3,1},{4,6},{5,7},{6,4},{7,5},{8,10},{9,11},{10,... | collective-permute-start | bytes 3342344 | tf_op jit(solution)/shard_map/ppermute | solution.py:662
  79.2 19.5 %collective-permute-start.17 = (bf16[256,2176]{1,0:T(8,128)(2,1)S(1)}, bf16[256,2176]{1,0:T(8,128)(2,1)S(1)}, u32[]{:S(2)}, u32[]{:S(2)}) collective-permute-start(bf16[256,2176]{1,0:T(8,128)(2,1)S(1)} %collective-permute-done.9.refs_2_), channel_id=1, source_target_pairs={{0,2},{1,3},{2,0},{3,1},{4,6},{5,7},{6,4},{7,5},{8,10},{9,11},{10,... | collective-permute-start | bytes 3342344 | tf_op jit(solution)/shard_map/ppermute | solution.py:662
  89.6 7.3 %collective-permute-start.12 = (bf16[64,2176]{1,0:T(8,128)(2,1)S(1)}, bf16[64,2176]{1,0:T(8,128)(2,1)S(1)}, u32[]{:S(2)}, u32[]{:S(2)}) collective-permute-start(bf16[64,2176]{1,0:T(8,128)(2,1)S(1)} %get-tuple-element.65), channel_id=1, source_target_pairs={{0,1},{1,0},{2,3},{3,2},{4,5},{5,4},{6,7},{7,6},{8,9},{9,8},{10,11... | collective-permute-start | bytes 835592 | tf_op jit(solution)/shard_map/ppermute | solution.py:662
  96.8 4.2 %collective-permute-start.13 = (bf16[192,2176]{1,0:T(8,128)(2,1)S(1)}, bf16[192,2176]{1,0:T(8,128)(2,1)S(1)}, u32[]{:S(2)}, u32[]{:S(2)}) collective-permute-start(bf16[192,2176]{1,0:T(8,128)(2,1)S(1)} %get-tuple-element.66.refs_0_), channel_id=1, source_target_pairs={{0,2},{1,3},{2,0},{3,1},{4,6},{5,7},{6,4},{7,5},{8,10},{9,11},{10,... | collective-permute-start | bytes 2506760 | tf_op jit(solution)/shard_map/ppermute | solution.py:662
  98.7 2.4 collective-permute-start.14
  142.9 8.3 %collective-permute-start.18 = (bf16[2064,1024]{1,0:T(8,128)(2,1)}, bf16[2064,1024]{1,0:T(8,128)(2,1)S(1)}, u32[]{:S(2)}, u32[]{:S(2)}) collective-permute-start(bf16[2064,1024]{1,0:T(8,128)(2,1)} %get-tuple-element.76), channel_id=1, source_target_pairs={{0,2},{1,3},{2,0},{3,1},{4,6},{5,7},{6,4},{7,5},{8,10},{9,11},{10,... | collective-permute-start | bytes 12681224 | tf_op jit(solution)/shard_map/ppermute | solution.py:662
  143.3 38.6 %collective-permute-start.20 = (bf16[256,2048]{1,0:T(8,128)(2,1)S(1)}, bf16[256,2048]{1,0:T(8,128)(2,1)S(1)}, u32[]{:S(2)}, u32[]{:S(2)}) collective-permute-start(bf16[256,2048]{1,0:T(8,128)(2,1)S(1)} %copy-done.9), channel_id=1, source_target_pairs={{0,1},{1,0},{2,3},{3,2},{4,5},{5,4},{6,7},{7,6},{8,9},{9,8},{10,11... | collective-permute-start | bytes 3145736 | tf_op jit(solution)/shard_map/ppermute | solution.py:662
  156.0 34.7 %collective-permute-start.23 = (bf16[1040,512]{1,0:T(8,128)(2,1)}, bf16[1040,512]{1,0:T(8,128)(2,1)S(1)}, u32[]{:S(2)}, u32[]{:S(2)}) collective-permute-start(bf16[1040,512]{1,0:T(8,128)(2,1)} %get-tuple-element.88), channel_id=1, source_target_pairs={{0,1},{1,0},{2,3},{3,2},{4,5},{5,4},{6,7},{7,6},{8,9},{9,8},{10,11... | collective-permute-start | bytes 3194888 | tf_op jit(solution)/shard_map/ppermute | solution.py:662
  157.4 33.3 %collective-permute-start.24 = (bf16[1040,512]{1,0:T(8,128)(2,1)}, bf16[1040,512]{1,0:T(8,128)(2,1)S(1)}, u32[]{:S(2)}, u32[]{:S(2)}) collective-permute-start(bf16[1040,512]{1,0:T(8,128)(2,1)} %get-tuple-element.90), channel_id=1, source_target_pairs={{0,4},{1,5},{2,6},{3,7},{4,0},{5,1},{6,2},{7,3},{8,12},{9,13},{10,... | collective-permute-start | bytes 3194888 | tf_op jit(solution)/shard_map/ppermute | solution.py:662
  166.8 15.0 %collective-permute-start.21 = (bf16[256,2048]{1,0:T(8,128)(2,1)}, bf16[256,2048]{1,0:T(8,128)(2,1)S(1)}, u32[]{:S(2)}, u32[]{:S(2)}) collective-permute-start(bf16[256,2048]{1,0:T(8,128)(2,1)} %get-tuple-element.84), channel_id=1, source_target_pairs={{0,2},{1,3},{2,0},{3,1},{4,6},{5,7},{6,4},{7,5},{8,10},{9,11},{10,... | collective-permute-start | bytes 3145736 | tf_op jit(solution)/shard_map/ppermute | solution.py:662
  192.9 24.1 %collective-permute-start.25 = (bf16[528,512]{1,0:T(8,128)(2,1)S(1)}, bf16[528,512]{1,0:T(8,128)(2,1)S(1)}, u32[]{:S(2)}, u32[]{:S(2)}) collective-permute-start(bf16[528,512]{1,0:T(8,128)(2,1)S(1)} %get-tuple-element.92), channel_id=1, source_target_pairs={{0,4},{1,5},{2,6},{3,7},{4,0},{5,1},{6,2},{7,3},{8,12},{9,13},{10,... | collective-permute-start | bytes 1622024 | tf_op jit(solution)/shard_map/ppermute | solution.py:662
  193.0 20.6 %collective-permute-start.26 = (bf16[512,512]{1,0:T(8,128)(2,1)S(1)}, bf16[512,512]{1,0:T(8,128)(2,1)S(1)}, u32[]{:S(2)}, u32[]{:S(2)}) collective-permute-start(bf16[512,512]{1,0:T(8,128)(2,1)S(1)} %get-tuple-element.94), channel_id=1, source_target_pairs={{0,1},{1,0},{2,3},{3,2},{4,5},{5,4},{6,7},{7,6},{8,9},{9,8},{10,11... | collective-permute-start | bytes 1572872 | tf_op jit(solution)/shard_map/ppermute | solution.py:662
  193.0 27.3 %collective-permute-start.19 = (bf16[256,2048]{1,0:T(8,128)(2,1)S(1)}, bf16[256,2048]{1,0:T(8,128)(2,1)S(1)}, u32[]{:S(2)}, u32[]{:S(2)}) collective-permute-start(bf16[256,2048]{1,0:T(8,128)(2,1)S(1)} %copy-done.8), channel_id=1, source_target_pairs={{0,2},{1,3},{2,0},{3,1},{4,6},{5,7},{6,4},{7,5},{8,10},{9,11},{10,... | collective-permute-start | bytes 3145736 | tf_op jit(solution)/shard_map/ppermute | solution.py:662
  194.3 35.4 %collective-permute-start.22 = (bf16[256,2048]{1,0:T(8,128)(2,1)S(1)}, bf16[256,2048]{1,0:T(8,128)(2,1)S(1)}, u32[]{:S(2)}, u32[]{:S(2)}) collective-permute-start(bf16[256,2048]{1,0:T(8,128)(2,1)S(1)} %get-tuple-element.85), channel_id=1, source_target_pairs={{0,30},{1,31},{2,4},{3,5},{4,2},{5,3},{6,8},{7,9},{8,6},{9,7},{10,... | collective-permute-start | bytes 3145736 | tf_op jit(solution)/shard_map/ppermute | solution.py:673
  217.7 22.9 %collective-permute-start.27 = (bf16[256,2048]{1,0:T(8,128)(2,1)S(1)}, bf16[256,2048]{1,0:T(8,128)(2,1)S(1)}, u32[]{:S(2)}, u32[]{:S(2)}) collective-permute-start(bf16[256,2048]{1,0:T(8,128)(2,1)S(1)} %tie.9), channel_id=1, source_target_pairs={{0,1},{1,0},{2,3},{3,2},{4,5},{5,4},{6,7},{7,6},{8,9},{9,8},{10,11... | collective-permute-start | bytes 3145736 | tf_op jit(solution)/shard_map/ppermute | solution.py:662
  217.8 27.7 %collective-permute-start.28 = (bf16[144,1024]{1,0:T(8,128)(2,1)S(1)}, bf16[144,1024]{1,0:T(8,128)(2,1)S(1)}, u32[]{:S(2)}, u32[]{:S(2)}) collective-permute-start(bf16[144,1024]{1,0:T(8,128)(2,1)S(1)} %get-tuple-element.102), channel_id=1, source_target_pairs={{0,8},{1,9},{2,10},{3,11},{4,12},{5,13},{6,14},{7,15},{8,16},{9,17... | collective-permute-start | bytes 884744 | tf_op jit(solution)/shard_map/ppermute | solution.py:662
  218.4 27.0 %collective-permute-start.29 = (bf16[144,1024]{1,0:T(8,128)(2,1)S(1)}, bf16[144,1024]{1,0:T(8,128)(2,1)S(1)}, u32[]{:S(2)}, u32[]{:S(2)}) collective-permute-start(bf16[144,1024]{1,0:T(8,128)(2,1)S(1)} %get-tuple-element.103), channel_id=1, source_target_pairs={{0,16},{1,17},{2,18},{3,19},{4,20},{5,21},{6,22},{7,23},{8,24},{9,... | collective-permute-start | bytes 884744 | tf_op jit(solution)/shard_map/ppermute | solution.py:662
  220.4 26.5 %collective-permute-start.30 = (bf16[144,1024]{1,0:T(8,128)(2,1)S(1)}, bf16[144,1024]{1,0:T(8,128)(2,1)S(1)}, u32[]{:S(2)}, u32[]{:S(2)}) collective-permute-start(bf16[144,1024]{1,0:T(8,128)(2,1)S(1)} %get-tuple-element.104), channel_id=1, source_target_pairs={{0,24},{1,25},{2,26},{3,27},{4,28},{5,29},{6,30},{7,31},{8,0},{9,1... | collective-permute-start | bytes 884744 | tf_op jit(solution)/shard_map/ppermute | solution.py:662
  247.5 2.7 %collective-permute-start.31 = (f32[72,1024]{1,0:T(8,128)S(1)}, f32[72,1024]{1,0:T(8,128)S(1)}, u32[]{:S(2)}, u32[]{:S(2)}) collective-permute-start(f32[72,1024]{1,0:T(8,128)S(1)} %get-tuple-element.107), channel_id=1, source_target_pairs={{0,2},{1,3},{2,0},{3,1},{4,6},{5,7},{6,4},{7,5},{8,10},{9,11},{10,... | collective-permute-start | bytes 884744 | tf_op jit(solution)/shard_map/ppermute | solution.py:662
  (13 other events, 219.9 us)

commit v7 on v6

--- a/solution.py
+++ b/solution.py
@@ -173,7 +173,7 @@
 def layer_kernel(at_ref, part_ref, c_ref, d_ref, cl_ref, same_ref, last_ref, inv_ref, ct_ref, *refs, tiles, numbers, planes):
     count = len(numbers)
     pieces, refs = refs[:count], refs[count + 1 :]
-    o_ref, agl_ref, m_all, gl_all, gb, far_ref, w, b, sem = refs
+    o_ref, agl_ref, m_all, gl_all, gb, far_low, far_high, w, b, sem = refs
     i = pl.program_id(0)
     h = part_ref.shape[1]
     copies = fetch(pieces, numbers, planes, w, sem, at_ref)
@@ -217,7 +217,9 @@
     @pl.when(i == tiles)
     def _():
         o_ref[...] = jnp.zeros_like(o_ref)
-        far_ref[...] = dot(cl_ref[...], agl_ref[...], 1, 0).astype(BF16)
+        away = dot(cl_ref[...], agl_ref[...], 1, 0).astype(BF16)
+        far_low[...] = away[: BOUND // 2]
+        far_high[...] = away[BOUND // 2 :]
 
 
 def weight_kernel(at_ref, m_all, gl_all, gb, *refs, mine):
@@ -295,7 +297,8 @@
                 WHOLE,
                 WHOLE,
                 resident((8, h)),
-                resident((BOUND, h)),
+                resident((BOUND // 2, h)),
+                resident((BOUND // 2, h)),
                 WHOLE,
             ],
             scratch_shapes=[
@@ -309,10 +312,11 @@
             pltpu.VMEM((live, h), BF16),
             pltpu.VMEM((live, h), BF16),
             jax.ShapeDtypeStruct((8, h), F32),
-            pltpu.HBM((BOUND, h), BF16),
+            pltpu.HBM((BOUND // 2, h), BF16),
+            pltpu.HBM((BOUND // 2, h), BF16),
             pltpu.VMEM(weight.shape, BF16),
         ],
-        input_output_aliases={9 + len(pieces): 6},
+        input_output_aliases={9 + len(pieces): 7},
         compiler_params=params(16),
         cost_estimate=cost(3 * live * h * h, live * h * 12),
         name="layer",
@@ -341,83 +345,52 @@
     return jnp.concatenate([rows[k : k + 1, :] for k in range(-(-total // n))], axis=1)[:, :total].astype(F32)
 
 
-def share_kernel(at_ref, kept_ref, came_ref, cb_ref, gb_ref, a_own, a_sent, b_own, b_sent, gb_out, *, rows):
-    t = pl.program_id(0)
-    last = pl.num_programs(0) - 1
-    n = a_own.shape[1]
-    groups = WIDE // (4 * rows)
-
-    @pl.when(t < last)
-    def _():
-        part = kept_ref[...].astype(F32) + came_ref[...].astype(F32)
-        for g in range(groups):
-            value = part[g * 4 * rows : (g + 1) * 4 * rows].astype(BF16)
-            mine, other = halves(at_ref, value[:, :n], rows)
-            at = slice(g * 2 * rows, (g + 1) * 2 * rows)
-            a_own[at, :] = mine
-            a_sent[at, :] = other
-            here = (t * groups + g) % 2 == at_ref[2]
-            at = slice(g // 2 * 4 * rows, (g // 2 + 1) * 4 * rows)
-
-            @pl.when(here)
-            def _():
-                b_own[at, :] = value[:, n:]
-
-            @pl.when(jnp.logical_not(here))
-            def _():
-                b_sent[at, :] = value[:, n:]
-
-    @pl.when(t == last)
-    def _():
-        total = gb_ref[0:1, :] + cb_ref[0:1, :].astype(F32)
-        gb_out[...] = jnp.broadcast_to(total, gb_out.shape)
-        a_sent[:SPARE, :] = spare_rows(total, n)
-        b_sent[:SPARE, :] = jnp.zeros((SPARE, b_sent.shape[1]), BF16)
-
-
-def share_rows(at, kept, came, bias, rows):
+def share_kernel(at_ref, kept_ref, came_ref, gb_ref, low_ref, high_ref, a_own, a_sent, b_own, b_sent, gb_out, *, rows):
+    h = kept_ref.shape[0]
+    n_a, n_b = a_own.shape[1], b_own.shape[1]
+    for g in range(h // (4 * rows)):
+        at = slice(g * 4 * rows, (g + 1) * 4 * rows)
+        value = (kept_ref[at, :].astype(F32) + came_ref[at, :].astype(F32)).astype(BF16)
+        mine, other = halves(at_ref, value[:, :n_a], rows)
+        at = slice(g * 2 * rows, (g + 1) * 2 * rows)
+        a_own[at, :] = mine
+        a_sent[at, :] = other
+        here = g % 2 == at_ref[2]
+        at = slice(g // 2 * 4 * rows, (g // 2 + 1) * 4 * rows)
+
+        @pl.when(here)
+        def _():
+            b_own[at, :] = value[:, n_a:]
+
+        @pl.when(jnp.logical_not(here))
+        def _():
+            b_sent[at, :] = value[:, n_a:]
+
+    total = gb_ref[0:1, :] + came_ref[h : h + 1, :].astype(F32)
+    gb_out[...] = jnp.broadcast_to(total, gb_out.shape)
+    a_sent[h // 2 :, :] = spare_rows(total, n_a)
+    b_sent[h // 2 :, :] = jnp.zeros((SPARE, n_b), BF16)
+
+
+def share_rows(at, kept, came, bias, rows, after):
     h, n = kept.shape
     n_a = n * FIRST // 8
     n_b = n - n_a
-    blocks = h // WIDE
-    b_rows = WIDE // 2
-
-    def tile(t):
-        return jnp.minimum(t, blocks - 1)
-
-    def plane(t, s):
-        return (tile(t), 0)
-
     return pl.pallas_call(
         functools.partial(share_kernel, rows=rows),
-        grid_spec=pltpu.PrefetchScalarGridSpec(
-            num_scalar_prefetch=1,
-            grid=(blocks + 1,),
-            in_specs=[
-                pl.BlockSpec((WIDE, n), lambda t, s: (tile(t), 0)),
-                pl.BlockSpec((WIDE, n), lambda t, s: (tile(t), 0)),
-                pl.BlockSpec((SPARE, n), lambda t, s: (h // SPARE, 0)),
-                resident((8, n)),
-            ],
-            out_specs=[
-                pl.BlockSpec((WIDE // 2, n_a), lambda t, s: (tile(t), 0)),
-                pl.BlockSpec((WIDE // 2, n_a), lambda t, s: (t, 0)),
-                pl.BlockSpec((b_rows, n_b), plane),
-                pl.BlockSpec((b_rows, n_b), lambda t, s: (t, 0)),
-                resident((8, n)),
-            ],
-        ),
+        in_specs=[SMEM] + [WHOLE] * 3 + [ANY] * 2,
+        out_specs=[WHOLE] * 5,
         out_shape=[
-            pltpu.HBM((h // 2, n_a), BF16),
-            pltpu.HBM((h // 2 + SPARE, n_a), BF16),
-            pltpu.HBM((h // 2, n_b), BF16),
-            pltpu.HBM((h // 2 + SPARE, n_b), BF16),
+            pltpu.VMEM((h // 2, n_a), BF16),
+            pltpu.VMEM((h // 2 + SPARE, n_a), BF16),
+            pltpu.VMEM((h // 2, n_b), BF16),
+            pltpu.VMEM((h // 2 + SPARE, n_b), BF16),
             jax.ShapeDtypeStruct((8, n), F32),
         ],
         compiler_params=params(10),
         cost_estimate=cost(0, h * n * 8),
         name="share",
-    )(at, kept, came, came, bias)
+    )(at, kept, came, bias, *after)
 
 
 def fold_kernel(at_ref, a_ref, a_came, b_ref, b_came, gb_ref, _, a_own, a_sent, b_own, b_sent, gb_out, *, rows):
@@ -455,7 +428,7 @@
         compiler_params=params(22),
         cost_estimate=cost(0, b_own.size * 9),
         name="fold",
-    )(at, far(a_own), a_came, far(b_own), b_came, bias, after)
+    )(at, a_own, a_came, b_own, b_came, bias, after)
 
 
 def part_kernel(at_ref, a_ref, a_came, b_ref, b_came, gb_ref, *refs, rows, planes):
@@ -598,23 +571,32 @@
     )(far(adjacency), grads, far(weight), *extra, *after)
 
 
-def back_kernel(a_ref, b_ref, c_ref, d_ref, _, o_ref, p_ref):
-    o_ref[...] = (a_ref[...].astype(F32) + b_ref[...].astype(F32)).astype(BF16)
-    p_ref[...] = (c_ref[...].astype(F32) + d_ref[...].astype(F32)).astype(BF16)
-
-
-def back(a, b, c, d, after):
-    block = pl.BlockSpec((64, a.shape[1]), lambda i: (i, 0))
+def back_kernel(outer_ref, low_ref, own_ref, came_ref, high_ref, _, outer_back, own_back):
+    i = pl.program_id(0)
+    half = pl.num_programs(0) // 2
+    early = (i < half).astype(F32)
+    outer_back[...] = (outer_ref[...].astype(F32) + early * low_ref[...].astype(F32)).astype(BF16)
+    own = own_ref[...].astype(F32) + came_ref[...].astype(F32)
+    own_back[...] = (own + (1 - early) * high_ref[...].astype(F32)).astype(BF16)
+
+
+def back(outer, low, own, came, high, after):
+    rows, h = own.shape
+    steps = 4
+    half = steps // 2
+    whole = pl.BlockSpec((rows // steps, h), lambda i: (i, 0))
+    first = pl.BlockSpec((rows // steps, h), lambda i: (jnp.minimum(i, half - 1), 0))
+    second = pl.BlockSpec((rows // steps, h), lambda i: (jnp.maximum(i - half, 0), 0))
     return pl.pallas_call(
         back_kernel,
-        grid=(a.shape[0] // 64,),
-        in_specs=[block] * 4 + [ANY],
-        out_specs=[block] * 2,
-        out_shape=[jax.ShapeDtypeStruct(a.shape, BF16)] * 2,
+        grid=(steps,),
+        in_specs=[whole, first, whole, whole, second, ANY],
+        out_specs=[whole] * 2,
+        out_shape=[jax.ShapeDtypeStruct((rows, h), BF16)] * 2,
         compiler_params=params(10),
-        cost_estimate=cost(0, a.size * 12),
+        cost_estimate=cost(0, own.size * 12),
         name="back",
-    )(far(a), b, far(c), d, after)
+    )(far(outer), low, far(own), came, high, after)
 
 
 def grad_lead_kernel(lead_ref, *refs):
@@ -717,7 +699,7 @@
     pieces = [sheet, half_sheet, row_sheet]
     pieces = pieces + [swap_core(value) for value in pieces]
     matrix = place(at, pieces, [(k, 0) for k in (0, 1, 2, 4, 5, 6)], n_hi)
-    output, grads, mixed, low, bias_sum, outer_other_g, matrix = layer(
+    output, grads, mixed, low, bias_sum, far_low, far_high, matrix = layer(
         at,
         part,
         adjacency,
@@ -734,15 +716,15 @@
     came = swap_core(sent)
     kept, bias_sum = weight_share(at, mixed, low, bias_sum, True, [token])
 
-    a, a_sent, b, b_sent, bias_sum = share_rows(at, kept, came, bias_sum, share)
+    far_low, far_high = swap_wa(far_low), swap_outer(far_high)
+    a, a_sent, b, b_sent, bias_sum = share_rows(at, kept, came, bias_sum, share, [far_low, far_high])
     a_came, b_came = swap_wa(a_sent), swap_lo(b_sent)
 
-    outer_came = swap_wa(outer_other_g)
     own_bound, inner_same_g, inner_other_g, outer_same_g = scatter_bound(adjacency, grads, [bias_sum])
     own_came, inner_came = swap_core(inner_other_g), swap_core(inner_same_g)
-    split, tiles = live // TILE // 2, -(-nodes // TILE)
+    split, tiles = live // TILE // 3, -(-nodes // TILE)
     grad_features, lead = grad_rows(adjacency, grads, matrix, nodes, 0, split, None, [far(own_bound)])
-    outer_back, own_back = back(outer_same_g, outer_came, own_bound, own_came, lead)
+    outer_back, own_back = back(outer_same_g, far_low, own_bound, own_came, far_high, lead)
     outer_back = swap_outer(outer_back)
     a, a_sent, b, b_sent, bias_sum = fold(at, a, a_came, b, b_came, bias_sum, share, own_back)
     a_came, b_came = swap_lo(a_sent), swap_wa(b_sent)
@@ -758,9 +740,10 @@
     grad_features, token = grad_lead(lead, returned, matrix, grad_features)
     mine, other = finish(at, bias_sum, own, rest, share, token)
     other = swap_core(other)
-    pair = jnp.where(core == 0, jnp.concatenate([mine, other], axis=1), jnp.concatenate([other, mine], axis=1))
-    grad_weight = pair[:share]
-    grad_bias = lax.dynamic_slice_in_dim(pair[share], (blk * n_wa + wa) * share, share)
+    first, second = jnp.where(core == 0, mine, other), jnp.where(core == 0, other, mine)
+    grad_weight = jnp.concatenate([first[:share], second[:share]], axis=1)
+    bias_row = jnp.concatenate([first[share], second[share]])
+    grad_bias = lax.dynamic_slice_in_dim(bias_row, (blk * n_wa + wa) * share, share)
     return (output, grad_features, grad_weight, grad_bias)
 
 

time: 253 us -> 249 us (0.984)
  Pallas kernels: 146 us -> 143 us
    ppermute x3 -> x4, waiting for transfers between devices: 9.08 us -> 8.01 us  [swap_outer(): lax.ppermute(value, axes, [(b * n_wa + w, t * n_wa + w) for b, t in chose...]
    ppermute x3 -> x4, starting transfers between devices: 6.89 us -> 6.77 us  [swap_outer(): lax.ppermute(value, axes, [(b * n_wa + w, t * n_wa + w) for b, t in chose...]
  transfers between devices with their start and end apart: 32 -> 33, of which waited for: 11 -> 12; matrix products, arithmetic and copies ran while one was open for 1% -> 1% of each run, Pallas kernels for 40% -> 39%
where the time goes in v7:
time: 249 us; the launch traced here: 247 us
  Pallas kernels  143 us (57%)
  waiting for transfers between devices  62.8 us (25%)
  starting transfers between devices  31.1 us (12%)
  local copies, waits for them, and re-layouts  5.31 us (2%)
  other arithmetic  2.91 us (1%)
    ppermute x29, waiting for transfers between devices, permute(): return lax.ppermute(value, axes, [(s, b * n_wa + w) for s, (b, w) in pairs])  54.8 us
    pallas_call x1, Pallas kernels, layer(): pl.pallas_call(functools.partial(layer_kernel, tiles=tiles, numbers=numbe...  32.9 us
    pallas_call x2, Pallas kernels, grad_rows(): pl.pallas_call(functools.partial(grad_rows_kernel, low=low, tiles=tiles),...  32 us
    ppermute x29, starting transfers between devices, permute(): return lax.ppermute(value, axes, [(s, b * n_wa + w) for s, (b, w) in pairs])  24.3 us
    pallas_call x1, Pallas kernels, gather(): pl.pallas_call(functools.partial(gather_kernel, count=len(blocks)), grid=...  21.4 us
    pallas_call x2, Pallas kernels, weight_share(): pl.pallas_call(functools.partial(weight_kernel, mine=mine), grid_spec=plt...  16.9 us
    pallas_call x1, Pallas kernels, counts(): pl.pallas_call(counts_kernel, grid=(tiles,), in_specs=[pl.BlockSpec((FANO...  16.4 us
    pallas_call x1, Pallas kernels, scatter_bound(): pl.pallas_call(functools.partial(scatter_bound_kernel, count=blocks), gri...  9.38 us
  transfers between devices with their start and end apart: 33, of which 12 were waited for; matrix products, arithmetic and copies ran while one was open for 1% of the time, Pallas kernels for 39%

profile of v7, /device:TPU:11, one launch (start us, length us, event | category | flops | bytes accessed | tf_op | source)
XLA Modules:
  0.0 247.4 jit_solution(9946524210523870198)
XLA Ops:
  0.7 2.4 slice.30.refs_1_
  3.0 3.7 %collective-permute-start.7 = (bf16[256,2048]{1,0:T(8,128)(2,1)}, bf16[256,2048]{1,0:T(8,128)(2,1)S(1)}, u32[]{:S(2)}, u32[]{:S(2)}) collective-permute-start(bf16[256,2048]{1,0:T(8,128)(2,1)} %slice.30.refs_1_), channel_id=1, source_target_pairs={{2,4},{3,5},{4,2},{5,3},{10,12},{11,13},{12,10},{13,11},{18,20},{1... | collective-permute-start | bytes 3145736 | tf_op jit(solution)/shard_map/ppermute | solution.py:655
  8.0 2.3 collective-permute-start.2
  10.3 2.2 collective-permute-start.1
  13.8 16.4 %counts.1.refs_5_.c_ref.d_ref.cl_ref = bf16[2816,1536]{1,0:T(8,128)(2,1)} custom-call(s32[16,1536]{1,0:T(8,128)S(1)} %fusion.2.index_ref, f32[1536,1]{1,0:T(8,128)S(1)} %broadcast_in_dim.27.refs_0_.inv_ref, s32[5]{0:T(128)S(1)} %stack.23.refs_1_.at_ref), custom_call_target="tpu_custom_call" | custom-call | bytes 4325376 | tf_op jit(solution)/shard_map/counts/pallas_call | solution.py:93
  30.3 3.2 %collective-permute-done.1.refs_2_ = bf16[64,2176]{1,0:T(8,128)(2,1)S(1)} collective-permute-done((bf16[64,2176]{1,0:T(8,128)(2,1)S(1)}, bf16[64,2176]{1,0:T(8,128)(2,1)S(1)}, u32[]{:S(2)}, u32[]{:S(2)}) %collective-permute-start.1) | collective-permute-done | bytes 278560 | tf_op jit(solution)/shard_map/ppermute | solution.py:644
  38.1 1.7 collective-permute-start.8
  39.7 3.7 %collective-permute-start.9 = (bf16[256,2176]{1,0:T(8,128)(2,1)S(1)}, bf16[256,2176]{1,0:T(8,128)(2,1)S(1)}, u32[]{:S(2)}, u32[]{:S(2)}) collective-permute-start(bf16[256,2176]{1,0:T(8,128)(2,1)S(1)} %pad_maximum_fusion.refs_0_), channel_id=1, source_target_pairs={{0,4},{1,5},{2,6},{3,7},{4,0},{5,1},{6,2},{7,3},{8,12},{9,13},{10,... | collective-permute-start | bytes 3342344 | tf_op jit(solution)/shard_map/ppermute | solution.py:644
  43.4 21.4 %gather.1.refs_3_.part_ref = f32[1536,2048]{1,0:T(8,128)} custom-call(bf16[2816,1536]{1,0:T(8,128)(2,1)} %counts.1.refs_5_.c_ref.d_ref.cl_ref, bf16[1664,2048]{1,0:T(8,128)(2,1)} %t_ref.1, bf16[256,2048]{1,0:T(8,128)(2,1)} %get-tuple-element.57.refs_0_, bf16[256,2048]{1,0:T(8,128)(2,1)} %collective-permute-done.4.refs_1_, ...), custom_call_target="tpu_custom_call" | custom-call | flops 905969664 | bytes 1179648 | tf_op jit(solution)/shard_map/gather/pallas_call | solution.py:118
  65.3 1.3 collective-permute-start.11
  67.2 11.9 %collective-permute-done.9.refs_2_ = bf16[256,2176]{1,0:T(8,128)(2,1)S(1)} collective-permute-done((bf16[256,2176]{1,0:T(8,128)(2,1)S(1)}, bf16[256,2176]{1,0:T(8,128)(2,1)S(1)}, u32[]{:S(2)}, u32[]{:S(2)}) %collective-permute-start.9) | collective-permute-done | bytes 1114144 | tf_op jit(solution)/shard_map/ppermute | solution.py:644
  79.2 10.3 %collective-permute-done.10.refs_1_ = bf16[256,2048]{1,0:T(8,128)(2,1)S(1)} collective-permute-done((bf16[256,2048]{1,0:T(8,128)(2,1)S(1)}, bf16[256,2048]{1,0:T(8,128)(2,1)S(1)}, u32[]{:S(2)}, u32[]{:S(2)}) %collective-permute-start.10) | collective-permute-done | bytes 1048608 | tf_op jit(solution)/shard_map/ppermute | solution.py:644
  89.6 7.1 %collective-permute-done.11.refs_0_ = bf16[192,2176]{1,0:T(8,128)(2,1)S(1)} collective-permute-done((bf16[192,2176]{1,0:T(8,128)(2,1)S(1)}, bf16[192,2176]{1,0:T(8,128)(2,1)S(1)}, u32[]{:S(2)}, u32[]{:S(2)}) %collective-permute-start.11) | collective-permute-done | bytes 835616 | tf_op jit(solution)/shard_map/ppermute | solution.py:644
  96.7 1.9 collective-permute-start.13
  98.7 1.9 place.1.refs_4_
  101.0 32.9 %layer.1 = (f32[1664,2048]{1,0:T(8,128)}, bf16[1536,2048]{1,0:T(8,128)(2,1)S(1)}, bf16[1536,2048]{1,0:T(8,128)(2,1)S(1)}, bf16[1536,2048]{1,0:T(8,128)(2,1)S(1)}...) custom-call(s32[5]{0:T(128)S(1)} %stack.23.refs_1_.at_ref, ...), custom_call_target="tpu_custom_call", output_to_operand_aliasing={{7}: (13, {})} | custom-call | flops 1207959552 | bytes 2359296 | tf_op jit(solution)/shard_map/layer/pallas_call | solution.py:277
  134.0 9.0 %weight_share.2 = (bf16[2064,1024]{1,0:T(8,128)(2,1)}, f32[8,1024]{1,0:T(8,128)S(1)}) custom-call(s32[5]{0:T(128)S(1)} %stack.23.refs_1_.at_ref, bf16[1536,2048]{1,0:T(8,128)(2,1)S(1)} %get-tuple-element.72.m_all, bf16[1536,2048]{1,0:T(8,128)(2,1)S(1)} %get-tuple-element.73.gl_all, f32[8,2048]{1,0:T(8,128)S(1)} %get-tuple-element.74.gb), custom_call_target="tpu_custom_call" | custom-call | flops 402653184 | bytes 786432 | tf_op jit(solution)/shard_map/weight_share/pallas_call | solution.py:250
  143.4 8.0 %weight_share.3 = (bf16[2048,1024]{1,0:T(8,128)(2,1)S(1)}, f32[8,1024]{1,0:T(8,128)S(1)}) custom-call(s32[5]{0:T(128)S(1)} %stack.23.refs_1_.at_ref, bf16[1536,2048]{1,0:T(8,128)(2,1)S(1)} %get-tuple-element.72.m_all, bf16[1536,2048]{1,0:T(8,128)(2,1)S(1)} %get-tuple-element.73.gl_all, f32[8,2048]{1,0:T(8,128)S(1)} %get-tuple-element.74.gb, ...), custom_call_target="tpu_custom_call" | custom-call | flops 402653184 | bytes 786432 | tf_op jit(solution)/shard_map/weight_share/pallas_call | solution.py:250
  151.4 5.3 %collective-permute-done.19.low_ref = bf16[128,2048]{1,0:T(8,128)(2,1)S(1)} collective-permute-done((bf16[128,2048]{1,0:T(8,128)(2,1)S(1)}, bf16[128,2048]{1,0:T(8,128)(2,1)S(1)}, u32[]{:S(2)}, u32[]{:S(2)}) %collective-permute-start.19) | collective-permute-done | bytes 524320 | tf_op jit(solution)/shard_map/ppermute | solution.py:644
  157.6 2.4 share.1
  160.0 1.5 collective-permute-start.24
  161.5 9.4 %scatter_bound.1 = (bf16[256,2048]{1,0:T(8,128)(2,1)}, bf16[256,2048]{1,0:T(8,128)(2,1)}, bf16[256,2048]{1,0:T(8,128)(2,1)}, bf16[256,2048]{1,0:T(8,128)(2,1)}) custom-call(bf16[2816,1536]{1,0:T(8,128)(2,1)} %counts.1.refs_5_.c_ref.d_ref.cl_ref, bf16[1536,2048]{1,0:T(8,128)(2,1)S(1)} %get-tuple-element.70.g_ref, f32[8,1024]{1,0:T(8,128)S(1)} %get-tuple-element.81.refs_0_.gb_ref), custom_call_target="tpu_custom_call" | custom-call | flops 402653184 | bytes 786432 | tf_op jit(solution)/shard_map/scatter_bound/pallas_call | solution.py:509
  171.5 10.1 %grad_rows.2 = (f32[1664,2048]{1,0:T(8,128)}, f32[256,2048]{1,0:T(8,128)S(1)}) custom-call(bf16[2816,1536]{1,0:T(8,128)(2,1)} %counts.1.refs_5_.c_ref.d_ref.cl_ref, bf16[1536,2048]{1,0:T(8,128)(2,1)S(1)} %get-tuple-element.70.g_ref, bf16[2048,2176]{1,0:T(8,128)(2,1)} %copy-done, bf16[256,2048]{1,0:T(8,128)(2,1)} %get-tuple-element.82.refs_1_.own_ref), custom_call_target="tpu_custom_call" | custom-call | flops 469762048 | bytes 1572864 | tf_op jit(solution)/shard_map/grad_rows/pallas_call | solution.py:555
  181.6 2.7 %back.1 = (bf16[256,2048]{1,0:T(8,128)(2,1)S(1)}, bf16[256,2048]{1,0:T(8,128)(2,1)S(1)}) custom-call(bf16[256,2048]{1,0:T(8,128)(2,1)} %get-tuple-element.85.outer_ref, bf16[128,2048]{1,0:T(8,128)(2,1)S(1)} %collective-permute-done.19.low_ref, bf16[256,2048]{1,0:T(8,128)(2,1)} %get-tuple-element.82.refs_1_.own_ref, ...), custom_call_target="tpu_custom_call" | custom-call | bytes 393216 | tf_op jit(solution)/shard_map/back/pallas_call | solution.py:590
  187.6 1.6 collective-permute-start.21
  189.2 1.3 collective-permute-start.23
  190.6 22.0 %grad_rows.3 = (f32[1664,2048]{1,0:T(8,128)}, f32[8,128]{1,0:T(8,128)S(1)}) custom-call(bf16[2816,1536]{1,0:T(8,128)(2,1)} %counts.1.refs_5_.c_ref.d_ref.cl_ref, bf16[1536,2048]{1,0:T(8,128)(2,1)S(1)} %get-tuple-element.70.g_ref, bf16[2048,2176]{1,0:T(8,128)(2,1)} %copy-done, ...), custom_call_target="tpu_custom_call", output_to_operand_aliasing={{0}: (3, {})} | custom-call | flops 1174405120 | bytes 1572864 | tf_op jit(solution)/shard_map/grad_rows/pallas_call | solution.py:555
  214.5 1.3 collective-permute-start.30
  216.9 7.1 %collective-permute-done.23.refs_1_ = bf16[256,2048]{1,0:T(8,128)(2,1)S(1)} collective-permute-done((bf16[256,2048]{1,0:T(8,128)(2,1)S(1)}, bf16[256,2048]{1,0:T(8,128)(2,1)S(1)}, u32[]{:S(2)}, u32[]{:S(2)}) %collective-permute-start.23) | collective-permute-done | bytes 1048608 | tf_op jit(solution)/shard_map/ppermute | solution.py:655
  224.0 13.4 %collective-permute-done.28.refs_2_ = bf16[256,2048]{1,0:T(8,128)(2,1)S(1)} collective-permute-done((bf16[256,2048]{1,0:T(8,128)(2,1)S(1)}, bf16[256,2048]{1,0:T(8,128)(2,1)S(1)}, u32[]{:S(2)}, u32[]{:S(2)}) %collective-permute-start.28) | collective-permute-done | bytes 1048608 | tf_op jit(solution)/shard_map/ppermute | solution.py:644
  237.5 4.9 %grad_lead.1 = (f32[1664,2048]{1,0:T(8,128)}, f32[8,128]{1,0:T(8,128)S(1)}) custom-call(f32[256,2048]{1,0:T(8,128)S(1)} %get-tuple-element.83._.lead_ref, bf16[256,2048]{1,0:T(8,128)(2,1)S(1)} %collective-permute-done.21.refs_0_, bf16[256,2048]{1,0:T(8,128)(2,1)S(1)} %collective-permute-done.23.refs_1_, ...), custom_call_target="tpu_custom_call", output_to_operand_aliasing={{0}: (5, {})} | custom-call | flops 134217728 | bytes 524288 | tf_op jit(solution)/shard_map/grad_lead/pallas_call | solution.py:618
  243.0 1.6 collective-permute-start.32
  (101 shorter events, 19.8 us)
Async XLA Ops:
  3.0 30.5 %collective-permute-start.7 = (bf16[256,2048]{1,0:T(8,128)(2,1)}, bf16[256,2048]{1,0:T(8,128)(2,1)S(1)}, u32[]{:S(2)}, u32[]{:S(2)}) collective-permute-start(bf16[256,2048]{1,0:T(8,128)(2,1)} %slice.30.refs_1_), channel_id=1, source_target_pairs={{2,4},{3,5},{4,2},{5,3},{10,12},{11,13},{12,10},{13,11},{18,20},{1... | collective-permute-start | bytes 3145736 | tf_op jit(solution)/shard_map/ppermute | solution.py:655
  6.7 26.8 %collective-permute-start = (bf16[256,2048]{1,0:T(8,128)(2,1)}, bf16[256,2048]{1,0:T(8,128)(2,1)}, u32[]{:S(2)}, u32[]{:S(2)}) collective-permute-start(bf16[256,2048]{1,0:T(8,128)(2,1)} %slice.30.refs_1_), channel_id=1, source_target_pairs={{0,1},{1,0},{2,3},{3,2},{4,5},{5,4},{6,7},{7,6},{8,9},{9,8},{10,11... | collective-permute-start | bytes 3145736 | tf_op jit(solution)/shard_map/ppermute | solution.py:644
  7.8 22.5 %collective-permute-start.3 = (bf16[64,2176]{1,0:T(8,128)(2,1)S(1)}, bf16[64,2176]{1,0:T(8,128)(2,1)S(1)}, u32[]{:S(2)}, u32[]{:S(2)}) collective-permute-start(bf16[64,2176]{1,0:T(8,128)(2,1)S(1)} %pad_maximum_fusion.2), channel_id=1, source_target_pairs={{0,24},{1,25},{2,26},{3,27},{4,28},{5,29},{6,30},{7,31},{8,0},{9,1... | collective-permute-start | bytes 835592 | tf_op jit(solution)/shard_map/ppermute | solution.py:644
  8.0 22.3 %collective-permute-start.2 = (bf16[64,2176]{1,0:T(8,128)(2,1)S(1)}, bf16[64,2176]{1,0:T(8,128)(2,1)S(1)}, u32[]{:S(2)}, u32[]{:S(2)}) collective-permute-start(bf16[64,2176]{1,0:T(8,128)(2,1)S(1)} %pad_maximum_fusion.2), channel_id=1, source_target_pairs={{0,16},{1,17},{2,18},{3,19},{4,20},{5,21},{6,22},{7,23},{8,24},{9,... | collective-permute-start | bytes 835592 | tf_op jit(solution)/shard_map/ppermute | solution.py:644
  10.3 23.1 %collective-permute-start.1 = (bf16[64,2176]{1,0:T(8,128)(2,1)S(1)}, bf16[64,2176]{1,0:T(8,128)(2,1)S(1)}, u32[]{:S(2)}, u32[]{:S(2)}) collective-permute-start(bf16[64,2176]{1,0:T(8,128)(2,1)S(1)} %pad_maximum_fusion.2), channel_id=1, source_target_pairs={{0,8},{1,9},{2,10},{3,11},{4,12},{5,13},{6,14},{7,15},{8,16},{9,17... | collective-permute-start | bytes 835592 | tf_op jit(solution)/shard_map/ppermute | solution.py:644
  35.2 8.2 %collective-permute-start.5 = (bf16[256,2048]{1,0:T(8,128)(2,1)}, bf16[256,2048]{1,0:T(8,128)(2,1)}, u32[]{:S(2)}, u32[]{:S(2)}) collective-permute-start(bf16[256,2048]{1,0:T(8,128)(2,1)} %get-tuple-element.57.refs_0_), channel_id=1, source_target_pairs={{0,2},{1,3},{2,0},{3,1},{4,6},{5,7},{6,4},{7,5},{8,10},{9,11},{10,... | collective-permute-start | bytes 3145736 | tf_op jit(solution)/shard_map/ppermute | solution.py:644
  35.2 8.2 %collective-permute-start.4 = (bf16[256,2048]{1,0:T(8,128)(2,1)}, bf16[256,2048]{1,0:T(8,128)(2,1)}, u32[]{:S(2)}, u32[]{:S(2)}) collective-permute-start(bf16[256,2048]{1,0:T(8,128)(2,1)} %get-tuple-element.58), channel_id=1, source_target_pairs={{0,2},{1,3},{2,0},{3,1},{4,6},{5,7},{6,4},{7,5},{8,10},{9,11},{10,... | collective-permute-start | bytes 3145736 | tf_op jit(solution)/shard_map/ppermute | solution.py:644
  36.8 28.0 %collective-permute-start.6 = (bf16[256,2176]{1,0:T(8,128)(2,1)S(1)}, bf16[256,2176]{1,0:T(8,128)(2,1)S(1)}, u32[]{:S(2)}, u32[]{:S(2)}) collective-permute-start(bf16[256,2176]{1,0:T(8,128)(2,1)S(1)} %pad_maximum_fusion.refs_0_), channel_id=1, source_target_pairs={{0,1},{1,0},{2,3},{3,2},{4,5},{5,4},{6,7},{7,6},{8,9},{9,8},{10,11... | collective-permute-start | bytes 3342344 | tf_op jit(solution)/shard_map/ppermute | solution.py:644
  38.1 26.7 %collective-permute-start.8 = (bf16[256,2048]{1,0:T(8,128)(2,1)}, bf16[256,2048]{1,0:T(8,128)(2,1)}, u32[]{:S(2)}, u32[]{:S(2)}) collective-permute-start(bf16[256,2048]{1,0:T(8,128)(2,1)} %get-tuple-element.58), channel_id=1, source_target_pairs={{0,30},{1,31},{6,8},{7,9},{8,6},{9,7},{14,16},{15,17},{16,14},{17,... | collective-permute-start | bytes 3145736 | tf_op jit(solution)/shard_map/ppermute | solution.py:655
  39.7 39.4 %collective-permute-start.9 = (bf16[256,2176]{1,0:T(8,128)(2,1)S(1)}, bf16[256,2176]{1,0:T(8,128)(2,1)S(1)}, u32[]{:S(2)}, u32[]{:S(2)}) collective-permute-start(bf16[256,2176]{1,0:T(8,128)(2,1)S(1)} %pad_maximum_fusion.refs_0_), channel_id=1, source_target_pairs={{0,4},{1,5},{2,6},{3,7},{4,0},{5,1},{6,2},{7,3},{8,12},{9,13},{10,... | collective-permute-start | bytes 3342344 | tf_op jit(solution)/shard_map/ppermute | solution.py:644
  64.9 24.6 %collective-permute-start.10 = (bf16[256,2048]{1,0:T(8,128)(2,1)S(1)}, bf16[256,2048]{1,0:T(8,128)(2,1)S(1)}, u32[]{:S(2)}, u32[]{:S(2)}) collective-permute-start(bf16[256,2048]{1,0:T(8,128)(2,1)S(1)} %broadcast_select_fusion.same_ref), channel_id=1, source_target_pairs={{0,1},{1,0},{2,3},{3,2},{4,5},{5,4},{6,7},{7,6},{8,9},{9,8},{10,11... | collective-permute-start | bytes 3145736 | tf_op jit(solution)/shard_map/ppermute | solution.py:644
  65.3 31.3 %collective-permute-start.11 = (bf16[192,2176]{1,0:T(8,128)(2,1)S(1)}, bf16[192,2176]{1,0:T(8,128)(2,1)S(1)}, u32[]{:S(2)}, u32[]{:S(2)}) collective-permute-start(bf16[192,2176]{1,0:T(8,128)(2,1)S(1)} %slice.32), channel_id=1, source_target_pairs={{0,4},{1,5},{2,6},{3,7},{4,0},{5,1},{6,2},{7,3},{8,12},{9,13},{10,... | collective-permute-start | bytes 2506760 | tf_op jit(solution)/shard_map/ppermute | solution.py:644
  66.7 32.0 %collective-permute-start.15 = (bf16[256,2176]{1,0:T(8,128)(2,1)S(1)}, bf16[256,2176]{1,0:T(8,128)(2,1)S(1)}, u32[]{:S(2)}, u32[]{:S(2)}) collective-permute-start(bf16[256,2176]{1,0:T(8,128)(2,1)S(1)} %pad_maximum_fusion.refs_0_), channel_id=1, source_target_pairs={{0,2},{1,3},{2,0},{3,1},{4,6},{5,7},{6,4},{7,5},{8,10},{9,11},{10,... | collective-permute-start | bytes 3342344 | tf_op jit(solution)/shard_map/ppermute | solution.py:644
  66.9 31.7 %collective-permute-start.16 = (bf16[256,2176]{1,0:T(8,128)(2,1)S(1)}, bf16[256,2176]{1,0:T(8,128)(2,1)S(1)}, u32[]{:S(2)}, u32[]{:S(2)}) collective-permute-start(bf16[256,2176]{1,0:T(8,128)(2,1)S(1)} %get-tuple-element.65.refs_1_), channel_id=1, source_target_pairs={{0,2},{1,3},{2,0},{3,1},{4,6},{5,7},{6,4},{7,5},{8,10},{9,11},{10,... | collective-permute-start | bytes 3342344 | tf_op jit(solution)/shard_map/ppermute | solution.py:644
  79.2 19.5 %collective-permute-start.17 = (bf16[256,2176]{1,0:T(8,128)(2,1)S(1)}, bf16[256,2176]{1,0:T(8,128)(2,1)S(1)}, u32[]{:S(2)}, u32[]{:S(2)}) collective-permute-start(bf16[256,2176]{1,0:T(8,128)(2,1)S(1)} %collective-permute-done.9.refs_2_), channel_id=1, source_target_pairs={{0,2},{1,3},{2,0},{3,1},{4,6},{5,7},{6,4},{7,5},{8,10},{9,11},{10,... | collective-permute-start | bytes 3342344 | tf_op jit(solution)/shard_map/ppermute | solution.py:644
  89.6 7.1 %collective-permute-start.12 = (bf16[64,2176]{1,0:T(8,128)(2,1)S(1)}, bf16[64,2176]{1,0:T(8,128)(2,1)S(1)}, u32[]{:S(2)}, u32[]{:S(2)}) collective-permute-start(bf16[64,2176]{1,0:T(8,128)(2,1)S(1)} %get-tuple-element.66), channel_id=1, source_target_pairs={{0,1},{1,0},{2,3},{3,2},{4,5},{5,4},{6,7},{7,6},{8,9},{9,8},{10,11... | collective-permute-start | bytes 835592 | tf_op jit(solution)/shard_map/ppermute | solution.py:644
  96.7 4.3 %collective-permute-start.13 = (bf16[192,2176]{1,0:T(8,128)(2,1)S(1)}, bf16[192,2176]{1,0:T(8,128)(2,1)S(1)}, u32[]{:S(2)}, u32[]{:S(2)}) collective-permute-start(bf16[192,2176]{1,0:T(8,128)(2,1)S(1)} %get-tuple-element.67.refs_0_), channel_id=1, source_target_pairs={{0,2},{1,3},{2,0},{3,1},{4,6},{5,7},{6,4},{7,5},{8,10},{9,11},{10,... | collective-permute-start | bytes 2506760 | tf_op jit(solution)/shard_map/ppermute | solution.py:644
  142.9 14.7 %collective-permute-start.18 = (bf16[2064,1024]{1,0:T(8,128)(2,1)}, bf16[2064,1024]{1,0:T(8,128)(2,1)S(1)}, u32[]{:S(2)}, u32[]{:S(2)}) collective-permute-start(bf16[2064,1024]{1,0:T(8,128)(2,1)} %get-tuple-element.77), channel_id=1, source_target_pairs={{0,2},{1,3},{2,0},{3,1},{4,6},{5,7},{6,4},{7,5},{8,10},{9,11},{10,... | collective-permute-start | bytes 12681224 | tf_op jit(solution)/shard_map/ppermute | solution.py:644
  143.3 13.4 %collective-permute-start.19 = (bf16[128,2048]{1,0:T(8,128)(2,1)S(1)}, bf16[128,2048]{1,0:T(8,128)(2,1)S(1)}, u32[]{:S(2)}, u32[]{:S(2)}) collective-permute-start(bf16[128,2048]{1,0:T(8,128)(2,1)S(1)} %copy-done.10), channel_id=1, source_target_pairs={{0,1},{1,0},{2,3},{3,2},{4,5},{5,4},{6,7},{7,6},{8,9},{9,8},{10,11... | collective-permute-start | bytes 1572872 | tf_op jit(solution)/shard_map/ppermute | solution.py:644
  143.3 14.3 %collective-permute-start.20 = (bf16[128,2048]{1,0:T(8,128)(2,1)S(1)}, bf16[128,2048]{1,0:T(8,128)(2,1)S(1)}, u32[]{:S(2)}, u32[]{:S(2)}) collective-permute-start(bf16[128,2048]{1,0:T(8,128)(2,1)S(1)} %copy-done.9), channel_id=1, source_target_pairs={{0,30},{1,31},{2,4},{3,5},{4,2},{5,3},{6,8},{7,9},{8,6},{9,7},{10,... | collective-permute-start | bytes 1572872 | tf_op jit(solution)/shard_map/ppermute | solution.py:655
  160.0 25.2 %collective-permute-start.24 = (bf16[1040,512]{1,0:T(8,128)(2,1)S(1)}, bf16[1040,512]{1,0:T(8,128)(2,1)S(1)}, u32[]{:S(2)}, u32[]{:S(2)}) collective-permute-start(bf16[1040,512]{1,0:T(8,128)(2,1)S(1)} %get-tuple-element.90), channel_id=1, source_target_pairs={{0,1},{1,0},{2,3},{3,2},{4,5},{5,4},{6,7},{7,6},{8,9},{9,8},{10,11... | collective-permute-start | bytes 3194888 | tf_op jit(solution)/shard_map/ppermute | solution.py:644
  161.5 24.6 %collective-permute-start.25 = (bf16[1040,512]{1,0:T(8,128)(2,1)S(1)}, bf16[1040,512]{1,0:T(8,128)(2,1)S(1)}, u32[]{:S(2)}, u32[]{:S(2)}) collective-permute-start(bf16[1040,512]{1,0:T(8,128)(2,1)S(1)} %get-tuple-element.92), channel_id=1, source_target_pairs={{0,4},{1,5},{2,6},{3,7},{4,0},{5,1},{6,2},{7,3},{8,12},{9,13},{10,... | collective-permute-start | bytes 3194888 | tf_op jit(solution)/shard_map/ppermute | solution.py:644
  170.9 10.7 %collective-permute-start.22 = (bf16[256,2048]{1,0:T(8,128)(2,1)}, bf16[256,2048]{1,0:T(8,128)(2,1)S(1)}, u32[]{:S(2)}, u32[]{:S(2)}) collective-permute-start(bf16[256,2048]{1,0:T(8,128)(2,1)} %get-tuple-element.86), channel_id=1, source_target_pairs={{0,2},{1,3},{2,0},{3,1},{4,6},{5,7},{6,4},{7,5},{8,10},{9,11},{10,... | collective-permute-start | bytes 3145736 | tf_op jit(solution)/shard_map/ppermute | solution.py:644
  187.2 25.3 %collective-permute-start.26 = (bf16[528,512]{1,0:T(8,128)(2,1)S(1)}, bf16[528,512]{1,0:T(8,128)(2,1)S(1)}, u32[]{:S(2)}, u32[]{:S(2)}) collective-permute-start(bf16[528,512]{1,0:T(8,128)(2,1)S(1)} %get-tuple-element.94), channel_id=1, source_target_pairs={{0,4},{1,5},{2,6},{3,7},{4,0},{5,1},{6,2},{7,3},{8,12},{9,13},{10,... | collective-permute-start | bytes 1622024 | tf_op jit(solution)/shard_map/ppermute | solution.py:644
  187.5 25.0 %collective-permute-start.27 = (bf16[512,512]{1,0:T(8,128)(2,1)S(1)}, bf16[512,512]{1,0:T(8,128)(2,1)S(1)}, u32[]{:S(2)}, u32[]{:S(2)}) collective-permute-start(bf16[512,512]{1,0:T(8,128)(2,1)S(1)} %get-tuple-element.96), channel_id=1, source_target_pairs={{0,1},{1,0},{2,3},{3,2},{4,5},{5,4},{6,7},{7,6},{8,9},{9,8},{10,11... | collective-permute-start | bytes 1572872 | tf_op jit(solution)/shard_map/ppermute | solution.py:644
  187.6 28.2 %collective-permute-start.21 = (bf16[256,2048]{1,0:T(8,128)(2,1)S(1)}, bf16[256,2048]{1,0:T(8,128)(2,1)S(1)}, u32[]{:S(2)}, u32[]{:S(2)}) collective-permute-start(bf16[256,2048]{1,0:T(8,128)(2,1)S(1)} %copy-done.8), channel_id=1, source_target_pairs={{0,2},{1,3},{2,0},{3,1},{4,6},{5,7},{6,4},{7,5},{8,10},{9,11},{10,... | collective-permute-start | bytes 3145736 | tf_op jit(solution)/shard_map/ppermute | solution.py:644
  189.2 34.8 %collective-permute-start.23 = (bf16[256,2048]{1,0:T(8,128)(2,1)S(1)}, bf16[256,2048]{1,0:T(8,128)(2,1)S(1)}, u32[]{:S(2)}, u32[]{:S(2)}) collective-permute-start(bf16[256,2048]{1,0:T(8,128)(2,1)S(1)} %get-tuple-element.87), channel_id=1, source_target_pairs={{0,30},{1,31},{2,4},{3,5},{4,2},{5,3},{6,8},{7,9},{8,6},{9,7},{10,... | collective-permute-start | bytes 3145736 | tf_op jit(solution)/shard_map/ppermute | solution.py:655
  213.3 24.1 %collective-permute-start.28 = (bf16[256,2048]{1,0:T(8,128)(2,1)S(1)}, bf16[256,2048]{1,0:T(8,128)(2,1)S(1)}, u32[]{:S(2)}, u32[]{:S(2)}) collective-permute-start(bf16[256,2048]{1,0:T(8,128)(2,1)S(1)} %tie.9), channel_id=1, source_target_pairs={{0,1},{1,0},{2,3},{3,2},{4,5},{5,4},{6,7},{7,6},{8,9},{9,8},{10,11... | collective-permute-start | bytes 3145736 | tf_op jit(solution)/shard_map/ppermute | solution.py:644
  213.6 28.7 %collective-permute-start.29 = (bf16[144,1024]{1,0:T(8,128)(2,1)S(1)}, bf16[144,1024]{1,0:T(8,128)(2,1)S(1)}, u32[]{:S(2)}, u32[]{:S(2)}) collective-permute-start(bf16[144,1024]{1,0:T(8,128)(2,1)S(1)} %get-tuple-element.104), channel_id=1, source_target_pairs={{0,8},{1,9},{2,10},{3,11},{4,12},{5,13},{6,14},{7,15},{8,16},{9,17... | collective-permute-start | bytes 884744 | tf_op jit(solution)/shard_map/ppermute | solution.py:644
  214.5 27.8 %collective-permute-start.30 = (bf16[144,1024]{1,0:T(8,128)(2,1)S(1)}, bf16[144,1024]{1,0:T(8,128)(2,1)S(1)}, u32[]{:S(2)}, u32[]{:S(2)}) collective-permute-start(bf16[144,1024]{1,0:T(8,128)(2,1)S(1)} %get-tuple-element.105), channel_id=1, source_target_pairs={{0,16},{1,17},{2,18},{3,19},{4,20},{5,21},{6,22},{7,23},{8,24},{9,... | collective-permute-start | bytes 884744 | tf_op jit(solution)/shard_map/ppermute | solution.py:644
  215.8 26.5 %collective-permute-start.31 = (bf16[144,1024]{1,0:T(8,128)(2,1)S(1)}, bf16[144,1024]{1,0:T(8,128)(2,1)S(1)}, u32[]{:S(2)}, u32[]{:S(2)}) collective-permute-start(bf16[144,1024]{1,0:T(8,128)(2,1)S(1)} %get-tuple-element.106), channel_id=1, source_target_pairs={{0,24},{1,25},{2,26},{3,27},{4,28},{5,29},{6,30},{7,31},{8,0},{9,1... | collective-permute-start | bytes 884744 | tf_op jit(solution)/shard_map/ppermute | solution.py:644
  243.0 2.8 %collective-permute-start.32 = (f32[72,1024]{1,0:T(8,128)S(1)}, f32[72,1024]{1,0:T(8,128)S(1)}, u32[]{:S(2)}, u32[]{:S(2)}) collective-permute-start(f32[72,1024]{1,0:T(8,128)S(1)} %get-tuple-element.109), channel_id=1, source_target_pairs={{0,2},{1,3},{2,0},{3,1},{4,6},{5,7},{6,4},{7,5},{8,10},{9,11},{10,... | collective-permute-start | bytes 884744 | tf_op jit(solution)/shard_map/ppermute | solution.py:644
  (15 other events, 237.1 us)

commit v8 on v7

--- a/solution.py
+++ b/solution.py
@@ -12,7 +12,7 @@
 BOUND = 256
 CMAX = 3016
 TILE = 256
-WIDE = 512
+WIDE = 1024
 F32 = jnp.float32
 BF16 = jnp.bfloat16
 MIB = 1024 * 1024
@@ -582,7 +582,7 @@
 
 def back(outer, low, own, came, high, after):
     rows, h = own.shape
-    steps = 4
+    steps = 2
     half = steps // 2
     whole = pl.BlockSpec((rows // steps, h), lambda i: (i, 0))
     first = pl.BlockSpec((rows // steps, h), lambda i: (jnp.minimum(i, half - 1), 0))
@@ -728,8 +728,9 @@
     outer_back = swap_outer(outer_back)
     a, a_sent, b, b_sent, bias_sum = fold(at, a, a_came, b, b_came, bias_sum, share, own_back)
     a_came, b_came = swap_lo(a_sent), swap_wa(b_sent)
+    late = live // TILE * 5 // 6
     grad_features, token = grad_rows(
-        adjacency, grads, matrix, nodes, split, tiles, grad_features, [bias_sum]
+        adjacency, grads, matrix, nodes, split, late, grad_features, [bias_sum]
     )
     bias_sum, own, *rest = part_planes(
         at, a, a_came, b, b_came, bias_sum, share, n_hi, [token]
@@ -737,6 +738,7 @@
     (own_back,) = tie([own_back], [own])
     returned = (inner_came, outer_back, swap_wa(own_back))
     rest = [rotate_hi(value, k + 1) for k, value in enumerate(rest)]
+    grad_features, _ = grad_rows(adjacency, grads, matrix, nodes, late, tiles, grad_features, [bias_sum])
     grad_features, token = grad_lead(lead, returned, matrix, grad_features)
     mine, other = finish(at, bias_sum, own, rest, share, token)
     other = swap_core(other)

time: 249 us -> 247 us (level)
  Pallas kernels: 143 us -> 146 us
    ppermute x4, waiting for transfers between devices: 8.01 us -> 0.92 us  [swap_outer(): lax.ppermute(value, axes, [(b * n_wa + w, t * n_wa + w) for b, t in chose...]
    ppermute x29, waiting for transfers between devices: 54.8 us -> 59.9 us  [permute(): return lax.ppermute(value, axes, [(s, b * n_wa + w) for s, (b, w) in pairs])]
    pallas_call x2 -> x3, Pallas kernels: 32 us -> 36.4 us  [grad_rows(): pl.pallas_call(functools.partial(grad_rows_kernel, low=low, tiles=tiles),...]
  transfers between devices with their start and end apart: 33 -> 33, of which waited for: 12 -> 12; matrix products, arithmetic and copies ran while one was open for 1% -> 1% of each run, Pallas kernels for 39% -> 41%
where the time goes in v8:
time: 247 us
  Pallas kernels  146 us (59%)
  waiting for transfers between devices  60.8 us (25%)
  starting transfers between devices  29.5 us (12%)
  local copies, waits for them, and re-layouts  5.31 us (2%)
  other arithmetic  2.91 us (1%)
    ppermute x29, waiting for transfers between devices, permute(): return lax.ppermute(value, axes, [(s, b * n_wa + w) for s, (b, w) in pairs])  59.9 us
    pallas_call x3, Pallas kernels, grad_rows(): pl.pallas_call(functools.partial(grad_rows_kernel, low=low, tiles=tiles),...  36.4 us
    pallas_call x1, Pallas kernels, layer(): pl.pallas_call(functools.partial(layer_kernel, tiles=tiles, numbers=numbe...  32.9 us
    ppermute x29, starting transfers between devices, permute(): return lax.ppermute(value, axes, [(s, b * n_wa + w) for s, (b, w) in pairs])  22.7 us
    pallas_call x1, Pallas kernels, gather(): pl.pallas_call(functools.partial(gather_kernel, count=len(blocks)), grid=...  21.2 us
    pallas_call x2, Pallas kernels, weight_share(): pl.pallas_call(functools.partial(weight_kernel, mine=mine), grid_spec=plt...  16.6 us
    pallas_call x1, Pallas kernels, counts(): pl.pallas_call(counts_kernel, grid=(tiles,), in_specs=[pl.BlockSpec((FANO...  16.4 us
    pallas_call x1, Pallas kernels, scatter_bound(): pl.pallas_call(functools.partial(scatter_bound_kernel, count=blocks), gri...  9.39 us
  transfers between devices with their start and end apart: 33, of which 12 were waited for; matrix products, arithmetic and copies ran while one was open for 1% of the time, Pallas kernels for 41%

profile of v8, /device:TPU:11, one launch (start us, length us, event | category | flops | bytes accessed | tf_op | source)
XLA Modules:
  0.0 246.8 jit_solution(11486848661664787124)
XLA Ops:
  0.7 2.4 slice.30.refs_1_
  3.0 3.7 %collective-permute-start.7 = (bf16[256,2048]{1,0:T(8,128)(2,1)}, bf16[256,2048]{1,0:T(8,128)(2,1)S(1)}, u32[]{:S(2)}, u32[]{:S(2)}) collective-permute-start(bf16[256,2048]{1,0:T(8,128)(2,1)} %slice.30.refs_1_), channel_id=1, source_target_pairs={{2,4},{3,5},{4,2},{5,3},{10,12},{11,13},{12,10},{13,11},{18,20},{1... | collective-permute-start | bytes 3145736 | tf_op jit(solution)/shard_map/ppermute | solution.py:655
  8.0 2.3 collective-permute-start.2
  10.3 2.2 collective-permute-start.1
  13.8 16.4 %counts.1.refs_5_.c_ref.d_ref.cl_ref = bf16[2816,1536]{1,0:T(8,128)(2,1)} custom-call(s32[16,1536]{1,0:T(8,128)S(1)} %fusion.2.index_ref, f32[1536,1]{1,0:T(8,128)S(1)} %broadcast_in_dim.27.refs_0_.inv_ref, s32[5]{0:T(128)S(1)} %stack.23.refs_1_.at_ref), custom_call_target="tpu_custom_call" | custom-call | bytes 4325376 | tf_op jit(solution)/shard_map/counts/pallas_call | solution.py:93
  30.3 3.2 %collective-permute-done.1.refs_2_ = bf16[64,2176]{1,0:T(8,128)(2,1)S(1)} collective-permute-done((bf16[64,2176]{1,0:T(8,128)(2,1)S(1)}, bf16[64,2176]{1,0:T(8,128)(2,1)S(1)}, u32[]{:S(2)}, u32[]{:S(2)}) %collective-permute-start.1) | collective-permute-done | bytes 278560 | tf_op jit(solution)/shard_map/ppermute | solution.py:644
  38.0 1.7 collective-permute-start.8
  39.7 3.9 %collective-permute-start.9 = (bf16[256,2176]{1,0:T(8,128)(2,1)S(1)}, bf16[256,2176]{1,0:T(8,128)(2,1)S(1)}, u32[]{:S(2)}, u32[]{:S(2)}) collective-permute-start(bf16[256,2176]{1,0:T(8,128)(2,1)S(1)} %pad_maximum_fusion.refs_0_), channel_id=1, source_target_pairs={{0,4},{1,5},{2,6},{3,7},{4,0},{5,1},{6,2},{7,3},{8,12},{9,13},{10,... | collective-permute-start | bytes 3342344 | tf_op jit(solution)/shard_map/ppermute | solution.py:644
  43.6 21.2 %gather.1.refs_3_.part_ref = f32[1536,2048]{1,0:T(8,128)} custom-call(bf16[2816,1536]{1,0:T(8,128)(2,1)} %counts.1.refs_5_.c_ref.d_ref.cl_ref, bf16[1664,2048]{1,0:T(8,128)(2,1)} %t_ref.1, bf16[256,2048]{1,0:T(8,128)(2,1)} %get-tuple-element.58.refs_0_, bf16[256,2048]{1,0:T(8,128)(2,1)} %collective-permute-done.4.refs_1_, ...), custom_call_target="tpu_custom_call" | custom-call | flops 905969664 | bytes 1179648 | tf_op jit(solution)/shard_map/gather/pallas_call | solution.py:118
  65.3 1.4 collective-permute-start.11
  67.2 11.9 %collective-permute-done.9.refs_2_ = bf16[256,2176]{1,0:T(8,128)(2,1)S(1)} collective-permute-done((bf16[256,2176]{1,0:T(8,128)(2,1)S(1)}, bf16[256,2176]{1,0:T(8,128)(2,1)S(1)}, u32[]{:S(2)}, u32[]{:S(2)}) %collective-permute-start.9) | collective-permute-done | bytes 1114144 | tf_op jit(solution)/shard_map/ppermute | solution.py:644
  79.2 10.3 %collective-permute-done.10.refs_1_ = bf16[256,2048]{1,0:T(8,128)(2,1)S(1)} collective-permute-done((bf16[256,2048]{1,0:T(8,128)(2,1)S(1)}, bf16[256,2048]{1,0:T(8,128)(2,1)S(1)}, u32[]{:S(2)}, u32[]{:S(2)}) %collective-permute-start.10) | collective-permute-done | bytes 1048608 | tf_op jit(solution)/shard_map/ppermute | solution.py:644
  89.6 7.3 %collective-permute-done.11.refs_0_ = bf16[192,2176]{1,0:T(8,128)(2,1)S(1)} collective-permute-done((bf16[192,2176]{1,0:T(8,128)(2,1)S(1)}, bf16[192,2176]{1,0:T(8,128)(2,1)S(1)}, u32[]{:S(2)}, u32[]{:S(2)}) %collective-permute-start.11) | collective-permute-done | bytes 835616 | tf_op jit(solution)/shard_map/ppermute | solution.py:644
  96.8 1.8 collective-permute-start.13
  98.7 1.9 place.1.refs_4_
  101.0 32.9 %layer.1 = (f32[1664,2048]{1,0:T(8,128)}, bf16[1536,2048]{1,0:T(8,128)(2,1)S(1)}, bf16[1536,2048]{1,0:T(8,128)(2,1)S(1)}, bf16[1536,2048]{1,0:T(8,128)(2,1)S(1)}...) custom-call(s32[5]{0:T(128)S(1)} %stack.23.refs_1_.at_ref, ...), custom_call_target="tpu_custom_call", output_to_operand_aliasing={{7}: (13, {})} | custom-call | flops 1207959552 | bytes 2359296 | tf_op jit(solution)/shard_map/layer/pallas_call | solution.py:277
  134.0 8.8 %weight_share.2 = (bf16[2064,1024]{1,0:T(8,128)(2,1)}, f32[8,1024]{1,0:T(8,128)S(1)}) custom-call(s32[5]{0:T(128)S(1)} %stack.23.refs_1_.at_ref, bf16[1536,2048]{1,0:T(8,128)(2,1)S(1)} %get-tuple-element.73.m_all, bf16[1536,2048]{1,0:T(8,128)(2,1)S(1)} %get-tuple-element.74.gl_all, f32[8,2048]{1,0:T(8,128)S(1)} %get-tuple-element.75.gb), custom_call_target="tpu_custom_call" | custom-call | flops 402653184 | bytes 786432 | tf_op jit(solution)/shard_map/weight_share/pallas_call | solution.py:250
  143.3 7.7 %weight_share.3 = (bf16[2048,1024]{1,0:T(8,128)(2,1)S(1)}, f32[8,1024]{1,0:T(8,128)S(1)}) custom-call(s32[5]{0:T(128)S(1)} %stack.23.refs_1_.at_ref, bf16[1536,2048]{1,0:T(8,128)(2,1)S(1)} %get-tuple-element.73.m_all, bf16[1536,2048]{1,0:T(8,128)(2,1)S(1)} %get-tuple-element.74.gl_all, f32[8,2048]{1,0:T(8,128)S(1)} %get-tuple-element.75.gb, ...), custom_call_target="tpu_custom_call" | custom-call | flops 402653184 | bytes 786432 | tf_op jit(solution)/shard_map/weight_share/pallas_call | solution.py:250
  151.0 5.6 %collective-permute-done.19.low_ref = bf16[128,2048]{1,0:T(8,128)(2,1)S(1)} collective-permute-done((bf16[128,2048]{1,0:T(8,128)(2,1)S(1)}, bf16[128,2048]{1,0:T(8,128)(2,1)S(1)}, u32[]{:S(2)}, u32[]{:S(2)}) %collective-permute-start.19) | collective-permute-done | bytes 524320 | tf_op jit(solution)/shard_map/ppermute | solution.py:644
  157.5 2.2 share.1
  159.7 1.5 collective-permute-start.24
  161.2 9.4 %scatter_bound.1 = (bf16[256,2048]{1,0:T(8,128)(2,1)}, bf16[256,2048]{1,0:T(8,128)(2,1)}, bf16[256,2048]{1,0:T(8,128)(2,1)}, bf16[256,2048]{1,0:T(8,128)(2,1)}) custom-call(bf16[2816,1536]{1,0:T(8,128)(2,1)} %counts.1.refs_5_.c_ref.d_ref.cl_ref, bf16[1536,2048]{1,0:T(8,128)(2,1)S(1)} %get-tuple-element.71.g_ref, f32[8,1024]{1,0:T(8,128)S(1)} %get-tuple-element.82.refs_0_.gb_ref), custom_call_target="tpu_custom_call" | custom-call | flops 402653184 | bytes 786432 | tf_op jit(solution)/shard_map/scatter_bound/pallas_call | solution.py:509
  171.1 10.1 %grad_rows.3 = (f32[1664,2048]{1,0:T(8,128)}, f32[256,2048]{1,0:T(8,128)S(1)}) custom-call(bf16[2816,1536]{1,0:T(8,128)(2,1)} %counts.1.refs_5_.c_ref.d_ref.cl_ref, bf16[1536,2048]{1,0:T(8,128)(2,1)S(1)} %get-tuple-element.71.g_ref, bf16[2048,2176]{1,0:T(8,128)(2,1)} %copy-done, bf16[256,2048]{1,0:T(8,128)(2,1)} %get-tuple-element.83.refs_1_.own_ref), custom_call_target="tpu_custom_call" | custom-call | flops 469762048 | bytes 1572864 | tf_op jit(solution)/shard_map/grad_rows/pallas_call | solution.py:555
  181.2 2.0 back.1
  183.2 1.6 collective-permute-done.24.a_came
  187.2 1.6 collective-permute-start.21
  190.2 16.7 %grad_rows.4 = (f32[1664,2048]{1,0:T(8,128)}, f32[8,128]{1,0:T(8,128)S(1)}) custom-call(bf16[2816,1536]{1,0:T(8,128)(2,1)} %counts.1.refs_5_.c_ref.d_ref.cl_ref, bf16[1536,2048]{1,0:T(8,128)(2,1)S(1)} %get-tuple-element.71.g_ref, bf16[2048,2176]{1,0:T(8,128)(2,1)} %copy-done, ...), custom_call_target="tpu_custom_call", output_to_operand_aliasing={{0}: (3, {})} | custom-call | flops 704643072 | bytes 1572864 | tf_op jit(solution)/shard_map/grad_rows/pallas_call | solution.py:555
  206.9 5.0 %collective-permute-done.26.a_came = bf16[528,512]{1,0:T(8,128)(2,1)S(1)} collective-permute-done((bf16[528,512]{1,0:T(8,128)(2,1)S(1)}, bf16[528,512]{1,0:T(8,128)(2,1)S(1)}, u32[]{:S(2)}, u32[]{:S(2)}) %collective-permute-start.26) | collective-permute-done | bytes 540704 | tf_op jit(solution)/shard_map/ppermute | solution.py:644
  214.2 9.7 %grad_rows.5 = (f32[1664,2048]{1,0:T(8,128)}, f32[8,128]{1,0:T(8,128)}) custom-call(bf16[2816,1536]{1,0:T(8,128)(2,1)} %counts.1.refs_5_.c_ref.d_ref.cl_ref, bf16[1536,2048]{1,0:T(8,128)(2,1)S(1)} %get-tuple-element.71.g_ref, bf16[2048,2176]{1,0:T(8,128)(2,1)} %copy-done, f32[1664,2048]{1,0:T(8,128)} %get-tuple-element.102.refs_1_, ...), custom_call_target="tpu_custom_call", output_to_operand_aliasing={{0}: (3, {})} | custom-call | flops 469762048 | bytes 1572864 | tf_op jit(solution)/shard_map/grad_rows/pallas_call | solution.py:555
  224.0 12.5 %collective-permute-done.28.refs_2_ = bf16[256,2048]{1,0:T(8,128)(2,1)S(1)} collective-permute-done((bf16[256,2048]{1,0:T(8,128)(2,1)S(1)}, bf16[256,2048]{1,0:T(8,128)(2,1)S(1)}, u32[]{:S(2)}, u32[]{:S(2)}) %collective-permute-start.28) | collective-permute-done | bytes 1048608 | tf_op jit(solution)/shard_map/ppermute | solution.py:644
  236.4 4.9 %grad_lead.1 = (f32[1664,2048]{1,0:T(8,128)}, f32[8,128]{1,0:T(8,128)S(1)}) custom-call(f32[256,2048]{1,0:T(8,128)S(1)} %get-tuple-element.84._.lead_ref, bf16[256,2048]{1,0:T(8,128)(2,1)S(1)} %collective-permute-done.21.refs_0_, bf16[256,2048]{1,0:T(8,128)(2,1)S(1)} %collective-permute-done.23.refs_1_, ...), custom_call_target="tpu_custom_call", output_to_operand_aliasing={{0}: (5, {})} | custom-call | flops 134217728 | bytes 524288 | tf_op jit(solution)/shard_map/grad_lead/pallas_call | solution.py:618
  242.1 1.9 collective-permute-start.32
  (102 shorter events, 19.5 us)
Async XLA Ops:
  3.0 30.5 %collective-permute-start.7 = (bf16[256,2048]{1,0:T(8,128)(2,1)}, bf16[256,2048]{1,0:T(8,128)(2,1)S(1)}, u32[]{:S(2)}, u32[]{:S(2)}) collective-permute-start(bf16[256,2048]{1,0:T(8,128)(2,1)} %slice.30.refs_1_), channel_id=1, source_target_pairs={{2,4},{3,5},{4,2},{5,3},{10,12},{11,13},{12,10},{13,11},{18,20},{1... | collective-permute-start | bytes 3145736 | tf_op jit(solution)/shard_map/ppermute | solution.py:655
  6.7 26.8 %collective-permute-start = (bf16[256,2048]{1,0:T(8,128)(2,1)}, bf16[256,2048]{1,0:T(8,128)(2,1)}, u32[]{:S(2)}, u32[]{:S(2)}) collective-permute-start(bf16[256,2048]{1,0:T(8,128)(2,1)} %slice.30.refs_1_), channel_id=1, source_target_pairs={{0,1},{1,0},{2,3},{3,2},{4,5},{5,4},{6,7},{7,6},{8,9},{9,8},{10,11... | collective-permute-start | bytes 3145736 | tf_op jit(solution)/shard_map/ppermute | solution.py:644
  7.8 22.5 %collective-permute-start.3 = (bf16[64,2176]{1,0:T(8,128)(2,1)S(1)}, bf16[64,2176]{1,0:T(8,128)(2,1)S(1)}, u32[]{:S(2)}, u32[]{:S(2)}) collective-permute-start(bf16[64,2176]{1,0:T(8,128)(2,1)S(1)} %pad_maximum_fusion.2), channel_id=1, source_target_pairs={{0,24},{1,25},{2,26},{3,27},{4,28},{5,29},{6,30},{7,31},{8,0},{9,1... | collective-permute-start | bytes 835592 | tf_op jit(solution)/shard_map/ppermute | solution.py:644
  8.0 22.3 %collective-permute-start.2 = (bf16[64,2176]{1,0:T(8,128)(2,1)S(1)}, bf16[64,2176]{1,0:T(8,128)(2,1)S(1)}, u32[]{:S(2)}, u32[]{:S(2)}) collective-permute-start(bf16[64,2176]{1,0:T(8,128)(2,1)S(1)} %pad_maximum_fusion.2), channel_id=1, source_target_pairs={{0,16},{1,17},{2,18},{3,19},{4,20},{5,21},{6,22},{7,23},{8,24},{9,... | collective-permute-start | bytes 835592 | tf_op jit(solution)/shard_map/ppermute | solution.py:644
  10.3 23.1 %collective-permute-start.1 = (bf16[64,2176]{1,0:T(8,128)(2,1)S(1)}, bf16[64,2176]{1,0:T(8,128)(2,1)S(1)}, u32[]{:S(2)}, u32[]{:S(2)}) collective-permute-start(bf16[64,2176]{1,0:T(8,128)(2,1)S(1)} %pad_maximum_fusion.2), channel_id=1, source_target_pairs={{0,8},{1,9},{2,10},{3,11},{4,12},{5,13},{6,14},{7,15},{8,16},{9,17... | collective-permute-start | bytes 835592 | tf_op jit(solution)/shard_map/ppermute | solution.py:644
  35.2 8.4 %collective-permute-start.5 = (bf16[256,2048]{1,0:T(8,128)(2,1)}, bf16[256,2048]{1,0:T(8,128)(2,1)}, u32[]{:S(2)}, u32[]{:S(2)}) collective-permute-start(bf16[256,2048]{1,0:T(8,128)(2,1)} %get-tuple-element.58.refs_0_), channel_id=1, source_target_pairs={{0,2},{1,3},{2,0},{3,1},{4,6},{5,7},{6,4},{7,5},{8,10},{9,11},{10,... | collective-permute-start | bytes 3145736 | tf_op jit(solution)/shard_map/ppermute | solution.py:644
  35.2 8.4 %collective-permute-start.4 = (bf16[256,2048]{1,0:T(8,128)(2,1)}, bf16[256,2048]{1,0:T(8,128)(2,1)}, u32[]{:S(2)}, u32[]{:S(2)}) collective-permute-start(bf16[256,2048]{1,0:T(8,128)(2,1)} %get-tuple-element.59), channel_id=1, source_target_pairs={{0,2},{1,3},{2,0},{3,1},{4,6},{5,7},{6,4},{7,5},{8,10},{9,11},{10,... | collective-permute-start | bytes 3145736 | tf_op jit(solution)/shard_map/ppermute | solution.py:644
  36.8 28.0 %collective-permute-start.6 = (bf16[256,2176]{1,0:T(8,128)(2,1)S(1)}, bf16[256,2176]{1,0:T(8,128)(2,1)S(1)}, u32[]{:S(2)}, u32[]{:S(2)}) collective-permute-start(bf16[256,2176]{1,0:T(8,128)(2,1)S(1)} %pad_maximum_fusion.refs_0_), channel_id=1, source_target_pairs={{0,1},{1,0},{2,3},{3,2},{4,5},{5,4},{6,7},{7,6},{8,9},{9,8},{10,11... | collective-permute-start | bytes 3342344 | tf_op jit(solution)/shard_map/ppermute | solution.py:644
  38.0 26.7 %collective-permute-start.8 = (bf16[256,2048]{1,0:T(8,128)(2,1)}, bf16[256,2048]{1,0:T(8,128)(2,1)}, u32[]{:S(2)}, u32[]{:S(2)}) collective-permute-start(bf16[256,2048]{1,0:T(8,128)(2,1)} %get-tuple-element.59), channel_id=1, source_target_pairs={{0,30},{1,31},{6,8},{7,9},{8,6},{9,7},{14,16},{15,17},{16,14},{17,... | collective-permute-start | bytes 3145736 | tf_op jit(solution)/shard_map/ppermute | solution.py:655
  39.7 39.4 %collective-permute-start.9 = (bf16[256,2176]{1,0:T(8,128)(2,1)S(1)}, bf16[256,2176]{1,0:T(8,128)(2,1)S(1)}, u32[]{:S(2)}, u32[]{:S(2)}) collective-permute-start(bf16[256,2176]{1,0:T(8,128)(2,1)S(1)} %pad_maximum_fusion.refs_0_), channel_id=1, source_target_pairs={{0,4},{1,5},{2,6},{3,7},{4,0},{5,1},{6,2},{7,3},{8,12},{9,13},{10,... | collective-permute-start | bytes 3342344 | tf_op jit(solution)/shard_map/ppermute | solution.py:644
  64.9 24.6 %collective-permute-start.10 = (bf16[256,2048]{1,0:T(8,128)(2,1)S(1)}, bf16[256,2048]{1,0:T(8,128)(2,1)S(1)}, u32[]{:S(2)}, u32[]{:S(2)}) collective-permute-start(bf16[256,2048]{1,0:T(8,128)(2,1)S(1)} %broadcast_select_fusion.same_ref), channel_id=1, source_target_pairs={{0,1},{1,0},{2,3},{3,2},{4,5},{5,4},{6,7},{7,6},{8,9},{9,8},{10,11... | collective-permute-start | bytes 3145736 | tf_op jit(solution)/shard_map/ppermute | solution.py:644
  65.3 31.5 %collective-permute-start.11 = (bf16[192,2176]{1,0:T(8,128)(2,1)S(1)}, bf16[192,2176]{1,0:T(8,128)(2,1)S(1)}, u32[]{:S(2)}, u32[]{:S(2)}) collective-permute-start(bf16[192,2176]{1,0:T(8,128)(2,1)S(1)} %slice.32), channel_id=1, source_target_pairs={{0,4},{1,5},{2,6},{3,7},{4,0},{5,1},{6,2},{7,3},{8,12},{9,13},{10,... | collective-permute-start | bytes 2506760 | tf_op jit(solution)/shard_map/ppermute | solution.py:644
  66.7 31.9 %collective-permute-start.15 = (bf16[256,2176]{1,0:T(8,128)(2,1)S(1)}, bf16[256,2176]{1,0:T(8,128)(2,1)S(1)}, u32[]{:S(2)}, u32[]{:S(2)}) collective-permute-start(bf16[256,2176]{1,0:T(8,128)(2,1)S(1)} %pad_maximum_fusion.refs_0_), channel_id=1, source_target_pairs={{0,2},{1,3},{2,0},{3,1},{4,6},{5,7},{6,4},{7,5},{8,10},{9,11},{10,... | collective-permute-start | bytes 3342344 | tf_op jit(solution)/shard_map/ppermute | solution.py:644
  66.9 31.7 %collective-permute-start.16 = (bf16[256,2176]{1,0:T(8,128)(2,1)S(1)}, bf16[256,2176]{1,0:T(8,128)(2,1)S(1)}, u32[]{:S(2)}, u32[]{:S(2)}) collective-permute-start(bf16[256,2176]{1,0:T(8,128)(2,1)S(1)} %get-tuple-element.66.refs_1_), channel_id=1, source_target_pairs={{0,2},{1,3},{2,0},{3,1},{4,6},{5,7},{6,4},{7,5},{8,10},{9,11},{10,... | collective-permute-start | bytes 3342344 | tf_op jit(solution)/shard_map/ppermute | solution.py:644
  79.1 19.5 %collective-permute-start.17 = (bf16[256,2176]{1,0:T(8,128)(2,1)S(1)}, bf16[256,2176]{1,0:T(8,128)(2,1)S(1)}, u32[]{:S(2)}, u32[]{:S(2)}) collective-permute-start(bf16[256,2176]{1,0:T(8,128)(2,1)S(1)} %collective-permute-done.9.refs_2_), channel_id=1, source_target_pairs={{0,2},{1,3},{2,0},{3,1},{4,6},{5,7},{6,4},{7,5},{8,10},{9,11},{10,... | collective-permute-start | bytes 3342344 | tf_op jit(solution)/shard_map/ppermute | solution.py:644
  89.6 7.3 %collective-permute-start.12 = (bf16[64,2176]{1,0:T(8,128)(2,1)S(1)}, bf16[64,2176]{1,0:T(8,128)(2,1)S(1)}, u32[]{:S(2)}, u32[]{:S(2)}) collective-permute-start(bf16[64,2176]{1,0:T(8,128)(2,1)S(1)} %get-tuple-element.67), channel_id=1, source_target_pairs={{0,1},{1,0},{2,3},{3,2},{4,5},{5,4},{6,7},{7,6},{8,9},{9,8},{10,11... | collective-permute-start | bytes 835592 | tf_op jit(solution)/shard_map/ppermute | solution.py:644
  96.8 4.2 %collective-permute-start.13 = (bf16[192,2176]{1,0:T(8,128)(2,1)S(1)}, bf16[192,2176]{1,0:T(8,128)(2,1)S(1)}, u32[]{:S(2)}, u32[]{:S(2)}) collective-permute-start(bf16[192,2176]{1,0:T(8,128)(2,1)S(1)} %get-tuple-element.68.refs_0_), channel_id=1, source_target_pairs={{0,2},{1,3},{2,0},{3,1},{4,6},{5,7},{6,4},{7,5},{8,10},{9,11},{10,... | collective-permute-start | bytes 2506760 | tf_op jit(solution)/shard_map/ppermute | solution.py:644
  142.8 14.7 %collective-permute-start.18 = (bf16[2064,1024]{1,0:T(8,128)(2,1)}, bf16[2064,1024]{1,0:T(8,128)(2,1)S(1)}, u32[]{:S(2)}, u32[]{:S(2)}) collective-permute-start(bf16[2064,1024]{1,0:T(8,128)(2,1)} %get-tuple-element.78), channel_id=1, source_target_pairs={{0,2},{1,3},{2,0},{3,1},{4,6},{5,7},{6,4},{7,5},{8,10},{9,11},{10,... | collective-permute-start | bytes 12681224 | tf_op jit(solution)/shard_map/ppermute | solution.py:644
  143.2 13.4 %collective-permute-start.19 = (bf16[128,2048]{1,0:T(8,128)(2,1)S(1)}, bf16[128,2048]{1,0:T(8,128)(2,1)S(1)}, u32[]{:S(2)}, u32[]{:S(2)}) collective-permute-start(bf16[128,2048]{1,0:T(8,128)(2,1)S(1)} %copy-done.10), channel_id=1, source_target_pairs={{0,1},{1,0},{2,3},{3,2},{4,5},{5,4},{6,7},{7,6},{8,9},{9,8},{10,11... | collective-permute-start | bytes 1572872 | tf_op jit(solution)/shard_map/ppermute | solution.py:644
  143.2 14.3 %collective-permute-start.20 = (bf16[128,2048]{1,0:T(8,128)(2,1)S(1)}, bf16[128,2048]{1,0:T(8,128)(2,1)S(1)}, u32[]{:S(2)}, u32[]{:S(2)}) collective-permute-start(bf16[128,2048]{1,0:T(8,128)(2,1)S(1)} %copy-done.9), channel_id=1, source_target_pairs={{0,30},{1,31},{2,4},{3,5},{4,2},{5,3},{6,8},{7,9},{8,6},{9,7},{10,... | collective-permute-start | bytes 1572872 | tf_op jit(solution)/shard_map/ppermute | solution.py:655
  159.7 25.2 %collective-permute-start.24 = (bf16[1040,512]{1,0:T(8,128)(2,1)S(1)}, bf16[1040,512]{1,0:T(8,128)(2,1)S(1)}, u32[]{:S(2)}, u32[]{:S(2)}) collective-permute-start(bf16[1040,512]{1,0:T(8,128)(2,1)S(1)} %get-tuple-element.91), channel_id=1, source_target_pairs={{0,1},{1,0},{2,3},{3,2},{4,5},{5,4},{6,7},{7,6},{8,9},{9,8},{10,11... | collective-permute-start | bytes 3194888 | tf_op jit(solution)/shard_map/ppermute | solution.py:644
  161.1 24.6 %collective-permute-start.25 = (bf16[1040,512]{1,0:T(8,128)(2,1)S(1)}, bf16[1040,512]{1,0:T(8,128)(2,1)S(1)}, u32[]{:S(2)}, u32[]{:S(2)}) collective-permute-start(bf16[1040,512]{1,0:T(8,128)(2,1)S(1)} %get-tuple-element.93), channel_id=1, source_target_pairs={{0,4},{1,5},{2,6},{3,7},{4,0},{5,1},{6,2},{7,3},{8,12},{9,13},{10,... | collective-permute-start | bytes 3194888 | tf_op jit(solution)/shard_map/ppermute | solution.py:644
  170.5 10.6 %collective-permute-start.22 = (bf16[256,2048]{1,0:T(8,128)(2,1)}, bf16[256,2048]{1,0:T(8,128)(2,1)S(1)}, u32[]{:S(2)}, u32[]{:S(2)}) collective-permute-start(bf16[256,2048]{1,0:T(8,128)(2,1)} %get-tuple-element.87), channel_id=1, source_target_pairs={{0,2},{1,3},{2,0},{3,1},{4,6},{5,7},{6,4},{7,5},{8,10},{9,11},{10,... | collective-permute-start | bytes 3145736 | tf_op jit(solution)/shard_map/ppermute | solution.py:644
  186.9 25.0 %collective-permute-start.26 = (bf16[528,512]{1,0:T(8,128)(2,1)S(1)}, bf16[528,512]{1,0:T(8,128)(2,1)S(1)}, u32[]{:S(2)}, u32[]{:S(2)}) collective-permute-start(bf16[528,512]{1,0:T(8,128)(2,1)S(1)} %get-tuple-element.95), channel_id=1, source_target_pairs={{0,4},{1,5},{2,6},{3,7},{4,0},{5,1},{6,2},{7,3},{8,12},{9,13},{10,... | collective-permute-start | bytes 1622024 | tf_op jit(solution)/shard_map/ppermute | solution.py:644
  187.2 19.7 %collective-permute-start.27 = (bf16[512,512]{1,0:T(8,128)(2,1)S(1)}, bf16[512,512]{1,0:T(8,128)(2,1)S(1)}, u32[]{:S(2)}, u32[]{:S(2)}) collective-permute-start(bf16[512,512]{1,0:T(8,128)(2,1)S(1)} %get-tuple-element.97), channel_id=1, source_target_pairs={{0,1},{1,0},{2,3},{3,2},{4,5},{5,4},{6,7},{7,6},{8,9},{9,8},{10,11... | collective-permute-start | bytes 1572872 | tf_op jit(solution)/shard_map/ppermute | solution.py:644
  187.2 26.6 %collective-permute-start.21 = (bf16[256,2048]{1,0:T(8,128)(2,1)S(1)}, bf16[256,2048]{1,0:T(8,128)(2,1)S(1)}, u32[]{:S(2)}, u32[]{:S(2)}) collective-permute-start(bf16[256,2048]{1,0:T(8,128)(2,1)S(1)} %copy-done.8), channel_id=1, source_target_pairs={{0,2},{1,3},{2,0},{3,1},{4,6},{5,7},{6,4},{7,5},{8,10},{9,11},{10,... | collective-permute-start | bytes 3145736 | tf_op jit(solution)/shard_map/ppermute | solution.py:644
  188.9 35.1 %collective-permute-start.23 = (bf16[256,2048]{1,0:T(8,128)(2,1)S(1)}, bf16[256,2048]{1,0:T(8,128)(2,1)S(1)}, u32[]{:S(2)}, u32[]{:S(2)}) collective-permute-start(bf16[256,2048]{1,0:T(8,128)(2,1)S(1)} %get-tuple-element.88), channel_id=1, source_target_pairs={{0,30},{1,31},{2,4},{3,5},{4,2},{5,3},{6,8},{7,9},{8,6},{9,7},{10,... | collective-permute-start | bytes 3145736 | tf_op jit(solution)/shard_map/ppermute | solution.py:655
  212.6 23.8 %collective-permute-start.28 = (bf16[256,2048]{1,0:T(8,128)(2,1)S(1)}, bf16[256,2048]{1,0:T(8,128)(2,1)S(1)}, u32[]{:S(2)}, u32[]{:S(2)}) collective-permute-start(bf16[256,2048]{1,0:T(8,128)(2,1)S(1)} %tie.9), channel_id=1, source_target_pairs={{0,1},{1,0},{2,3},{3,2},{4,5},{5,4},{6,7},{7,6},{8,9},{9,8},{10,11... | collective-permute-start | bytes 3145736 | tf_op jit(solution)/shard_map/ppermute | solution.py:644
  212.7 28.6 %collective-permute-start.29 = (bf16[144,1024]{1,0:T(8,128)(2,1)S(1)}, bf16[144,1024]{1,0:T(8,128)(2,1)S(1)}, u32[]{:S(2)}, u32[]{:S(2)}) collective-permute-start(bf16[144,1024]{1,0:T(8,128)(2,1)S(1)} %get-tuple-element.106), channel_id=1, source_target_pairs={{0,8},{1,9},{2,10},{3,11},{4,12},{5,13},{6,14},{7,15},{8,16},{9,17... | collective-permute-start | bytes 884744 | tf_op jit(solution)/shard_map/ppermute | solution.py:644
  212.8 28.6 %collective-permute-start.30 = (bf16[144,1024]{1,0:T(8,128)(2,1)S(1)}, bf16[144,1024]{1,0:T(8,128)(2,1)S(1)}, u32[]{:S(2)}, u32[]{:S(2)}) collective-permute-start(bf16[144,1024]{1,0:T(8,128)(2,1)S(1)} %get-tuple-element.107), channel_id=1, source_target_pairs={{0,16},{1,17},{2,18},{3,19},{4,20},{5,21},{6,22},{7,23},{8,24},{9,... | collective-permute-start | bytes 884744 | tf_op jit(solution)/shard_map/ppermute | solution.py:644
  213.8 27.5 %collective-permute-start.31 = (bf16[144,1024]{1,0:T(8,128)(2,1)S(1)}, bf16[144,1024]{1,0:T(8,128)(2,1)S(1)}, u32[]{:S(2)}, u32[]{:S(2)}) collective-permute-start(bf16[144,1024]{1,0:T(8,128)(2,1)S(1)} %get-tuple-element.108), channel_id=1, source_target_pairs={{0,24},{1,25},{2,26},{3,27},{4,28},{5,29},{6,30},{7,31},{8,0},{9,1... | collective-permute-start | bytes 884744 | tf_op jit(solution)/shard_map/ppermute | solution.py:644
  242.1 3.1 %collective-permute-start.32 = (f32[72,1024]{1,0:T(8,128)S(1)}, f32[72,1024]{1,0:T(8,128)S(1)}, u32[]{:S(2)}, u32[]{:S(2)}) collective-permute-start(f32[72,1024]{1,0:T(8,128)S(1)} %get-tuple-element.111), channel_id=1, source_target_pairs={{0,2},{1,3},{2,0},{3,1},{4,6},{5,7},{6,4},{7,5},{8,10},{9,11},{10,... | collective-permute-start | bytes 884744 | tf_op jit(solution)/shard_map/ppermute | solution.py:644
  (15 other events, 162.6 us)

commit v9 on v8

--- a/solution.py
+++ b/solution.py
@@ -617,9 +617,9 @@
     rows, h = lead.shape
     return pl.pallas_call(
         grad_lead_kernel,
-        grid=(4,),
-        in_specs=[resident((rows, h))] * 4 + [pl.BlockSpec((h // 4, h), lambda i: (i, 0)), ANY],
-        out_specs=[pl.BlockSpec((rows, h // 4), lambda i: (0, i)), resident((8, 128))],
+        grid=(1,),
+        in_specs=[resident((rows, h))] * 4 + [pl.BlockSpec((h, h), lambda i: (i, 0)), ANY],
+        out_specs=[pl.BlockSpec((rows, h), lambda i: (0, i)), resident((8, 128))],
         out_shape=[jax.ShapeDtypeStruct(grads.shape, F32), TOKEN],
         scratch_shapes=[pltpu.VMEM((rows, h), BF16)],
         input_output_aliases={5: 0},

time: 247 us -> 246 us (level)
  transfers between devices with their start and end apart: 33 -> 33, of which waited for: 12 -> 13; matrix products, arithmetic and copies ran while one was open for 1% -> 1% of each run, Pallas kernels for 41% -> 41%
where the time goes in v9:
time: 246 us
  Pallas kernels  145 us (59%)
  waiting for transfers between devices  60.9 us (25%)
  starting transfers between devices  29.5 us (12%)
  local copies, waits for them, and re-layouts  5.31 us (2%)
  other arithmetic  2.91 us (1%)
    ppermute x29, waiting for transfers between devices, permute(): return lax.ppermute(value, axes, [(s, b * n_wa + w) for s, (b, w) in pairs])  60 us
    pallas_call x3, Pallas kernels, grad_rows(): pl.pallas_call(functools.partial(grad_rows_kernel, low=low, tiles=tiles),...  36.4 us
    pallas_call x1, Pallas kernels, layer(): pl.pallas_call(functools.partial(layer_kernel, tiles=tiles, numbers=numbe...  32.9 us
    ppermute x29, starting transfers between devices, permute(): return lax.ppermute(value, axes, [(s, b * n_wa + w) for s, (b, w) in pairs])  22.7 us
    pallas_call x1, Pallas kernels, gather(): pl.pallas_call(functools.partial(gather_kernel, count=len(blocks)), grid=...  21.2 us
    pallas_call x2, Pallas kernels, weight_share(): pl.pallas_call(functools.partial(weight_kernel, mine=mine), grid_spec=plt...  16.6 us
    pallas_call x1, Pallas kernels, counts(): pl.pallas_call(counts_kernel, grid=(tiles,), in_specs=[pl.BlockSpec((FANO...  16.4 us
    pallas_call x1, Pallas kernels, scatter_bound(): pl.pallas_call(functools.partial(scatter_bound_kernel, count=blocks), gri...  9.39 us
  transfers between devices with their start and end apart: 33, of which 13 were waited for; matrix products, arithmetic and copies ran while one was open for 1% of the time, Pallas kernels for 41%

profile of v9, /device:TPU:11, one launch (start us, length us, event | category | flops | bytes accessed | tf_op | source)
XLA Modules:
  0.0 245.6 jit_solution(6981993726004211720)
XLA Ops:
  0.7 2.4 slice.30.refs_1_
  3.0 3.7 %collective-permute-start.7 = (bf16[256,2048]{1,0:T(8,128)(2,1)}, bf16[256,2048]{1,0:T(8,128)(2,1)S(1)}, u32[]{:S(2)}, u32[]{:S(2)}) collective-permute-start(bf16[256,2048]{1,0:T(8,128)(2,1)} %slice.30.refs_1_), channel_id=1, source_target_pairs={{2,4},{3,5},{4,2},{5,3},{10,12},{11,13},{12,10},{13,11},{18,20},{1... | collective-permute-start | bytes 3145736 | tf_op jit(solution)/shard_map/ppermute | solution.py:655
  8.0 2.3 collective-permute-start.2
  10.3 2.2 collective-permute-start.1
  13.8 16.4 %counts.1.refs_5_.c_ref.d_ref.cl_ref = bf16[2816,1536]{1,0:T(8,128)(2,1)} custom-call(s32[16,1536]{1,0:T(8,128)S(1)} %fusion.2.index_ref, f32[1536,1]{1,0:T(8,128)S(1)} %broadcast_in_dim.27.refs_0_.inv_ref, s32[5]{0:T(128)S(1)} %stack.23.refs_1_.at_ref), custom_call_target="tpu_custom_call" | custom-call | bytes 4325376 | tf_op jit(solution)/shard_map/counts/pallas_call | solution.py:93
  30.3 3.2 %collective-permute-done.1.refs_2_ = bf16[64,2176]{1,0:T(8,128)(2,1)S(1)} collective-permute-done((bf16[64,2176]{1,0:T(8,128)(2,1)S(1)}, bf16[64,2176]{1,0:T(8,128)(2,1)S(1)}, u32[]{:S(2)}, u32[]{:S(2)}) %collective-permute-start.1) | collective-permute-done | bytes 278560 | tf_op jit(solution)/shard_map/ppermute | solution.py:644
  38.0 1.7 collective-permute-start.8
  39.7 3.9 %collective-permute-start.9 = (bf16[256,2176]{1,0:T(8,128)(2,1)S(1)}, bf16[256,2176]{1,0:T(8,128)(2,1)S(1)}, u32[]{:S(2)}, u32[]{:S(2)}) collective-permute-start(bf16[256,2176]{1,0:T(8,128)(2,1)S(1)} %pad_maximum_fusion.refs_0_), channel_id=1, source_target_pairs={{0,4},{1,5},{2,6},{3,7},{4,0},{5,1},{6,2},{7,3},{8,12},{9,13},{10,... | collective-permute-start | bytes 3342344 | tf_op jit(solution)/shard_map/ppermute | solution.py:644
  43.6 21.2 %gather.1.refs_3_.part_ref = f32[1536,2048]{1,0:T(8,128)} custom-call(bf16[2816,1536]{1,0:T(8,128)(2,1)} %counts.1.refs_5_.c_ref.d_ref.cl_ref, bf16[1664,2048]{1,0:T(8,128)(2,1)} %t_ref.1, bf16[256,2048]{1,0:T(8,128)(2,1)} %get-tuple-element.58.refs_0_, bf16[256,2048]{1,0:T(8,128)(2,1)} %collective-permute-done.4.refs_1_, ...), custom_call_target="tpu_custom_call" | custom-call | flops 905969664 | bytes 1179648 | tf_op jit(solution)/shard_map/gather/pallas_call | solution.py:118
  65.3 1.4 collective-permute-start.11
  67.2 11.9 %collective-permute-done.9.refs_2_ = bf16[256,2176]{1,0:T(8,128)(2,1)S(1)} collective-permute-done((bf16[256,2176]{1,0:T(8,128)(2,1)S(1)}, bf16[256,2176]{1,0:T(8,128)(2,1)S(1)}, u32[]{:S(2)}, u32[]{:S(2)}) %collective-permute-start.9) | collective-permute-done | bytes 1114144 | tf_op jit(solution)/shard_map/ppermute | solution.py:644
  79.2 10.3 %collective-permute-done.10.refs_1_ = bf16[256,2048]{1,0:T(8,128)(2,1)S(1)} collective-permute-done((bf16[256,2048]{1,0:T(8,128)(2,1)S(1)}, bf16[256,2048]{1,0:T(8,128)(2,1)S(1)}, u32[]{:S(2)}, u32[]{:S(2)}) %collective-permute-start.10) | collective-permute-done | bytes 1048608 | tf_op jit(solution)/shard_map/ppermute | solution.py:644
  89.6 7.3 %collective-permute-done.11.refs_0_ = bf16[192,2176]{1,0:T(8,128)(2,1)S(1)} collective-permute-done((bf16[192,2176]{1,0:T(8,128)(2,1)S(1)}, bf16[192,2176]{1,0:T(8,128)(2,1)S(1)}, u32[]{:S(2)}, u32[]{:S(2)}) %collective-permute-start.11) | collective-permute-done | bytes 835616 | tf_op jit(solution)/shard_map/ppermute | solution.py:644
  96.8 1.8 collective-permute-start.13
  98.7 1.9 place.1.refs_4_
  101.0 32.9 %layer.1 = (f32[1664,2048]{1,0:T(8,128)}, bf16[1536,2048]{1,0:T(8,128)(2,1)S(1)}, bf16[1536,2048]{1,0:T(8,128)(2,1)S(1)}, bf16[1536,2048]{1,0:T(8,128)(2,1)S(1)}...) custom-call(s32[5]{0:T(128)S(1)} %stack.23.refs_1_.at_ref, ...), custom_call_target="tpu_custom_call", output_to_operand_aliasing={{7}: (13, {})} | custom-call | flops 1207959552 | bytes 2359296 | tf_op jit(solution)/shard_map/layer/pallas_call | solution.py:277
  134.0 8.8 %weight_share.2 = (bf16[2064,1024]{1,0:T(8,128)(2,1)}, f32[8,1024]{1,0:T(8,128)S(1)}) custom-call(s32[5]{0:T(128)S(1)} %stack.23.refs_1_.at_ref, bf16[1536,2048]{1,0:T(8,128)(2,1)S(1)} %get-tuple-element.73.m_all, bf16[1536,2048]{1,0:T(8,128)(2,1)S(1)} %get-tuple-element.74.gl_all, f32[8,2048]{1,0:T(8,128)S(1)} %get-tuple-element.75.gb), custom_call_target="tpu_custom_call" | custom-call | flops 402653184 | bytes 786432 | tf_op jit(solution)/shard_map/weight_share/pallas_call | solution.py:250
  143.3 7.7 %weight_share.3 = (bf16[2048,1024]{1,0:T(8,128)(2,1)S(1)}, f32[8,1024]{1,0:T(8,128)S(1)}) custom-call(s32[5]{0:T(128)S(1)} %stack.23.refs_1_.at_ref, bf16[1536,2048]{1,0:T(8,128)(2,1)S(1)} %get-tuple-element.73.m_all, bf16[1536,2048]{1,0:T(8,128)(2,1)S(1)} %get-tuple-element.74.gl_all, f32[8,2048]{1,0:T(8,128)S(1)} %get-tuple-element.75.gb, ...), custom_call_target="tpu_custom_call" | custom-call | flops 402653184 | bytes 786432 | tf_op jit(solution)/shard_map/weight_share/pallas_call | solution.py:250
  151.0 5.6 %collective-permute-done.19.low_ref = bf16[128,2048]{1,0:T(8,128)(2,1)S(1)} collective-permute-done((bf16[128,2048]{1,0:T(8,128)(2,1)S(1)}, bf16[128,2048]{1,0:T(8,128)(2,1)S(1)}, u32[]{:S(2)}, u32[]{:S(2)}) %collective-permute-start.19) | collective-permute-done | bytes 524320 | tf_op jit(solution)/shard_map/ppermute | solution.py:644
  157.5 2.2 share.1
  159.7 1.5 collective-permute-start.24
  161.2 9.4 %scatter_bound.1 = (bf16[256,2048]{1,0:T(8,128)(2,1)}, bf16[256,2048]{1,0:T(8,128)(2,1)}, bf16[256,2048]{1,0:T(8,128)(2,1)}, bf16[256,2048]{1,0:T(8,128)(2,1)}) custom-call(bf16[2816,1536]{1,0:T(8,128)(2,1)} %counts.1.refs_5_.c_ref.d_ref.cl_ref, bf16[1536,2048]{1,0:T(8,128)(2,1)S(1)} %get-tuple-element.71.g_ref, f32[8,1024]{1,0:T(8,128)S(1)} %get-tuple-element.82.refs_0_.gb_ref), custom_call_target="tpu_custom_call" | custom-call | flops 402653184 | bytes 786432 | tf_op jit(solution)/shard_map/scatter_bound/pallas_call | solution.py:509
  171.1 10.1 %grad_rows.3 = (f32[1664,2048]{1,0:T(8,128)}, f32[256,2048]{1,0:T(8,128)S(1)}) custom-call(bf16[2816,1536]{1,0:T(8,128)(2,1)} %counts.1.refs_5_.c_ref.d_ref.cl_ref, bf16[1536,2048]{1,0:T(8,128)(2,1)S(1)} %get-tuple-element.71.g_ref, bf16[2048,2176]{1,0:T(8,128)(2,1)} %copy-done, bf16[256,2048]{1,0:T(8,128)(2,1)} %get-tuple-element.83.refs_1_.own_ref), custom_call_target="tpu_custom_call" | custom-call | flops 469762048 | bytes 1572864 | tf_op jit(solution)/shard_map/grad_rows/pallas_call | solution.py:555
  181.2 2.0 back.1
  183.2 1.6 collective-permute-done.24.a_came
  187.2 1.6 collective-permute-start.21
  190.2 16.7 %grad_rows.4 = (f32[1664,2048]{1,0:T(8,128)}, f32[8,128]{1,0:T(8,128)S(1)}) custom-call(bf16[2816,1536]{1,0:T(8,128)(2,1)} %counts.1.refs_5_.c_ref.d_ref.cl_ref, bf16[1536,2048]{1,0:T(8,128)(2,1)S(1)} %get-tuple-element.71.g_ref, bf16[2048,2176]{1,0:T(8,128)(2,1)} %copy-done, ...), custom_call_target="tpu_custom_call", output_to_operand_aliasing={{0}: (3, {})} | custom-call | flops 704643072 | bytes 1572864 | tf_op jit(solution)/shard_map/grad_rows/pallas_call | solution.py:555
  206.9 5.0 %collective-permute-done.26.a_came = bf16[528,512]{1,0:T(8,128)(2,1)S(1)} collective-permute-done((bf16[528,512]{1,0:T(8,128)(2,1)S(1)}, bf16[528,512]{1,0:T(8,128)(2,1)S(1)}, u32[]{:S(2)}, u32[]{:S(2)}) %collective-permute-start.26) | collective-permute-done | bytes 540704 | tf_op jit(solution)/shard_map/ppermute | solution.py:644
  214.2 9.7 %grad_rows.5 = (f32[1664,2048]{1,0:T(8,128)}, f32[8,128]{1,0:T(8,128)}) custom-call(bf16[2816,1536]{1,0:T(8,128)(2,1)} %counts.1.refs_5_.c_ref.d_ref.cl_ref, bf16[1536,2048]{1,0:T(8,128)(2,1)S(1)} %get-tuple-element.71.g_ref, bf16[2048,2176]{1,0:T(8,128)(2,1)} %copy-done, f32[1664,2048]{1,0:T(8,128)} %get-tuple-element.102.refs_1_, ...), custom_call_target="tpu_custom_call", output_to_operand_aliasing={{0}: (3, {})} | custom-call | flops 469762048 | bytes 1572864 | tf_op jit(solution)/shard_map/grad_rows/pallas_call | solution.py:555
  224.0 12.5 %collective-permute-done.28.refs_2_ = bf16[256,2048]{1,0:T(8,128)(2,1)S(1)} collective-permute-done((bf16[256,2048]{1,0:T(8,128)(2,1)S(1)}, bf16[256,2048]{1,0:T(8,128)(2,1)S(1)}, u32[]{:S(2)}, u32[]{:S(2)}) %collective-permute-start.28) | collective-permute-done | bytes 1048608 | tf_op jit(solution)/shard_map/ppermute | solution.py:644
  236.4 3.8 %grad_lead.1 = (f32[1664,2048]{1,0:T(8,128)}, f32[8,128]{1,0:T(8,128)S(1)}) custom-call(f32[256,2048]{1,0:T(8,128)S(1)} %get-tuple-element.84._.lead_ref, bf16[256,2048]{1,0:T(8,128)(2,1)S(1)} %collective-permute-done.21.refs_0_, bf16[256,2048]{1,0:T(8,128)(2,1)S(1)} %collective-permute-done.23.refs_1_, ...), custom_call_target="tpu_custom_call", output_to_operand_aliasing={{0}: (5, {})} | custom-call | flops 134217728 | bytes 524288 | tf_op jit(solution)/shard_map/grad_lead/pallas_call | solution.py:618
  241.0 1.9 collective-permute-start.32
  (102 shorter events, 19.5 us)
Async XLA Ops:
  3.0 30.5 %collective-permute-start.7 = (bf16[256,2048]{1,0:T(8,128)(2,1)}, bf16[256,2048]{1,0:T(8,128)(2,1)S(1)}, u32[]{:S(2)}, u32[]{:S(2)}) collective-permute-start(bf16[256,2048]{1,0:T(8,128)(2,1)} %slice.30.refs_1_), channel_id=1, source_target_pairs={{2,4},{3,5},{4,2},{5,3},{10,12},{11,13},{12,10},{13,11},{18,20},{1... | collective-permute-start | bytes 3145736 | tf_op jit(solution)/shard_map/ppermute | solution.py:655
  6.7 26.8 %collective-permute-start = (bf16[256,2048]{1,0:T(8,128)(2,1)}, bf16[256,2048]{1,0:T(8,128)(2,1)}, u32[]{:S(2)}, u32[]{:S(2)}) collective-permute-start(bf16[256,2048]{1,0:T(8,128)(2,1)} %slice.30.refs_1_), channel_id=1, source_target_pairs={{0,1},{1,0},{2,3},{3,2},{4,5},{5,4},{6,7},{7,6},{8,9},{9,8},{10,11... | collective-permute-start | bytes 3145736 | tf_op jit(solution)/shard_map/ppermute | solution.py:644
  7.8 22.5 %collective-permute-start.3 = (bf16[64,2176]{1,0:T(8,128)(2,1)S(1)}, bf16[64,2176]{1,0:T(8,128)(2,1)S(1)}, u32[]{:S(2)}, u32[]{:S(2)}) collective-permute-start(bf16[64,2176]{1,0:T(8,128)(2,1)S(1)} %pad_maximum_fusion.2), channel_id=1, source_target_pairs={{0,24},{1,25},{2,26},{3,27},{4,28},{5,29},{6,30},{7,31},{8,0},{9,1... | collective-permute-start | bytes 835592 | tf_op jit(solution)/shard_map/ppermute | solution.py:644
  8.0 22.3 %collective-permute-start.2 = (bf16[64,2176]{1,0:T(8,128)(2,1)S(1)}, bf16[64,2176]{1,0:T(8,128)(2,1)S(1)}, u32[]{:S(2)}, u32[]{:S(2)}) collective-permute-start(bf16[64,2176]{1,0:T(8,128)(2,1)S(1)} %pad_maximum_fusion.2), channel_id=1, source_target_pairs={{0,16},{1,17},{2,18},{3,19},{4,20},{5,21},{6,22},{7,23},{8,24},{9,... | collective-permute-start | bytes 835592 | tf_op jit(solution)/shard_map/ppermute | solution.py:644
  10.3 23.1 %collective-permute-start.1 = (bf16[64,2176]{1,0:T(8,128)(2,1)S(1)}, bf16[64,2176]{1,0:T(8,128)(2,1)S(1)}, u32[]{:S(2)}, u32[]{:S(2)}) collective-permute-start(bf16[64,2176]{1,0:T(8,128)(2,1)S(1)} %pad_maximum_fusion.2), channel_id=1, source_target_pairs={{0,8},{1,9},{2,10},{3,11},{4,12},{5,13},{6,14},{7,15},{8,16},{9,17... | collective-permute-start | bytes 835592 | tf_op jit(solution)/shard_map/ppermute | solution.py:644
  35.2 8.4 %collective-permute-start.5 = (bf16[256,2048]{1,0:T(8,128)(2,1)}, bf16[256,2048]{1,0:T(8,128)(2,1)}, u32[]{:S(2)}, u32[]{:S(2)}) collective-permute-start(bf16[256,2048]{1,0:T(8,128)(2,1)} %get-tuple-element.58.refs_0_), channel_id=1, source_target_pairs={{0,2},{1,3},{2,0},{3,1},{4,6},{5,7},{6,4},{7,5},{8,10},{9,11},{10,... | collective-permute-start | bytes 3145736 | tf_op jit(solution)/shard_map/ppermute | solution.py:644
  35.2 8.4 %collective-permute-start.4 = (bf16[256,2048]{1,0:T(8,128)(2,1)}, bf16[256,2048]{1,0:T(8,128)(2,1)}, u32[]{:S(2)}, u32[]{:S(2)}) collective-permute-start(bf16[256,2048]{1,0:T(8,128)(2,1)} %get-tuple-element.59), channel_id=1, source_target_pairs={{0,2},{1,3},{2,0},{3,1},{4,6},{5,7},{6,4},{7,5},{8,10},{9,11},{10,... | collective-permute-start | bytes 3145736 | tf_op jit(solution)/shard_map/ppermute | solution.py:644
  36.8 28.0 %collective-permute-start.6 = (bf16[256,2176]{1,0:T(8,128)(2,1)S(1)}, bf16[256,2176]{1,0:T(8,128)(2,1)S(1)}, u32[]{:S(2)}, u32[]{:S(2)}) collective-permute-start(bf16[256,2176]{1,0:T(8,128)(2,1)S(1)} %pad_maximum_fusion.refs_0_), channel_id=1, source_target_pairs={{0,1},{1,0},{2,3},{3,2},{4,5},{5,4},{6,7},{7,6},{8,9},{9,8},{10,11... | collective-permute-start | bytes 3342344 | tf_op jit(solution)/shard_map/ppermute | solution.py:644
  38.0 26.7 %collective-permute-start.8 = (bf16[256,2048]{1,0:T(8,128)(2,1)}, bf16[256,2048]{1,0:T(8,128)(2,1)}, u32[]{:S(2)}, u32[]{:S(2)}) collective-permute-start(bf16[256,2048]{1,0:T(8,128)(2,1)} %get-tuple-element.59), channel_id=1, source_target_pairs={{0,30},{1,31},{6,8},{7,9},{8,6},{9,7},{14,16},{15,17},{16,14},{17,... | collective-permute-start | bytes 3145736 | tf_op jit(solution)/shard_map/ppermute | solution.py:655
  39.7 39.4 %collective-permute-start.9 = (bf16[256,2176]{1,0:T(8,128)(2,1)S(1)}, bf16[256,2176]{1,0:T(8,128)(2,1)S(1)}, u32[]{:S(2)}, u32[]{:S(2)}) collective-permute-start(bf16[256,2176]{1,0:T(8,128)(2,1)S(1)} %pad_maximum_fusion.refs_0_), channel_id=1, source_target_pairs={{0,4},{1,5},{2,6},{3,7},{4,0},{5,1},{6,2},{7,3},{8,12},{9,13},{10,... | collective-permute-start | bytes 3342344 | tf_op jit(solution)/shard_map/ppermute | solution.py:644
  64.9 24.6 %collective-permute-start.10 = (bf16[256,2048]{1,0:T(8,128)(2,1)S(1)}, bf16[256,2048]{1,0:T(8,128)(2,1)S(1)}, u32[]{:S(2)}, u32[]{:S(2)}) collective-permute-start(bf16[256,2048]{1,0:T(8,128)(2,1)S(1)} %broadcast_select_fusion.same_ref), channel_id=1, source_target_pairs={{0,1},{1,0},{2,3},{3,2},{4,5},{5,4},{6,7},{7,6},{8,9},{9,8},{10,11... | collective-permute-start | bytes 3145736 | tf_op jit(solution)/shard_map/ppermute | solution.py:644
  65.3 31.5 %collective-permute-start.11 = (bf16[192,2176]{1,0:T(8,128)(2,1)S(1)}, bf16[192,2176]{1,0:T(8,128)(2,1)S(1)}, u32[]{:S(2)}, u32[]{:S(2)}) collective-permute-start(bf16[192,2176]{1,0:T(8,128)(2,1)S(1)} %slice.32), channel_id=1, source_target_pairs={{0,4},{1,5},{2,6},{3,7},{4,0},{5,1},{6,2},{7,3},{8,12},{9,13},{10,... | collective-permute-start | bytes 2506760 | tf_op jit(solution)/shard_map/ppermute | solution.py:644
  66.7 31.9 %collective-permute-start.15 = (bf16[256,2176]{1,0:T(8,128)(2,1)S(1)}, bf16[256,2176]{1,0:T(8,128)(2,1)S(1)}, u32[]{:S(2)}, u32[]{:S(2)}) collective-permute-start(bf16[256,2176]{1,0:T(8,128)(2,1)S(1)} %pad_maximum_fusion.refs_0_), channel_id=1, source_target_pairs={{0,2},{1,3},{2,0},{3,1},{4,6},{5,7},{6,4},{7,5},{8,10},{9,11},{10,... | collective-permute-start | bytes 3342344 | tf_op jit(solution)/shard_map/ppermute | solution.py:644
  66.9 31.7 %collective-permute-start.16 = (bf16[256,2176]{1,0:T(8,128)(2,1)S(1)}, bf16[256,2176]{1,0:T(8,128)(2,1)S(1)}, u32[]{:S(2)}, u32[]{:S(2)}) collective-permute-start(bf16[256,2176]{1,0:T(8,128)(2,1)S(1)} %get-tuple-element.66.refs_1_), channel_id=1, source_target_pairs={{0,2},{1,3},{2,0},{3,1},{4,6},{5,7},{6,4},{7,5},{8,10},{9,11},{10,... | collective-permute-start | bytes 3342344 | tf_op jit(solution)/shard_map/ppermute | solution.py:644
  79.1 19.5 %collective-permute-start.17 = (bf16[256,2176]{1,0:T(8,128)(2,1)S(1)}, bf16[256,2176]{1,0:T(8,128)(2,1)S(1)}, u32[]{:S(2)}, u32[]{:S(2)}) collective-permute-start(bf16[256,2176]{1,0:T(8,128)(2,1)S(1)} %collective-permute-done.9.refs_2_), channel_id=1, source_target_pairs={{0,2},{1,3},{2,0},{3,1},{4,6},{5,7},{6,4},{7,5},{8,10},{9,11},{10,... | collective-permute-start | bytes 3342344 | tf_op jit(solution)/shard_map/ppermute | solution.py:644
  89.6 7.3 %collective-permute-start.12 = (bf16[64,2176]{1,0:T(8,128)(2,1)S(1)}, bf16[64,2176]{1,0:T(8,128)(2,1)S(1)}, u32[]{:S(2)}, u32[]{:S(2)}) collective-permute-start(bf16[64,2176]{1,0:T(8,128)(2,1)S(1)} %get-tuple-element.67), channel_id=1, source_target_pairs={{0,1},{1,0},{2,3},{3,2},{4,5},{5,4},{6,7},{7,6},{8,9},{9,8},{10,11... | collective-permute-start | bytes 835592 | tf_op jit(solution)/shard_map/ppermute | solution.py:644
  96.8 4.2 %collective-permute-start.13 = (bf16[192,2176]{1,0:T(8,128)(2,1)S(1)}, bf16[192,2176]{1,0:T(8,128)(2,1)S(1)}, u32[]{:S(2)}, u32[]{:S(2)}) collective-permute-start(bf16[192,2176]{1,0:T(8,128)(2,1)S(1)} %get-tuple-element.68.refs_0_), channel_id=1, source_target_pairs={{0,2},{1,3},{2,0},{3,1},{4,6},{5,7},{6,4},{7,5},{8,10},{9,11},{10,... | collective-permute-start | bytes 2506760 | tf_op jit(solution)/shard_map/ppermute | solution.py:644
  142.8 14.7 %collective-permute-start.18 = (bf16[2064,1024]{1,0:T(8,128)(2,1)}, bf16[2064,1024]{1,0:T(8,128)(2,1)S(1)}, u32[]{:S(2)}, u32[]{:S(2)}) collective-permute-start(bf16[2064,1024]{1,0:T(8,128)(2,1)} %get-tuple-element.78), channel_id=1, source_target_pairs={{0,2},{1,3},{2,0},{3,1},{4,6},{5,7},{6,4},{7,5},{8,10},{9,11},{10,... | collective-permute-start | bytes 12681224 | tf_op jit(solution)/shard_map/ppermute | solution.py:644
  143.2 13.4 %collective-permute-start.19 = (bf16[128,2048]{1,0:T(8,128)(2,1)S(1)}, bf16[128,2048]{1,0:T(8,128)(2,1)S(1)}, u32[]{:S(2)}, u32[]{:S(2)}) collective-permute-start(bf16[128,2048]{1,0:T(8,128)(2,1)S(1)} %copy-done.10), channel_id=1, source_target_pairs={{0,1},{1,0},{2,3},{3,2},{4,5},{5,4},{6,7},{7,6},{8,9},{9,8},{10,11... | collective-permute-start | bytes 1572872 | tf_op jit(solution)/shard_map/ppermute | solution.py:644
  143.2 14.3 %collective-permute-start.20 = (bf16[128,2048]{1,0:T(8,128)(2,1)S(1)}, bf16[128,2048]{1,0:T(8,128)(2,1)S(1)}, u32[]{:S(2)}, u32[]{:S(2)}) collective-permute-start(bf16[128,2048]{1,0:T(8,128)(2,1)S(1)} %copy-done.9), channel_id=1, source_target_pairs={{0,30},{1,31},{2,4},{3,5},{4,2},{5,3},{6,8},{7,9},{8,6},{9,7},{10,... | collective-permute-start | bytes 1572872 | tf_op jit(solution)/shard_map/ppermute | solution.py:655
  159.7 25.2 %collective-permute-start.24 = (bf16[1040,512]{1,0:T(8,128)(2,1)S(1)}, bf16[1040,512]{1,0:T(8,128)(2,1)S(1)}, u32[]{:S(2)}, u32[]{:S(2)}) collective-permute-start(bf16[1040,512]{1,0:T(8,128)(2,1)S(1)} %get-tuple-element.91), channel_id=1, source_target_pairs={{0,1},{1,0},{2,3},{3,2},{4,5},{5,4},{6,7},{7,6},{8,9},{9,8},{10,11... | collective-permute-start | bytes 3194888 | tf_op jit(solution)/shard_map/ppermute | solution.py:644
  161.1 24.6 %collective-permute-start.25 = (bf16[1040,512]{1,0:T(8,128)(2,1)S(1)}, bf16[1040,512]{1,0:T(8,128)(2,1)S(1)}, u32[]{:S(2)}, u32[]{:S(2)}) collective-permute-start(bf16[1040,512]{1,0:T(8,128)(2,1)S(1)} %get-tuple-element.93), channel_id=1, source_target_pairs={{0,4},{1,5},{2,6},{3,7},{4,0},{5,1},{6,2},{7,3},{8,12},{9,13},{10,... | collective-permute-start | bytes 3194888 | tf_op jit(solution)/shard_map/ppermute | solution.py:644
  170.5 10.6 %collective-permute-start.22 = (bf16[256,2048]{1,0:T(8,128)(2,1)}, bf16[256,2048]{1,0:T(8,128)(2,1)S(1)}, u32[]{:S(2)}, u32[]{:S(2)}) collective-permute-start(bf16[256,2048]{1,0:T(8,128)(2,1)} %get-tuple-element.87), channel_id=1, source_target_pairs={{0,2},{1,3},{2,0},{3,1},{4,6},{5,7},{6,4},{7,5},{8,10},{9,11},{10,... | collective-permute-start | bytes 3145736 | tf_op jit(solution)/shard_map/ppermute | solution.py:644
  186.9 25.0 %collective-permute-start.26 = (bf16[528,512]{1,0:T(8,128)(2,1)S(1)}, bf16[528,512]{1,0:T(8,128)(2,1)S(1)}, u32[]{:S(2)}, u32[]{:S(2)}) collective-permute-start(bf16[528,512]{1,0:T(8,128)(2,1)S(1)} %get-tuple-element.95), channel_id=1, source_target_pairs={{0,4},{1,5},{2,6},{3,7},{4,0},{5,1},{6,2},{7,3},{8,12},{9,13},{10,... | collective-permute-start | bytes 1622024 | tf_op jit(solution)/shard_map/ppermute | solution.py:644
  187.2 19.7 %collective-permute-start.27 = (bf16[512,512]{1,0:T(8,128)(2,1)S(1)}, bf16[512,512]{1,0:T(8,128)(2,1)S(1)}, u32[]{:S(2)}, u32[]{:S(2)}) collective-permute-start(bf16[512,512]{1,0:T(8,128)(2,1)S(1)} %get-tuple-element.97), channel_id=1, source_target_pairs={{0,1},{1,0},{2,3},{3,2},{4,5},{5,4},{6,7},{7,6},{8,9},{9,8},{10,11... | collective-permute-start | bytes 1572872 | tf_op jit(solution)/shard_map/ppermute | solution.py:644
  187.2 26.6 %collective-permute-start.21 = (bf16[256,2048]{1,0:T(8,128)(2,1)S(1)}, bf16[256,2048]{1,0:T(8,128)(2,1)S(1)}, u32[]{:S(2)}, u32[]{:S(2)}) collective-permute-start(bf16[256,2048]{1,0:T(8,128)(2,1)S(1)} %copy-done.8), channel_id=1, source_target_pairs={{0,2},{1,3},{2,0},{3,1},{4,6},{5,7},{6,4},{7,5},{8,10},{9,11},{10,... | collective-permute-start | bytes 3145736 | tf_op jit(solution)/shard_map/ppermute | solution.py:644
  188.9 35.1 %collective-permute-start.23 = (bf16[256,2048]{1,0:T(8,128)(2,1)S(1)}, bf16[256,2048]{1,0:T(8,128)(2,1)S(1)}, u32[]{:S(2)}, u32[]{:S(2)}) collective-permute-start(bf16[256,2048]{1,0:T(8,128)(2,1)S(1)} %get-tuple-element.88), channel_id=1, source_target_pairs={{0,30},{1,31},{2,4},{3,5},{4,2},{5,3},{6,8},{7,9},{8,6},{9,7},{10,... | collective-permute-start | bytes 3145736 | tf_op jit(solution)/shard_map/ppermute | solution.py:655
  212.6 23.8 %collective-permute-start.28 = (bf16[256,2048]{1,0:T(8,128)(2,1)S(1)}, bf16[256,2048]{1,0:T(8,128)(2,1)S(1)}, u32[]{:S(2)}, u32[]{:S(2)}) collective-permute-start(bf16[256,2048]{1,0:T(8,128)(2,1)S(1)} %tie.9), channel_id=1, source_target_pairs={{0,1},{1,0},{2,3},{3,2},{4,5},{5,4},{6,7},{7,6},{8,9},{9,8},{10,11... | collective-permute-start | bytes 3145736 | tf_op jit(solution)/shard_map/ppermute | solution.py:644
  212.7 27.5 %collective-permute-start.29 = (bf16[144,1024]{1,0:T(8,128)(2,1)S(1)}, bf16[144,1024]{1,0:T(8,128)(2,1)S(1)}, u32[]{:S(2)}, u32[]{:S(2)}) collective-permute-start(bf16[144,1024]{1,0:T(8,128)(2,1)S(1)} %get-tuple-element.106), channel_id=1, source_target_pairs={{0,8},{1,9},{2,10},{3,11},{4,12},{5,13},{6,14},{7,15},{8,16},{9,17... | collective-permute-start | bytes 884744 | tf_op jit(solution)/shard_map/ppermute | solution.py:644
  212.8 27.5 %collective-permute-start.30 = (bf16[144,1024]{1,0:T(8,128)(2,1)S(1)}, bf16[144,1024]{1,0:T(8,128)(2,1)S(1)}, u32[]{:S(2)}, u32[]{:S(2)}) collective-permute-start(bf16[144,1024]{1,0:T(8,128)(2,1)S(1)} %get-tuple-element.107), channel_id=1, source_target_pairs={{0,16},{1,17},{2,18},{3,19},{4,20},{5,21},{6,22},{7,23},{8,24},{9,... | collective-permute-start | bytes 884744 | tf_op jit(solution)/shard_map/ppermute | solution.py:644
  213.8 26.5 %collective-permute-start.31 = (bf16[144,1024]{1,0:T(8,128)(2,1)S(1)}, bf16[144,1024]{1,0:T(8,128)(2,1)S(1)}, u32[]{:S(2)}, u32[]{:S(2)}) collective-permute-start(bf16[144,1024]{1,0:T(8,128)(2,1)S(1)} %get-tuple-element.108), channel_id=1, source_target_pairs={{0,24},{1,25},{2,26},{3,27},{4,28},{5,29},{6,30},{7,31},{8,0},{9,1... | collective-permute-start | bytes 884744 | tf_op jit(solution)/shard_map/ppermute | solution.py:644
  241.0 3.1 %collective-permute-start.32 = (f32[72,1024]{1,0:T(8,128)S(1)}, f32[72,1024]{1,0:T(8,128)S(1)}, u32[]{:S(2)}, u32[]{:S(2)}) collective-permute-start(f32[72,1024]{1,0:T(8,128)S(1)} %get-tuple-element.111), channel_id=1, source_target_pairs={{0,2},{1,3},{2,0},{3,1},{4,6},{5,7},{6,4},{7,5},{8,10},{9,11},{10,... | collective-permute-start | bytes 884744 | tf_op jit(solution)/shard_map/ppermute | solution.py:644
  (15 other events, 162.6 us)

commit v10 on v9

--- a/solution.py
+++ b/solution.py
@@ -258,7 +258,7 @@
                 resident((8, n)),
             ],
         ),
-        out_shape=[(pltpu.VMEM if mine else pltpu.HBM)((rows, n), BF16), jax.ShapeDtypeStruct((8, n), F32)],
+        out_shape=[pltpu.VMEM((rows, n), BF16), jax.ShapeDtypeStruct((8, n), F32)],
         compiler_params=params(12),
         cost_estimate=cost(live * h * h, live * h * 4),
         name="weight_share",

time: 246 us -> 245 us (level)
  no operation moved by 1% of the time
where the time goes in v10:
time: 245 us
  Pallas kernels  144 us (59%)
  waiting for transfers between devices  60.9 us (25%)
  starting transfers between devices  29.5 us (12%)
  local copies, waits for them, and re-layouts  5.31 us (2%)
  other arithmetic  2.91 us (1%)
    ppermute x29, waiting for transfers between devices, permute(): return lax.ppermute(value, axes, [(s, b * n_wa + w) for s, (b, w) in pairs])  60 us
    pallas_call x3, Pallas kernels, grad_rows(): pl.pallas_call(functools.partial(grad_rows_kernel, low=low, tiles=tiles),...  36.4 us
    pallas_call x1, Pallas kernels, layer(): pl.pallas_call(functools.partial(layer_kernel, tiles=tiles, numbers=numbe...  32.9 us
    ppermute x29, starting transfers between devices, permute(): return lax.ppermute(value, axes, [(s, b * n_wa + w) for s, (b, w) in pairs])  22.8 us
    pallas_call x1, Pallas kernels, gather(): pl.pallas_call(functools.partial(gather_kernel, count=len(blocks)), grid=...  21.2 us
    pallas_call x1, Pallas kernels, counts(): pl.pallas_call(counts_kernel, grid=(tiles,), in_specs=[pl.BlockSpec((FANO...  16.4 us
    pallas_call x2, Pallas kernels, weight_share(): pl.pallas_call(functools.partial(weight_kernel, mine=mine), grid_spec=plt...  15.6 us
    pallas_call x1, Pallas kernels, scatter_bound(): pl.pallas_call(functools.partial(scatter_bound_kernel, count=blocks), gri...  9.39 us
  transfers between devices with their start and end apart: 33, of which 13 were waited for; matrix products, arithmetic and copies ran while one was open for 1% of the time, Pallas kernels for 41%

profile of v10, /device:TPU:11, one launch (start us, length us, event | category | flops | bytes accessed | tf_op | source)
XLA Modules:
  0.0 244.8 jit_solution(359684097383864201)
XLA Ops:
  0.7 2.4 slice.30.refs_1_
  3.0 3.7 %collective-permute-start.7 = (bf16[256,2048]{1,0:T(8,128)(2,1)}, bf16[256,2048]{1,0:T(8,128)(2,1)S(1)}, u32[]{:S(2)}, u32[]{:S(2)}) collective-permute-start(bf16[256,2048]{1,0:T(8,128)(2,1)} %slice.30.refs_1_), channel_id=1, source_target_pairs={{2,4},{3,5},{4,2},{5,3},{10,12},{11,13},{12,10},{13,11},{18,20},{1... | collective-permute-start | bytes 3145736 | tf_op jit(solution)/shard_map/ppermute | solution.py:655
  8.0 2.3 collective-permute-start.2
  10.3 2.2 collective-permute-start.1
  13.8 16.4 %counts.1.refs_5_.c_ref.d_ref.cl_ref = bf16[2816,1536]{1,0:T(8,128)(2,1)} custom-call(s32[16,1536]{1,0:T(8,128)S(1)} %fusion.2.index_ref, f32[1536,1]{1,0:T(8,128)S(1)} %broadcast_in_dim.27.refs_0_.inv_ref, s32[5]{0:T(128)S(1)} %stack.23.refs_1_.at_ref), custom_call_target="tpu_custom_call" | custom-call | bytes 4325376 | tf_op jit(solution)/shard_map/counts/pallas_call | solution.py:93
  30.3 3.2 %collective-permute-done.1.refs_2_ = bf16[64,2176]{1,0:T(8,128)(2,1)S(1)} collective-permute-done((bf16[64,2176]{1,0:T(8,128)(2,1)S(1)}, bf16[64,2176]{1,0:T(8,128)(2,1)S(1)}, u32[]{:S(2)}, u32[]{:S(2)}) %collective-permute-start.1) | collective-permute-done | bytes 278560 | tf_op jit(solution)/shard_map/ppermute | solution.py:644
  38.0 1.7 collective-permute-start.8
  39.7 3.9 %collective-permute-start.9 = (bf16[256,2176]{1,0:T(8,128)(2,1)S(1)}, bf16[256,2176]{1,0:T(8,128)(2,1)S(1)}, u32[]{:S(2)}, u32[]{:S(2)}) collective-permute-start(bf16[256,2176]{1,0:T(8,128)(2,1)S(1)} %pad_maximum_fusion.refs_0_), channel_id=1, source_target_pairs={{0,4},{1,5},{2,6},{3,7},{4,0},{5,1},{6,2},{7,3},{8,12},{9,13},{10,... | collective-permute-start | bytes 3342344 | tf_op jit(solution)/shard_map/ppermute | solution.py:644
  43.6 21.2 %gather.1.refs_3_.part_ref = f32[1536,2048]{1,0:T(8,128)} custom-call(bf16[2816,1536]{1,0:T(8,128)(2,1)} %counts.1.refs_5_.c_ref.d_ref.cl_ref, bf16[1664,2048]{1,0:T(8,128)(2,1)} %t_ref.1, bf16[256,2048]{1,0:T(8,128)(2,1)} %get-tuple-element.58.refs_0_, bf16[256,2048]{1,0:T(8,128)(2,1)} %collective-permute-done.4.refs_1_, ...), custom_call_target="tpu_custom_call" | custom-call | flops 905969664 | bytes 1179648 | tf_op jit(solution)/shard_map/gather/pallas_call | solution.py:118
  65.3 1.4 collective-permute-start.11
  67.2 11.9 %collective-permute-done.9.refs_2_ = bf16[256,2176]{1,0:T(8,128)(2,1)S(1)} collective-permute-done((bf16[256,2176]{1,0:T(8,128)(2,1)S(1)}, bf16[256,2176]{1,0:T(8,128)(2,1)S(1)}, u32[]{:S(2)}, u32[]{:S(2)}) %collective-permute-start.9) | collective-permute-done | bytes 1114144 | tf_op jit(solution)/shard_map/ppermute | solution.py:644
  79.2 10.3 %collective-permute-done.10.refs_1_ = bf16[256,2048]{1,0:T(8,128)(2,1)S(1)} collective-permute-done((bf16[256,2048]{1,0:T(8,128)(2,1)S(1)}, bf16[256,2048]{1,0:T(8,128)(2,1)S(1)}, u32[]{:S(2)}, u32[]{:S(2)}) %collective-permute-start.10) | collective-permute-done | bytes 1048608 | tf_op jit(solution)/shard_map/ppermute | solution.py:644
  89.6 7.3 %collective-permute-done.11.refs_0_ = bf16[192,2176]{1,0:T(8,128)(2,1)S(1)} collective-permute-done((bf16[192,2176]{1,0:T(8,128)(2,1)S(1)}, bf16[192,2176]{1,0:T(8,128)(2,1)S(1)}, u32[]{:S(2)}, u32[]{:S(2)}) %collective-permute-start.11) | collective-permute-done | bytes 835616 | tf_op jit(solution)/shard_map/ppermute | solution.py:644
  96.8 1.8 collective-permute-start.13
  98.7 1.9 place.1.refs_4_
  101.0 32.9 %layer.1 = (f32[1664,2048]{1,0:T(8,128)}, bf16[1536,2048]{1,0:T(8,128)(2,1)S(1)}, bf16[1536,2048]{1,0:T(8,128)(2,1)S(1)}, bf16[1536,2048]{1,0:T(8,128)(2,1)S(1)}...) custom-call(s32[5]{0:T(128)S(1)} %stack.23.refs_1_.at_ref, ...), custom_call_target="tpu_custom_call", output_to_operand_aliasing={{7}: (13, {})} | custom-call | flops 1207959552 | bytes 2359296 | tf_op jit(solution)/shard_map/layer/pallas_call | solution.py:277
  134.0 7.9 %weight_share.2 = (bf16[2064,1024]{1,0:T(8,128)(2,1)S(1)}, f32[8,1024]{1,0:T(8,128)S(1)}) custom-call(s32[5]{0:T(128)S(1)} %stack.23.refs_1_.at_ref, bf16[1536,2048]{1,0:T(8,128)(2,1)S(1)} %get-tuple-element.73.m_all, bf16[1536,2048]{1,0:T(8,128)(2,1)S(1)} %get-tuple-element.74.gl_all, f32[8,2048]{1,0:T(8,128)S(1)} %get-tuple-element.75.gb), custom_call_target="tpu_custom_call" | custom-call | flops 402653184 | bytes 786432 | tf_op jit(solution)/shard_map/weight_share/pallas_call | solution.py:250
  142.4 7.7 %weight_share.3 = (bf16[2048,1024]{1,0:T(8,128)(2,1)S(1)}, f32[8,1024]{1,0:T(8,128)S(1)}) custom-call(s32[5]{0:T(128)S(1)} %stack.23.refs_1_.at_ref, bf16[1536,2048]{1,0:T(8,128)(2,1)S(1)} %get-tuple-element.73.m_all, bf16[1536,2048]{1,0:T(8,128)(2,1)S(1)} %get-tuple-element.74.gl_all, f32[8,2048]{1,0:T(8,128)S(1)} %get-tuple-element.75.gb, ...), custom_call_target="tpu_custom_call" | custom-call | flops 402653184 | bytes 786432 | tf_op jit(solution)/shard_map/weight_share/pallas_call | solution.py:250
  150.1 5.6 %collective-permute-done.19.low_ref = bf16[128,2048]{1,0:T(8,128)(2,1)S(1)} collective-permute-done((bf16[128,2048]{1,0:T(8,128)(2,1)S(1)}, bf16[128,2048]{1,0:T(8,128)(2,1)S(1)}, u32[]{:S(2)}, u32[]{:S(2)}) %collective-permute-start.19) | collective-permute-done | bytes 524320 | tf_op jit(solution)/shard_map/ppermute | solution.py:644
  156.6 2.2 share.1
  158.8 1.5 collective-permute-start.24
  160.3 9.4 %scatter_bound.1 = (bf16[256,2048]{1,0:T(8,128)(2,1)}, bf16[256,2048]{1,0:T(8,128)(2,1)}, bf16[256,2048]{1,0:T(8,128)(2,1)}, bf16[256,2048]{1,0:T(8,128)(2,1)}) custom-call(bf16[2816,1536]{1,0:T(8,128)(2,1)} %counts.1.refs_5_.c_ref.d_ref.cl_ref, bf16[1536,2048]{1,0:T(8,128)(2,1)S(1)} %get-tuple-element.71.g_ref, f32[8,1024]{1,0:T(8,128)S(1)} %get-tuple-element.82.refs_0_.gb_ref), custom_call_target="tpu_custom_call" | custom-call | flops 402653184 | bytes 786432 | tf_op jit(solution)/shard_map/scatter_bound/pallas_call | solution.py:509
  170.2 10.1 %grad_rows.3 = (f32[1664,2048]{1,0:T(8,128)}, f32[256,2048]{1,0:T(8,128)S(1)}) custom-call(bf16[2816,1536]{1,0:T(8,128)(2,1)} %counts.1.refs_5_.c_ref.d_ref.cl_ref, bf16[1536,2048]{1,0:T(8,128)(2,1)S(1)} %get-tuple-element.71.g_ref, bf16[2048,2176]{1,0:T(8,128)(2,1)} %copy-done, bf16[256,2048]{1,0:T(8,128)(2,1)} %get-tuple-element.83.refs_1_.own_ref), custom_call_target="tpu_custom_call" | custom-call | flops 469762048 | bytes 1572864 | tf_op jit(solution)/shard_map/grad_rows/pallas_call | solution.py:555
  180.3 2.0 back.1
  182.3 1.6 collective-permute-done.24.a_came
  186.4 1.6 collective-permute-start.21
  189.3 16.7 %grad_rows.4 = (f32[1664,2048]{1,0:T(8,128)}, f32[8,128]{1,0:T(8,128)S(1)}) custom-call(bf16[2816,1536]{1,0:T(8,128)(2,1)} %counts.1.refs_5_.c_ref.d_ref.cl_ref, bf16[1536,2048]{1,0:T(8,128)(2,1)S(1)} %get-tuple-element.71.g_ref, bf16[2048,2176]{1,0:T(8,128)(2,1)} %copy-done, ...), custom_call_target="tpu_custom_call", output_to_operand_aliasing={{0}: (3, {})} | custom-call | flops 704643072 | bytes 1572864 | tf_op jit(solution)/shard_map/grad_rows/pallas_call | solution.py:555
  206.0 5.0 %collective-permute-done.26.a_came = bf16[528,512]{1,0:T(8,128)(2,1)S(1)} collective-permute-done((bf16[528,512]{1,0:T(8,128)(2,1)S(1)}, bf16[528,512]{1,0:T(8,128)(2,1)S(1)}, u32[]{:S(2)}, u32[]{:S(2)}) %collective-permute-start.26) | collective-permute-done | bytes 540704 | tf_op jit(solution)/shard_map/ppermute | solution.py:644
  213.4 9.7 %grad_rows.5 = (f32[1664,2048]{1,0:T(8,128)}, f32[8,128]{1,0:T(8,128)}) custom-call(bf16[2816,1536]{1,0:T(8,128)(2,1)} %counts.1.refs_5_.c_ref.d_ref.cl_ref, bf16[1536,2048]{1,0:T(8,128)(2,1)S(1)} %get-tuple-element.71.g_ref, bf16[2048,2176]{1,0:T(8,128)(2,1)} %copy-done, f32[1664,2048]{1,0:T(8,128)} %get-tuple-element.102.refs_1_, ...), custom_call_target="tpu_custom_call", output_to_operand_aliasing={{0}: (3, {})} | custom-call | flops 469762048 | bytes 1572864 | tf_op jit(solution)/shard_map/grad_rows/pallas_call | solution.py:555
  223.1 12.5 %collective-permute-done.28.refs_2_ = bf16[256,2048]{1,0:T(8,128)(2,1)S(1)} collective-permute-done((bf16[256,2048]{1,0:T(8,128)(2,1)S(1)}, bf16[256,2048]{1,0:T(8,128)(2,1)S(1)}, u32[]{:S(2)}, u32[]{:S(2)}) %collective-permute-start.28) | collective-permute-done | bytes 1048608 | tf_op jit(solution)/shard_map/ppermute | solution.py:644
  235.5 3.8 %grad_lead.1 = (f32[1664,2048]{1,0:T(8,128)}, f32[8,128]{1,0:T(8,128)S(1)}) custom-call(f32[256,2048]{1,0:T(8,128)S(1)} %get-tuple-element.84._.lead_ref, bf16[256,2048]{1,0:T(8,128)(2,1)S(1)} %collective-permute-done.21.refs_0_, bf16[256,2048]{1,0:T(8,128)(2,1)S(1)} %collective-permute-done.23.refs_1_, ...), custom_call_target="tpu_custom_call", output_to_operand_aliasing={{0}: (5, {})} | custom-call | flops 134217728 | bytes 524288 | tf_op jit(solution)/shard_map/grad_lead/pallas_call | solution.py:618
  240.1 1.9 collective-permute-start.32
  (102 shorter events, 19.6 us)
Async XLA Ops:
  3.0 30.5 %collective-permute-start.7 = (bf16[256,2048]{1,0:T(8,128)(2,1)}, bf16[256,2048]{1,0:T(8,128)(2,1)S(1)}, u32[]{:S(2)}, u32[]{:S(2)}) collective-permute-start(bf16[256,2048]{1,0:T(8,128)(2,1)} %slice.30.refs_1_), channel_id=1, source_target_pairs={{2,4},{3,5},{4,2},{5,3},{10,12},{11,13},{12,10},{13,11},{18,20},{1... | collective-permute-start | bytes 3145736 | tf_op jit(solution)/shard_map/ppermute | solution.py:655
  6.7 26.8 %collective-permute-start = (bf16[256,2048]{1,0:T(8,128)(2,1)}, bf16[256,2048]{1,0:T(8,128)(2,1)}, u32[]{:S(2)}, u32[]{:S(2)}) collective-permute-start(bf16[256,2048]{1,0:T(8,128)(2,1)} %slice.30.refs_1_), channel_id=1, source_target_pairs={{0,1},{1,0},{2,3},{3,2},{4,5},{5,4},{6,7},{7,6},{8,9},{9,8},{10,11... | collective-permute-start | bytes 3145736 | tf_op jit(solution)/shard_map/ppermute | solution.py:644
  7.8 22.5 %collective-permute-start.3 = (bf16[64,2176]{1,0:T(8,128)(2,1)S(1)}, bf16[64,2176]{1,0:T(8,128)(2,1)S(1)}, u32[]{:S(2)}, u32[]{:S(2)}) collective-permute-start(bf16[64,2176]{1,0:T(8,128)(2,1)S(1)} %pad_maximum_fusion.2), channel_id=1, source_target_pairs={{0,24},{1,25},{2,26},{3,27},{4,28},{5,29},{6,30},{7,31},{8,0},{9,1... | collective-permute-start | bytes 835592 | tf_op jit(solution)/shard_map/ppermute | solution.py:644
  8.0 22.3 %collective-permute-start.2 = (bf16[64,2176]{1,0:T(8,128)(2,1)S(1)}, bf16[64,2176]{1,0:T(8,128)(2,1)S(1)}, u32[]{:S(2)}, u32[]{:S(2)}) collective-permute-start(bf16[64,2176]{1,0:T(8,128)(2,1)S(1)} %pad_maximum_fusion.2), channel_id=1, source_target_pairs={{0,16},{1,17},{2,18},{3,19},{4,20},{5,21},{6,22},{7,23},{8,24},{9,... | collective-permute-start | bytes 835592 | tf_op jit(solution)/shard_map/ppermute | solution.py:644
  10.3 23.1 %collective-permute-start.1 = (bf16[64,2176]{1,0:T(8,128)(2,1)S(1)}, bf16[64,2176]{1,0:T(8,128)(2,1)S(1)}, u32[]{:S(2)}, u32[]{:S(2)}) collective-permute-start(bf16[64,2176]{1,0:T(8,128)(2,1)S(1)} %pad_maximum_fusion.2), channel_id=1, source_target_pairs={{0,8},{1,9},{2,10},{3,11},{4,12},{5,13},{6,14},{7,15},{8,16},{9,17... | collective-permute-start | bytes 835592 | tf_op jit(solution)/shard_map/ppermute | solution.py:644
  35.2 8.4 %collective-permute-start.5 = (bf16[256,2048]{1,0:T(8,128)(2,1)}, bf16[256,2048]{1,0:T(8,128)(2,1)}, u32[]{:S(2)}, u32[]{:S(2)}) collective-permute-start(bf16[256,2048]{1,0:T(8,128)(2,1)} %get-tuple-element.58.refs_0_), channel_id=1, source_target_pairs={{0,2},{1,3},{2,0},{3,1},{4,6},{5,7},{6,4},{7,5},{8,10},{9,11},{10,... | collective-permute-start | bytes 3145736 | tf_op jit(solution)/shard_map/ppermute | solution.py:644
  35.2 8.4 %collective-permute-start.4 = (bf16[256,2048]{1,0:T(8,128)(2,1)}, bf16[256,2048]{1,0:T(8,128)(2,1)}, u32[]{:S(2)}, u32[]{:S(2)}) collective-permute-start(bf16[256,2048]{1,0:T(8,128)(2,1)} %get-tuple-element.59), channel_id=1, source_target_pairs={{0,2},{1,3},{2,0},{3,1},{4,6},{5,7},{6,4},{7,5},{8,10},{9,11},{10,... | collective-permute-start | bytes 3145736 | tf_op jit(solution)/shard_map/ppermute | solution.py:644
  36.8 28.0 %collective-permute-start.6 = (bf16[256,2176]{1,0:T(8,128)(2,1)S(1)}, bf16[256,2176]{1,0:T(8,128)(2,1)S(1)}, u32[]{:S(2)}, u32[]{:S(2)}) collective-permute-start(bf16[256,2176]{1,0:T(8,128)(2,1)S(1)} %pad_maximum_fusion.refs_0_), channel_id=1, source_target_pairs={{0,1},{1,0},{2,3},{3,2},{4,5},{5,4},{6,7},{7,6},{8,9},{9,8},{10,11... | collective-permute-start | bytes 3342344 | tf_op jit(solution)/shard_map/ppermute | solution.py:644
  38.0 26.7 %collective-permute-start.8 = (bf16[256,2048]{1,0:T(8,128)(2,1)}, bf16[256,2048]{1,0:T(8,128)(2,1)}, u32[]{:S(2)}, u32[]{:S(2)}) collective-permute-start(bf16[256,2048]{1,0:T(8,128)(2,1)} %get-tuple-element.59), channel_id=1, source_target_pairs={{0,30},{1,31},{6,8},{7,9},{8,6},{9,7},{14,16},{15,17},{16,14},{17,... | collective-permute-start | bytes 3145736 | tf_op jit(solution)/shard_map/ppermute | solution.py:655
  39.7 39.4 %collective-permute-start.9 = (bf16[256,2176]{1,0:T(8,128)(2,1)S(1)}, bf16[256,2176]{1,0:T(8,128)(2,1)S(1)}, u32[]{:S(2)}, u32[]{:S(2)}) collective-permute-start(bf16[256,2176]{1,0:T(8,128)(2,1)S(1)} %pad_maximum_fusion.refs_0_), channel_id=1, source_target_pairs={{0,4},{1,5},{2,6},{3,7},{4,0},{5,1},{6,2},{7,3},{8,12},{9,13},{10,... | collective-permute-start | bytes 3342344 | tf_op jit(solution)/shard_map/ppermute | solution.py:644
  64.9 24.6 %collective-permute-start.10 = (bf16[256,2048]{1,0:T(8,128)(2,1)S(1)}, bf16[256,2048]{1,0:T(8,128)(2,1)S(1)}, u32[]{:S(2)}, u32[]{:S(2)}) collective-permute-start(bf16[256,2048]{1,0:T(8,128)(2,1)S(1)} %broadcast_select_fusion.same_ref), channel_id=1, source_target_pairs={{0,1},{1,0},{2,3},{3,2},{4,5},{5,4},{6,7},{7,6},{8,9},{9,8},{10,11... | collective-permute-start | bytes 3145736 | tf_op jit(solution)/shard_map/ppermute | solution.py:644
  65.3 31.5 %collective-permute-start.11 = (bf16[192,2176]{1,0:T(8,128)(2,1)S(1)}, bf16[192,2176]{1,0:T(8,128)(2,1)S(1)}, u32[]{:S(2)}, u32[]{:S(2)}) collective-permute-start(bf16[192,2176]{1,0:T(8,128)(2,1)S(1)} %slice.32), channel_id=1, source_target_pairs={{0,4},{1,5},{2,6},{3,7},{4,0},{5,1},{6,2},{7,3},{8,12},{9,13},{10,... | collective-permute-start | bytes 2506760 | tf_op jit(solution)/shard_map/ppermute | solution.py:644
  66.7 31.9 %collective-permute-start.15 = (bf16[256,2176]{1,0:T(8,128)(2,1)S(1)}, bf16[256,2176]{1,0:T(8,128)(2,1)S(1)}, u32[]{:S(2)}, u32[]{:S(2)}) collective-permute-start(bf16[256,2176]{1,0:T(8,128)(2,1)S(1)} %pad_maximum_fusion.refs_0_), channel_id=1, source_target_pairs={{0,2},{1,3},{2,0},{3,1},{4,6},{5,7},{6,4},{7,5},{8,10},{9,11},{10,... | collective-permute-start | bytes 3342344 | tf_op jit(solution)/shard_map/ppermute | solution.py:644
  66.9 31.7 %collective-permute-start.16 = (bf16[256,2176]{1,0:T(8,128)(2,1)S(1)}, bf16[256,2176]{1,0:T(8,128)(2,1)S(1)}, u32[]{:S(2)}, u32[]{:S(2)}) collective-permute-start(bf16[256,2176]{1,0:T(8,128)(2,1)S(1)} %get-tuple-element.66.refs_1_), channel_id=1, source_target_pairs={{0,2},{1,3},{2,0},{3,1},{4,6},{5,7},{6,4},{7,5},{8,10},{9,11},{10,... | collective-permute-start | bytes 3342344 | tf_op jit(solution)/shard_map/ppermute | solution.py:644
  79.1 19.5 %collective-permute-start.17 = (bf16[256,2176]{1,0:T(8,128)(2,1)S(1)}, bf16[256,2176]{1,0:T(8,128)(2,1)S(1)}, u32[]{:S(2)}, u32[]{:S(2)}) collective-permute-start(bf16[256,2176]{1,0:T(8,128)(2,1)S(1)} %collective-permute-done.9.refs_2_), channel_id=1, source_target_pairs={{0,2},{1,3},{2,0},{3,1},{4,6},{5,7},{6,4},{7,5},{8,10},{9,11},{10,... | collective-permute-start | bytes 3342344 | tf_op jit(solution)/shard_map/ppermute | solution.py:644
  89.6 7.3 %collective-permute-start.12 = (bf16[64,2176]{1,0:T(8,128)(2,1)S(1)}, bf16[64,2176]{1,0:T(8,128)(2,1)S(1)}, u32[]{:S(2)}, u32[]{:S(2)}) collective-permute-start(bf16[64,2176]{1,0:T(8,128)(2,1)S(1)} %get-tuple-element.67), channel_id=1, source_target_pairs={{0,1},{1,0},{2,3},{3,2},{4,5},{5,4},{6,7},{7,6},{8,9},{9,8},{10,11... | collective-permute-start | bytes 835592 | tf_op jit(solution)/shard_map/ppermute | solution.py:644
  96.8 4.2 %collective-permute-start.13 = (bf16[192,2176]{1,0:T(8,128)(2,1)S(1)}, bf16[192,2176]{1,0:T(8,128)(2,1)S(1)}, u32[]{:S(2)}, u32[]{:S(2)}) collective-permute-start(bf16[192,2176]{1,0:T(8,128)(2,1)S(1)} %get-tuple-element.68.refs_0_), channel_id=1, source_target_pairs={{0,2},{1,3},{2,0},{3,1},{4,6},{5,7},{6,4},{7,5},{8,10},{9,11},{10,... | collective-permute-start | bytes 2506760 | tf_op jit(solution)/shard_map/ppermute | solution.py:644
  141.8 14.7 %collective-permute-start.18 = (bf16[2064,1024]{1,0:T(8,128)(2,1)S(1)}, bf16[2064,1024]{1,0:T(8,128)(2,1)S(1)}, u32[]{:S(2)}, u32[]{:S(2)}) collective-permute-start(bf16[2064,1024]{1,0:T(8,128)(2,1)S(1)} %get-tuple-element.78), channel_id=1, source_target_pairs={{0,2},{1,3},{2,0},{3,1},{4,6},{5,7},{6,4},{7,5},{8,10},{9,11},{10,... | collective-permute-start | bytes 12681224 | tf_op jit(solution)/shard_map/ppermute | solution.py:644
  142.3 13.4 %collective-permute-start.19 = (bf16[128,2048]{1,0:T(8,128)(2,1)S(1)}, bf16[128,2048]{1,0:T(8,128)(2,1)S(1)}, u32[]{:S(2)}, u32[]{:S(2)}) collective-permute-start(bf16[128,2048]{1,0:T(8,128)(2,1)S(1)} %copy-done.10), channel_id=1, source_target_pairs={{0,1},{1,0},{2,3},{3,2},{4,5},{5,4},{6,7},{7,6},{8,9},{9,8},{10,11... | collective-permute-start | bytes 1572872 | tf_op jit(solution)/shard_map/ppermute | solution.py:644
  142.3 14.3 %collective-permute-start.20 = (bf16[128,2048]{1,0:T(8,128)(2,1)S(1)}, bf16[128,2048]{1,0:T(8,128)(2,1)S(1)}, u32[]{:S(2)}, u32[]{:S(2)}) collective-permute-start(bf16[128,2048]{1,0:T(8,128)(2,1)S(1)} %copy-done.9), channel_id=1, source_target_pairs={{0,30},{1,31},{2,4},{3,5},{4,2},{5,3},{6,8},{7,9},{8,6},{9,7},{10,... | collective-permute-start | bytes 1572872 | tf_op jit(solution)/shard_map/ppermute | solution.py:655
  158.8 25.2 %collective-permute-start.24 = (bf16[1040,512]{1,0:T(8,128)(2,1)S(1)}, bf16[1040,512]{1,0:T(8,128)(2,1)S(1)}, u32[]{:S(2)}, u32[]{:S(2)}) collective-permute-start(bf16[1040,512]{1,0:T(8,128)(2,1)S(1)} %get-tuple-element.91), channel_id=1, source_target_pairs={{0,1},{1,0},{2,3},{3,2},{4,5},{5,4},{6,7},{7,6},{8,9},{9,8},{10,11... | collective-permute-start | bytes 3194888 | tf_op jit(solution)/shard_map/ppermute | solution.py:644
  160.3 24.6 %collective-permute-start.25 = (bf16[1040,512]{1,0:T(8,128)(2,1)S(1)}, bf16[1040,512]{1,0:T(8,128)(2,1)S(1)}, u32[]{:S(2)}, u32[]{:S(2)}) collective-permute-start(bf16[1040,512]{1,0:T(8,128)(2,1)S(1)} %get-tuple-element.93), channel_id=1, source_target_pairs={{0,4},{1,5},{2,6},{3,7},{4,0},{5,1},{6,2},{7,3},{8,12},{9,13},{10,... | collective-permute-start | bytes 3194888 | tf_op jit(solution)/shard_map/ppermute | solution.py:644
  169.7 10.6 %collective-permute-start.22 = (bf16[256,2048]{1,0:T(8,128)(2,1)}, bf16[256,2048]{1,0:T(8,128)(2,1)S(1)}, u32[]{:S(2)}, u32[]{:S(2)}) collective-permute-start(bf16[256,2048]{1,0:T(8,128)(2,1)} %get-tuple-element.87), channel_id=1, source_target_pairs={{0,2},{1,3},{2,0},{3,1},{4,6},{5,7},{6,4},{7,5},{8,10},{9,11},{10,... | collective-permute-start | bytes 3145736 | tf_op jit(solution)/shard_map/ppermute | solution.py:644
  186.0 25.0 %collective-permute-start.26 = (bf16[528,512]{1,0:T(8,128)(2,1)S(1)}, bf16[528,512]{1,0:T(8,128)(2,1)S(1)}, u32[]{:S(2)}, u32[]{:S(2)}) collective-permute-start(bf16[528,512]{1,0:T(8,128)(2,1)S(1)} %get-tuple-element.95), channel_id=1, source_target_pairs={{0,4},{1,5},{2,6},{3,7},{4,0},{5,1},{6,2},{7,3},{8,12},{9,13},{10,... | collective-permute-start | bytes 1622024 | tf_op jit(solution)/shard_map/ppermute | solution.py:644
  186.3 19.7 %collective-permute-start.27 = (bf16[512,512]{1,0:T(8,128)(2,1)S(1)}, bf16[512,512]{1,0:T(8,128)(2,1)S(1)}, u32[]{:S(2)}, u32[]{:S(2)}) collective-permute-start(bf16[512,512]{1,0:T(8,128)(2,1)S(1)} %get-tuple-element.97), channel_id=1, source_target_pairs={{0,1},{1,0},{2,3},{3,2},{4,5},{5,4},{6,7},{7,6},{8,9},{9,8},{10,11... | collective-permute-start | bytes 1572872 | tf_op jit(solution)/shard_map/ppermute | solution.py:644
  186.4 26.6 %collective-permute-start.21 = (bf16[256,2048]{1,0:T(8,128)(2,1)S(1)}, bf16[256,2048]{1,0:T(8,128)(2,1)S(1)}, u32[]{:S(2)}, u32[]{:S(2)}) collective-permute-start(bf16[256,2048]{1,0:T(8,128)(2,1)S(1)} %copy-done.8), channel_id=1, source_target_pairs={{0,2},{1,3},{2,0},{3,1},{4,6},{5,7},{6,4},{7,5},{8,10},{9,11},{10,... | collective-permute-start | bytes 3145736 | tf_op jit(solution)/shard_map/ppermute | solution.py:644
  188.0 35.1 %collective-permute-start.23 = (bf16[256,2048]{1,0:T(8,128)(2,1)S(1)}, bf16[256,2048]{1,0:T(8,128)(2,1)S(1)}, u32[]{:S(2)}, u32[]{:S(2)}) collective-permute-start(bf16[256,2048]{1,0:T(8,128)(2,1)S(1)} %get-tuple-element.88), channel_id=1, source_target_pairs={{0,30},{1,31},{2,4},{3,5},{4,2},{5,3},{6,8},{7,9},{8,6},{9,7},{10,... | collective-permute-start | bytes 3145736 | tf_op jit(solution)/shard_map/ppermute | solution.py:655
  211.8 23.8 %collective-permute-start.28 = (bf16[256,2048]{1,0:T(8,128)(2,1)S(1)}, bf16[256,2048]{1,0:T(8,128)(2,1)S(1)}, u32[]{:S(2)}, u32[]{:S(2)}) collective-permute-start(bf16[256,2048]{1,0:T(8,128)(2,1)S(1)} %tie.9), channel_id=1, source_target_pairs={{0,1},{1,0},{2,3},{3,2},{4,5},{5,4},{6,7},{7,6},{8,9},{9,8},{10,11... | collective-permute-start | bytes 3145736 | tf_op jit(solution)/shard_map/ppermute | solution.py:644
  211.8 27.5 %collective-permute-start.29 = (bf16[144,1024]{1,0:T(8,128)(2,1)S(1)}, bf16[144,1024]{1,0:T(8,128)(2,1)S(1)}, u32[]{:S(2)}, u32[]{:S(2)}) collective-permute-start(bf16[144,1024]{1,0:T(8,128)(2,1)S(1)} %get-tuple-element.106), channel_id=1, source_target_pairs={{0,8},{1,9},{2,10},{3,11},{4,12},{5,13},{6,14},{7,15},{8,16},{9,17... | collective-permute-start | bytes 884744 | tf_op jit(solution)/shard_map/ppermute | solution.py:644
  211.9 27.5 %collective-permute-start.30 = (bf16[144,1024]{1,0:T(8,128)(2,1)S(1)}, bf16[144,1024]{1,0:T(8,128)(2,1)S(1)}, u32[]{:S(2)}, u32[]{:S(2)}) collective-permute-start(bf16[144,1024]{1,0:T(8,128)(2,1)S(1)} %get-tuple-element.107), channel_id=1, source_target_pairs={{0,16},{1,17},{2,18},{3,19},{4,20},{5,21},{6,22},{7,23},{8,24},{9,... | collective-permute-start | bytes 884744 | tf_op jit(solution)/shard_map/ppermute | solution.py:644
  212.9 26.5 %collective-permute-start.31 = (bf16[144,1024]{1,0:T(8,128)(2,1)S(1)}, bf16[144,1024]{1,0:T(8,128)(2,1)S(1)}, u32[]{:S(2)}, u32[]{:S(2)}) collective-permute-start(bf16[144,1024]{1,0:T(8,128)(2,1)S(1)} %get-tuple-element.108), channel_id=1, source_target_pairs={{0,24},{1,25},{2,26},{3,27},{4,28},{5,29},{6,30},{7,31},{8,0},{9,1... | collective-permute-start | bytes 884744 | tf_op jit(solution)/shard_map/ppermute | solution.py:644
  240.1 3.1 %collective-permute-start.32 = (f32[72,1024]{1,0:T(8,128)S(1)}, f32[72,1024]{1,0:T(8,128)S(1)}, u32[]{:S(2)}, u32[]{:S(2)}) collective-permute-start(f32[72,1024]{1,0:T(8,128)S(1)} %get-tuple-element.111), channel_id=1, source_target_pairs={{0,2},{1,3},{2,0},{3,1},{4,6},{5,7},{6,4},{7,5},{8,10},{9,11},{10,... | collective-permute-start | bytes 884744 | tf_op jit(solution)/shard_map/ppermute | solution.py:644
  (15 other events, 159.8 us)
